TPU v7x, 32 devices: a whole 2x2x4 slice. The times are simulated.
32 devices in a mesh: grp: 8 (over z, y), tok: 4 (over x, core).
Axes of the slice: x: 2, y: 2, z: 4, core: 2. Of those that a mesh axis runs over, the one named last changes fastest.
Arguments:
- queries: bfloat16 [4096, 5120], P(('grp', 'tok')), may hold values from -6 to 6
- rotated_keys_values: bfloat16 [4096, 2048], P(('grp', 'tok')), may hold values from -6 to 6
- prompt_window_index: int32 [8, 512], P('grp', 'tok'), may hold values from 0 to 1, never falling along the last dimension, each value on 1 to 384 neighbouring positions
- residual: bfloat16 [4096, 5120], P(('grp', 'tok')), may hold values from -8 to 8
- ffn_gain: float32 [5120], replicated, may hold values from 0.1 to 1.9
- gate_weight: bfloat16 [5120, 8192], P(None, 'grp'), may hold values from -0.078125 to 0.078125
- up_weight: bfloat16 [5120, 8192], P(None, 'grp'), may hold values from -0.078125 to 0.078125
- paged_cache: bfloat16 [512, 16, 2048], P(('grp', 'tok')), may hold values from -6 to 6
- page_table: int32 [8, 64], P('grp'), may hold values from 0 to 63, each once within a row
Outputs:
- attended: bfloat16 [4096, 5120], P(('grp', 'tok'))
- hidden: bfloat16 [4096, 8192], P(('grp', 'tok'))
- cache_out: bfloat16 [512, 16, 2048], P(('grp', 'tok'))
All inputs are finite; a program needn't handle non-finite values.
Results may differ from a plain program's by a relative error of at most 0.012.
Values may be sent and summed in bfloat16 or wider, within the bound.
No kernel may reach another device: no remote copies, remote signals or barrier semaphores. Data moves between devices by JAX's collectives and lax.ppermute only.
A program may use at most 128 MiB of HBM per device.

v0:
```python
import math

import jax
import jax.numpy as jnp
from jax import lax
from jax.sharding import PartitionSpec as P

QUERY_HEADS = 40
KEY_VALUE_HEADS = 8
HEAD_SIZE = 128
PAGE_TOKENS = 16


MASK_FILLER = -1e30


def on_device(
    queries,
    rotated_keys_values,
    prompt_window_index,
    residual,
    ffn_gain,
    gate_weight,
    up_weight,
    paged_cache,
    page_table,
):
    count_of_rows = queries.shape[0]
    kv_width = rotated_keys_values.shape[1]
    group_split = QUERY_HEADS // KEY_VALUE_HEADS
    slot_count = paged_cache.shape[0]
    tok_index = lax.axis_index("tok")
    first_row = tok_index * count_of_rows
    grouped_rows = queries.reshape(count_of_rows, KEY_VALUE_HEADS, group_split, HEAD_SIZE)
    own_segment = prompt_window_index[0]
    own_place = first_row + jnp.arange(count_of_rows)
    slot_table = page_table[0]
    score_scale = 1.0 / math.sqrt(HEAD_SIZE)
    initial = (
        jnp.full((count_of_rows, KEY_VALUE_HEADS, group_split), MASK_FILLER, jnp.float32),
        jnp.zeros((count_of_rows, KEY_VALUE_HEADS, group_split), jnp.float32),
        jnp.zeros((count_of_rows, KEY_VALUE_HEADS, group_split, HEAD_SIZE), jnp.float32),
        paged_cache,
    )
    key_value_portion = lax.all_gather(rotated_keys_values, "tok", axis=0, tiled=True)
    seg_piece = lax.all_gather(own_segment, "tok", axis=0, tiled=True)
    count_of_keys = key_value_portion.shape[0]
    rows_of_keys = key_value_portion[:, : KEY_VALUE_HEADS * HEAD_SIZE].reshape(
        count_of_keys, KEY_VALUE_HEADS, HEAD_SIZE
    )
    rows_of_values = key_value_portion[:, KEY_VALUE_HEADS * HEAD_SIZE :].reshape(
        count_of_keys, KEY_VALUE_HEADS, HEAD_SIZE
    )
    key_place = jnp.arange(count_of_keys)
    live_mask = (seg_piece[None, :] == own_segment[:, None]) & (
        key_place[None, :] <= own_place[:, None]
    )
    running = (initial[0], initial[1], initial[2])
    run_max, run_sum, partial_value = running
    scores = (
        jnp.einsum("qgrd,kgd->qgrk", grouped_rows, rows_of_keys, preferred_element_type=jnp.float32)
        * score_scale
    )
    scores = jnp.where(live_mask[:, None, None, :], scores, MASK_FILLER)
    new_max = jnp.maximum(run_max, jnp.max(scores, axis=-1))
    weights = jnp.where(live_mask[:, None, None, :], jnp.exp(scores - new_max[..., None]), 0.0)
    run_sum = jnp.sum(weights, axis=-1)
    partial_value = jnp.einsum(
        "qgrk,kgd->qgrd",
        weights.astype(jnp.bfloat16),
        rows_of_values,
        preferred_element_type=jnp.float32,
    )
    running = (new_max, run_sum, partial_value)
    page_count = count_of_keys // PAGE_TOKENS
    targets = (
        lax.dynamic_slice_in_dim(slot_table, jnp.int32(0) // PAGE_TOKENS, page_count)
        - tok_index * slot_count
    )
    onehot = targets[None, :] == jnp.arange(slot_count)[:, None]
    placed = jnp.dot(
        onehot.astype(jnp.bfloat16),
        key_value_portion.reshape(page_count, PAGE_TOKENS * kv_width),
        preferred_element_type=jnp.float32,
    )
    placed = placed.astype(jnp.bfloat16).reshape(slot_count, PAGE_TOKENS, kv_width)
    written = jnp.where(jnp.any(onehot, axis=1)[:, None, None], placed, initial[3])
    run_sum = running[1]
    partial_value = running[2]
    attention = (
        (partial_value / run_sum[..., None])
        .reshape(count_of_rows, QUERY_HEADS * HEAD_SIZE)
        .astype(jnp.bfloat16)
    )
    attended = (residual.astype(jnp.float32) + attention.astype(jnp.float32)).astype(jnp.bfloat16)
    widened = attended.astype(jnp.float32)
    normed = (
        widened * lax.rsqrt(jnp.mean(widened * widened, axis=-1, keepdims=True) + 1e-06) * ffn_gain
    ).astype(jnp.bfloat16)
    tok_count = lax.axis_size("tok")
    grp_count = lax.axis_size("grp")
    col_width = gate_weight.shape[1] // tok_count
    gate_cols = lax.dynamic_slice_in_dim(gate_weight, tok_index * col_width, col_width, 1)
    up_cols = lax.dynamic_slice_in_dim(up_weight, tok_index * col_width, col_width, 1)
    gate_all, up_all = (
        lax.all_gather(gate_cols, "grp", axis=1, tiled=True),
        lax.all_gather(up_cols, "grp", axis=1, tiled=True),
    )
    shards = lax.all_gather(normed, "tok", axis=0, tiled=True)
    gate_sum = jnp.dot(shards, gate_all, preferred_element_type=jnp.float32)
    up_sum = jnp.dot(shards, up_all, preferred_element_type=jnp.float32)
    produced = (jax.nn.silu(gate_sum) * up_sum).astype(jnp.bfloat16)
    returned = lax.all_to_all(produced, "tok", split_axis=0, concat_axis=1, tiled=True)
    hidden = (
        returned.reshape(count_of_rows, tok_count, grp_count, col_width)
        .transpose(0, 2, 1, 3)
        .reshape(count_of_rows, tok_count * grp_count * col_width)
    )
    return (attended, hidden, written)


def solution(mesh):
    in_specs = (
        P(("grp", "tok"), None),
        P(("grp", "tok"), None),
        P("grp", "tok"),
        P(("grp", "tok"), None),
        P(),
        P(None, "grp"),
        P(None, "grp"),
        P(("grp", "tok"), None, None),
        P("grp", None),
    )
    out_specs = (P(("grp", "tok"), None), P(("grp", "tok"), None), P(("grp", "tok"), None, None))
    return jax.shard_map(
        on_device, mesh=mesh, in_specs=in_specs, out_specs=out_specs, check_vma=False
    )
```

profile of v0, /device:TPU:0, one launch (start us, length us, event | category | flops | bytes accessed | tf_op | source)
XLA Modules:
  0.0 966.0 jit_solution(4111490794621667463)
XLA Ops:
  7.2 0.0 copy-start.4
  7.2 0.0 all-gather.6.cloned.1.call-start
  7.2 2.0 copy.32
  9.3 0.0 all-gather.6.cloned.1.call-update
  9.3 0.0 all-gather.8.cloned.1.call-start
  9.3 1.8 copy.33
  11.1 0.0 copy-done.4
  11.1 6.0 all-gather
  17.1 0.1 fusion.12
  17.2 18.5 %all-gather.6.cloned.1.call-done = bf16[512,2048]{0,1:T(8,128)(2,1)} async-done(((bf16[128,2048]{0,1:T(8,128)(2,1)}), bf16[512,2048]{0,1:T(8,128)(2,1)}) %all-gather.6.cloned.1.call-update) | async-done | bytes 2097168 | tf_op jit(solution)/shard_map/all_gather | solution.py:45
  35.7 1.7 fusion.18
  37.4 1.7 fusion
  39.2 2.6 fusion.1
  41.8 3.2 fusion.9
  45.0 1.8 bitcast_convert_fusion
  46.7 0.0 copy-start.3
  46.7 2.2 copy.37
  48.9 1.8 fusion.6
  50.7 0.0 copy-start.1
  50.7 1.0 copy-done.1
  51.8 0.0 copy-done.3
  51.8 1.4 fusion.8
  53.2 0.0 all-gather.8.cloned.1.call-update
  53.2 0.0 all-gather.10.cloned.1.call-start
  53.3 3.4 constant_dynamic-slice_fusion.1
  56.7 0.0 all-gather.10.cloned.1.call-update
  56.7 0.2 all-gather.12.cloned.1.call-start
  56.9 3.5 constant_dynamic-slice_fusion
  60.4 0.0 all-gather.12.cloned.1.call-update
  60.4 33.4 %all-gather.8.cloned.1.call-done = bf16[512,5120]{1,0:T(8,128)(2,1)} async-done(((bf16[128,5120]{1,0:T(8,128)(2,1)}), bf16[512,5120]{1,0:T(8,128)(2,1)}) %all-gather.8.cloned.1.call-update) | async-done | bytes 5242896 | tf_op jit(solution)/shard_map/all_gather | solution.py:109
  93.8 404.6 %all-gather.10.cloned.1.call-done = bf16[5120,2048]{1,0:T(8,128)(2,1)} async-done(((bf16[5120,256]{1,0:T(8,128)(2,1)}), bf16[5120,2048]{1,0:T(8,128)(2,1)}) %all-gather.10.cloned.1.call-update) | async-done | bytes 20971536 | tf_op jit(solution)/shard_map/all_gather | solution.py:106
  498.4 18.1 %fusion.19 = f32[512,2048]{1,0:T(8,128)} fusion(bf16[512,5120]{1,0:T(8,128)(2,1)} %all-gather.8.cloned.1.call-done, bf16[5120,2048]{1,0:T(8,128)(2,1)} %all-gather.10.cloned.1.call-done), kind=kOutput, calls=%fused_computation.35 | convolution fusion | flops 10737418240 | bytes 30408704 | tf_op jit(solution)/shard_map/dot_general | solution.py:110
  516.5 386.4 %all-gather.12.cloned.1.call-done = bf16[5120,2048]{1,0:T(8,128)(2,1)} async-done(((bf16[5120,256]{1,0:T(8,128)(2,1)}), bf16[5120,2048]{1,0:T(8,128)(2,1)}) %all-gather.12.cloned.1.call-update) | async-done | bytes 20971536 | tf_op jit(solution)/shard_map/all_gather | solution.py:107
  902.9 18.4 %multiply_convert_fusion = bf16[512,2048]{1,0:T(8,128)(2,1)} fusion(f32[512,2048]{1,0:T(8,128)} %fusion.19, bf16[512,5120]{1,0:T(8,128)(2,1)} %all-gather.8.cloned.1.call-done, bf16[5120,2048]{1,0:T(8,128)(2,1)} %all-gather.12.cloned.1.call-done), kind=kOutput, calls=%fused_computation.8 | convolution fusion | flops 10743709696 | bytes 32505856 | tf_op jit(solution)/shard_map/dot_general | solution.py:111
  921.4 0.0 copy-start.5
  921.4 0.0 copy-start
  921.4 4.8 all-to-all-start
  926.2 0.0 copy-done.5
  926.2 0.1 fusion.13
  926.3 0.0 copy-done
  926.3 2.5 copy.39
  928.8 0.0 copy-start.2
  928.8 3.0 reshape.103
  931.8 0.4 convolution_convert_fusion
  932.2 0.6 copy.47
  932.8 0.0 copy-done.2
  932.8 1.1 bitcast_select_fusion.1
  933.9 17.8 %all-to-all-done = bf16[4,128,2048]{2,1,0:T(8,128)(2,1)} async-done(((bf16[4,128,2048]{2,1,0:T(8,128)(2,1)}), bf16[4,128,2048]{2,1,0:T(8,128)(2,1)}, u32[]{:S(2)}, u32[]{:S(2)}) %all-to-all-start) | async-done | bytes 2097184 | tf_op jit(solution)/shard_map/all_to_all | solution.py:113
  951.7 2.3 copy.46
  954.0 2.7 copy.49
  956.7 2.8 reshape.102
  (4 shorter events, 0.0 us)
Async XLA Ops:
  7.2 4.0 copy-start.4
  7.2 28.5 %all-gather.6.cloned.1.call-start = ((), (), s32[]{:S(2)}) async-start(), calls=%async_computation.1 | async-start | bytes 2621440 | tf_op jit(solution)/shard_map/all_gather | solution.py:45
  9.3 84.6 %all-gather.8.cloned.1.call-start = ((), (), s32[]{:S(2)}) async-start(), calls=%async_computation.2 | async-start | bytes 6553600 | tf_op jit(solution)/shard_map/all_gather | solution.py:109
  46.7 5.0 copy-start.3
  50.7 1.1 copy-start.1
  53.2 445.2 %all-gather.10.cloned.1.call-start = ((), (), s32[]{:S(2)}) async-start(), calls=%async_computation.3 | async-start | bytes 23592960 | tf_op jit(solution)/shard_map/all_gather | solution.py:106
  56.7 846.2 %all-gather.12.cloned.1.call-start = ((), (), s32[]{:S(2)}) async-start(), calls=%async_computation.4 | async-start | bytes 23592960 | tf_op jit(solution)/shard_map/all_gather | solution.py:107
  921.4 4.8 copy-start.5
  921.4 4.9 copy-start
  921.4 30.3 %all-to-all-start = ((bf16[4,128,2048]{2,1,0:T(8,128)(2,1)}), bf16[4,128,2048]{2,1,0:T(8,128)(2,1)}, u32[]{:S(2)}, u32[]{:S(2)}) async-start(bf16[4,128,2048]{2,1,0:T(8,128)(2,1)} %bitcast.62), calls=%async_computation | async-start | bytes 4194304 | tf_op jit(solution)/shard_map/all_to_all | solution.py:113
  928.8 4.0 copy-start.2
Sparse Core Ops, SparseCore 0:
  10.1 25.5 all-gather.5
  53.4 40.4 all-gather.7
  95.3 403.0 all-gather.9
  499.8 403.1 all-gather.11
where the time goes:
time: 966 us
  waiting for transfers between devices  861 us (89%)
  matrix products  41.9 us (4%)
  local copies, waits for them, and re-layouts  29.3 us (3%)
  between operations  13.9 us (1%)
    all_gather x1, waiting for transfers between devices, on_device(): lax.all_gather(gate_cols, 'grp', axis=1, tiled=True)  405 us
    all_gather x1, waiting for transfers between devices, on_device(): lax.all_gather(up_cols, 'grp', axis=1, tiled=True)  386 us
    all_gather x1, waiting for transfers between devices, on_device(): shards = lax.all_gather(normed, 'tok', axis=0, tiled=True)  33.4 us
  transfers between devices with their start and end apart: 5, of which 5 were waited for; matrix products, arithmetic and copies ran while one was open for 4% of the time, Pallas kernels for 0%

commit v1 on v0

--- a/solution.py
+++ b/solution.py
@@ -97,25 +97,11 @@
     normed = (
         widened * lax.rsqrt(jnp.mean(widened * widened, axis=-1, keepdims=True) + 1e-06) * ffn_gain
     ).astype(jnp.bfloat16)
-    tok_count = lax.axis_size("tok")
-    grp_count = lax.axis_size("grp")
-    col_width = gate_weight.shape[1] // tok_count
-    gate_cols = lax.dynamic_slice_in_dim(gate_weight, tok_index * col_width, col_width, 1)
-    up_cols = lax.dynamic_slice_in_dim(up_weight, tok_index * col_width, col_width, 1)
-    gate_all, up_all = (
-        lax.all_gather(gate_cols, "grp", axis=1, tiled=True),
-        lax.all_gather(up_cols, "grp", axis=1, tiled=True),
-    )
-    shards = lax.all_gather(normed, "tok", axis=0, tiled=True)
-    gate_sum = jnp.dot(shards, gate_all, preferred_element_type=jnp.float32)
-    up_sum = jnp.dot(shards, up_all, preferred_element_type=jnp.float32)
+    shards = lax.all_gather(normed, "grp", axis=0, tiled=True)
+    gate_sum = jnp.dot(shards, gate_weight, preferred_element_type=jnp.float32)
+    up_sum = jnp.dot(shards, up_weight, preferred_element_type=jnp.float32)
     produced = (jax.nn.silu(gate_sum) * up_sum).astype(jnp.bfloat16)
-    returned = lax.all_to_all(produced, "tok", split_axis=0, concat_axis=1, tiled=True)
-    hidden = (
-        returned.reshape(count_of_rows, tok_count, grp_count, col_width)
-        .transpose(0, 2, 1, 3)
-        .reshape(count_of_rows, tok_count * grp_count * col_width)
-    )
+    hidden = lax.all_to_all(produced, "grp", split_axis=0, concat_axis=1, tiled=True)
     return (attended, hidden, written)
 
 

time: 966 us -> 298 us (0.31)
  waiting for transfers between devices: 861 us -> 210 us
  local copies, waits for them, and re-layouts: 29.3 us -> 17.9 us
    all_gather x3 -> x1, waiting for transfers between devices: 824 us -> 151 us  [on_device(): shards = lax.all_gather(normed, 'grp', axis=0, tiled=True)]
    all_to_all x1, waiting for transfers between devices: 17.8 us -> 40.3 us  [on_device(): lax.all_to_all(produced, 'grp', split_axis=0, concat_axis=1, tiled=True)]
  transfers between devices with their start and end apart: 5 -> 3, of which waited for: 5 -> 3; matrix products, arithmetic and copies ran while one was open for 4% -> 3% of each run, Pallas kernels for 0% -> 0%
where the time goes in v1:
time: 298 us
  waiting for transfers between devices  210 us (70%)
  matrix products  36.2 us (12%)
  local copies, waits for them, and re-layouts  17.9 us (6%)
  between operations  14.2 us (5%)
  other arithmetic  9.06 us (3%)
  blocking collectives  5.95 us (2%)
  starting transfers between devices  4.56 us (2%)
    all_gather x1, waiting for transfers between devices, on_device(): shards = lax.all_gather(normed, 'grp', axis=0, tiled=True)  151 us
    all_to_all x1, waiting for transfers between devices, on_device(): lax.all_to_all(produced, 'grp', split_axis=0, concat_axis=1, tiled=True)  40.3 us
    all_gather x1, waiting for transfers between devices, on_device(): lax.all_gather(rotated_keys_values, 'tok', axis=0, tiled=True)  18.5 us
    dot_general x1, matrix products, on_device(): gate_sum = jnp.dot(shards, gate_weight, preferred_element_type=jnp.float32)  15.5 us
    dot_general x1, matrix products, on_device(): up_sum = jnp.dot(shards, up_weight, preferred_element_type=jnp.float32)  15.1 us
  transfers between devices with their start and end apart: 3, of which 3 were waited for; matrix products, arithmetic and copies ran while one was open for 3% of the time, Pallas kernels for 0%

profile of v1, /device:TPU:0, one launch (start us, length us, event | category | flops | bytes accessed | tf_op | source)
XLA Modules:
  0.0 297.7 jit_solution(10952795545649887813)
XLA Ops:
  7.2 0.0 copy-start.4
  7.2 0.0 all-gather.4.cloned.1.call-start
  7.2 2.0 copy.32
  9.3 0.0 all-gather.4.cloned.1.call-update
  9.3 0.0 all-gather.6.cloned.1.call-start
  9.3 1.8 copy.33
  11.1 0.0 copy-done.4
  11.1 6.0 %all-gather = s32[1,512]{1,0:T(1,128)S(1)} all-gather(s32[1,128]{1,0:T(1,128)S(1)} %copy-done.4), channel_id=2, replica_groups=mesh['grp'=8,'tok'=4] {'tok'}, dimensions={1}, use_global_device_ids=true | all-gather | bytes 2560 | tf_op jit(solution)/shard_map/all_gather | solution.py:46
  17.1 0.1 fusion.12
  17.2 18.5 %all-gather.4.cloned.1.call-done = bf16[512,2048]{0,1:T(8,128)(2,1)} async-done(((bf16[128,2048]{0,1:T(8,128)(2,1)}), bf16[512,2048]{0,1:T(8,128)(2,1)}) %all-gather.4.cloned.1.call-update) | async-done | bytes 2097168 | tf_op jit(solution)/shard_map/all_gather | solution.py:45
  35.7 1.7 fusion.18
  37.4 1.7 fusion
  39.2 2.6 fusion.1
  41.8 3.4 %fusion.9 = bf16[128,8,5,128]{0,3,2,1:T(8,128)(2,1)S(1)} fusion(bf16[512,8,128,1]{0,2,3,1:T(8,128)(2,1)S(1)} %bitcast.55, f32[8,512,128,5]{2,1,3,0:T(8,128)S(1)} %get-tuple-element.8, f32[128,8,5]{0,2,1:T(8,128)S(1)} %broadcast_maximum_fusion, pred[128,512]{0,1:T(8,128)(4,1)S(1)} %fusion.12, f32[128,8,5]{0,2,1:T(8,128)S(1)} %fusion.1), kind=kOutput, calls=%fused_computation.15 | convolution fusion | flops 685506560 | bytes 12951552 | tf_op jit(solution)/shard_map/qgrk,kgd->qgrd/dot_general | solution.py:68
  45.1 1.8 bitcast_convert_fusion
  46.9 0.0 copy-start.3
  46.9 2.2 copy.37
  49.1 1.8 fusion.6
  50.9 0.0 copy-start.1
  50.9 1.0 copy-done.1
  52.0 0.0 copy-done.3
  52.0 1.4 fusion.8
  53.4 0.0 all-gather.6.cloned.1.call-update
  53.4 151.0 %all-gather.6.cloned.1.call-done = bf16[1024,5120]{1,0:T(8,128)(2,1)} async-done(((bf16[128,5120]{1,0:T(8,128)(2,1)}), bf16[1024,5120]{1,0:T(8,128)(2,1)}) %all-gather.6.cloned.1.call-update) | async-done | bytes 10485776 | tf_op jit(solution)/shard_map/all_gather | solution.py:100
  204.4 0.0 copy-start.5
  204.4 15.5 %fusion.19 = f32[1024,1024]{1,0:T(8,128)S(1)} fusion(bf16[1024,5120]{1,0:T(8,128)(2,1)} %all-gather.6.cloned.1.call-done, bf16[5120,1024]{1,0:T(8,128)(2,1)} %param.14), kind=kOutput, calls=%fused_computation.32 | convolution fusion | flops 10737418240 | bytes 25165824 | tf_op jit(solution)/shard_map/dot_general | solution.py:101
  220.0 0.0 copy-done.5
  220.0 15.1 %multiply_convert_fusion = bf16[1024,1024]{1,0:T(8,128)(2,1)} fusion(f32[1024,1024]{1,0:T(8,128)S(1)} %fusion.19, bf16[1024,5120]{1,0:T(8,128)(2,1)S(1)} %copy-done.5, bf16[5120,1024]{1,0:T(8,128)(2,1)} %param.15), kind=kOutput, calls=%fused_computation.8 | convolution fusion | flops 10743709696 | bytes 27262976 | tf_op jit(solution)/shard_map/dot_general | solution.py:102
  235.1 0.0 copy-start.6
  235.1 0.0 copy-start
  235.1 4.5 %all-to-all-start = ((bf16[8,128,1024]{2,1,0:T(8,128)(2,1)}), bf16[8,128,1024]{2,1,0:T(8,128)(2,1)}, u32[]{:S(2)}, u32[]{:S(2)}) async-start(bf16[8,128,1024]{2,1,0:T(8,128)(2,1)} %bitcast.53), calls=%async_computation | async-start | bytes 4194304 | tf_op jit(solution)/shard_map/all_to_all | solution.py:104
  239.6 0.0 copy-done.6
  239.6 0.1 fusion.13
  239.8 0.0 copy-done
  239.8 2.5 copy.39
  242.3 0.0 copy-start.2
  242.3 3.0 reshape.94
  245.2 0.4 convolution_convert_fusion
  245.7 0.6 copy.47
  246.2 0.0 copy-done.2
  246.3 1.1 bitcast_select_fusion.1
  247.4 40.3 %all-to-all-done = bf16[8,128,1024]{2,1,0:T(8,128)(2,1)} async-done(((bf16[8,128,1024]{2,1,0:T(8,128)(2,1)}), bf16[8,128,1024]{2,1,0:T(8,128)(2,1)}, u32[]{:S(2)}, u32[]{:S(2)}) %all-to-all-start) | async-done | bytes 2097184 | tf_op jit(solution)/shard_map/all_to_all | solution.py:104
  287.7 3.1 %copy.46 = bf16[8,16,8,1024]{3,2,0,1:T(8,128)(2,1)} copy(bf16[8,16,8,1024]{3,2,1,0:T(8,128)(2,1)} %bitcast.20) | data formatting | bytes 4194304 | tf_op jit(solution)/shard_map/all_to_all | solution.py:104
  (4 shorter events, 0.0 us)
Async XLA Ops:
  7.2 4.0 %copy-start.4 = (s32[1,128]{1,0:T(1,128)S(1)}, s32[1,128]{1,0:T(1,128)}, u32[]{:S(2)}) copy-start(s32[1,128]{1,0:T(1,128)} %param.11) | copy-start | bytes 1540
  7.2 28.5 %all-gather.4.cloned.1.call-start = ((), (), s32[]{:S(2)}) async-start(), calls=%async_computation.1 | async-start | bytes 2621440 | tf_op jit(solution)/shard_map/all_gather | solution.py:45
  9.3 195.2 %all-gather.6.cloned.1.call-start = ((), (), s32[]{:S(2)}) async-start(), calls=%async_computation.2 | async-start | bytes 11796480 | tf_op jit(solution)/shard_map/all_gather | solution.py:100
  46.9 5.0 %copy-start.3 = (f32[5120]{0:T(1024)S(1)}, f32[5120]{0:T(1024)}, u32[]{:S(2)}) copy-start(f32[5120]{0:T(1024)} %param.13) | copy-start | bytes 61444
  50.9 1.1 copy-start.1
  204.4 15.5 %copy-start.5 = (bf16[1024,5120]{1,0:T(8,128)(2,1)S(1)}, bf16[1024,5120]{1,0:T(8,128)(2,1)}, u32[]{:S(2)}) copy-start(bf16[1024,5120]{1,0:T(8,128)(2,1)} %all-gather.6.cloned.1.call-done) | copy-start | bytes 31457284
  235.1 4.5 %copy-start.6 = (s32[1,64]{1,0:T(1,128)S(1)}, s32[1,64]{1,0:T(1,128)}, u32[]{:S(2)}) copy-start(s32[1,64]{1,0:T(1,128)} %param.17) | copy-start | bytes 772
  235.1 4.6 %copy-start = (bf16[512,2048]{0,1:T(8,128)(2,1)S(1)}, bf16[512,2048]{0,1:T(8,128)(2,1)}, u32[]{:S(2)}) copy-start(bf16[512,2048]{0,1:T(8,128)(2,1)} %all-gather.4.cloned.1.call-done) | copy-start | bytes 6291460
  235.1 52.6 %all-to-all-start = ((bf16[8,128,1024]{2,1,0:T(8,128)(2,1)}), bf16[8,128,1024]{2,1,0:T(8,128)(2,1)}, u32[]{:S(2)}, u32[]{:S(2)}) async-start(bf16[8,128,1024]{2,1,0:T(8,128)(2,1)} %bitcast.53), calls=%async_computation | async-start | bytes 4194304 | tf_op jit(solution)/shard_map/all_to_all | solution.py:104
  242.3 4.0 %copy-start.2 = (bf16[16,16,2048]{2,1,0:T(8,128)(2,1)S(1)}, bf16[16,16,2048]{2,1,0:T(8,128)(2,1)}, u32[]{:S(2)}) copy-start(bf16[16,16,2048]{2,1,0:T(8,128)(2,1)} %param.16) | copy-start | bytes 3145732
Sparse Core Ops, SparseCore 0:
  10.1 25.5 all-gather.3
  53.6 150.8 all-gather.5

commit v2 on v1

--- a/solution.py
+++ b/solution.py
@@ -3,6 +3,8 @@
 import jax
 import jax.numpy as jnp
 from jax import lax
+from jax.experimental import pallas as pl
+from jax.experimental.pallas import tpu as pltpu
 from jax.sharding import PartitionSpec as P
 
 QUERY_HEADS = 40
@@ -12,6 +14,56 @@
 
 
 MASK_FILLER = -1e30
+
+
+def ring_order(count):
+    return list(range(0, 1)) + list(range(1, count, 2)) + list(range((count - 1) // 2 * 2, 0, -2))
+
+
+def ring_tables(count):
+    order = ring_order(count)
+    spot = {place: i for i, place in enumerate(order)}
+    return [[order[(spot[z] + s) % count] for z in range(count)] for s in range(count)]
+
+
+def gated_kernel(own_ref, other_ref, gate_ref, up_ref, own_out, other_out, rows_ref):
+    half = own_ref.shape[0]
+
+    @pl.when(pl.program_id(0) == 0)
+    def _():
+        rows_ref[:half] = own_ref[...]
+        rows_ref[half:] = other_ref[...]
+
+    rows = rows_ref[...]
+    gate_sum = jnp.dot(rows, gate_ref[...], preferred_element_type=jnp.float32)
+    up_sum = jnp.dot(rows, up_ref[...], preferred_element_type=jnp.float32)
+    made = (gate_sum / (1.0 + jnp.exp(-gate_sum)) * up_sum).astype(jnp.bfloat16)
+    own_out[...] = made[:half]
+    other_out[...] = made[half:]
+
+
+def gated(own, other, gate_weight, up_weight):
+    rows, width = own.shape
+    units = gate_weight.shape[1]
+    block = 256
+    whole = pl.BlockSpec((rows, width), lambda i: (0, 0))
+    columns = pl.BlockSpec((width, block), lambda i: (0, i))
+    out = pl.BlockSpec((rows, block), lambda i: (0, i))
+    shape = jax.ShapeDtypeStruct((rows, units), jnp.bfloat16)
+    return pl.pallas_call(
+        gated_kernel,
+        grid=(units // block,),
+        in_specs=[whole, whole, columns, columns],
+        out_specs=[out, out],
+        out_shape=[shape, shape],
+        scratch_shapes=[pltpu.VMEM((2 * rows, width), jnp.bfloat16)],
+        compiler_params=pltpu.CompilerParams(vmem_limit_bytes=48 * 1024 * 1024),
+        cost_estimate=pl.CostEstimate(
+            flops=8 * rows * width * units,
+            bytes_accessed=4 * width * units + 4 * rows * (width + units),
+            transcendentals=2 * rows * units,
+        ),
+    )(own, other, gate_weight, up_weight)
 
 
 def on_device(
@@ -97,11 +149,37 @@
     normed = (
         widened * lax.rsqrt(jnp.mean(widened * widened, axis=-1, keepdims=True) + 1e-06) * ffn_gain
     ).astype(jnp.bfloat16)
-    shards = lax.all_gather(normed, "grp", axis=0, tiled=True)
-    gate_sum = jnp.dot(shards, gate_weight, preferred_element_type=jnp.float32)
-    up_sum = jnp.dot(shards, up_weight, preferred_element_type=jnp.float32)
-    produced = (jax.nn.silu(gate_sum) * up_sum).astype(jnp.bfloat16)
-    hidden = lax.all_to_all(produced, "grp", split_axis=0, concat_axis=1, tiled=True)
+    grp_count = lax.axis_size("grp")
+    grp_index = lax.axis_index("grp")
+    line, column = grp_index // 2, grp_index % 2
+    line_count = grp_count // 2
+    ahead = ring_tables(line_count)
+    units = gate_weight.shape[1]
+
+    def send(array, steps, flip):
+        pairs = []
+        for z in range(line_count):
+            for y in range(2):
+                pairs.append((2 * z + y, 2 * ahead[steps][z] + (1 - y if flip else y)))
+        return lax.ppermute(array, "grp", pairs)
+
+    hidden = jnp.zeros((count_of_rows, grp_count * units), jnp.bfloat16)
+
+    def place(hidden, block, steps, flip):
+        source = jnp.asarray(ahead[steps], jnp.int32)[line] * 2 + (1 - column if flip else column)
+        return lax.dynamic_update_slice_in_dim(hidden, block, source * units, 1)
+
+    held = normed
+    for step in range(line_count):
+        other = send(held, 0, True)
+        following = send(held, 1, False) if step + 1 < line_count else None
+        own_block, other_block = gated(held, other, gate_weight, up_weight)
+        if step:
+            own_block = send(own_block, line_count - step, False)
+        other_block = send(other_block, (line_count - step) % line_count, True)
+        hidden = place(hidden, own_block, step, False)
+        hidden = place(hidden, other_block, step, True)
+        held = following
     return (attended, hidden, written)
 
 

time: 298 us -> 248 us (0.83)
  waiting for transfers between devices: 210 us -> 128 us
  Pallas kernels: 0 us -> 42.2 us
  matrix products: 36.2 us -> 6.95 us
  starting transfers between devices: 4.56 us -> 21.2 us
    all_gather x1 -> x0, waiting for transfers between devices: 151 us -> none  [on_device(): shards = lax.all_gather(normed, 'grp', axis=0, tiled=True)]
    ppermute x0 -> x14, waiting for transfers between devices: none -> 108 us  [send(): return lax.ppermute(array, 'grp', pairs)]
    pallas_call x0 -> x4, Pallas kernels: none -> 42.2 us  [gated(): pl.pallas_call(gated_kernel, grid=(units // block,), in_specs=[whole, who...]
    all_to_all x1 -> x0, waiting for transfers between devices: 40.3 us -> none  [on_device(): lax.all_to_all(produced, 'grp', split_axis=0, concat_axis=1, tiled=True)]
    dot_general x2 -> x0, matrix products: 30.7 us -> none  [the longest x1 15.5 us: on_device(): gate_sum = jnp.dot(shards, gate_weight, preferred_element_type=jnp.float32)]
    ppermute x0 -> x14, starting transfers between devices: none -> 21.1 us  [send(): return lax.ppermute(array, 'grp', pairs)]
    all_to_all x1 -> x0, starting transfers between devices: 4.48 us -> none  [on_device(): lax.all_to_all(produced, 'grp', split_axis=0, concat_axis=1, tiled=True)]
    all_to_all x1 -> x0, local copies, waits for them, and re-layouts: 3.15 us -> none  [on_device(): lax.all_to_all(produced, 'grp', split_axis=0, concat_axis=1, tiled=True)]
  transfers between devices with their start and end apart: 3 -> 15, of which waited for: 3 -> 9; matrix products, arithmetic and copies ran while one was open for 3% -> 6% of each run, Pallas kernels for 0% -> 17%
where the time goes in v2:
time: 248 us; the launch traced here: 247 us
  waiting for transfers between devices  128 us (52%)
  Pallas kernels  42.2 us (17%)
  starting transfers between devices  21.2 us (9%)
  local copies, waits for them, and re-layouts  19 us (8%)
  between operations  16.4 us (7%)
  other arithmetic  7.97 us (3%)
  matrix products  6.95 us (3%)
  blocking collectives  5.95 us (2%)
    ppermute x14, waiting for transfers between devices, send(): return lax.ppermute(array, 'grp', pairs)  108 us
    pallas_call x4, Pallas kernels, gated(): pl.pallas_call(gated_kernel, grid=(units // block,), in_specs=[whole, who...  42.2 us
    ppermute x14, starting transfers between devices, send(): return lax.ppermute(array, 'grp', pairs)  21.1 us
    all_gather x1, waiting for transfers between devices, on_device(): lax.all_gather(rotated_keys_values, 'tok', axis=0, tiled=True)  19.4 us
    all_gather x1, blocking collectives, on_device(): seg_piece = lax.all_gather(own_segment, 'tok', axis=0, tiled=True)  5.95 us
  transfers between devices with their start and end apart: 15, of which 9 were waited for; matrix products, arithmetic and copies ran while one was open for 6% of the time, Pallas kernels for 17%

profile of v2, /device:TPU:0, one launch (start us, length us, event | category | flops | bytes accessed | tf_op | source)
XLA Modules:
  0.0 247.4 jit_solution(12063392009997506205)
XLA Ops:
  7.2 0.0 all-gather.3.cloned.1.call-start
  7.2 2.1 copy.37
  9.4 0.0 all-gather.3.cloned.1.call-update
  9.4 0.8 copy.38
  10.2 6.0 %all-gather = s32[1,512]{1,0:T(1,128)S(1)} all-gather(s32[1,128]{1,0:T(1,128)S(1)} %copy-done.5), channel_id=2, replica_groups=mesh['grp'=8,'tok'=4] {'tok'}, dimensions={1}, use_global_device_ids=true | all-gather | bytes 2560 | tf_op jit(solution)/shard_map/all_gather | solution.py:98
  16.2 0.1 fusion.12
  16.3 19.4 %all-gather.3.cloned.1.call-done = bf16[512,2048]{0,1:T(8,128)(2,1)} async-done(((bf16[128,2048]{0,1:T(8,128)(2,1)}), bf16[512,2048]{0,1:T(8,128)(2,1)}) %all-gather.3.cloned.1.call-update) | async-done | bytes 2097168 | tf_op jit(solution)/shard_map/all_gather | solution.py:97
  35.7 1.7 fusion.18
  37.4 1.7 fusion
  39.2 2.6 %fusion.1 = f32[128,8,5]{0,2,1:T(8,128)S(1)} fusion(f32[8,512,128,5]{2,1,3,0:T(8,128)S(1)} %get-tuple-element.24, f32[128,8,5]{0,2,1:T(8,128)S(1)} %broadcast_maximum_fusion, pred[128,512]{0,1:T(8,128)(4,1)S(1)} %fusion.12), kind=kLoop, calls=%fused_computation.4 | loop fusion | flops 13102080 | bytes 10592256 | tf_op jit(solution)/shard_map/reduce_sum | solution.py:119
  41.8 3.2 %fusion.9 = bf16[128,8,5,128]{0,3,2,1:T(8,128)(2,1)S(1)} fusion(bf16[512,8,128,1]{0,2,3,1:T(8,128)(2,1)S(1)} %bitcast.48, f32[8,512,128,5]{2,1,3,0:T(8,128)S(1)} %get-tuple-element.24, f32[128,8,5]{0,2,1:T(8,128)S(1)} %broadcast_maximum_fusion, pred[128,512]{0,1:T(8,128)(4,1)S(1)} %fusion.12, f32[128,8,5]{0,2,1:T(8,128)S(1)} %fusion.1), kind=kOutput, calls=%fused_computation.14 | convolution fusion | flops 685506560 | bytes 12951552 | tf_op jit(solution)/shard_map/qgrk,kgd->qgrd/dot_general | solution.py:120
  45.0 1.8 bitcast_convert_fusion
  46.7 2.1 copy.42
  48.9 0.0 copy-start.4
  48.9 1.8 fusion.6
  50.7 0.0 copy-start
  50.7 0.0 copy-start.9
  50.7 0.0 copy-start.8
  50.7 0.0 copy-start.7
  50.8 0.0 copy-start.6
  50.8 0.4 fusion.8.own_ref
  51.2 1.5 collective-permute-start.2
  52.7 30.5 %collective-permute-done.2.own_ref = bf16[128,5120]{1,0:T(8,128)(2,1)} collective-permute-done((bf16[128,5120]{1,0:T(8,128)(2,1)S(1)}, bf16[128,5120]{1,0:T(8,128)(2,1)}, u32[]{:S(2)}, u32[]{:S(2)}) %collective-permute-start.2) | collective-permute-done | bytes 1310752 | tf_op jit(solution)/shard_map/ppermute | solution.py:164
  83.2 0.6 collective-permute-start.6
  83.8 1.5 collective-permute-start
  85.2 0.6 collective-permute-start.3
  85.8 0.6 dynamic_slice.29
  87.1 0.6 dynamic_slice.31
  88.3 0.6 dynamic_slice.33
  89.7 0.1 fusion.13
  89.8 3.9 %copy.43 = bf16[512,2048]{1,0:T(8,128)(2,1)} copy(bf16[512,2048]{0,1:T(8,128)(2,1)} %all-gather.3.cloned.1.call-done) | data formatting | bytes 4194304 | tf_op jit(solution)/shard_map/all_gather | solution.py:97
  93.7 20.7 %collective-permute-done.6.own_ref = bf16[128,5120]{1,0:T(8,128)(2,1)S(1)} collective-permute-done((bf16[128,5120]{1,0:T(8,128)(2,1)}, bf16[128,5120]{1,0:T(8,128)(2,1)S(1)}, u32[]{:S(2)}, u32[]{:S(2)}) %collective-permute-start.6) | collective-permute-done | bytes 1310752 | tf_op jit(solution)/shard_map/ppermute | solution.py:164
  114.4 0.6 collective-permute-start.10
  115.0 4.3 %reshape.107 = bf16[32,32768]{1,0:T(8,128)(2,1)} reshape(bf16[512,2048]{1,0:T(8,128)(2,1)} %copy.43) | data formatting | bytes 4194304 | tf_op jit(solution)/shard_map/reshape | solution.py:135
  119.3 2.0 convolution_convert_fusion
  121.3 0.6 copy.50
  121.9 0.0 collective-permute-done.other_ref
  121.9 10.6 %shard_map.184 = (bf16[128,1024]{1,0:T(8,128)(2,1)S(1)}, bf16[128,1024]{1,0:T(8,128)(2,1)S(1)}) custom-call(bf16[128,5120]{1,0:T(8,128)(2,1)S(1)} %fusion.8.own_ref, bf16[128,5120]{1,0:T(8,128)(2,1)} %collective-permute-done.other_ref, bf16[5120,1024]{1,0:T(8,128)(2,1)} %gate_ref.7, bf16[5120,1024]{1,0:T(8,128)(2,1)} %up_ref.7), custom_call_target="tpu_custom_call" | custom-call | flops 5368709120 | bytes 24117248 | tf_op jit(solution)/shard_map/pallas_call | solution.py:53
  132.5 0.0 copy-start.3
  132.5 1.5 collective-permute-start.1
  134.0 0.5 collective-permute-start.7
  134.6 9.1 %collective-permute-done.3.other_ref = bf16[128,5120]{1,0:T(8,128)(2,1)} collective-permute-done((bf16[128,5120]{1,0:T(8,128)(2,1)}, bf16[128,5120]{1,0:T(8,128)(2,1)}, u32[]{:S(2)}, u32[]{:S(2)}) %collective-permute-start.3) | collective-permute-done | bytes 1310752 | tf_op jit(solution)/shard_map/ppermute | solution.py:164
  143.7 10.9 %shard_map.185 = (bf16[128,1024]{1,0:T(8,128)(2,1)S(1)}, bf16[128,1024]{1,0:T(8,128)(2,1)S(1)}) custom-call(bf16[128,5120]{1,0:T(8,128)(2,1)} %collective-permute-done.2.own_ref, bf16[128,5120]{1,0:T(8,128)(2,1)} %collective-permute-done.3.other_ref, bf16[5120,1024]{1,0:T(8,128)(2,1)} %gate_ref.7, bf16[5120,1024]{1,0:T(8,128)(2,1)} %up_ref.7), custom_call_target="tpu_custom_call" | custom-call | flops 5368709120 | bytes 24117248 | tf_op jit(solution)/shard_map/pallas_call | solution.py:53
  154.6 2.4 collective-permute-start.4
  157.0 0.0 collective-permute-done.10.own_ref
  157.0 1.5 collective-permute-start.11
  158.5 1.1 bitcast_select_fusion.1
  159.6 0.2 broadcast_in_dim.48
  159.9 0.0 collective-permute-done.1
  159.9 1.0 collective-permute-start.5
  160.9 3.1 %collective-permute-done.4 = bf16[128,1024]{1,0:T(8,128)(2,1)S(1)} collective-permute-done((bf16[128,1024]{1,0:T(8,128)(2,1)S(1)}, bf16[128,1024]{1,0:T(8,128)(2,1)S(1)}, u32[]{:S(2)}, u32[]{:S(2)}) %collective-permute-start.4) | collective-permute-done | bytes 262176 | tf_op jit(solution)/shard_map/ppermute | solution.py:164
  164.1 18.9 %collective-permute-done.7.other_ref = bf16[128,5120]{1,0:T(8,128)(2,1)S(1)} collective-permute-done((bf16[128,5120]{1,0:T(8,128)(2,1)S(1)}, bf16[128,5120]{1,0:T(8,128)(2,1)S(1)}, u32[]{:S(2)}, u32[]{:S(2)}) %collective-permute-start.7) | collective-permute-done | bytes 1310752 | tf_op jit(solution)/shard_map/ppermute | solution.py:164
  182.9 10.2 %shard_map.186 = (bf16[128,1024]{1,0:T(8,128)(2,1)S(1)}, bf16[128,1024]{1,0:T(8,128)(2,1)S(1)}) custom-call(bf16[128,5120]{1,0:T(8,128)(2,1)S(1)} %collective-permute-done.6.own_ref, bf16[128,5120]{1,0:T(8,128)(2,1)S(1)} %collective-permute-done.7.other_ref, bf16[5120,1024]{1,0:T(8,128)(2,1)} %gate_ref.7, bf16[5120,1024]{1,0:T(8,128)(2,1)} %up_ref.7), custom_call_target="tpu_custom_call" | custom-call | flops 5368709120 | bytes 24117248 | tf_op jit(solution)/shard_map/pallas_call | solution.py:53
  193.1 2.8 %collective-permute-start.8 = (bf16[128,1024]{1,0:T(8,128)(2,1)S(1)}, bf16[128,1024]{1,0:T(8,128)(2,1)S(1)}, u32[]{:S(2)}, u32[]{:S(2)}) collective-permute-start(bf16[128,1024]{1,0:T(8,128)(2,1)S(1)} %get-tuple-element.15), channel_id=1, source_target_pairs={{0,24},{4,28},{8,16},{12,20},{16,8},{20,12},{24,0},{28,4},{1,25},{... | collective-permute-start | bytes 786440 | tf_op jit(solution)/shard_map/ppermute | solution.py:164
  195.9 2.0 collective-permute-start.9
  197.9 16.9 %collective-permute-done.11.other_ref = bf16[128,5120]{1,0:T(8,128)(2,1)S(1)} collective-permute-done((bf16[128,5120]{1,0:T(8,128)(2,1)}, bf16[128,5120]{1,0:T(8,128)(2,1)S(1)}, u32[]{:S(2)}, u32[]{:S(2)}) %collective-permute-start.11) | collective-permute-done | bytes 1310752 | tf_op jit(solution)/shard_map/ppermute | solution.py:164
  214.7 10.6 %shard_map.187 = (bf16[128,1024]{1,0:T(8,128)(2,1)S(1)}, bf16[128,1024]{1,0:T(8,128)(2,1)S(1)}) custom-call(bf16[128,5120]{1,0:T(8,128)(2,1)} %collective-permute-done.10.own_ref, bf16[128,5120]{1,0:T(8,128)(2,1)S(1)} %collective-permute-done.11.other_ref, bf16[5120,1024]{1,0:T(8,128)(2,1)} %gate_ref.7, bf16[5120,1024]{1,0:T(8,128)(2,1)} %up_ref.7), custom_call_target="tpu_custom_call" | custom-call | flops 5368709120 | bytes 24117248 | tf_op jit(solution)/shard_map/pallas_call | solution.py:53
  225.3 3.4 %collective-permute-start.12 = (bf16[128,1024]{1,0:T(8,128)(2,1)S(1)}, bf16[128,1024]{1,0:T(8,128)(2,1)S(1)}, u32[]{:S(2)}, u32[]{:S(2)}) collective-permute-start(bf16[128,1024]{1,0:T(8,128)(2,1)S(1)} %get-tuple-element.17), channel_id=1, source_target_pairs={{0,8},{4,12},{8,24},{12,28},{16,0},{20,4},{24,16},{28,20},{1,9},{5... | collective-permute-start | bytes 786440 | tf_op jit(solution)/shard_map/ppermute | solution.py:164
  228.7 0.0 collective-permute-done.5
  228.7 1.2 collective-permute-start.13
  230.0 5.5 %collective-permute-done.12 = bf16[128,1024]{1,0:T(8,128)(2,1)S(1)} collective-permute-done((bf16[128,1024]{1,0:T(8,128)(2,1)S(1)}, bf16[128,1024]{1,0:T(8,128)(2,1)S(1)}, u32[]{:S(2)}, u32[]{:S(2)}) %collective-permute-start.12) | collective-permute-done | bytes 262176 | tf_op jit(solution)/shard_map/ppermute | solution.py:164
  235.5 3.7 %collective-permute-done.13 = bf16[128,1024]{1,0:T(8,128)(2,1)S(1)} collective-permute-done((bf16[128,1024]{1,0:T(8,128)(2,1)S(1)}, bf16[128,1024]{1,0:T(8,128)(2,1)S(1)}, u32[]{:S(2)}, u32[]{:S(2)}) %collective-permute-start.13) | collective-permute-done | bytes 262176 | tf_op jit(solution)/shard_map/ppermute | solution.py:164
  239.3 0.0 copy-start.1
  239.3 1.3 copy-done.1
  (25 shorter events, 0.2 us)
Async XLA Ops:
  7.2 2.2 copy-start.2
  7.2 3.0 %copy-start.5 = (s32[1,128]{1,0:T(1,128)S(1)}, s32[1,128]{1,0:T(1,128)}, u32[]{:S(2)}) copy-start(s32[1,128]{1,0:T(1,128)} %param.19) | copy-start | bytes 1540
  7.2 28.5 %all-gather.3.cloned.1.call-start = ((), (), s32[]{:S(2)}) async-start(), calls=%async_computation | async-start | bytes 2621440 | tf_op jit(solution)/shard_map/all_gather | solution.py:97
  48.9 1.9 copy-start.4
  50.7 32.5 %copy-start = (bf16[128,5120]{1,0:T(8,128)(2,1)}, bf16[128,5120]{1,0:T(8,128)(2,1)S(1)}, u32[]{:S(2)}) copy-start(bf16[128,5120]{1,0:T(8,128)(2,1)S(1)} %get-tuple-element.20) | copy-start | bytes 3932164
  50.7 35.1 %copy-start.9 = (s32[4]{0:T(128)S(1)}, s32[4]{0:T(128)}, u32[]{:S(2)}) copy-start(s32[4]{0:T(128)} %constant.95.clone) | copy-start | bytes 52
  50.7 36.3 %copy-start.8 = (s32[4]{0:T(128)S(1)}, s32[4]{0:T(128)}, u32[]{:S(2)}) copy-start(s32[4]{0:T(128)} %constant.96.clone) | copy-start | bytes 52
  50.7 37.6 %copy-start.7 = (s32[4]{0:T(128)S(1)}, s32[4]{0:T(128)}, u32[]{:S(2)}) copy-start(s32[4]{0:T(128)} %constant.97.clone) | copy-start | bytes 52
  50.8 38.9 %copy-start.6 = (s32[1,64]{1,0:T(1,128)S(1)}, s32[1,64]{1,0:T(1,128)}, u32[]{:S(2)}) copy-start(s32[1,64]{1,0:T(1,128)} %param.25) | copy-start | bytes 772
  51.2 32.0 %collective-permute-start.2 = (bf16[128,5120]{1,0:T(8,128)(2,1)S(1)}, bf16[128,5120]{1,0:T(8,128)(2,1)}, u32[]{:S(2)}, u32[]{:S(2)}) collective-permute-start(bf16[128,5120]{1,0:T(8,128)(2,1)S(1)} %fusion.8.own_ref), channel_id=1, source_target_pairs={{0,8},{4,12},{8,24},{12,28},{16,0},{20,4},{24,16},{28,20},{1,9},{5... | collective-permute-start | bytes 3932168 | tf_op jit(solution)/shard_map/ppermute | solution.py:164
  83.2 31.2 %collective-permute-start.6 = (bf16[128,5120]{1,0:T(8,128)(2,1)}, bf16[128,5120]{1,0:T(8,128)(2,1)S(1)}, u32[]{:S(2)}, u32[]{:S(2)}) collective-permute-start(bf16[128,5120]{1,0:T(8,128)(2,1)} %collective-permute-done.2.own_ref), channel_id=1, source_target_pairs={{0,8},{4,12},{8,24},{12,28},{16,0},{20,4},{24,16},{28,20},{1,9},{5... | collective-permute-start | bytes 3932168 | tf_op jit(solution)/shard_map/ppermute | solution.py:164
  83.8 38.1 %collective-permute-start = (bf16[128,5120]{1,0:T(8,128)(2,1)S(1)}, bf16[128,5120]{1,0:T(8,128)(2,1)}, u32[]{:S(2)}, u32[]{:S(2)}) collective-permute-start(bf16[128,5120]{1,0:T(8,128)(2,1)S(1)} %fusion.8.own_ref), channel_id=1, source_target_pairs={{0,4},{4,0},{8,12},{12,8},{16,20},{20,16},{24,28},{28,24},{1,5},{5... | collective-permute-start | bytes 3932168 | tf_op jit(solution)/shard_map/ppermute | solution.py:164
  85.2 58.4 %collective-permute-start.3 = (bf16[128,5120]{1,0:T(8,128)(2,1)}, bf16[128,5120]{1,0:T(8,128)(2,1)}, u32[]{:S(2)}, u32[]{:S(2)}) collective-permute-start(bf16[128,5120]{1,0:T(8,128)(2,1)} %collective-permute-done.2.own_ref), channel_id=1, source_target_pairs={{0,4},{4,0},{8,12},{12,8},{16,20},{20,16},{24,28},{28,24},{1,5},{5... | collective-permute-start | bytes 3932168 | tf_op jit(solution)/shard_map/ppermute | solution.py:164
  114.4 42.6 %collective-permute-start.10 = (bf16[128,5120]{1,0:T(8,128)(2,1)S(1)}, bf16[128,5120]{1,0:T(8,128)(2,1)}, u32[]{:S(2)}, u32[]{:S(2)}) collective-permute-start(bf16[128,5120]{1,0:T(8,128)(2,1)S(1)} %collective-permute-done.6.own_ref), channel_id=1, source_target_pairs={{0,8},{4,12},{8,24},{12,28},{16,0},{20,4},{24,16},{28,20},{1,9},{5... | collective-permute-start | bytes 3932168 | tf_op jit(solution)/shard_map/ppermute | solution.py:164
  132.5 26.0 %copy-start.3 = (bf16[16,16,2048]{2,1,0:T(8,128)(2,1)S(1)}, bf16[16,16,2048]{2,1,0:T(8,128)(2,1)}, u32[]{:S(2)}) copy-start(bf16[16,16,2048]{2,1,0:T(8,128)(2,1)} %param.24) | copy-start | bytes 3145732
  132.5 27.4 %collective-permute-start.1 = (bf16[128,1024]{1,0:T(8,128)(2,1)S(1)}, bf16[128,1024]{1,0:T(8,128)(2,1)S(1)}, u32[]{:S(2)}, u32[]{:S(2)}) collective-permute-start(bf16[128,1024]{1,0:T(8,128)(2,1)S(1)} %get-tuple-element.12), channel_id=1, source_target_pairs={{0,4},{4,0},{8,12},{12,8},{16,20},{20,16},{24,28},{28,24},{1,5},{5... | collective-permute-start | bytes 786440 | tf_op jit(solution)/shard_map/ppermute | solution.py:164
  134.0 48.9 %collective-permute-start.7 = (bf16[128,5120]{1,0:T(8,128)(2,1)S(1)}, bf16[128,5120]{1,0:T(8,128)(2,1)S(1)}, u32[]{:S(2)}, u32[]{:S(2)}) collective-permute-start(bf16[128,5120]{1,0:T(8,128)(2,1)S(1)} %collective-permute-done.6.own_ref), channel_id=1, source_target_pairs={{0,4},{4,0},{8,12},{12,8},{16,20},{20,16},{24,28},{28,24},{1,5},{5... | collective-permute-start | bytes 3932168 | tf_op jit(solution)/shard_map/ppermute | solution.py:164
  154.6 9.4 %collective-permute-start.4 = (bf16[128,1024]{1,0:T(8,128)(2,1)S(1)}, bf16[128,1024]{1,0:T(8,128)(2,1)S(1)}, u32[]{:S(2)}, u32[]{:S(2)}) collective-permute-start(bf16[128,1024]{1,0:T(8,128)(2,1)S(1)} %get-tuple-element.13), channel_id=1, source_target_pairs={{0,16},{4,20},{8,0},{12,4},{16,24},{20,28},{24,8},{28,12},{1,17},{... | collective-permute-start | bytes 786440 | tf_op jit(solution)/shard_map/ppermute | solution.py:164
  157.0 57.7 %collective-permute-start.11 = (bf16[128,5120]{1,0:T(8,128)(2,1)}, bf16[128,5120]{1,0:T(8,128)(2,1)S(1)}, u32[]{:S(2)}, u32[]{:S(2)}) collective-permute-start(bf16[128,5120]{1,0:T(8,128)(2,1)} %collective-permute-done.10.own_ref), channel_id=1, source_target_pairs={{0,4},{4,0},{8,12},{12,8},{16,20},{20,16},{24,28},{28,24},{1,5},{5... | collective-permute-start | bytes 3932168 | tf_op jit(solution)/shard_map/ppermute | solution.py:164
  159.9 68.7 %collective-permute-start.5 = (bf16[128,1024]{1,0:T(8,128)(2,1)S(1)}, bf16[128,1024]{1,0:T(8,128)(2,1)S(1)}, u32[]{:S(2)}, u32[]{:S(2)}) collective-permute-start(bf16[128,1024]{1,0:T(8,128)(2,1)S(1)} %get-tuple-element.14), channel_id=1, source_target_pairs={{0,20},{4,16},{8,4},{12,0},{16,28},{20,24},{24,12},{28,8},{1,21},{... | collective-permute-start | bytes 786440 | tf_op jit(solution)/shard_map/ppermute | solution.py:164
  193.1 36.9 %collective-permute-start.8 = (bf16[128,1024]{1,0:T(8,128)(2,1)S(1)}, bf16[128,1024]{1,0:T(8,128)(2,1)S(1)}, u32[]{:S(2)}, u32[]{:S(2)}) collective-permute-start(bf16[128,1024]{1,0:T(8,128)(2,1)S(1)} %get-tuple-element.15), channel_id=1, source_target_pairs={{0,24},{4,28},{8,16},{12,20},{16,8},{20,12},{24,0},{28,4},{1,25},{... | collective-permute-start | bytes 786440 | tf_op jit(solution)/shard_map/ppermute | solution.py:164
  195.9 34.1 %collective-permute-start.9 = (bf16[128,1024]{1,0:T(8,128)(2,1)S(1)}, bf16[128,1024]{1,0:T(8,128)(2,1)S(1)}, u32[]{:S(2)}, u32[]{:S(2)}) collective-permute-start(bf16[128,1024]{1,0:T(8,128)(2,1)S(1)} %get-tuple-element.16), channel_id=1, source_target_pairs={{0,28},{4,24},{8,20},{12,16},{16,12},{20,8},{24,4},{28,0},{1,29},{... | collective-permute-start | bytes 786440 | tf_op jit(solution)/shard_map/ppermute | solution.py:164
  225.3 10.2 %collective-permute-start.12 = (bf16[128,1024]{1,0:T(8,128)(2,1)S(1)}, bf16[128,1024]{1,0:T(8,128)(2,1)S(1)}, u32[]{:S(2)}, u32[]{:S(2)}) collective-permute-start(bf16[128,1024]{1,0:T(8,128)(2,1)S(1)} %get-tuple-element.17), channel_id=1, source_target_pairs={{0,8},{4,12},{8,24},{12,28},{16,0},{20,4},{24,16},{28,20},{1,9},{5... | collective-permute-start | bytes 786440 | tf_op jit(solution)/shard_map/ppermute | solution.py:164
  228.7 10.5 %collective-permute-start.13 = (bf16[128,1024]{1,0:T(8,128)(2,1)S(1)}, bf16[128,1024]{1,0:T(8,128)(2,1)S(1)}, u32[]{:S(2)}, u32[]{:S(2)}) collective-permute-start(bf16[128,1024]{1,0:T(8,128)(2,1)S(1)} %get-tuple-element.18), channel_id=1, source_target_pairs={{0,12},{4,8},{8,28},{12,24},{16,4},{20,0},{24,20},{28,16},{1,13},{... | collective-permute-start | bytes 786440 | tf_op jit(solution)/shard_map/ppermute | solution.py:164
  239.3 1.3 copy-start.1
Sparse Core Ops, SparseCore 0:
  10.1 25.5 all-gather.2

commit v3 on v2

v3 whole, which is shorter than its diff:
```python
import functools
import math

import jax
import jax.numpy as jnp
from jax import lax
from jax.experimental import pallas as pl
from jax.experimental.pallas import tpu as pltpu
from jax.sharding import PartitionSpec as P

QUERY_HEADS = 40
KEY_VALUE_HEADS = 8
HEAD_SIZE = 128
PAGE_TOKENS = 16
GROUP_SPLIT = QUERY_HEADS // KEY_VALUE_HEADS
HEAD_CHUNKS = (2, 2, 2, 2)
SEG_ROWS = 16
SCALE_COLUMNS = 128
MASK_FILLER = -1e30
MIB = 1024 * 1024


def ring_order(count):
    return [0] + list(range(1, count, 2)) + list(range((count - 1) // 2 * 2, 0, -2))


def ring_tables(count):
    order = ring_order(count)
    spot = {place: i for i, place in enumerate(order)}
    return [[order[(spot[z] + s) % count] for z in range(count)] for s in range(count)]


def pack_kernel(kv_ref, seg_ref, *out_refs):
    rows = kv_ref.shape[0]
    key_width = KEY_VALUE_HEADS * HEAD_SIZE
    first = 0
    for out_ref, heads in zip(out_refs, HEAD_CHUNKS):
        width = heads * HEAD_SIZE
        out_ref[:rows, :width] = kv_ref[:, first : first + width]
        out_ref[:rows, width:] = kv_ref[:, key_width + first : key_width + first + width]
        first += width
    ids = jnp.broadcast_to(seg_ref[...], (SEG_ROWS, rows)).astype(jnp.float32)
    tail = jnp.concatenate([ids] * (out_refs[0].shape[1] // rows), axis=1)
    out_refs[0][rows:, :] = tail.astype(jnp.bfloat16)


def pack(kv, seg):
    rows = kv.shape[0]
    shapes = [
        jax.ShapeDtypeStruct(
            (rows + (SEG_ROWS if i == 0 else 0), 2 * heads * HEAD_SIZE), jnp.bfloat16
        )
        for i, heads in enumerate(HEAD_CHUNKS)
    ]
    return pl.pallas_call(
        pack_kernel,
        out_shape=shapes,
        cost_estimate=pl.CostEstimate(flops=0, bytes_accessed=4 * kv.size, transcendentals=0),
    )(kv, seg)


def attend_kernel(chunk, shard_count, width_all, *refs):
    heads = HEAD_CHUNKS[chunk]
    first, last = chunk == 0, chunk == len(HEAD_CHUNKS) - 1
    refs = list(refs)
    q_ref, res_ref, gain_ref = refs[:3]
    kv_refs = refs[3 : 3 + shard_count]
    rest = refs[3 + shard_count :]
    rows = q_ref.shape[0]
    if first:
        place_ref, own_seg_ref = rest[:2]
        attended_ref, scaled_ref, square_ref, bias_ref = rest[2:]
        row = lax.broadcasted_iota(jnp.int32, (rows, rows), 0)
        col = lax.broadcasted_iota(jnp.int32, (rows, rows), 1)
        place = place_ref[0]
        for m in range(shard_count):
            ids = kv_refs[m][rows:, :rows].astype(jnp.float32)[:1]
            apart = ((place ^ m) - place) * rows
            live = (own_seg_ref[...] == ids) & (col + apart <= row)
            bias_ref[:, m * rows : (m + 1) * rows] = jnp.where(live, 0.0, MASK_FILLER)
        total = jnp.zeros((rows, 1), jnp.float32)
    else:
        bias_ref, square_in, _ = rest[:3]
        attended_ref, scaled_ref = rest[3:5]
        square_ref = None if last else rest[5]
        total = square_in[:, :1]
    bias = bias_ref[...]
    bias = jnp.concatenate([bias] * GROUP_SPLIT, axis=0)
    for h in range(heads):
        keys = jnp.concatenate(
            [r[:rows, h * HEAD_SIZE : (h + 1) * HEAD_SIZE] for r in kv_refs], axis=0
        )
        values = jnp.concatenate(
            [r[:rows, (heads + h) * HEAD_SIZE : (heads + h + 1) * HEAD_SIZE] for r in kv_refs],
            axis=0,
        )
        base = h * GROUP_SPLIT * HEAD_SIZE
        query = jnp.concatenate(
            [q_ref[:, base + g * HEAD_SIZE : base + (g + 1) * HEAD_SIZE] for g in range(GROUP_SPLIT)],
            axis=0,
        )
        scores = lax.dot_general(
            query, keys, (((1,), (1,)), ((), ())), preferred_element_type=jnp.float32
        )
        scores = scores * (1.0 / math.sqrt(HEAD_SIZE)) + bias
        weights = jnp.exp(scores - jnp.max(scores, axis=1, keepdims=True))
        denominator = jnp.sum(weights, axis=1, keepdims=True)
        summed = jnp.dot(weights.astype(jnp.bfloat16), values, preferred_element_type=jnp.float32)
        attention = (summed / denominator).astype(jnp.bfloat16).astype(jnp.float32)
        for g in range(GROUP_SPLIT):
            columns = slice(base + g * HEAD_SIZE, base + (g + 1) * HEAD_SIZE)
            attended = res_ref[:, columns].astype(jnp.float32) + attention[g * rows : (g + 1) * rows]
            attended = attended.astype(jnp.bfloat16)
            attended_ref[:, columns] = attended
            widened = attended.astype(jnp.float32)
            scaled_ref[:, columns] = (widened * gain_ref[:, columns]).astype(jnp.bfloat16)
            total = total + jnp.sum(widened * widened, axis=1, keepdims=True)
    if last:
        scale = lax.rsqrt(total * (1.0 / width_all) + 1e-06)
        high = scale.astype(jnp.bfloat16)
        low = (scale - high.astype(jnp.float32)).astype(jnp.bfloat16)
        lane = lax.broadcasted_iota(jnp.int32, (rows, SCALE_COLUMNS), 1)
        both = jnp.where(
            lane < SCALE_COLUMNS // 2, high.astype(jnp.float32), low.astype(jnp.float32)
        )
        scaled_ref[:, heads * GROUP_SPLIT * HEAD_SIZE :] = both.astype(jnp.bfloat16)
    else:
        square_ref[...] = jnp.broadcast_to(total, square_ref.shape)


def attend(chunk, queries, residual, gain, kv_chunks, place, own_seg, carried):
    heads = HEAD_CHUNKS[chunk]
    rows, width_all = queries.shape
    first, last = chunk == 0, chunk == len(HEAD_CHUNKS) - 1
    width = heads * GROUP_SPLIT * HEAD_SIZE
    before = sum(HEAD_CHUNKS[:chunk]) * GROUP_SPLIT * HEAD_SIZE
    assert before % width == 0
    shard_count = len(kv_chunks)

    def whole(shape):
        return pl.BlockSpec(shape, lambda i: (0, 0))

    columns = pl.BlockSpec((rows, width), lambda i: (0, before // width))
    in_specs = [columns, columns, pl.BlockSpec((1, width), lambda i: (0, before // width))]
    in_specs += [whole(a.shape) for a in kv_chunks]
    operands = [queries, residual, gain] + list(kv_chunks)
    sent = width + (SCALE_COLUMNS if last else 0)
    shapes = [
        jax.ShapeDtypeStruct((rows, width_all), jnp.bfloat16),
        jax.ShapeDtypeStruct((rows, sent), jnp.bfloat16),
    ]
    out_specs = [columns, whole((rows, sent))]
    square = jax.ShapeDtypeStruct((rows, 128), jnp.float32)
    bias = jax.ShapeDtypeStruct((rows, rows * shard_count), jnp.float32)
    aliases = {}
    if first:
        operands += [place, own_seg]
        in_specs += [pl.BlockSpec(memory_space=pltpu.SMEM), whole(own_seg.shape)]
        shapes += [square, bias]
        out_specs += [whole(square.shape), whole(bias.shape)]
    else:
        attended_so_far, square_so_far, bias_array = carried
        operands += [bias_array, square_so_far, attended_so_far]
        in_specs += [whole(bias.shape), whole(square.shape), pl.BlockSpec(memory_space=pl.ANY)]
        aliases = {len(operands) - 1: 0}
        if not last:
            shapes += [square]
            out_specs += [whole(square.shape)]
    keys = rows * shard_count
    return pl.pallas_call(
        functools.partial(attend_kernel, chunk, shard_count, width_all),
        grid=(1,),
        in_specs=in_specs,
        out_specs=out_specs,
        out_shape=shapes,
        input_output_aliases=aliases,
        compiler_params=pltpu.CompilerParams(vmem_limit_bytes=32 * MIB),
        cost_estimate=pl.CostEstimate(
            flops=4 * rows * width * keys,
            bytes_accessed=8 * rows * width + 4 * keys * heads * HEAD_SIZE,
            transcendentals=rows * keys * heads * GROUP_SPLIT,
        ),
    )(*operands)


def gated_kernel(shard_count, chunk_count, *refs):
    shards = [refs[i * chunk_count : (i + 1) * chunk_count] for i in range(shard_count)]
    rest = refs[shard_count * chunk_count :]
    gate_ref, up_ref = rest[:2]
    out_refs = rest[2 : 2 + shard_count]
    rows_ref, scale_ref = rest[2 + shard_count :]
    rows = shards[0][0].shape[0]

    @pl.when(pl.program_id(0) == 0)
    def _():
        for i, chunks in enumerate(shards):
            span = slice(i * rows, (i + 1) * rows)
            first = 0
            for j, ref in enumerate(chunks):
                width = ref.shape[1] - (SCALE_COLUMNS if j == chunk_count - 1 else 0)
                rows_ref[span, first : first + width] = ref[:, :width]
                first += width
            both = chunks[-1][:, -SCALE_COLUMNS:].astype(jnp.float32)
            scale = both[:, :1] + both[:, SCALE_COLUMNS // 2 : SCALE_COLUMNS // 2 + 1]
            scale_ref[span, :] = jnp.broadcast_to(scale, (rows, 128))

    tokens = rows_ref[...]
    scale = scale_ref[:, :1]
    gate_sum = jnp.dot(tokens, gate_ref[...], preferred_element_type=jnp.float32) * scale
    up_sum = jnp.dot(tokens, up_ref[...], preferred_element_type=jnp.float32) * scale
    made = (gate_sum / (1.0 + jnp.exp(-gate_sum)) * up_sum).astype(jnp.bfloat16)
    for i in range(shard_count):
        out_refs[i][...] = made[i * rows : (i + 1) * rows]


def gated(shards, gate_weight, up_weight):
    rows = shards[0][0].shape[0]
    width, units = gate_weight.shape
    block = 256
    count = len(shards)
    operands = [a for shard in shards for a in shard]
    columns = pl.BlockSpec((width, block), lambda i: (0, i))
    out = pl.BlockSpec((rows, block), lambda i: (0, i))
    shape = jax.ShapeDtypeStruct((rows, units), jnp.bfloat16)
    return pl.pallas_call(
        functools.partial(gated_kernel, count, len(shards[0])),
        grid=(units // block,),
        in_specs=[pl.BlockSpec(a.shape, lambda i: (0, 0)) for a in operands] + [columns] * 2,
        out_specs=[out] * count,
        out_shape=[shape] * count,
        scratch_shapes=[
            pltpu.VMEM((count * rows, width), jnp.bfloat16),
            pltpu.VMEM((count * rows, 128), jnp.float32),
        ],
        compiler_params=pltpu.CompilerParams(vmem_limit_bytes=40 * MIB),
        cost_estimate=pl.CostEstimate(
            flops=4 * count * rows * width * units,
            bytes_accessed=4 * width * units + 2 * count * rows * (width + units),
            transcendentals=count * rows * units,
        ),
    )(*operands, gate_weight, up_weight)


def cache_kernel(page_ref, kv_ref, cache_ref, out_ref, sems):
    slots = out_ref.shape[0]

    def fresh(i, page):
        rows = pl.ds(pl.multiple_of(page * PAGE_TOKENS, PAGE_TOKENS), PAGE_TOKENS)
        return pltpu.make_async_copy(kv_ref.at[rows], out_ref.at[i], sems.at[i])

    def kept(i):
        return pltpu.make_async_copy(cache_ref.at[i], out_ref.at[i], sems.at[i])

    for i in range(slots):
        page = page_ref[i]

        @pl.when(page >= 0)
        def _():
            fresh(i, page).start()

        @pl.when(page < 0)
        def _():
            kept(i).start()

    for i in range(slots):
        kept(i).wait()


def write_cache(pages, kv, cache):
    return pl.pallas_call(
        cache_kernel,
        in_specs=[
            pl.BlockSpec(memory_space=pltpu.SMEM),
            pl.BlockSpec(memory_space=pl.ANY),
            pl.BlockSpec(memory_space=pl.ANY),
        ],
        out_specs=pl.BlockSpec(memory_space=pl.ANY),
        out_shape=jax.ShapeDtypeStruct(cache.shape, cache.dtype),
        scratch_shapes=[pltpu.SemaphoreType.DMA((cache.shape[0],))],
        cost_estimate=pl.CostEstimate(flops=0, bytes_accessed=4 * cache.size, transcendentals=0),
    )(pages, kv, cache)


def on_device(
    queries,
    rotated_keys_values,
    prompt_window_index,
    residual,
    ffn_gain,
    gate_weight,
    up_weight,
    paged_cache,
    page_table,
):
    rows, width = queries.shape
    tok_index = lax.axis_index("tok")
    tok_count = lax.axis_size("tok")
    grp_index = lax.axis_index("grp")
    grp_count = lax.axis_size("grp")
    line, column = grp_index // 2, grp_index % 2
    line_count = grp_count // 2
    ahead = ring_tables(line_count)
    units = gate_weight.shape[1]
    chunks = range(len(HEAD_CHUNKS))

    def swap(array, mask):
        return lax.ppermute(array, "tok", [(t, t ^ mask) for t in range(tok_count)])

    def send(array, steps, flip):
        pairs = []
        for z in range(line_count):
            for y in range(2):
                pairs.append((2 * z + y, 2 * ahead[steps][z] + (1 - y if flip else y)))
        return lax.ppermute(array, "grp", pairs)

    packed = pack(rotated_keys_values, prompt_window_index)
    group_chunks = []
    for c in chunks:
        held = {0: packed[c]}
        mask = tok_count // 2
        while mask:
            held.update({m ^ mask: swap(a, mask) for m, a in held.items()})
            mask //= 2
        group_chunks.append([held[m] for m in range(tok_count)])

    own_seg = jnp.broadcast_to(prompt_window_index[0].astype(jnp.float32)[:, None], (rows, rows))
    place = tok_index.astype(jnp.int32).reshape(1)
    gain = ffn_gain.reshape(1, width)
    scaled, carried = [], None
    for c in chunks:
        made = attend(c, queries, residual, gain, group_chunks[c], place, own_seg, carried)
        if c == 0:
            bias = made[3]
        if c < len(HEAD_CHUNKS) - 1:
            carried = (made[0], made[2], bias)
        scaled.append(made[1])
    attended = made[0]

    late_kv, _ = lax.optimization_barrier((rotated_keys_values, scaled[-1]))
    group_kv = lax.all_gather(late_kv, "tok", axis=0, tiled=True)
    slot_count = paged_cache.shape[0]
    page_count = group_kv.shape[0] // PAGE_TOKENS
    targets = page_table[0, :page_count] - tok_index * slot_count
    onehot = targets[None, :] == jnp.arange(slot_count)[:, None]
    page = jnp.where(onehot, jnp.arange(page_count, dtype=jnp.int32)[None, :] + 1, 0)
    pages = jnp.max(page, axis=1) - 1
    written = write_cache(pages, group_kv, paged_cache)

    hidden = jnp.zeros((rows, grp_count * units), jnp.bfloat16)

    def put(hidden, block, steps, flip):
        source = jnp.asarray(ahead[steps], jnp.int32)[line] * 2 + (1 - column if flip else column)
        return lax.dynamic_update_slice_in_dim(hidden, block, source * units, 1)

    held = scaled
    for step in range(line_count):
        other, following = [], []
        for c in chunks:
            swapped = send(held[c], 0, True)
            if step + 1 < line_count:
                forwarded = send(held[c], 1, False)
                swapped, forwarded = lax.optimization_barrier((swapped, forwarded))
                following.append(forwarded)
            other.append(swapped)
        own_block, other_block = gated([held, other], gate_weight, up_weight)
        if step:
            own_block = send(own_block, line_count - step, False)
        other_block = send(other_block, (line_count - step) % line_count, True)
        hidden = put(hidden, own_block, step, False)
        hidden = put(hidden, other_block, step, True)
        held = following
    return (attended, hidden, written)


def solution(mesh):
    in_specs = (
        P(("grp", "tok"), None),
        P(("grp", "tok"), None),
        P("grp", "tok"),
        P(("grp", "tok"), None),
        P(),
        P(None, "grp"),
        P(None, "grp"),
        P(("grp", "tok"), None, None),
        P("grp", None),
    )
    out_specs = (P(("grp", "tok"), None), P(("grp", "tok"), None), P(("grp", "tok"), None, None))
    return jax.shard_map(
        on_device, mesh=mesh, in_specs=in_specs, out_specs=out_specs, check_vma=False
    )
```

time: 248 us -> 235 us (0.948)
  waiting for transfers between devices: 128 us -> 39 us
  Pallas kernels: 42.2 us -> 84.2 us
  starting transfers between devices: 21.2 us -> 54.5 us
  local copies, waits for them, and re-layouts: 19 us -> 38.9 us
  matrix products: 6.95 us -> 0 us
  other arithmetic: 7.97 us -> 1.35 us
  blocking collectives: 5.95 us -> 0 us
    ppermute x14 -> x35, waiting for transfers between devices: 108 us -> 35.3 us  [send(): return lax.ppermute(array, 'grp', pairs)]
    pallas_call x4 -> x10, Pallas kernels: 42.2 us -> 84.2 us  [the longest x4 40.1 us: gated(): pl.pallas_call(functools.partial(gated_kernel, count, len(shards[0])), gr...]
    ppermute x14 -> x35, starting transfers between devices: 21.1 us -> 48 us  [send(): return lax.ppermute(array, 'grp', pairs)]
    unnamed x23 -> x94, local copies, waits for them, and re-layouts: 4.86 us -> 29.8 us
    all_gather x1, waiting for transfers between devices: 19.4 us -> 0.01 us  [on_device(): group_kv = lax.all_gather(late_kv, 'tok', axis=0, tiled=True)]
    dot_general x3 -> x0, matrix products: 6.95 us -> none  [the longest x1 3.19 us: on_device(): jnp.einsum('qgrk,kgd->qgrd', weights.astype(jnp.bfloat16), rows_of_values...]
    ppermute x0 -> x12, starting transfers between devices: none -> 6.54 us  [swap(): return lax.ppermute(array, 'tok', [(t, t ^ mask) for t in range(tok_count)])]
    all_gather x1 -> x0, blocking collectives: 5.95 us -> none  [on_device(): seg_piece = lax.all_gather(own_segment, 'tok', axis=0, tiled=True)]
  transfers between devices with their start and end apart: 15 -> 48, of which waited for: 9 -> 20; matrix products, arithmetic and copies ran while one was open for 6% -> 4% of each run, Pallas kernels for 17% -> 21%
where the time goes in v3:
time: 235 us; the launch traced here: 234 us
  Pallas kernels  84.2 us (36%)
  starting transfers between devices  54.5 us (23%)
  waiting for transfers between devices  39 us (17%)
  local copies, waits for them, and re-layouts  38.9 us (17%)
  between operations  16.3 us (7%)
    ppermute x35, starting transfers between devices, send(): return lax.ppermute(array, 'grp', pairs)  48 us
    pallas_call x4, Pallas kernels, gated(): pl.pallas_call(functools.partial(gated_kernel, count, len(shards[0])), gr...  40.1 us
    ppermute x35, waiting for transfers between devices, send(): return lax.ppermute(array, 'grp', pairs)  35.3 us
    pallas_call x1, Pallas kernels, write_cache(): pl.pallas_call(cache_kernel, in_specs=[pl.BlockSpec(memory_space=pltpu.SM...  33.7 us
    unnamed x94, local copies, waits for them, and re-layouts  29.8 us
    pallas_call x4, Pallas kernels, attend(): pl.pallas_call(functools.partial(attend_kernel, chunk, shard_count, width...  8.62 us
    ppermute x12, starting transfers between devices, swap(): return lax.ppermute(array, 'tok', [(t, t ^ mask) for t in range(tok_count)])  6.54 us
    dynamic_update_slice x8, local copies, waits for them, and re-layouts, put(): return lax.dynamic_update_slice_in_dim(hidden, block, source * units, 1)  5.76 us
  transfers between devices with their start and end apart: 48, of which 20 were waited for; matrix products, arithmetic and copies ran while one was open for 4% of the time, Pallas kernels for 21%

profile of v3, /device:TPU:0, one launch (start us, length us, event | category | flops | bytes accessed | tf_op | source)
XLA Modules:
  0.0 234.3 jit_solution(4443911126265049360)
XLA Ops:
  7.2 1.9 shard_map.184
  9.1 2.9 %collective-permute-start.4 = (bf16[144,512]{1,0:T(8,128)(2,1)}, bf16[144,512]{1,0:T(8,128)(2,1)S(1)}, u32[]{:S(2)}, u32[]{:S(2)}) collective-permute-start(bf16[144,512]{1,0:T(8,128)(2,1)} %get-tuple-element.53.refs_3_), channel_id=1, source_target_pairs={{0,2},{1,3},{2,0},{3,1},{4,6},{5,7},{6,4},{7,5},{8,10},{9,11},{10,... | collective-permute-start | bytes 442376 | tf_op jit(solution)/shard_map/ppermute | solution.py:307
  12.1 2.0 collective-permute-start.7
  14.1 2.6 %collective-permute-done.4.refs_5_ = bf16[144,512]{1,0:T(8,128)(2,1)S(1)} collective-permute-done((bf16[144,512]{1,0:T(8,128)(2,1)}, bf16[144,512]{1,0:T(8,128)(2,1)S(1)}, u32[]{:S(2)}, u32[]{:S(2)}) %collective-permute-start.4) | collective-permute-done | bytes 147488 | tf_op jit(solution)/shard_map/ppermute | solution.py:307
  18.2 1.3 copy-done.3
  19.5 1.3 copy-done.5
  21.6 0.9 copy-done.35
  22.5 2.1 shard_map.185
  24.6 2.1 collective-permute-start.12
  28.6 2.2 shard_map.186
  30.8 1.6 collective-permute-start.13
  32.9 2.6 %collective-permute-start.15 = (bf16[128,1280]{1,0:T(8,128)(2,1)S(1)}, bf16[128,1280]{1,0:T(8,128)(2,1)}, u32[]{:S(2)}, u32[]{:S(2)}) collective-permute-start(bf16[128,1280]{1,0:T(8,128)(2,1)S(1)} %get-tuple-element.65.refs_1_), channel_id=1, source_target_pairs={{0,8},{4,12},{8,24},{12,28},{16,0},{20,4},{24,16},{28,20},{1,9},{5... | collective-permute-start | bytes 983048 | tf_op jit(solution)/shard_map/ppermute | solution.py:314
  35.5 2.2 shard_map.187
  37.7 1.6 collective-permute-start.16
  39.7 2.2 shard_map.188
  43.7 2.6 %collective-permute-start.19 = (bf16[128,1408]{1,0:T(8,128)(2,1)S(1)}, bf16[128,1408]{1,0:T(8,128)(2,1)S(1)}, u32[]{:S(2)}, u32[]{:S(2)}) collective-permute-start(bf16[128,1408]{1,0:T(8,128)(2,1)S(1)} %get-tuple-element.67.refs_3_), channel_id=1, source_target_pairs={{0,8},{4,12},{8,24},{12,28},{16,0},{20,4},{24,16},{28,20},{1,9},{5... | collective-permute-start | bytes 1081352 | tf_op jit(solution)/shard_map/ppermute | solution.py:314
  46.3 3.1 %collective-permute-done.15.refs_1_ = bf16[128,1280]{1,0:T(8,128)(2,1)} collective-permute-done((bf16[128,1280]{1,0:T(8,128)(2,1)S(1)}, bf16[128,1280]{1,0:T(8,128)(2,1)}, u32[]{:S(2)}, u32[]{:S(2)}) %collective-permute-start.15) | collective-permute-done | bytes 327712 | tf_op jit(solution)/shard_map/ppermute | solution.py:314
  50.7 2.6 %collective-permute-start.22 = (bf16[128,1280]{1,0:T(8,128)(2,1)S(1)}, bf16[128,1280]{1,0:T(8,128)(2,1)}, u32[]{:S(2)}, u32[]{:S(2)}) collective-permute-start(bf16[128,1280]{1,0:T(8,128)(2,1)S(1)} %collective-permute-done.13.refs_0_), channel_id=1, source_target_pairs={{0,8},{4,12},{8,24},{12,28},{16,0},{20,4},{24,16},{28,20},{1,9},{5... | collective-permute-start | bytes 983048 | tf_op jit(solution)/shard_map/ppermute | solution.py:314
  54.1 2.3 collective-permute-done.17.refs_2_
  56.7 1.0 collective-permute-done.18.refs_7_
  58.5 2.6 %collective-permute-start.24 = (bf16[128,1280]{1,0:T(8,128)(2,1)}, bf16[128,1280]{1,0:T(8,128)(2,1)}, u32[]{:S(2)}, u32[]{:S(2)}) collective-permute-start(bf16[128,1280]{1,0:T(8,128)(2,1)} %collective-permute-done.15.refs_1_), channel_id=1, source_target_pairs={{0,8},{4,12},{8,24},{12,28},{16,0},{20,4},{24,16},{28,20},{1,9},{5... | collective-permute-start | bytes 983048 | tf_op jit(solution)/shard_map/ppermute | solution.py:314
  61.0 3.0 %collective-permute-done.19.refs_3_ = bf16[128,1408]{1,0:T(8,128)(2,1)S(1)} collective-permute-done((bf16[128,1408]{1,0:T(8,128)(2,1)S(1)}, bf16[128,1408]{1,0:T(8,128)(2,1)S(1)}, u32[]{:S(2)}, u32[]{:S(2)}) %collective-permute-start.19) | collective-permute-done | bytes 360480 | tf_op jit(solution)/shard_map/ppermute | solution.py:314
  65.5 2.6 %collective-permute-start.26 = (bf16[128,1280]{1,0:T(8,128)(2,1)}, bf16[128,1280]{1,0:T(8,128)(2,1)}, u32[]{:S(2)}, u32[]{:S(2)}) collective-permute-start(bf16[128,1280]{1,0:T(8,128)(2,1)} %collective-permute-done.17.refs_2_), channel_id=1, source_target_pairs={{0,8},{4,12},{8,24},{12,28},{16,0},{20,4},{24,16},{28,20},{1,9},{5... | collective-permute-start | bytes 983048 | tf_op jit(solution)/shard_map/ppermute | solution.py:314
  68.1 3.1 %collective-permute-done.22.refs_0_ = bf16[128,1280]{1,0:T(8,128)(2,1)} collective-permute-done((bf16[128,1280]{1,0:T(8,128)(2,1)S(1)}, bf16[128,1280]{1,0:T(8,128)(2,1)}, u32[]{:S(2)}, u32[]{:S(2)}) %collective-permute-start.22) | collective-permute-done | bytes 327712 | tf_op jit(solution)/shard_map/ppermute | solution.py:314
  72.5 2.6 %collective-permute-start.28 = (bf16[128,1408]{1,0:T(8,128)(2,1)S(1)}, bf16[128,1408]{1,0:T(8,128)(2,1)S(1)}, u32[]{:S(2)}, u32[]{:S(2)}) collective-permute-start(bf16[128,1408]{1,0:T(8,128)(2,1)S(1)} %collective-permute-done.19.refs_3_), channel_id=1, source_target_pairs={{0,8},{4,12},{8,24},{12,28},{16,0},{20,4},{24,16},{28,20},{1,9},{5... | collective-permute-start | bytes 1081352 | tf_op jit(solution)/shard_map/ppermute | solution.py:314
  75.1 4.0 %copy-done = bf16[5120,1024]{1,0:T(8,128)(2,1)S(1)} copy-done((bf16[5120,1024]{1,0:T(8,128)(2,1)S(1)}, bf16[5120,1024]{1,0:T(8,128)(2,1)}, u32[]{:S(2)}) %copy-start) | copy-done | bytes 10485784
  79.1 1.0 copy-done.8
  80.1 1.0 copy-done.10
  81.1 1.0 copy-done.14
  82.1 1.0 copy-done.16
  83.1 1.0 copy-done.20
  84.0 1.0 copy-done.22
  85.0 1.0 copy-done.24
  86.0 1.0 copy-done.28
  86.9 10.2 %shard_map.189 = (bf16[128,1024]{1,0:T(8,128)(2,1)S(1)}, bf16[128,1024]{1,0:T(8,128)(2,1)}) custom-call(bf16[128,1280]{1,0:T(8,128)(2,1)S(1)} %copy-done.14, bf16[128,1280]{1,0:T(8,128)(2,1)S(1)} %copy-done.20, bf16[128,1280]{1,0:T(8,128)(2,1)S(1)} %copy-done.24, bf16[128,1408]{1,0:T(8,128)(2,1)S(1)} %copy-done.8, bf16[128,1280]{1,0:T(8,128)(2,1)S(1)} %copy-done.16, ...), custom_call_target="tpu_custom_call" | custom-call | flops 5368709120 | bytes 24117248 | tf_op jit(solution)/shard_map/pallas_call | solution.py:225
  98.5 1.6 collective-permute-start.31
  100.0 1.4 collective-permute-start.32
  101.5 1.5 collective-permute-start.33
  103.4 1.0 copy-done.18
  104.3 1.0 copy-done.26
  105.3 1.0 copy-done.30
  106.3 10.4 %shard_map.190 = (bf16[128,1024]{1,0:T(8,128)(2,1)}, bf16[128,1024]{1,0:T(8,128)(2,1)S(1)}) custom-call(bf16[128,1280]{1,0:T(8,128)(2,1)S(1)} %copy-done.18, bf16[128,1280]{1,0:T(8,128)(2,1)} %collective-permute-done.15.refs_1_, bf16[128,1280]{1,0:T(8,128)(2,1)} %collective-permute-done.17.refs_2_, bf16[128,1408]{1,0:T(8,128)(2,1)S(1)} %collective-permute-done.19.refs_3_, ...), custom_call_target="tpu_custom_call" | custom-call | flops 5368709120 | bytes 24117248 | tf_op jit(solution)/shard_map/pallas_call | solution.py:225
  119.3 2.5 %collective-permute-start.29 = (bf16[128,1024]{1,0:T(8,128)(2,1)}, bf16[128,1024]{1,0:T(8,128)(2,1)S(1)}, u32[]{:S(2)}, u32[]{:S(2)}) collective-permute-start(bf16[128,1024]{1,0:T(8,128)(2,1)} %get-tuple-element.82), channel_id=1, source_target_pairs={{0,16},{4,20},{8,0},{12,4},{16,24},{20,28},{24,8},{28,12},{1,17},{... | collective-permute-start | bytes 786440 | tf_op jit(solution)/shard_map/ppermute | solution.py:314
  122.3 1.4 collective-permute-start.37
  123.7 0.8 collective-permute-start.38
  128.4 1.5 broadcast_in_dim.25
  131.4 2.2 collective-permute-start.30
  133.5 1.3 collective-permute-done.36.refs_2_
  134.9 0.8 collective-permute-start.41
  135.6 1.5 collective-permute-done.29
  137.1 1.2 collective-permute-start.42
  139.0 0.9 collective-permute-start.43
  139.9 3.0 %collective-permute-done.38.refs_3_ = bf16[128,1408]{1,0:T(8,128)(2,1)S(1)} collective-permute-done((bf16[128,1408]{1,0:T(8,128)(2,1)S(1)}, bf16[128,1408]{1,0:T(8,128)(2,1)S(1)}, u32[]{:S(2)}, u32[]{:S(2)}) %collective-permute-start.38) | collective-permute-done | bytes 360480 | tf_op jit(solution)/shard_map/ppermute | solution.py:314
  142.9 1.1 collective-permute-start.44
  144.0 4.0 %copy-done.2 = bf16[5120,1024]{1,0:T(8,128)(2,1)S(1)} copy-done((bf16[5120,1024]{1,0:T(8,128)(2,1)S(1)}, bf16[5120,1024]{1,0:T(8,128)(2,1)}, u32[]{:S(2)}) %copy-start.2) | copy-done | bytes 10485784
  147.9 9.8 %shard_map.191 = (bf16[128,1024]{1,0:T(8,128)(2,1)S(1)}, bf16[128,1024]{1,0:T(8,128)(2,1)S(1)}) custom-call(bf16[128,1280]{1,0:T(8,128)(2,1)} %collective-permute-done.22.refs_0_, bf16[128,1280]{1,0:T(8,128)(2,1)} %collective-permute-done.24.refs_1_, bf16[128,1280]{1,0:T(8,128)(2,1)} %collective-permute-done.26.refs_2_, ...), custom_call_target="tpu_custom_call" | custom-call | flops 5368709120 | bytes 24117248 | tf_op jit(solution)/shard_map/pallas_call | solution.py:225
  157.8 4.2 %collective-permute-start.39 = (bf16[128,1024]{1,0:T(8,128)(2,1)S(1)}, bf16[128,1024]{1,0:T(8,128)(2,1)S(1)}, u32[]{:S(2)}, u32[]{:S(2)}) collective-permute-start(bf16[128,1024]{1,0:T(8,128)(2,1)S(1)} %get-tuple-element.92), channel_id=1, source_target_pairs={{0,24},{4,28},{8,16},{12,20},{16,8},{20,12},{24,0},{28,4},{1,25},{... | collective-permute-start | bytes 786440 | tf_op jit(solution)/shard_map/ppermute | solution.py:314
  162.7 3.7 %collective-permute-done.43.refs_6_ = bf16[128,1280]{1,0:T(8,128)(2,1)S(1)} collective-permute-done((bf16[128,1280]{1,0:T(8,128)(2,1)S(1)}, bf16[128,1280]{1,0:T(8,128)(2,1)S(1)}, u32[]{:S(2)}, u32[]{:S(2)}) %collective-permute-start.43) | collective-permute-done | bytes 327712 | tf_op jit(solution)/shard_map/ppermute | solution.py:314
  166.4 6.7 %collective-permute-done.44.refs_7_ = bf16[128,1408]{1,0:T(8,128)(2,1)S(1)} collective-permute-done((bf16[128,1408]{1,0:T(8,128)(2,1)S(1)}, bf16[128,1408]{1,0:T(8,128)(2,1)S(1)}, u32[]{:S(2)}, u32[]{:S(2)}) %collective-permute-start.44) | collective-permute-done | bytes 360480 | tf_op jit(solution)/shard_map/ppermute | solution.py:314
  173.0 9.6 %shard_map.192 = (bf16[128,1024]{1,0:T(8,128)(2,1)S(1)}, bf16[128,1024]{1,0:T(8,128)(2,1)S(1)}) custom-call(bf16[128,1280]{1,0:T(8,128)(2,1)} %collective-permute-done.32.refs_0_, bf16[128,1280]{1,0:T(8,128)(2,1)} %collective-permute-done.34.refs_1_, bf16[128,1280]{1,0:T(8,128)(2,1)S(1)} %collective-permute-done.36.refs_2_, ...), custom_call_target="tpu_custom_call" | custom-call | flops 5368709120 | bytes 24117248 | tf_op jit(solution)/shard_map/pallas_call | solution.py:225
  183.5 3.3 %collective-permute-start.46 = (bf16[128,1024]{1,0:T(8,128)(2,1)S(1)}, bf16[128,1024]{1,0:T(8,128)(2,1)S(1)}, u32[]{:S(2)}, u32[]{:S(2)}) collective-permute-start(bf16[128,1024]{1,0:T(8,128)(2,1)S(1)} %get-tuple-element.99), channel_id=1, source_target_pairs={{0,12},{4,8},{8,28},{12,24},{16,4},{20,0},{24,20},{28,16},{1,13},{... | collective-permute-start | bytes 786440 | tf_op jit(solution)/shard_map/ppermute | solution.py:314
  188.2 1.8 collective-permute-done.45
  190.7 2.3 collective-permute-done.46
  193.7 33.7 %shard_map.193 = bf16[16,16,2048]{2,1,0:T(8,128)(2,1)} custom-call(s32[16]{0:T(128)} %broadcast_add_fusion.page_ref, bf16[512,2048]{1,0:T(8,128)(2,1)} %all-gather.2.cloned.1.call-done.kv_ref, bf16[16,16,2048]{2,1,0:T(8,128)(2,1)} %cache_ref.1), custom_call_target="tpu_custom_call" | custom-call | bytes 2097152 | tf_op jit(solution)/shard_map/pallas_call | solution.py:270
  (155 shorter events, 26.1 us)
Async XLA Ops:
  7.2 21.4 %copy-start.32 = (f32[5120]{0:T(1024)S(1)}, f32[5120]{0:T(1024)}, u32[]{:S(2)}) copy-start(f32[5120]{0:T(1024)} %param.21) | copy-start | bytes 61444
  7.2 186.5 %all-gather.2.cloned.1.call-start = ((), (), s32[]{:S(2)}) async-start(), calls=%async_computation | async-start | bytes 2621440 | tf_op jit(solution)/shard_map/all_gather | solution.py:340
  9.1 7.7 %collective-permute-start.4 = (bf16[144,512]{1,0:T(8,128)(2,1)}, bf16[144,512]{1,0:T(8,128)(2,1)S(1)}, u32[]{:S(2)}, u32[]{:S(2)}) collective-permute-start(bf16[144,512]{1,0:T(8,128)(2,1)} %get-tuple-element.53.refs_3_), channel_id=1, source_target_pairs={{0,2},{1,3},{2,0},{3,1},{4,6},{5,7},{6,4},{7,5},{8,10},{9,11},{10,... | collective-permute-start | bytes 442376 | tf_op jit(solution)/shard_map/ppermute | solution.py:307
  12.0 5.4 %collective-permute-start.3 = (bf16[144,512]{1,0:T(8,128)(2,1)}, bf16[144,512]{1,0:T(8,128)(2,1)S(1)}, u32[]{:S(2)}, u32[]{:S(2)}) collective-permute-start(bf16[144,512]{1,0:T(8,128)(2,1)} %get-tuple-element.53.refs_3_), channel_id=1, source_target_pairs={{0,1},{1,0},{2,3},{3,2},{4,5},{5,4},{6,7},{7,6},{8,9},{9,8},{10,11... | collective-permute-start | bytes 442376 | tf_op jit(solution)/shard_map/ppermute | solution.py:307
  12.0 15.2 %collective-permute-start.1 = (bf16[128,512]{1,0:T(8,128)(2,1)}, bf16[128,512]{1,0:T(8,128)(2,1)S(1)}, u32[]{:S(2)}, u32[]{:S(2)}) collective-permute-start(bf16[128,512]{1,0:T(8,128)(2,1)} %get-tuple-element.52.refs_3_), channel_id=1, source_target_pairs={{0,2},{1,3},{2,0},{3,1},{4,6},{5,7},{6,4},{7,5},{8,10},{9,11},{10,... | collective-permute-start | bytes 393224 | tf_op jit(solution)/shard_map/ppermute | solution.py:307
  12.1 15.2 %collective-permute-start.7 = (bf16[128,512]{1,0:T(8,128)(2,1)}, bf16[128,512]{1,0:T(8,128)(2,1)S(1)}, u32[]{:S(2)}, u32[]{:S(2)}) collective-permute-start(bf16[128,512]{1,0:T(8,128)(2,1)} %get-tuple-element.55.refs_3_), channel_id=1, source_target_pairs={{0,2},{1,3},{2,0},{3,1},{4,6},{5,7},{6,4},{7,5},{8,10},{9,11},{10,... | collective-permute-start | bytes 393224 | tf_op jit(solution)/shard_map/ppermute | solution.py:307
  14.1 12.7 %collective-permute-start.10 = (bf16[128,512]{1,0:T(8,128)(2,1)}, bf16[128,512]{1,0:T(8,128)(2,1)S(1)}, u32[]{:S(2)}, u32[]{:S(2)}) collective-permute-start(bf16[128,512]{1,0:T(8,128)(2,1)} %get-tuple-element.56.refs_3_), channel_id=1, source_target_pairs={{0,2},{1,3},{2,0},{3,1},{4,6},{5,7},{6,4},{7,5},{8,10},{9,11},{10,... | collective-permute-start | bytes 393224 | tf_op jit(solution)/shard_map/ppermute | solution.py:307
  16.7 1.4 collective-permute-start.5
  22.5 4.8 %copy-start.37 = (bf16[128,512]{1,0:T(8,128)(2,1)S(1)}, bf16[128,512]{1,0:T(8,128)(2,1)}, u32[]{:S(2)}) copy-start(bf16[128,512]{1,0:T(8,128)(2,1)} %get-tuple-element.55.refs_3_) | copy-start | bytes 393220
  22.5 6.1 %copy-start.4 = (bf16[128,5120]{1,0:T(8,128)(2,1)S(1)}, bf16[128,5120]{1,0:T(8,128)(2,1)}, u32[]{:S(2)}) copy-start(bf16[128,5120]{1,0:T(8,128)(2,1)} %refs_0_.7) | copy-start | bytes 3932164
  22.5 6.1 %copy-start.6 = (bf16[128,5120]{1,0:T(8,128)(2,1)S(1)}, bf16[128,5120]{1,0:T(8,128)(2,1)}, u32[]{:S(2)}) copy-start(bf16[128,5120]{1,0:T(8,128)(2,1)} %refs_1_.7) | copy-start | bytes 3932164
  24.6 6.1 %copy-start.13 = (bf16[128,1280]{1,0:T(8,128)(2,1)}, bf16[128,1280]{1,0:T(8,128)(2,1)S(1)}, u32[]{:S(2)}) copy-start(bf16[128,1280]{1,0:T(8,128)(2,1)S(1)} %get-tuple-element.64.refs_0_) | copy-start | bytes 983044
  24.6 14.6 %collective-permute-start.12 = (bf16[128,1280]{1,0:T(8,128)(2,1)S(1)}, bf16[128,1280]{1,0:T(8,128)(2,1)S(1)}, u32[]{:S(2)}, u32[]{:S(2)}) collective-permute-start(bf16[128,1280]{1,0:T(8,128)(2,1)S(1)} %get-tuple-element.64.refs_0_), channel_id=1, source_target_pairs={{0,4},{4,0},{8,12},{12,8},{16,20},{20,16},{24,28},{28,24},{1,5},{5... | collective-permute-start | bytes 983048 | tf_op jit(solution)/shard_map/ppermute | solution.py:314
  26.7 1.3 collective-permute-start.9
  26.7 1.5 collective-permute-start.11
  27.2 3.5 %collective-permute-start = (bf16[128,512]{1,0:T(8,128)(2,1)S(1)}, bf16[128,512]{1,0:T(8,128)(2,1)S(1)}, u32[]{:S(2)}, u32[]{:S(2)}) collective-permute-start(bf16[128,512]{1,0:T(8,128)(2,1)S(1)} %copy-done.36), channel_id=1, source_target_pairs={{0,1},{1,0},{2,3},{3,2},{4,5},{5,4},{6,7},{7,6},{8,9},{9,8},{10,11... | collective-permute-start | bytes 393224 | tf_op jit(solution)/shard_map/ppermute | solution.py:307
  27.3 5.1 %collective-permute-start.6 = (bf16[128,512]{1,0:T(8,128)(2,1)S(1)}, bf16[128,512]{1,0:T(8,128)(2,1)S(1)}, u32[]{:S(2)}, u32[]{:S(2)}) collective-permute-start(bf16[128,512]{1,0:T(8,128)(2,1)S(1)} %copy-done.37), channel_id=1, source_target_pairs={{0,1},{1,0},{2,3},{3,2},{4,5},{5,4},{6,7},{7,6},{8,9},{9,8},{10,11... | collective-permute-start | bytes 393224 | tf_op jit(solution)/shard_map/ppermute | solution.py:307
  28.1 4.8 %collective-permute-start.8 = (bf16[128,512]{1,0:T(8,128)(2,1)S(1)}, bf16[128,512]{1,0:T(8,128)(2,1)S(1)}, u32[]{:S(2)}, u32[]{:S(2)}) collective-permute-start(bf16[128,512]{1,0:T(8,128)(2,1)S(1)} %collective-permute-done.7.refs_5_), channel_id=1, source_target_pairs={{0,1},{1,0},{2,3},{3,2},{4,5},{5,4},{6,7},{7,6},{8,9},{9,8},{10,11... | collective-permute-start | bytes 393224 | tf_op jit(solution)/shard_map/ppermute | solution.py:307
  28.2 9.4 %collective-permute-start.2 = (bf16[128,512]{1,0:T(8,128)(2,1)S(1)}, bf16[128,512]{1,0:T(8,128)(2,1)S(1)}, u32[]{:S(2)}, u32[]{:S(2)}) collective-permute-start(bf16[128,512]{1,0:T(8,128)(2,1)S(1)} %collective-permute-done.1.refs_5_), channel_id=1, source_target_pairs={{0,1},{1,0},{2,3},{3,2},{4,5},{5,4},{6,7},{7,6},{8,9},{9,8},{10,11... | collective-permute-start | bytes 393224 | tf_op jit(solution)/shard_map/ppermute | solution.py:307
  30.7 6.9 %copy-start.19 = (bf16[128,1280]{1,0:T(8,128)(2,1)}, bf16[128,1280]{1,0:T(8,128)(2,1)S(1)}, u32[]{:S(2)}) copy-start(bf16[128,1280]{1,0:T(8,128)(2,1)S(1)} %get-tuple-element.65.refs_1_) | copy-start | bytes 983044
  30.8 11.5 %collective-permute-start.13 = (bf16[128,1280]{1,0:T(8,128)(2,1)S(1)}, bf16[128,1280]{1,0:T(8,128)(2,1)S(1)}, u32[]{:S(2)}, u32[]{:S(2)}) collective-permute-start(bf16[128,1280]{1,0:T(8,128)(2,1)S(1)} %get-tuple-element.64.refs_0_), channel_id=1, source_target_pairs={{0,8},{4,12},{8,24},{12,28},{16,0},{20,4},{24,16},{28,20},{1,9},{5... | collective-permute-start | bytes 983048 | tf_op jit(solution)/shard_map/ppermute | solution.py:314
  32.4 10.6 %collective-permute-start.14 = (bf16[128,1280]{1,0:T(8,128)(2,1)S(1)}, bf16[128,1280]{1,0:T(8,128)(2,1)S(1)}, u32[]{:S(2)}, u32[]{:S(2)}) collective-permute-start(bf16[128,1280]{1,0:T(8,128)(2,1)S(1)} %get-tuple-element.65.refs_1_), channel_id=1, source_target_pairs={{0,4},{4,0},{8,12},{12,8},{16,20},{20,16},{24,28},{28,24},{1,5},{5... | collective-permute-start | bytes 983048 | tf_op jit(solution)/shard_map/ppermute | solution.py:314
  32.9 16.5 %collective-permute-start.15 = (bf16[128,1280]{1,0:T(8,128)(2,1)S(1)}, bf16[128,1280]{1,0:T(8,128)(2,1)}, u32[]{:S(2)}, u32[]{:S(2)}) collective-permute-start(bf16[128,1280]{1,0:T(8,128)(2,1)S(1)} %get-tuple-element.65.refs_1_), channel_id=1, source_target_pairs={{0,8},{4,12},{8,24},{12,28},{16,0},{20,4},{24,16},{28,20},{1,9},{5... | collective-permute-start | bytes 983048 | tf_op jit(solution)/shard_map/ppermute | solution.py:314
  37.7 12.3 %collective-permute-start.16 = (bf16[128,1280]{1,0:T(8,128)(2,1)S(1)}, bf16[128,1280]{1,0:T(8,128)(2,1)S(1)}, u32[]{:S(2)}, u32[]{:S(2)}) collective-permute-start(bf16[128,1280]{1,0:T(8,128)(2,1)S(1)} %get-tuple-element.66.refs_2_), channel_id=1, source_target_pairs={{0,4},{4,0},{8,12},{12,8},{16,20},{20,16},{24,28},{28,24},{1,5},{5... | collective-permute-start | bytes 983048 | tf_op jit(solution)/shard_map/ppermute | solution.py:314
  39.2 17.2 %collective-permute-start.17 = (bf16[128,1280]{1,0:T(8,128)(2,1)S(1)}, bf16[128,1280]{1,0:T(8,128)(2,1)}, u32[]{:S(2)}, u32[]{:S(2)}) collective-permute-start(bf16[128,1280]{1,0:T(8,128)(2,1)S(1)} %get-tuple-element.66.refs_2_), channel_id=1, source_target_pairs={{0,8},{4,12},{8,24},{12,28},{16,0},{20,4},{24,16},{28,20},{1,9},{5... | collective-permute-start | bytes 983048 | tf_op jit(solution)/shard_map/ppermute | solution.py:314
  39.7 16.8 %copy-start.43 = (s32[1,64]{1,0:T(1,128)S(1)}, s32[1,64]{1,0:T(1,128)}, u32[]{:S(2)}) copy-start(s32[1,64]{1,0:T(1,128)} %param.25) | copy-start | bytes 772
  41.9 29.9 %copy-start.7 = (bf16[128,1408]{1,0:T(8,128)(2,1)}, bf16[128,1408]{1,0:T(8,128)(2,1)S(1)}, u32[]{:S(2)}) copy-start(bf16[128,1408]{1,0:T(8,128)(2,1)S(1)} %get-tuple-element.67.refs_3_) | copy-start | bytes 1081348
  42.3 15.5 %collective-permute-start.18 = (bf16[128,1408]{1,0:T(8,128)(2,1)S(1)}, bf16[128,1408]{1,0:T(8,128)(2,1)S(1)}, u32[]{:S(2)}, u32[]{:S(2)}) collective-permute-start(bf16[128,1408]{1,0:T(8,128)(2,1)S(1)} %get-tuple-element.67.refs_3_), channel_id=1, source_target_pairs={{0,4},{4,0},{8,12},{12,8},{16,20},{20,16},{24,28},{28,24},{1,5},{5... | collective-permute-start | bytes 1081352 | tf_op jit(solution)/shard_map/ppermute | solution.py:314
  43.7 20.3 %collective-permute-start.19 = (bf16[128,1408]{1,0:T(8,128)(2,1)S(1)}, bf16[128,1408]{1,0:T(8,128)(2,1)S(1)}, u32[]{:S(2)}, u32[]{:S(2)}) collective-permute-start(bf16[128,1408]{1,0:T(8,128)(2,1)S(1)} %get-tuple-element.67.refs_3_), channel_id=1, source_target_pairs={{0,8},{4,12},{8,24},{12,28},{16,0},{20,4},{24,16},{28,20},{1,9},{5... | collective-permute-start | bytes 1081352 | tf_op jit(solution)/shard_map/ppermute | solution.py:314
  49.4 15.4 %collective-permute-start.21 = (bf16[128,1280]{1,0:T(8,128)(2,1)S(1)}, bf16[128,1280]{1,0:T(8,128)(2,1)S(1)}, u32[]{:S(2)}, u32[]{:S(2)}) collective-permute-start(bf16[128,1280]{1,0:T(8,128)(2,1)S(1)} %collective-permute-done.13.refs_0_), channel_id=1, source_target_pairs={{0,4},{4,0},{8,12},{12,8},{16,20},{20,16},{24,28},{28,24},{1,5},{5... | collective-permute-start | bytes 983048 | tf_op jit(solution)/shard_map/ppermute | solution.py:314
  50.7 20.4 %collective-permute-start.22 = (bf16[128,1280]{1,0:T(8,128)(2,1)S(1)}, bf16[128,1280]{1,0:T(8,128)(2,1)}, u32[]{:S(2)}, u32[]{:S(2)}) collective-permute-start(bf16[128,1280]{1,0:T(8,128)(2,1)S(1)} %collective-permute-done.13.refs_0_), channel_id=1, source_target_pairs={{0,8},{4,12},{8,24},{12,28},{16,0},{20,4},{24,16},{28,20},{1,9},{5... | collective-permute-start | bytes 983048 | tf_op jit(solution)/shard_map/ppermute | solution.py:314
  56.4 15.4 %collective-permute-start.23 = (bf16[128,1280]{1,0:T(8,128)(2,1)}, bf16[128,1280]{1,0:T(8,128)(2,1)S(1)}, u32[]{:S(2)}, u32[]{:S(2)}) collective-permute-start(bf16[128,1280]{1,0:T(8,128)(2,1)} %collective-permute-done.15.refs_1_), channel_id=1, source_target_pairs={{0,4},{4,0},{8,12},{12,8},{16,20},{20,16},{24,28},{28,24},{1,5},{5... | collective-permute-start | bytes 983048 | tf_op jit(solution)/shard_map/ppermute | solution.py:314
  58.5 39.4 %collective-permute-start.24 = (bf16[128,1280]{1,0:T(8,128)(2,1)}, bf16[128,1280]{1,0:T(8,128)(2,1)}, u32[]{:S(2)}, u32[]{:S(2)}) collective-permute-start(bf16[128,1280]{1,0:T(8,128)(2,1)} %collective-permute-done.15.refs_1_), channel_id=1, source_target_pairs={{0,8},{4,12},{8,24},{12,28},{16,0},{20,4},{24,16},{28,20},{1,9},{5... | collective-permute-start | bytes 983048 | tf_op jit(solution)/shard_map/ppermute | solution.py:314
  64.0 34.5 %collective-permute-start.25 = (bf16[128,1280]{1,0:T(8,128)(2,1)}, bf16[128,1280]{1,0:T(8,128)(2,1)}, u32[]{:S(2)}, u32[]{:S(2)}) collective-permute-start(bf16[128,1280]{1,0:T(8,128)(2,1)} %collective-permute-done.17.refs_2_), channel_id=1, source_target_pairs={{0,4},{4,0},{8,12},{12,8},{16,20},{20,16},{24,28},{28,24},{1,5},{5... | collective-permute-start | bytes 983048 | tf_op jit(solution)/shard_map/ppermute | solution.py:314
  65.5 34.5 %collective-permute-start.26 = (bf16[128,1280]{1,0:T(8,128)(2,1)}, bf16[128,1280]{1,0:T(8,128)(2,1)}, u32[]{:S(2)}, u32[]{:S(2)}) collective-permute-start(bf16[128,1280]{1,0:T(8,128)(2,1)} %collective-permute-done.17.refs_2_), channel_id=1, source_target_pairs={{0,8},{4,12},{8,24},{12,28},{16,0},{20,4},{24,16},{28,20},{1,9},{5... | collective-permute-start | bytes 983048 | tf_op jit(solution)/shard_map/ppermute | solution.py:314
  71.1 30.3 %collective-permute-start.27 = (bf16[128,1408]{1,0:T(8,128)(2,1)S(1)}, bf16[128,1408]{1,0:T(8,128)(2,1)}, u32[]{:S(2)}, u32[]{:S(2)}) collective-permute-start(bf16[128,1408]{1,0:T(8,128)(2,1)S(1)} %collective-permute-done.19.refs_3_), channel_id=1, source_target_pairs={{0,4},{4,0},{8,12},{12,8},{16,20},{20,16},{24,28},{28,24},{1,5},{5... | collective-permute-start | bytes 1081352 | tf_op jit(solution)/shard_map/ppermute | solution.py:314
  72.5 30.5 %collective-permute-start.28 = (bf16[128,1408]{1,0:T(8,128)(2,1)S(1)}, bf16[128,1408]{1,0:T(8,128)(2,1)S(1)}, u32[]{:S(2)}, u32[]{:S(2)}) collective-permute-start(bf16[128,1408]{1,0:T(8,128)(2,1)S(1)} %collective-permute-done.19.refs_3_), channel_id=1, source_target_pairs={{0,8},{4,12},{8,24},{12,28},{16,0},{20,4},{24,16},{28,20},{1,9},{5... | collective-permute-start | bytes 1081352 | tf_op jit(solution)/shard_map/ppermute | solution.py:314
  86.9 16.4 %copy-start.1 = (bf16[5120,1024]{1,0:T(8,128)(2,1)S(1)}, bf16[5120,1024]{1,0:T(8,128)(2,1)}, u32[]{:S(2)}) copy-start(bf16[5120,1024]{1,0:T(8,128)(2,1)} %refs_8_.7) | copy-start | bytes 31457284
  97.9 26.7 %copy-start.46 = (s32[4]{0:T(128)S(1)}, s32[4]{0:T(128)}, u32[]{:S(2)}) copy-start(s32[4]{0:T(128)} %constant.67.clone) | copy-start | bytes 52
  97.9 27.9 %copy-start.45 = (s32[4]{0:T(128)S(1)}, s32[4]{0:T(128)}, u32[]{:S(2)}) copy-start(s32[4]{0:T(128)} %constant.68.clone) | copy-start | bytes 52
  97.9 29.2 %copy-start.44 = (s32[4]{0:T(128)S(1)}, s32[4]{0:T(128)}, u32[]{:S(2)}) copy-start(s32[4]{0:T(128)} %constant.69.clone) | copy-start | bytes 52
  97.9 19.5 %collective-permute-start.20 = (bf16[128,1024]{1,0:T(8,128)(2,1)}, bf16[128,1024]{1,0:T(8,128)(2,1)S(1)}, u32[]{:S(2)}, u32[]{:S(2)}) collective-permute-start(bf16[128,1024]{1,0:T(8,128)(2,1)} %get-tuple-element.73), channel_id=1, source_target_pairs={{0,4},{4,0},{8,12},{12,8},{16,20},{20,16},{24,28},{28,24},{1,5},{5... | collective-permute-start | bytes 786440 | tf_op jit(solution)/shard_map/ppermute | solution.py:314
  98.5 19.5 %collective-permute-start.31 = (bf16[128,1280]{1,0:T(8,128)(2,1)}, bf16[128,1280]{1,0:T(8,128)(2,1)S(1)}, u32[]{:S(2)}, u32[]{:S(2)}) collective-permute-start(bf16[128,1280]{1,0:T(8,128)(2,1)} %collective-permute-done.22.refs_0_), channel_id=1, source_target_pairs={{0,4},{4,0},{8,12},{12,8},{16,20},{20,16},{24,28},{28,24},{1,5},{5... | collective-permute-start | bytes 983048 | tf_op jit(solution)/shard_map/ppermute | solution.py:314
  100.0 19.2 %collective-permute-start.32 = (bf16[128,1280]{1,0:T(8,128)(2,1)}, bf16[128,1280]{1,0:T(8,128)(2,1)}, u32[]{:S(2)}, u32[]{:S(2)}) collective-permute-start(bf16[128,1280]{1,0:T(8,128)(2,1)} %collective-permute-done.22.refs_0_), channel_id=1, source_target_pairs={{0,8},{4,12},{8,24},{12,28},{16,0},{20,4},{24,16},{28,20},{1,9},{5... | collective-permute-start | bytes 983048 | tf_op jit(solution)/shard_map/ppermute | solution.py:314
  101.5 20.9 %collective-permute-start.33 = (bf16[128,1280]{1,0:T(8,128)(2,1)}, bf16[128,1280]{1,0:T(8,128)(2,1)}, u32[]{:S(2)}, u32[]{:S(2)}) collective-permute-start(bf16[128,1280]{1,0:T(8,128)(2,1)} %collective-permute-done.24.refs_1_), channel_id=1, source_target_pairs={{0,4},{4,0},{8,12},{12,8},{16,20},{20,16},{24,28},{28,24},{1,5},{5... | collective-permute-start | bytes 983048 | tf_op jit(solution)/shard_map/ppermute | solution.py:314
  103.0 20.7 %collective-permute-start.34 = (bf16[128,1280]{1,0:T(8,128)(2,1)}, bf16[128,1280]{1,0:T(8,128)(2,1)}, u32[]{:S(2)}, u32[]{:S(2)}) collective-permute-start(bf16[128,1280]{1,0:T(8,128)(2,1)} %collective-permute-done.24.refs_1_), channel_id=1, source_target_pairs={{0,8},{4,12},{8,24},{12,28},{16,0},{20,4},{24,16},{28,20},{1,9},{5... | collective-permute-start | bytes 983048 | tf_op jit(solution)/shard_map/ppermute | solution.py:314
  117.4 12.5 %copy-start.34 = (bf16[128,1024]{1,0:T(8,128)(2,1)S(1)}, bf16[128,1024]{1,0:T(8,128)(2,1)}, u32[]{:S(2)}) copy-start(bf16[128,1024]{1,0:T(8,128)(2,1)} %copy-done.33) | copy-start | bytes 786436
  117.4 13.9 %copy-start.40 = (bf16[128,1024]{1,0:T(8,128)(2,1)S(1)}, bf16[128,1024]{1,0:T(8,128)(2,1)}, u32[]{:S(2)}) copy-start(bf16[128,1024]{1,0:T(8,128)(2,1)} %copy-done.39) | copy-start | bytes 786436
  117.4 13.9 %collective-permute-start.35 = (bf16[128,1280]{1,0:T(8,128)(2,1)}, bf16[128,1280]{1,0:T(8,128)(2,1)S(1)}, u32[]{:S(2)}, u32[]{:S(2)}) collective-permute-start(bf16[128,1280]{1,0:T(8,128)(2,1)} %collective-permute-done.26.refs_2_), channel_id=1, source_target_pairs={{0,4},{4,0},{8,12},{12,8},{16,20},{20,16},{24,28},{28,24},{1,5},{5... | collective-permute-start | bytes 983048 | tf_op jit(solution)/shard_map/ppermute | solution.py:314
  118.8 16.0 %collective-permute-start.36 = (bf16[128,1280]{1,0:T(8,128)(2,1)}, bf16[128,1280]{1,0:T(8,128)(2,1)S(1)}, u32[]{:S(2)}, u32[]{:S(2)}) collective-permute-start(bf16[128,1280]{1,0:T(8,128)(2,1)} %collective-permute-done.26.refs_2_), channel_id=1, source_target_pairs={{0,8},{4,12},{8,24},{12,28},{16,0},{20,4},{24,16},{28,20},{1,9},{5... | collective-permute-start | bytes 983048 | tf_op jit(solution)/shard_map/ppermute | solution.py:314
  119.2 11.4 %copy-start.42 = (bf16[128,1024]{1,0:T(8,128)(2,1)S(1)}, bf16[128,1024]{1,0:T(8,128)(2,1)}, u32[]{:S(2)}) copy-start(bf16[128,1024]{1,0:T(8,128)(2,1)} %copy-done.41) | copy-start | bytes 786436
  119.2 24.7 %copy-start.12 = (bf16[128,1280]{1,0:T(8,128)(2,1)S(1)}, bf16[128,1280]{1,0:T(8,128)(2,1)}, u32[]{:S(2)}) copy-start(bf16[128,1280]{1,0:T(8,128)(2,1)} %copy-done.11) | copy-start | bytes 983044
  119.3 17.9 %collective-permute-start.29 = (bf16[128,1024]{1,0:T(8,128)(2,1)}, bf16[128,1024]{1,0:T(8,128)(2,1)S(1)}, u32[]{:S(2)}, u32[]{:S(2)}) collective-permute-start(bf16[128,1024]{1,0:T(8,128)(2,1)} %get-tuple-element.82), channel_id=1, source_target_pairs={{0,16},{4,20},{8,0},{12,4},{16,24},{20,28},{24,8},{28,12},{1,17},{... | collective-permute-start | bytes 786440 | tf_op jit(solution)/shard_map/ppermute | solution.py:314
  122.3 16.7 %collective-permute-start.37 = (bf16[128,1408]{1,0:T(8,128)(2,1)S(1)}, bf16[128,1408]{1,0:T(8,128)(2,1)S(1)}, u32[]{:S(2)}, u32[]{:S(2)}) collective-permute-start(bf16[128,1408]{1,0:T(8,128)(2,1)S(1)} %collective-permute-done.28.refs_3_), channel_id=1, source_target_pairs={{0,4},{4,0},{8,12},{12,8},{16,20},{20,16},{24,28},{28,24},{1,5},{5... | collective-permute-start | bytes 1081352 | tf_op jit(solution)/shard_map/ppermute | solution.py:314
  123.7 19.1 %collective-permute-start.38 = (bf16[128,1408]{1,0:T(8,128)(2,1)S(1)}, bf16[128,1408]{1,0:T(8,128)(2,1)S(1)}, u32[]{:S(2)}, u32[]{:S(2)}) collective-permute-start(bf16[128,1408]{1,0:T(8,128)(2,1)S(1)} %collective-permute-done.28.refs_3_), channel_id=1, source_target_pairs={{0,8},{4,12},{8,24},{12,28},{16,0},{20,4},{24,16},{28,20},{1,9},{5... | collective-permute-start | bytes 1081352 | tf_op jit(solution)/shard_map/ppermute | solution.py:314
  131.4 51.4 %collective-permute-start.30 = (bf16[128,1024]{1,0:T(8,128)(2,1)S(1)}, bf16[128,1024]{1,0:T(8,128)(2,1)S(1)}, u32[]{:S(2)}, u32[]{:S(2)}) collective-permute-start(bf16[128,1024]{1,0:T(8,128)(2,1)S(1)} %copy-done.40), channel_id=1, source_target_pairs={{0,20},{4,16},{8,4},{12,0},{16,28},{20,24},{24,12},{28,8},{1,21},{... | collective-permute-start | bytes 786440 | tf_op jit(solution)/shard_map/ppermute | solution.py:314
  134.9 22.9 %collective-permute-start.41 = (bf16[128,1280]{1,0:T(8,128)(2,1)}, bf16[128,1280]{1,0:T(8,128)(2,1)S(1)}, u32[]{:S(2)}, u32[]{:S(2)}) collective-permute-start(bf16[128,1280]{1,0:T(8,128)(2,1)} %collective-permute-done.32.refs_0_), channel_id=1, source_target_pairs={{0,4},{4,0},{8,12},{12,8},{16,20},{20,16},{24,28},{28,24},{1,5},{5... | collective-permute-start | bytes 983048 | tf_op jit(solution)/shard_map/ppermute | solution.py:314
  137.1 24.9 %collective-permute-start.42 = (bf16[128,1280]{1,0:T(8,128)(2,1)}, bf16[128,1280]{1,0:T(8,128)(2,1)S(1)}, u32[]{:S(2)}, u32[]{:S(2)}) collective-permute-start(bf16[128,1280]{1,0:T(8,128)(2,1)} %collective-permute-done.34.refs_1_), channel_id=1, source_target_pairs={{0,4},{4,0},{8,12},{12,8},{16,20},{20,16},{24,28},{28,24},{1,5},{5... | collective-permute-start | bytes 983048 | tf_op jit(solution)/shard_map/ppermute | solution.py:314
  139.0 27.3 %collective-permute-start.43 = (bf16[128,1280]{1,0:T(8,128)(2,1)S(1)}, bf16[128,1280]{1,0:T(8,128)(2,1)S(1)}, u32[]{:S(2)}, u32[]{:S(2)}) collective-permute-start(bf16[128,1280]{1,0:T(8,128)(2,1)S(1)} %collective-permute-done.36.refs_2_), channel_id=1, source_target_pairs={{0,4},{4,0},{8,12},{12,8},{16,20},{20,16},{24,28},{28,24},{1,5},{5... | collective-permute-start | bytes 983048 | tf_op jit(solution)/shard_map/ppermute | solution.py:314
  142.9 30.2 %collective-permute-start.44 = (bf16[128,1408]{1,0:T(8,128)(2,1)S(1)}, bf16[128,1408]{1,0:T(8,128)(2,1)S(1)}, u32[]{:S(2)}, u32[]{:S(2)}) collective-permute-start(bf16[128,1408]{1,0:T(8,128)(2,1)S(1)} %collective-permute-done.38.refs_3_), channel_id=1, source_target_pairs={{0,4},{4,0},{8,12},{12,8},{16,20},{20,16},{24,28},{28,24},{1,5},{5... | collective-permute-start | bytes 1081352 | tf_op jit(solution)/shard_map/ppermute | solution.py:314
  157.8 29.0 %collective-permute-start.39 = (bf16[128,1024]{1,0:T(8,128)(2,1)S(1)}, bf16[128,1024]{1,0:T(8,128)(2,1)S(1)}, u32[]{:S(2)}, u32[]{:S(2)}) collective-permute-start(bf16[128,1024]{1,0:T(8,128)(2,1)S(1)} %get-tuple-element.92), channel_id=1, source_target_pairs={{0,24},{4,28},{8,16},{12,20},{16,8},{20,12},{24,0},{28,4},{1,25},{... | collective-permute-start | bytes 786440 | tf_op jit(solution)/shard_map/ppermute | solution.py:314
  162.0 25.4 %collective-permute-start.40 = (bf16[128,1024]{1,0:T(8,128)(2,1)S(1)}, bf16[128,1024]{1,0:T(8,128)(2,1)S(1)}, u32[]{:S(2)}, u32[]{:S(2)}) collective-permute-start(bf16[128,1024]{1,0:T(8,128)(2,1)S(1)} %get-tuple-element.93), channel_id=1, source_target_pairs={{0,28},{4,24},{8,20},{12,16},{16,12},{20,8},{24,4},{28,0},{1,29},{... | collective-permute-start | bytes 786440 | tf_op jit(solution)/shard_map/ppermute | solution.py:314
  182.7 7.3 %collective-permute-start.45 = (bf16[128,1024]{1,0:T(8,128)(2,1)S(1)}, bf16[128,1024]{1,0:T(8,128)(2,1)S(1)}, u32[]{:S(2)}, u32[]{:S(2)}) collective-permute-start(bf16[128,1024]{1,0:T(8,128)(2,1)S(1)} %get-tuple-element.98), channel_id=1, source_target_pairs={{0,8},{4,12},{8,24},{12,28},{16,0},{20,4},{24,16},{28,20},{1,9},{5... | collective-permute-start | bytes 786440 | tf_op jit(solution)/shard_map/ppermute | solution.py:314
  183.5 9.5 %collective-permute-start.46 = (bf16[128,1024]{1,0:T(8,128)(2,1)S(1)}, bf16[128,1024]{1,0:T(8,128)(2,1)S(1)}, u32[]{:S(2)}, u32[]{:S(2)}) collective-permute-start(bf16[128,1024]{1,0:T(8,128)(2,1)S(1)} %get-tuple-element.99), channel_id=1, source_target_pairs={{0,12},{4,8},{8,28},{12,24},{16,4},{20,0},{24,20},{28,16},{1,13},{... | collective-permute-start | bytes 786440 | tf_op jit(solution)/shard_map/ppermute | solution.py:314
  (31 other events, 46.2 us)
Sparse Core Ops, SparseCore 0:
  56.8 24.3 all-gather.1

commit v4 on v3

--- a/solution.py
+++ b/solution.py
@@ -17,7 +17,7 @@
 SEG_ROWS = 16
 SCALE_COLUMNS = 128
 MASK_FILLER = -1e30
-MIB = 1024 * 1024
+VMEM_LIMIT = 60 * 1024 * 1024
 
 
 def ring_order(count):
@@ -55,6 +55,7 @@
     return pl.pallas_call(
         pack_kernel,
         out_shape=shapes,
+        compiler_params=pltpu.CompilerParams(vmem_limit_bytes=VMEM_LIMIT),
         cost_estimate=pl.CostEstimate(flops=0, bytes_accessed=4 * kv.size, transcendentals=0),
     )(kv, seg)
 
@@ -174,7 +175,7 @@
         out_specs=out_specs,
         out_shape=shapes,
         input_output_aliases=aliases,
-        compiler_params=pltpu.CompilerParams(vmem_limit_bytes=32 * MIB),
+        compiler_params=pltpu.CompilerParams(vmem_limit_bytes=VMEM_LIMIT),
         cost_estimate=pl.CostEstimate(
             flops=4 * rows * width * keys,
             bytes_accessed=8 * rows * width + 4 * keys * heads * HEAD_SIZE,
@@ -232,7 +233,7 @@
             pltpu.VMEM((count * rows, width), jnp.bfloat16),
             pltpu.VMEM((count * rows, 128), jnp.float32),
         ],
-        compiler_params=pltpu.CompilerParams(vmem_limit_bytes=40 * MIB),
+        compiler_params=pltpu.CompilerParams(vmem_limit_bytes=VMEM_LIMIT),
         cost_estimate=pl.CostEstimate(
             flops=4 * count * rows * width * units,
             bytes_accessed=4 * width * units + 2 * count * rows * (width + units),
@@ -241,29 +242,18 @@
     )(*operands, gate_weight, up_weight)
 
 
-def cache_kernel(page_ref, kv_ref, cache_ref, out_ref, sems):
-    slots = out_ref.shape[0]
-
-    def fresh(i, page):
-        rows = pl.ds(pl.multiple_of(page * PAGE_TOKENS, PAGE_TOKENS), PAGE_TOKENS)
-        return pltpu.make_async_copy(kv_ref.at[rows], out_ref.at[i], sems.at[i])
-
-    def kept(i):
-        return pltpu.make_async_copy(cache_ref.at[i], out_ref.at[i], sems.at[i])
-
-    for i in range(slots):
+def cache_kernel(page_ref, kv_ref, cache_ref, out_ref):
+    for i in range(out_ref.shape[0]):
         page = page_ref[i]
 
         @pl.when(page >= 0)
         def _():
-            fresh(i, page).start()
+            first = pl.multiple_of(jnp.maximum(page, 0) * PAGE_TOKENS, PAGE_TOKENS)
+            out_ref[i] = kv_ref[pl.ds(first, PAGE_TOKENS), :]
 
         @pl.when(page < 0)
         def _():
-            kept(i).start()
-
-    for i in range(slots):
-        kept(i).wait()
+            out_ref[i] = cache_ref[i]
 
 
 def write_cache(pages, kv, cache):
@@ -271,13 +261,13 @@
         cache_kernel,
         in_specs=[
             pl.BlockSpec(memory_space=pltpu.SMEM),
-            pl.BlockSpec(memory_space=pl.ANY),
-            pl.BlockSpec(memory_space=pl.ANY),
+            pl.BlockSpec(memory_space=pltpu.VMEM),
+            pl.BlockSpec(memory_space=pltpu.VMEM),
         ],
-        out_specs=pl.BlockSpec(memory_space=pl.ANY),
+        out_specs=pl.BlockSpec(memory_space=pltpu.VMEM),
         out_shape=jax.ShapeDtypeStruct(cache.shape, cache.dtype),
-        scratch_shapes=[pltpu.SemaphoreType.DMA((cache.shape[0],))],
-        cost_estimate=pl.CostEstimate(flops=0, bytes_accessed=4 * cache.size, transcendentals=0),
+        compiler_params=pltpu.CompilerParams(vmem_limit_bytes=VMEM_LIMIT),
+        cost_estimate=pl.CostEstimate(flops=0, bytes_accessed=8 * cache.size, transcendentals=0),
     )(pages, kv, cache)
 
 
@@ -349,7 +339,8 @@
     hidden = jnp.zeros((rows, grp_count * units), jnp.bfloat16)
 
     def put(hidden, block, steps, flip):
-        source = jnp.asarray(ahead[steps], jnp.int32)[line] * 2 + (1 - column if flip else column)
+        source = sum(jnp.where(line == z, ahead[steps][z] * 2, 0) for z in range(line_count))
+        source = source + (1 - column if flip else column)
         return lax.dynamic_update_slice_in_dim(hidden, block, source * units, 1)
 
     held = scaled
@@ -362,7 +353,12 @@
                 swapped, forwarded = lax.optimization_barrier((swapped, forwarded))
                 following.append(forwarded)
             other.append(swapped)
-        own_block, other_block = gated([held, other], gate_weight, up_weight)
+        if step + 1 < line_count:
+            own_block, other_block = gated([held, other], gate_weight, up_weight)
+        else:
+            (own_block,) = gated([held], gate_weight, up_weight)
+            other[-1], written = lax.optimization_barrier((other[-1], written))
+            (other_block,) = gated([other], gate_weight, up_weight)
         if step:
             own_block = send(own_block, line_count - step, False)
         other_block = send(other_block, (line_count - step) % line_count, True)

time: 235 us -> 203 us (0.86)
  local copies, waits for them, and re-layouts: 38.9 us -> 7.96 us
  waiting for transfers between devices: 39 us -> 58.5 us
  Pallas kernels: 84.2 us -> 73.9 us
  starting transfers between devices: 54.5 us -> 46.8 us
    pallas_call x1, Pallas kernels: 33.7 us -> 3.13 us  [write_cache(): pl.pallas_call(cache_kernel, in_specs=[pl.BlockSpec(memory_space=pltpu.SM...]
    unnamed x94 -> x80, local copies, waits for them, and re-layouts: 29.8 us -> 3.08 us
    ppermute x35, waiting for transfers between devices: 35.3 us -> 51.5 us  [send(): return lax.ppermute(array, 'grp', pairs)]
    pallas_call x4 -> x5, Pallas kernels: 40.1 us -> 54.6 us  [gated(): pl.pallas_call(functools.partial(gated_kernel, count, len(shards[0])), gr...]
    ppermute x35, starting transfers between devices: 48 us -> 38.4 us  [send(): return lax.ppermute(array, 'grp', pairs)]
    pallas_call x4, Pallas kernels: 8.62 us -> 14.4 us  [attend(): pl.pallas_call(functools.partial(attend_kernel, chunk, shard_count, width...]
    ppermute x12, waiting for transfers between devices: 3.68 us -> 6.96 us  [swap(): return lax.ppermute(array, 'tok', [(t, t ^ mask) for t in range(tok_count)])]
  transfers between devices with their start and end apart: 48 -> 48, of which waited for: 20 -> 12; matrix products, arithmetic and copies ran while one was open for 4% -> 3% of each run, Pallas kernels for 21% -> 36%
where the time goes in v4:
time: 203 us
  Pallas kernels  73.9 us (36%)
  waiting for transfers between devices  58.5 us (29%)
  starting transfers between devices  46.8 us (23%)
  between operations  14.4 us (7%)
  local copies, waits for them, and re-layouts  7.96 us (4%)
    pallas_call x5, Pallas kernels, gated(): pl.pallas_call(functools.partial(gated_kernel, count, len(shards[0])), gr...  54.6 us
    ppermute x35, waiting for transfers between devices, send(): return lax.ppermute(array, 'grp', pairs)  51.5 us
    ppermute x35, starting transfers between devices, send(): return lax.ppermute(array, 'grp', pairs)  38.4 us
    pallas_call x4, Pallas kernels, attend(): pl.pallas_call(functools.partial(attend_kernel, chunk, shard_count, width...  14.4 us
    ppermute x12, starting transfers between devices, swap(): return lax.ppermute(array, 'tok', [(t, t ^ mask) for t in range(tok_count)])  8.44 us
    ppermute x12, waiting for transfers between devices, swap(): return lax.ppermute(array, 'tok', [(t, t ^ mask) for t in range(tok_count)])  6.96 us
  transfers between devices with their start and end apart: 48, of which 12 were waited for; matrix products, arithmetic and copies ran while one was open for 3% of the time, Pallas kernels for 36%

profile of v4, /device:TPU:0, one launch (start us, length us, event | category | flops | bytes accessed | tf_op | source)
XLA Modules:
  0.0 202.9 jit_solution(17314287552287158685)
XLA Ops:
  7.2 1.9 shard_map.112
  9.5 2.5 %collective-permute-start.4 = (bf16[144,512]{1,0:T(8,128)(2,1)}, bf16[144,512]{1,0:T(8,128)(2,1)S(1)}, u32[]{:S(2)}, u32[]{:S(2)}) collective-permute-start(bf16[144,512]{1,0:T(8,128)(2,1)} %get-tuple-element.53.refs_3_), channel_id=1, source_target_pairs={{0,2},{1,3},{2,0},{3,1},{4,6},{5,7},{6,4},{7,5},{8,10},{9,11},{10,... | collective-permute-start | bytes 442376 | tf_op jit(solution)/shard_map/ppermute | solution.py:297
  12.3 1.8 collective-permute-start.1
  14.0 5.7 %collective-permute-done.10.refs_5_ = bf16[128,512]{1,0:T(8,128)(2,1)S(1)} collective-permute-done((bf16[128,512]{1,0:T(8,128)(2,1)}, bf16[128,512]{1,0:T(8,128)(2,1)S(1)}, u32[]{:S(2)}, u32[]{:S(2)}) %collective-permute-start.10) | collective-permute-done | bytes 131104 | tf_op jit(solution)/shard_map/ppermute | solution.py:297
  19.7 1.9 collective-permute-start.7
  21.7 0.5 collective-permute-start.5
  22.2 0.7 convert_bitcast_fusion
  23.2 0.7 broadcast_in_dim.24.refs_8_
  24.0 3.6 %shard_map.113 = (bf16[128,5120]{1,0:T(8,128)(2,1)}, bf16[128,1280]{1,0:T(8,128)(2,1)}, f32[128,128]{1,0:T(8,128)}, f32[128,512]{1,0:T(8,128)}) custom-call(bf16[128,5120]{1,0:T(8,128)(2,1)} %refs_0_.7, bf16[128,5120]{1,0:T(8,128)(2,1)} %refs_1_.7, f32[1,5120]{1,0:T(1,128)} %bitcast.6, bf16[144,512]{1,0:T(8,128)(2,1)} %get-tuple-element.53.refs_3_, ...), custom_call_target="tpu_custom_call" | custom-call | flops 335544320 | bytes 1835008 | tf_op jit(solution)/shard_map/pallas_call | solution.py:171
  27.5 1.5 collective-permute-start.12
  29.0 1.6 collective-permute-start.13
  30.6 0.6 copy-done.34
  31.3 3.6 %shard_map.114 = (bf16[128,5120]{1,0:T(8,128)(2,1)}, bf16[128,1280]{1,0:T(8,128)(2,1)}, f32[128,128]{1,0:T(8,128)}) custom-call(bf16[128,5120]{1,0:T(8,128)(2,1)} %refs_0_.7, bf16[128,5120]{1,0:T(8,128)(2,1)} %refs_1_.7, f32[1,5120]{1,0:T(1,128)} %bitcast.7, bf16[128,512]{1,0:T(8,128)(2,1)} %get-tuple-element.56.refs_3_, ...), custom_call_target="tpu_custom_call", output_to_operand_aliasing={{0}: (9, {})} | custom-call | flops 335544320 | bytes 1835008 | tf_op jit(solution)/shard_map/pallas_call | solution.py:171
  34.9 0.5 collective-permute-start.14
  35.5 0.5 collective-permute-start.8
  36.0 0.8 collective-permute-done.6.refs_4_
  37.6 3.5 %shard_map.115 = (bf16[128,5120]{1,0:T(8,128)(2,1)}, bf16[128,1280]{1,0:T(8,128)(2,1)}, f32[128,128]{1,0:T(8,128)}) custom-call(bf16[128,5120]{1,0:T(8,128)(2,1)} %refs_0_.7, bf16[128,5120]{1,0:T(8,128)(2,1)} %refs_1_.7, f32[1,5120]{1,0:T(1,128)} %bitcast.8, bf16[128,512]{1,0:T(8,128)(2,1)} %get-tuple-element.55.refs_3_, ...), custom_call_target="tpu_custom_call", output_to_operand_aliasing={{0}: (9, {})} | custom-call | flops 335544320 | bytes 1835008 | tf_op jit(solution)/shard_map/pallas_call | solution.py:171
  41.2 0.6 copy-done.36
  41.9 3.7 %shard_map.116 = (bf16[128,5120]{1,0:T(8,128)(2,1)}, bf16[128,1408]{1,0:T(8,128)(2,1)}) custom-call(bf16[128,5120]{1,0:T(8,128)(2,1)} %refs_0_.7, bf16[128,5120]{1,0:T(8,128)(2,1)} %refs_1_.7, f32[1,5120]{1,0:T(1,128)} %bitcast.9, bf16[128,512]{1,0:T(8,128)(2,1)} %get-tuple-element.52.refs_3_, ...), custom_call_target="tpu_custom_call", output_to_operand_aliasing={{0}: (9, {})} | custom-call | flops 335544320 | bytes 1835008 | tf_op jit(solution)/shard_map/pallas_call | solution.py:171
  45.5 1.5 collective-permute-start.18
  47.1 2.6 %collective-permute-start.19 = (bf16[128,1408]{1,0:T(8,128)(2,1)}, bf16[128,1408]{1,0:T(8,128)(2,1)S(1)}, u32[]{:S(2)}, u32[]{:S(2)}) collective-permute-start(bf16[128,1408]{1,0:T(8,128)(2,1)} %get-tuple-element.67.refs_3_), channel_id=1, source_target_pairs={{0,8},{4,12},{8,24},{12,28},{16,0},{20,4},{24,16},{28,20},{1,9},{5... | collective-permute-start | bytes 1081352 | tf_op jit(solution)/shard_map/ppermute | solution.py:304
  49.7 0.5 collective-permute-start.15
  50.2 0.6 collective-permute-start.16
  51.1 15.3 %collective-permute-done.15.refs_1_ = bf16[128,1280]{1,0:T(8,128)(2,1)S(1)} collective-permute-done((bf16[128,1280]{1,0:T(8,128)(2,1)S(1)}, bf16[128,1280]{1,0:T(8,128)(2,1)S(1)}, u32[]{:S(2)}, u32[]{:S(2)}) %collective-permute-start.15) | collective-permute-done | bytes 327712 | tf_op jit(solution)/shard_map/ppermute | solution.py:304
  66.5 0.5 collective-permute-start.21
  67.0 1.7 collective-permute-start.22
  68.7 4.9 %collective-permute-done.17.refs_2_ = bf16[128,1280]{1,0:T(8,128)(2,1)} collective-permute-done((bf16[128,1280]{1,0:T(8,128)(2,1)S(1)}, bf16[128,1280]{1,0:T(8,128)(2,1)}, u32[]{:S(2)}, u32[]{:S(2)}) %collective-permute-start.17) | collective-permute-done | bytes 327712 | tf_op jit(solution)/shard_map/ppermute | solution.py:304
  73.6 0.5 collective-permute-start.23
  74.1 1.7 collective-permute-start.24
  75.8 1.5 collective-permute-start.25
  77.3 11.7 %shard_map.117 = (bf16[128,1024]{1,0:T(8,128)(2,1)}, bf16[128,1024]{1,0:T(8,128)(2,1)}) custom-call(bf16[128,1280]{1,0:T(8,128)(2,1)} %get-tuple-element.64.refs_0_, bf16[128,1280]{1,0:T(8,128)(2,1)} %get-tuple-element.65.refs_1_, bf16[128,1280]{1,0:T(8,128)(2,1)} %get-tuple-element.66.refs_2_, bf16[128,1408]{1,0:T(8,128)(2,1)} %get-tuple-element.67.refs_3_, ...), custom_call_target="tpu_custom_call" | custom-call | flops 5368709120 | bytes 24117248 | tf_op jit(solution)/shard_map/pallas_call | solution.py:226
  89.1 1.4 collective-permute-start.26
  90.5 0.5 collective-permute-start.27
  91.2 1.4 collective-permute-start.20
  92.8 0.7 collective-permute-start.31
  93.5 7.5 %collective-permute-done.26.refs_2_ = bf16[128,1280]{1,0:T(8,128)(2,1)} collective-permute-done((bf16[128,1280]{1,0:T(8,128)(2,1)}, bf16[128,1280]{1,0:T(8,128)(2,1)}, u32[]{:S(2)}, u32[]{:S(2)}) %collective-permute-start.26) | collective-permute-done | bytes 327712 | tf_op jit(solution)/shard_map/ppermute | solution.py:304
  101.8 0.5 collective-permute-start.33
  102.3 6.3 %collective-permute-done.28.refs_3_ = bf16[128,1408]{1,0:T(8,128)(2,1)S(1)} collective-permute-done((bf16[128,1408]{1,0:T(8,128)(2,1)S(1)}, bf16[128,1408]{1,0:T(8,128)(2,1)S(1)}, u32[]{:S(2)}, u32[]{:S(2)}) %collective-permute-start.28) | collective-permute-done | bytes 360480 | tf_op jit(solution)/shard_map/ppermute | solution.py:304
  109.1 0.5 collective-permute-start.35
  109.6 11.7 %shard_map.118 = (bf16[128,1024]{1,0:T(8,128)(2,1)}, bf16[128,1024]{1,0:T(8,128)(2,1)}) custom-call(bf16[128,1280]{1,0:T(8,128)(2,1)} %copy-done.17, bf16[128,1280]{1,0:T(8,128)(2,1)} %copy-done.19, bf16[128,1280]{1,0:T(8,128)(2,1)} %collective-permute-done.17.refs_2_, bf16[128,1408]{1,0:T(8,128)(2,1)} %copy-done.2, bf16[128,1280]{1,0:T(8,128)(2,1)} %copy-done.22, ...), custom_call_target="tpu_custom_call" | custom-call | flops 5368709120 | bytes 24117248 | tf_op jit(solution)/shard_map/pallas_call | solution.py:226
  121.3 1.3 collective-permute-start.36
  122.6 1.8 collective-permute-start.29
  124.4 0.5 broadcast_add_fusion.page_ref
  125.0 1.5 collective-permute-start.37
  126.7 2.0 collective-permute-done.35.refs_6_
  128.7 1.4 collective-permute-start.30
  130.3 1.0 constant_dynamic-update-slice_fusion.7
  131.2 1.0 constant_dynamic-update-slice_fusion.6
  132.2 6.5 %collective-permute-done.36.refs_2_ = bf16[128,1280]{1,0:T(8,128)(2,1)} collective-permute-done((bf16[128,1280]{1,0:T(8,128)(2,1)}, bf16[128,1280]{1,0:T(8,128)(2,1)}, u32[]{:S(2)}, u32[]{:S(2)}) %collective-permute-start.36) | collective-permute-done | bytes 327712 | tf_op jit(solution)/shard_map/ppermute | solution.py:304
  138.7 2.0 collective-permute-start.43
  140.7 1.0 constant_dynamic-update-slice_fusion.5
  141.7 3.4 %collective-permute-done.30 = bf16[128,1024]{1,0:T(8,128)(2,1)S(1)} collective-permute-done((bf16[128,1024]{1,0:T(8,128)(2,1)}, bf16[128,1024]{1,0:T(8,128)(2,1)S(1)}, u32[]{:S(2)}, u32[]{:S(2)}) %collective-permute-start.30) | collective-permute-done | bytes 262176 | tf_op jit(solution)/shard_map/ppermute | solution.py:304
  145.1 1.3 collective-permute-start.44
  146.5 0.7 collective-permute-start.45
  147.3 11.7 %shard_map.119 = (bf16[128,1024]{1,0:T(8,128)(2,1)}, bf16[128,1024]{1,0:T(8,128)(2,1)}) custom-call(bf16[128,1280]{1,0:T(8,128)(2,1)} %copy-done.8, bf16[128,1280]{1,0:T(8,128)(2,1)} %copy-done.9, bf16[128,1280]{1,0:T(8,128)(2,1)} %collective-permute-done.26.refs_2_, bf16[128,1408]{1,0:T(8,128)(2,1)} %copy-done.1, bf16[128,1280]{1,0:T(8,128)(2,1)} %copy-done.14, ...), custom_call_target="tpu_custom_call" | custom-call | flops 5368709120 | bytes 24117248 | tf_op jit(solution)/shard_map/pallas_call | solution.py:226
  158.9 1.6 collective-permute-start.39
  160.6 9.8 %shard_map.120 = bf16[128,1024]{1,0:T(8,128)(2,1)} custom-call(bf16[128,1280]{1,0:T(8,128)(2,1)} %copy-done.10, bf16[128,1280]{1,0:T(8,128)(2,1)} %copy-done.12, bf16[128,1280]{1,0:T(8,128)(2,1)} %collective-permute-done.36.refs_2_, bf16[128,1408]{1,0:T(8,128)(2,1)} %copy-done.3, bf16[5120,1024]{1,0:T(8,128)(2,1)} %refs_4_.3, bf16[5120,1024]{1,0:T(8,128)(2,1)} %refs_5_.3), custom_call_target="tpu_custom_call" | custom-call | flops 2684354560 | bytes 22544384 | tf_op jit(solution)/shard_map/pallas_call | solution.py:226
  170.3 3.1 %shard_map.121 = bf16[16,16,2048]{2,1,0:T(8,128)(2,1)} custom-call(s32[16]{0:T(128)} %broadcast_add_fusion.page_ref, bf16[512,2048]{1,0:T(8,128)(2,1)} %all-gather.2.cloned.1.call-done.kv_ref, bf16[16,16,2048]{2,1,0:T(8,128)(2,1)} %cache_ref.1), custom_call_target="tpu_custom_call" | custom-call | bytes 4194304 | tf_op jit(solution)/shard_map/pallas_call | solution.py:260
  173.5 3.1 %collective-permute-start.40 = (bf16[128,1024]{1,0:T(8,128)(2,1)}, bf16[128,1024]{1,0:T(8,128)(2,1)S(1)}, u32[]{:S(2)}, u32[]{:S(2)}) collective-permute-start(bf16[128,1024]{1,0:T(8,128)(2,1)} %get-tuple-element.93), channel_id=1, source_target_pairs={{0,28},{4,24},{8,20},{12,16},{16,12},{20,8},{24,4},{28,0},{1,29},{... | collective-permute-start | bytes 786440 | tf_op jit(solution)/shard_map/ppermute | solution.py:304
  176.6 9.8 %shard_map.122 = bf16[128,1024]{1,0:T(8,128)(2,1)} custom-call(bf16[128,1280]{1,0:T(8,128)(2,1)} %collective-permute-done.42.refs_0_, bf16[128,1280]{1,0:T(8,128)(2,1)} %collective-permute-done.43.refs_1_, bf16[128,1280]{1,0:T(8,128)(2,1)} %collective-permute-done.44.refs_2_, bf16[128,1408]{1,0:T(8,128)(2,1)} %copy-done.7, bf16[5120,1024]{1,0:T(8,128)(2,1)} %refs_4_.3, ...), custom_call_target="tpu_custom_call" | custom-call | flops 2684354560 | bytes 22544384 | tf_op jit(solution)/shard_map/pallas_call | solution.py:226
  186.4 2.2 %collective-permute-start.46 = (bf16[128,1024]{1,0:T(8,128)(2,1)}, bf16[128,1024]{1,0:T(8,128)(2,1)S(1)}, u32[]{:S(2)}, u32[]{:S(2)}) collective-permute-start(bf16[128,1024]{1,0:T(8,128)(2,1)} %shard_map.122), channel_id=1, source_target_pairs={{0,12},{4,8},{8,28},{12,24},{16,4},{20,0},{24,20},{28,16},{1,13},{... | collective-permute-start | bytes 786440 | tf_op jit(solution)/shard_map/ppermute | solution.py:304
  188.6 1.0 constant_dynamic-update-slice_fusion.3
  189.6 5.1 %collective-permute-done.46 = bf16[128,1024]{1,0:T(8,128)(2,1)S(1)} collective-permute-done((bf16[128,1024]{1,0:T(8,128)(2,1)}, bf16[128,1024]{1,0:T(8,128)(2,1)S(1)}, u32[]{:S(2)}, u32[]{:S(2)}) %collective-permute-start.46) | collective-permute-done | bytes 262176 | tf_op jit(solution)/shard_map/ppermute | solution.py:304
  194.8 1.3 copy-done
  (139 shorter events, 4.8 us)
Async XLA Ops:
  7.2 163.2 %all-gather.2.cloned.1.call-start = ((), (), s32[]{:S(2)}) async-start(), calls=%async_computation | async-start | bytes 2621440 | tf_op jit(solution)/shard_map/all_gather | solution.py:330
  9.1 12.6 %collective-permute-start.3 = (bf16[144,512]{1,0:T(8,128)(2,1)}, bf16[144,512]{1,0:T(8,128)(2,1)S(1)}, u32[]{:S(2)}, u32[]{:S(2)}) collective-permute-start(bf16[144,512]{1,0:T(8,128)(2,1)} %get-tuple-element.53.refs_3_), channel_id=1, source_target_pairs={{0,1},{1,0},{2,3},{3,2},{4,5},{5,4},{6,7},{7,6},{8,9},{9,8},{10,11... | collective-permute-start | bytes 442376 | tf_op jit(solution)/shard_map/ppermute | solution.py:297
  9.5 12.2 %collective-permute-start.4 = (bf16[144,512]{1,0:T(8,128)(2,1)}, bf16[144,512]{1,0:T(8,128)(2,1)S(1)}, u32[]{:S(2)}, u32[]{:S(2)}) collective-permute-start(bf16[144,512]{1,0:T(8,128)(2,1)} %get-tuple-element.53.refs_3_), channel_id=1, source_target_pairs={{0,2},{1,3},{2,0},{3,1},{4,6},{5,7},{6,4},{7,5},{8,10},{9,11},{10,... | collective-permute-start | bytes 442376 | tf_op jit(solution)/shard_map/ppermute | solution.py:297
  12.0 7.7 %collective-permute-start.10 = (bf16[128,512]{1,0:T(8,128)(2,1)}, bf16[128,512]{1,0:T(8,128)(2,1)S(1)}, u32[]{:S(2)}, u32[]{:S(2)}) collective-permute-start(bf16[128,512]{1,0:T(8,128)(2,1)} %get-tuple-element.56.refs_3_), channel_id=1, source_target_pairs={{0,2},{1,3},{2,0},{3,1},{4,6},{5,7},{6,4},{7,5},{8,10},{9,11},{10,... | collective-permute-start | bytes 393224 | tf_op jit(solution)/shard_map/ppermute | solution.py:297
  12.1 17.0 %collective-permute-start.9 = (bf16[128,512]{1,0:T(8,128)(2,1)}, bf16[128,512]{1,0:T(8,128)(2,1)S(1)}, u32[]{:S(2)}, u32[]{:S(2)}) collective-permute-start(bf16[128,512]{1,0:T(8,128)(2,1)} %get-tuple-element.56.refs_3_), channel_id=1, source_target_pairs={{0,1},{1,0},{2,3},{3,2},{4,5},{5,4},{6,7},{7,6},{8,9},{9,8},{10,11... | collective-permute-start | bytes 393224 | tf_op jit(solution)/shard_map/ppermute | solution.py:297
  12.3 23.1 %collective-permute-start.1 = (bf16[128,512]{1,0:T(8,128)(2,1)}, bf16[128,512]{1,0:T(8,128)(2,1)S(1)}, u32[]{:S(2)}, u32[]{:S(2)}) collective-permute-start(bf16[128,512]{1,0:T(8,128)(2,1)} %get-tuple-element.52.refs_3_), channel_id=1, source_target_pairs={{0,2},{1,3},{2,0},{3,1},{4,6},{5,7},{6,4},{7,5},{8,10},{9,11},{10,... | collective-permute-start | bytes 393224 | tf_op jit(solution)/shard_map/ppermute | solution.py:297
  19.7 10.9 %copy-start.32 = (bf16[128,512]{1,0:T(8,128)(2,1)}, bf16[128,512]{1,0:T(8,128)(2,1)S(1)}, u32[]{:S(2)}) copy-start(bf16[128,512]{1,0:T(8,128)(2,1)S(1)} %collective-permute-done.10.refs_5_) | copy-start | bytes 393220
  19.7 15.7 %collective-permute-start.7 = (bf16[128,512]{1,0:T(8,128)(2,1)}, bf16[128,512]{1,0:T(8,128)(2,1)S(1)}, u32[]{:S(2)}, u32[]{:S(2)}) collective-permute-start(bf16[128,512]{1,0:T(8,128)(2,1)} %get-tuple-element.55.refs_3_), channel_id=1, source_target_pairs={{0,2},{1,3},{2,0},{3,1},{4,6},{5,7},{6,4},{7,5},{8,10},{9,11},{10,... | collective-permute-start | bytes 393224 | tf_op jit(solution)/shard_map/ppermute | solution.py:297
  21.7 8.9 %collective-permute-start.11 = (bf16[128,512]{1,0:T(8,128)(2,1)S(1)}, bf16[128,512]{1,0:T(8,128)(2,1)S(1)}, u32[]{:S(2)}, u32[]{:S(2)}) collective-permute-start(bf16[128,512]{1,0:T(8,128)(2,1)S(1)} %collective-permute-done.10.refs_5_), channel_id=1, source_target_pairs={{0,1},{1,0},{2,3},{3,2},{4,5},{5,4},{6,7},{7,6},{8,9},{9,8},{10,11... | collective-permute-start | bytes 393224 | tf_op jit(solution)/shard_map/ppermute | solution.py:297
  21.7 1.5 collective-permute-start.5
  27.5 22.1 %collective-permute-start.12 = (bf16[128,1280]{1,0:T(8,128)(2,1)}, bf16[128,1280]{1,0:T(8,128)(2,1)S(1)}, u32[]{:S(2)}, u32[]{:S(2)}) collective-permute-start(bf16[128,1280]{1,0:T(8,128)(2,1)} %get-tuple-element.64.refs_0_), channel_id=1, source_target_pairs={{0,4},{4,0},{8,12},{12,8},{16,20},{20,16},{24,28},{28,24},{1,5},{5... | collective-permute-start | bytes 983048 | tf_op jit(solution)/shard_map/ppermute | solution.py:304
  29.0 21.1 %collective-permute-start.13 = (bf16[128,1280]{1,0:T(8,128)(2,1)}, bf16[128,1280]{1,0:T(8,128)(2,1)S(1)}, u32[]{:S(2)}, u32[]{:S(2)}) collective-permute-start(bf16[128,1280]{1,0:T(8,128)(2,1)} %get-tuple-element.64.refs_0_), channel_id=1, source_target_pairs={{0,8},{4,12},{8,24},{12,28},{16,0},{20,4},{24,16},{28,20},{1,9},{5... | collective-permute-start | bytes 983048 | tf_op jit(solution)/shard_map/ppermute | solution.py:304
  34.9 15.9 %collective-permute-start.14 = (bf16[128,1280]{1,0:T(8,128)(2,1)}, bf16[128,1280]{1,0:T(8,128)(2,1)S(1)}, u32[]{:S(2)}, u32[]{:S(2)}) collective-permute-start(bf16[128,1280]{1,0:T(8,128)(2,1)} %get-tuple-element.65.refs_1_), channel_id=1, source_target_pairs={{0,4},{4,0},{8,12},{12,8},{16,20},{20,16},{24,28},{28,24},{1,5},{5... | collective-permute-start | bytes 983048 | tf_op jit(solution)/shard_map/ppermute | solution.py:304
  35.4 1.4 collective-permute-start.6
  35.5 1.5 collective-permute-start.8
  36.8 4.4 %collective-permute-start = (bf16[128,512]{1,0:T(8,128)(2,1)S(1)}, bf16[128,512]{1,0:T(8,128)(2,1)S(1)}, u32[]{:S(2)}, u32[]{:S(2)}) collective-permute-start(bf16[128,512]{1,0:T(8,128)(2,1)S(1)} %copy-done.28), channel_id=1, source_target_pairs={{0,1},{1,0},{2,3},{3,2},{4,5},{5,4},{6,7},{7,6},{8,9},{9,8},{10,11... | collective-permute-start | bytes 393224 | tf_op jit(solution)/shard_map/ppermute | solution.py:297
  37.0 4.2 %collective-permute-start.2 = (bf16[128,512]{1,0:T(8,128)(2,1)S(1)}, bf16[128,512]{1,0:T(8,128)(2,1)S(1)}, u32[]{:S(2)}, u32[]{:S(2)}) collective-permute-start(bf16[128,512]{1,0:T(8,128)(2,1)S(1)} %collective-permute-done.1.refs_5_), channel_id=1, source_target_pairs={{0,1},{1,0},{2,3},{3,2},{4,5},{5,4},{6,7},{7,6},{8,9},{9,8},{10,11... | collective-permute-start | bytes 393224 | tf_op jit(solution)/shard_map/ppermute | solution.py:297
  41.9 7.8 %copy-start.20 = (bf16[128,1280]{1,0:T(8,128)(2,1)S(1)}, bf16[128,1280]{1,0:T(8,128)(2,1)}, u32[]{:S(2)}) copy-start(bf16[128,1280]{1,0:T(8,128)(2,1)} %get-tuple-element.65.refs_1_) | copy-start | bytes 983044
  41.9 8.3 %copy-start.23 = (bf16[128,1280]{1,0:T(8,128)(2,1)S(1)}, bf16[128,1280]{1,0:T(8,128)(2,1)}, u32[]{:S(2)}) copy-start(bf16[128,1280]{1,0:T(8,128)(2,1)} %get-tuple-element.66.refs_2_) | copy-start | bytes 983044
  45.5 28.6 %collective-permute-start.18 = (bf16[128,1408]{1,0:T(8,128)(2,1)}, bf16[128,1408]{1,0:T(8,128)(2,1)S(1)}, u32[]{:S(2)}, u32[]{:S(2)}) collective-permute-start(bf16[128,1408]{1,0:T(8,128)(2,1)} %get-tuple-element.67.refs_3_), channel_id=1, source_target_pairs={{0,4},{4,0},{8,12},{12,8},{16,20},{20,16},{24,28},{28,24},{1,5},{5... | collective-permute-start | bytes 1081352 | tf_op jit(solution)/shard_map/ppermute | solution.py:304
  47.1 28.7 %collective-permute-start.19 = (bf16[128,1408]{1,0:T(8,128)(2,1)}, bf16[128,1408]{1,0:T(8,128)(2,1)S(1)}, u32[]{:S(2)}, u32[]{:S(2)}) collective-permute-start(bf16[128,1408]{1,0:T(8,128)(2,1)} %get-tuple-element.67.refs_3_), channel_id=1, source_target_pairs={{0,8},{4,12},{8,24},{12,28},{16,0},{20,4},{24,16},{28,20},{1,9},{5... | collective-permute-start | bytes 1081352 | tf_op jit(solution)/shard_map/ppermute | solution.py:304
  49.7 27.7 %copy-start.18 = (bf16[128,1280]{1,0:T(8,128)(2,1)}, bf16[128,1280]{1,0:T(8,128)(2,1)S(1)}, u32[]{:S(2)}) copy-start(bf16[128,1280]{1,0:T(8,128)(2,1)S(1)} %collective-permute-done.12.refs_4_) | copy-start | bytes 983044
  49.7 16.8 %collective-permute-start.15 = (bf16[128,1280]{1,0:T(8,128)(2,1)S(1)}, bf16[128,1280]{1,0:T(8,128)(2,1)S(1)}, u32[]{:S(2)}, u32[]{:S(2)}) collective-permute-start(bf16[128,1280]{1,0:T(8,128)(2,1)S(1)} %copy-done.20), channel_id=1, source_target_pairs={{0,8},{4,12},{8,24},{12,28},{16,0},{20,4},{24,16},{28,20},{1,9},{5... | collective-permute-start | bytes 983048 | tf_op jit(solution)/shard_map/ppermute | solution.py:304
  50.2 38.9 %copy-start.17 = (bf16[128,1280]{1,0:T(8,128)(2,1)}, bf16[128,1280]{1,0:T(8,128)(2,1)S(1)}, u32[]{:S(2)}) copy-start(bf16[128,1280]{1,0:T(8,128)(2,1)S(1)} %collective-permute-done.13.refs_0_) | copy-start | bytes 983044
  50.2 16.8 %collective-permute-start.16 = (bf16[128,1280]{1,0:T(8,128)(2,1)S(1)}, bf16[128,1280]{1,0:T(8,128)(2,1)}, u32[]{:S(2)}, u32[]{:S(2)}) collective-permute-start(bf16[128,1280]{1,0:T(8,128)(2,1)S(1)} %copy-done.23), channel_id=1, source_target_pairs={{0,4},{4,0},{8,12},{12,8},{16,20},{20,16},{24,28},{28,24},{1,5},{5... | collective-permute-start | bytes 983048 | tf_op jit(solution)/shard_map/ppermute | solution.py:304
  50.7 26.6 %copy-start.21 = (bf16[128,1280]{1,0:T(8,128)(2,1)}, bf16[128,1280]{1,0:T(8,128)(2,1)S(1)}, u32[]{:S(2)}) copy-start(bf16[128,1280]{1,0:T(8,128)(2,1)S(1)} %collective-permute-done.14.refs_5_) | copy-start | bytes 983044
  50.7 22.9 %collective-permute-start.17 = (bf16[128,1280]{1,0:T(8,128)(2,1)S(1)}, bf16[128,1280]{1,0:T(8,128)(2,1)}, u32[]{:S(2)}, u32[]{:S(2)}) collective-permute-start(bf16[128,1280]{1,0:T(8,128)(2,1)S(1)} %copy-done.23), channel_id=1, source_target_pairs={{0,8},{4,12},{8,24},{12,28},{16,0},{20,4},{24,16},{28,20},{1,9},{5... | collective-permute-start | bytes 983048 | tf_op jit(solution)/shard_map/ppermute | solution.py:304
  51.1 41.6 %copy-start.39 = (s32[1,64]{1,0:T(1,128)S(1)}, s32[1,64]{1,0:T(1,128)}, u32[]{:S(2)}) copy-start(s32[1,64]{1,0:T(1,128)} %param.17) | copy-start | bytes 772
  66.5 22.6 %copy-start.19 = (bf16[128,1280]{1,0:T(8,128)(2,1)}, bf16[128,1280]{1,0:T(8,128)(2,1)S(1)}, u32[]{:S(2)}) copy-start(bf16[128,1280]{1,0:T(8,128)(2,1)S(1)} %collective-permute-done.15.refs_1_) | copy-start | bytes 983044
  66.5 22.6 %collective-permute-start.21 = (bf16[128,1280]{1,0:T(8,128)(2,1)S(1)}, bf16[128,1280]{1,0:T(8,128)(2,1)S(1)}, u32[]{:S(2)}, u32[]{:S(2)}) collective-permute-start(bf16[128,1280]{1,0:T(8,128)(2,1)S(1)} %collective-permute-done.13.refs_0_), channel_id=1, source_target_pairs={{0,4},{4,0},{8,12},{12,8},{16,20},{20,16},{24,28},{28,24},{1,5},{5... | collective-permute-start | bytes 983048 | tf_op jit(solution)/shard_map/ppermute | solution.py:304
  67.0 23.5 %collective-permute-start.22 = (bf16[128,1280]{1,0:T(8,128)(2,1)S(1)}, bf16[128,1280]{1,0:T(8,128)(2,1)S(1)}, u32[]{:S(2)}, u32[]{:S(2)}) collective-permute-start(bf16[128,1280]{1,0:T(8,128)(2,1)S(1)} %collective-permute-done.13.refs_0_), channel_id=1, source_target_pairs={{0,8},{4,12},{8,24},{12,28},{16,0},{20,4},{24,16},{28,20},{1,9},{5... | collective-permute-start | bytes 983048 | tf_op jit(solution)/shard_map/ppermute | solution.py:304
  73.6 17.4 %collective-permute-start.23 = (bf16[128,1280]{1,0:T(8,128)(2,1)S(1)}, bf16[128,1280]{1,0:T(8,128)(2,1)}, u32[]{:S(2)}, u32[]{:S(2)}) collective-permute-start(bf16[128,1280]{1,0:T(8,128)(2,1)S(1)} %collective-permute-done.15.refs_1_), channel_id=1, source_target_pairs={{0,4},{4,0},{8,12},{12,8},{16,20},{20,16},{24,28},{28,24},{1,5},{5... | collective-permute-start | bytes 983048 | tf_op jit(solution)/shard_map/ppermute | solution.py:304
  74.1 17.1 %collective-permute-start.24 = (bf16[128,1280]{1,0:T(8,128)(2,1)S(1)}, bf16[128,1280]{1,0:T(8,128)(2,1)S(1)}, u32[]{:S(2)}, u32[]{:S(2)}) collective-permute-start(bf16[128,1280]{1,0:T(8,128)(2,1)S(1)} %collective-permute-done.15.refs_1_), channel_id=1, source_target_pairs={{0,8},{4,12},{8,24},{12,28},{16,0},{20,4},{24,16},{28,20},{1,9},{5... | collective-permute-start | bytes 983048 | tf_op jit(solution)/shard_map/ppermute | solution.py:304
  75.8 15.2 %copy-start.2 = (bf16[128,1408]{1,0:T(8,128)(2,1)}, bf16[128,1408]{1,0:T(8,128)(2,1)S(1)}, u32[]{:S(2)}) copy-start(bf16[128,1408]{1,0:T(8,128)(2,1)S(1)} %collective-permute-done.19.refs_3_) | copy-start | bytes 1081348
  75.8 17.0 %collective-permute-start.25 = (bf16[128,1280]{1,0:T(8,128)(2,1)}, bf16[128,1280]{1,0:T(8,128)(2,1)}, u32[]{:S(2)}, u32[]{:S(2)}) collective-permute-start(bf16[128,1280]{1,0:T(8,128)(2,1)} %collective-permute-done.17.refs_2_), channel_id=1, source_target_pairs={{0,4},{4,0},{8,12},{12,8},{16,20},{20,16},{24,28},{28,24},{1,5},{5... | collective-permute-start | bytes 983048 | tf_op jit(solution)/shard_map/ppermute | solution.py:304
  89.1 11.9 %collective-permute-start.26 = (bf16[128,1280]{1,0:T(8,128)(2,1)}, bf16[128,1280]{1,0:T(8,128)(2,1)}, u32[]{:S(2)}, u32[]{:S(2)}) collective-permute-start(bf16[128,1280]{1,0:T(8,128)(2,1)} %collective-permute-done.17.refs_2_), channel_id=1, source_target_pairs={{0,8},{4,12},{8,24},{12,28},{16,0},{20,4},{24,16},{28,20},{1,9},{5... | collective-permute-start | bytes 983048 | tf_op jit(solution)/shard_map/ppermute | solution.py:304
  90.5 30.8 %copy-start.8 = (bf16[128,1280]{1,0:T(8,128)(2,1)}, bf16[128,1280]{1,0:T(8,128)(2,1)S(1)}, u32[]{:S(2)}) copy-start(bf16[128,1280]{1,0:T(8,128)(2,1)S(1)} %collective-permute-done.22.refs_0_) | copy-start | bytes 983044
  90.5 11.4 %collective-permute-start.27 = (bf16[128,1408]{1,0:T(8,128)(2,1)S(1)}, bf16[128,1408]{1,0:T(8,128)(2,1)S(1)}, u32[]{:S(2)}, u32[]{:S(2)}) collective-permute-start(bf16[128,1408]{1,0:T(8,128)(2,1)S(1)} %collective-permute-done.19.refs_3_), channel_id=1, source_target_pairs={{0,4},{4,0},{8,12},{12,8},{16,20},{20,16},{24,28},{28,24},{1,5},{5... | collective-permute-start | bytes 1081352 | tf_op jit(solution)/shard_map/ppermute | solution.py:304
  91.0 17.6 %collective-permute-start.28 = (bf16[128,1408]{1,0:T(8,128)(2,1)S(1)}, bf16[128,1408]{1,0:T(8,128)(2,1)S(1)}, u32[]{:S(2)}, u32[]{:S(2)}) collective-permute-start(bf16[128,1408]{1,0:T(8,128)(2,1)S(1)} %collective-permute-done.19.refs_3_), channel_id=1, source_target_pairs={{0,8},{4,12},{8,24},{12,28},{16,0},{20,4},{24,16},{28,20},{1,9},{5... | collective-permute-start | bytes 1081352 | tf_op jit(solution)/shard_map/ppermute | solution.py:304
  91.2 30.0 %copy-start.9 = (bf16[128,1280]{1,0:T(8,128)(2,1)}, bf16[128,1280]{1,0:T(8,128)(2,1)S(1)}, u32[]{:S(2)}) copy-start(bf16[128,1280]{1,0:T(8,128)(2,1)S(1)} %collective-permute-done.24.refs_1_) | copy-start | bytes 983044
  91.2 17.8 %collective-permute-start.20 = (bf16[128,1024]{1,0:T(8,128)(2,1)}, bf16[128,1024]{1,0:T(8,128)(2,1)}, u32[]{:S(2)}, u32[]{:S(2)}) collective-permute-start(bf16[128,1024]{1,0:T(8,128)(2,1)} %get-tuple-element.73), channel_id=1, source_target_pairs={{0,4},{4,0},{8,12},{12,8},{16,20},{20,16},{24,28},{28,24},{1,5},{5... | collective-permute-start | bytes 786440 | tf_op jit(solution)/shard_map/ppermute | solution.py:304
  92.8 28.5 %collective-permute-start.31 = (bf16[128,1280]{1,0:T(8,128)(2,1)S(1)}, bf16[128,1280]{1,0:T(8,128)(2,1)S(1)}, u32[]{:S(2)}, u32[]{:S(2)}) collective-permute-start(bf16[128,1280]{1,0:T(8,128)(2,1)S(1)} %collective-permute-done.22.refs_0_), channel_id=1, source_target_pairs={{0,4},{4,0},{8,12},{12,8},{16,20},{20,16},{24,28},{28,24},{1,5},{5... | collective-permute-start | bytes 983048 | tf_op jit(solution)/shard_map/ppermute | solution.py:304
  101.0 21.6 %collective-permute-start.32 = (bf16[128,1280]{1,0:T(8,128)(2,1)S(1)}, bf16[128,1280]{1,0:T(8,128)(2,1)S(1)}, u32[]{:S(2)}, u32[]{:S(2)}) collective-permute-start(bf16[128,1280]{1,0:T(8,128)(2,1)S(1)} %collective-permute-done.22.refs_0_), channel_id=1, source_target_pairs={{0,8},{4,12},{8,24},{12,28},{16,0},{20,4},{24,16},{28,20},{1,9},{5... | collective-permute-start | bytes 983048 | tf_op jit(solution)/shard_map/ppermute | solution.py:304
  101.8 23.1 %collective-permute-start.33 = (bf16[128,1280]{1,0:T(8,128)(2,1)S(1)}, bf16[128,1280]{1,0:T(8,128)(2,1)S(1)}, u32[]{:S(2)}, u32[]{:S(2)}) collective-permute-start(bf16[128,1280]{1,0:T(8,128)(2,1)S(1)} %collective-permute-done.24.refs_1_), channel_id=1, source_target_pairs={{0,4},{4,0},{8,12},{12,8},{16,20},{20,16},{24,28},{28,24},{1,5},{5... | collective-permute-start | bytes 983048 | tf_op jit(solution)/shard_map/ppermute | solution.py:304
  108.6 17.9 %copy-start.1 = (bf16[128,1408]{1,0:T(8,128)(2,1)}, bf16[128,1408]{1,0:T(8,128)(2,1)S(1)}, u32[]{:S(2)}) copy-start(bf16[128,1408]{1,0:T(8,128)(2,1)S(1)} %collective-permute-done.28.refs_3_) | copy-start | bytes 1081348
  108.6 17.9 %collective-permute-start.34 = (bf16[128,1280]{1,0:T(8,128)(2,1)S(1)}, bf16[128,1280]{1,0:T(8,128)(2,1)S(1)}, u32[]{:S(2)}, u32[]{:S(2)}) collective-permute-start(bf16[128,1280]{1,0:T(8,128)(2,1)S(1)} %collective-permute-done.24.refs_1_), channel_id=1, source_target_pairs={{0,8},{4,12},{8,24},{12,28},{16,0},{20,4},{24,16},{28,20},{1,9},{5... | collective-permute-start | bytes 983048 | tf_op jit(solution)/shard_map/ppermute | solution.py:304
  109.1 19.6 %collective-permute-start.35 = (bf16[128,1280]{1,0:T(8,128)(2,1)}, bf16[128,1280]{1,0:T(8,128)(2,1)S(1)}, u32[]{:S(2)}, u32[]{:S(2)}) collective-permute-start(bf16[128,1280]{1,0:T(8,128)(2,1)} %collective-permute-done.26.refs_2_), channel_id=1, source_target_pairs={{0,4},{4,0},{8,12},{12,8},{16,20},{20,16},{24,28},{28,24},{1,5},{5... | collective-permute-start | bytes 983048 | tf_op jit(solution)/shard_map/ppermute | solution.py:304
  121.3 8.8 %copy-start.14 = (bf16[128,1280]{1,0:T(8,128)(2,1)}, bf16[128,1280]{1,0:T(8,128)(2,1)S(1)}, u32[]{:S(2)}) copy-start(bf16[128,1280]{1,0:T(8,128)(2,1)S(1)} %collective-permute-done.31.refs_4_) | copy-start | bytes 983044
  121.3 17.4 %collective-permute-start.36 = (bf16[128,1280]{1,0:T(8,128)(2,1)}, bf16[128,1280]{1,0:T(8,128)(2,1)}, u32[]{:S(2)}, u32[]{:S(2)}) collective-permute-start(bf16[128,1280]{1,0:T(8,128)(2,1)} %collective-permute-done.26.refs_2_), channel_id=1, source_target_pairs={{0,8},{4,12},{8,24},{12,28},{16,0},{20,4},{24,16},{28,20},{1,9},{5... | collective-permute-start | bytes 983048 | tf_op jit(solution)/shard_map/ppermute | solution.py:304
  122.6 16.1 %collective-permute-start.29 = (bf16[128,1024]{1,0:T(8,128)(2,1)}, bf16[128,1024]{1,0:T(8,128)(2,1)}, u32[]{:S(2)}, u32[]{:S(2)}) collective-permute-start(bf16[128,1024]{1,0:T(8,128)(2,1)} %get-tuple-element.82), channel_id=1, source_target_pairs={{0,16},{4,20},{8,0},{12,4},{16,24},{20,28},{24,8},{28,12},{1,17},{... | collective-permute-start | bytes 786440 | tf_op jit(solution)/shard_map/ppermute | solution.py:304
  125.0 21.5 %collective-permute-start.37 = (bf16[128,1408]{1,0:T(8,128)(2,1)S(1)}, bf16[128,1408]{1,0:T(8,128)(2,1)S(1)}, u32[]{:S(2)}, u32[]{:S(2)}) collective-permute-start(bf16[128,1408]{1,0:T(8,128)(2,1)S(1)} %collective-permute-done.28.refs_3_), channel_id=1, source_target_pairs={{0,4},{4,0},{8,12},{12,8},{16,20},{20,16},{24,28},{28,24},{1,5},{5... | collective-permute-start | bytes 1081352 | tf_op jit(solution)/shard_map/ppermute | solution.py:304
  126.5 12.2 %copy-start.11 = (bf16[128,1280]{1,0:T(8,128)(2,1)S(1)}, bf16[128,1280]{1,0:T(8,128)(2,1)}, u32[]{:S(2)}) copy-start(bf16[128,1280]{1,0:T(8,128)(2,1)} %copy-done.10) | copy-start | bytes 983044
  126.5 20.0 %collective-permute-start.38 = (bf16[128,1408]{1,0:T(8,128)(2,1)S(1)}, bf16[128,1408]{1,0:T(8,128)(2,1)S(1)}, u32[]{:S(2)}, u32[]{:S(2)}) collective-permute-start(bf16[128,1408]{1,0:T(8,128)(2,1)S(1)} %collective-permute-done.28.refs_3_), channel_id=1, source_target_pairs={{0,8},{4,12},{8,24},{12,28},{16,0},{20,4},{24,16},{28,20},{1,9},{5... | collective-permute-start | bytes 1081352 | tf_op jit(solution)/shard_map/ppermute | solution.py:304
  128.7 16.5 %collective-permute-start.30 = (bf16[128,1024]{1,0:T(8,128)(2,1)}, bf16[128,1024]{1,0:T(8,128)(2,1)S(1)}, u32[]{:S(2)}, u32[]{:S(2)}) collective-permute-start(bf16[128,1024]{1,0:T(8,128)(2,1)} %get-tuple-element.83), channel_id=1, source_target_pairs={{0,20},{4,16},{8,4},{12,0},{16,28},{20,24},{24,12},{28,8},{1,21},{... | collective-permute-start | bytes 786440 | tf_op jit(solution)/shard_map/ppermute | solution.py:304
  130.0 8.6 %copy-start.13 = (bf16[128,1280]{1,0:T(8,128)(2,1)S(1)}, bf16[128,1280]{1,0:T(8,128)(2,1)}, u32[]{:S(2)}) copy-start(bf16[128,1280]{1,0:T(8,128)(2,1)} %copy-done.12) | copy-start | bytes 983044
  138.7 37.9 %collective-permute-start.42 = (bf16[128,1280]{1,0:T(8,128)(2,1)S(1)}, bf16[128,1280]{1,0:T(8,128)(2,1)}, u32[]{:S(2)}, u32[]{:S(2)}) collective-permute-start(bf16[128,1280]{1,0:T(8,128)(2,1)S(1)} %copy-done.11), channel_id=1, source_target_pairs={{0,4},{4,0},{8,12},{12,8},{16,20},{20,16},{24,28},{28,24},{1,5},{5... | collective-permute-start | bytes 983048 | tf_op jit(solution)/shard_map/ppermute | solution.py:304
  138.7 37.8 %collective-permute-start.43 = (bf16[128,1280]{1,0:T(8,128)(2,1)S(1)}, bf16[128,1280]{1,0:T(8,128)(2,1)}, u32[]{:S(2)}, u32[]{:S(2)}) collective-permute-start(bf16[128,1280]{1,0:T(8,128)(2,1)S(1)} %copy-done.13), channel_id=1, source_target_pairs={{0,4},{4,0},{8,12},{12,8},{16,20},{20,16},{24,28},{28,24},{1,5},{5... | collective-permute-start | bytes 983048 | tf_op jit(solution)/shard_map/ppermute | solution.py:304
  145.1 31.4 %collective-permute-start.44 = (bf16[128,1280]{1,0:T(8,128)(2,1)}, bf16[128,1280]{1,0:T(8,128)(2,1)}, u32[]{:S(2)}, u32[]{:S(2)}) collective-permute-start(bf16[128,1280]{1,0:T(8,128)(2,1)} %collective-permute-done.36.refs_2_), channel_id=1, source_target_pairs={{0,4},{4,0},{8,12},{12,8},{16,20},{20,16},{24,28},{28,24},{1,5},{5... | collective-permute-start | bytes 983048 | tf_op jit(solution)/shard_map/ppermute | solution.py:304
  146.5 12.4 %copy-start.3 = (bf16[128,1408]{1,0:T(8,128)(2,1)}, bf16[128,1408]{1,0:T(8,128)(2,1)S(1)}, u32[]{:S(2)}) copy-start(bf16[128,1408]{1,0:T(8,128)(2,1)S(1)} %collective-permute-done.38.refs_3_) | copy-start | bytes 1081348
  146.5 26.9 %collective-permute-start.45 = (bf16[128,1408]{1,0:T(8,128)(2,1)S(1)}, bf16[128,1408]{1,0:T(8,128)(2,1)S(1)}, u32[]{:S(2)}, u32[]{:S(2)}) collective-permute-start(bf16[128,1408]{1,0:T(8,128)(2,1)S(1)} %collective-permute-done.38.refs_3_), channel_id=1, source_target_pairs={{0,4},{4,0},{8,12},{12,8},{16,20},{20,16},{24,28},{28,24},{1,5},{5... | collective-permute-start | bytes 1081352 | tf_op jit(solution)/shard_map/ppermute | solution.py:304
  158.9 29.6 %collective-permute-start.39 = (bf16[128,1024]{1,0:T(8,128)(2,1)}, bf16[128,1024]{1,0:T(8,128)(2,1)}, u32[]{:S(2)}, u32[]{:S(2)}) collective-permute-start(bf16[128,1024]{1,0:T(8,128)(2,1)} %get-tuple-element.92), channel_id=1, source_target_pairs={{0,24},{4,28},{8,16},{12,20},{16,8},{20,12},{24,0},{28,4},{1,25},{... | collective-permute-start | bytes 786440 | tf_op jit(solution)/shard_map/ppermute | solution.py:304
  173.5 16.1 %collective-permute-start.40 = (bf16[128,1024]{1,0:T(8,128)(2,1)}, bf16[128,1024]{1,0:T(8,128)(2,1)S(1)}, u32[]{:S(2)}, u32[]{:S(2)}) collective-permute-start(bf16[128,1024]{1,0:T(8,128)(2,1)} %get-tuple-element.93), channel_id=1, source_target_pairs={{0,28},{4,24},{8,20},{12,16},{16,12},{20,8},{24,4},{28,0},{1,29},{... | collective-permute-start | bytes 786440 | tf_op jit(solution)/shard_map/ppermute | solution.py:304
  176.5 13.0 %collective-permute-start.41 = (bf16[128,1024]{1,0:T(8,128)(2,1)S(1)}, bf16[128,1024]{1,0:T(8,128)(2,1)S(1)}, u32[]{:S(2)}, u32[]{:S(2)}) collective-permute-start(bf16[128,1024]{1,0:T(8,128)(2,1)S(1)} %copy-done.24), channel_id=1, source_target_pairs={{0,8},{4,12},{8,24},{12,28},{16,0},{20,4},{24,16},{28,20},{1,9},{5... | collective-permute-start | bytes 786440 | tf_op jit(solution)/shard_map/ppermute | solution.py:304
  186.4 8.4 %collective-permute-start.46 = (bf16[128,1024]{1,0:T(8,128)(2,1)}, bf16[128,1024]{1,0:T(8,128)(2,1)S(1)}, u32[]{:S(2)}, u32[]{:S(2)}) collective-permute-start(bf16[128,1024]{1,0:T(8,128)(2,1)} %shard_map.122), channel_id=1, source_target_pairs={{0,12},{4,8},{8,28},{12,24},{16,4},{20,0},{24,20},{28,16},{1,13},{... | collective-permute-start | bytes 786440 | tf_op jit(solution)/shard_map/ppermute | solution.py:304
  (24 other events, 65.5 us)
Sparse Core Ops, SparseCore 0:
  51.2 22.8 all-gather.1

commit v5 on v4

--- a/solution.py
+++ b/solution.py
@@ -17,7 +17,7 @@
 SEG_ROWS = 16
 SCALE_COLUMNS = 128
 MASK_FILLER = -1e30
-VMEM_LIMIT = 60 * 1024 * 1024
+VMEM_LIMIT = 28 * 1024 * 1024
 
 
 def ring_order(count):
@@ -259,12 +259,13 @@
 def write_cache(pages, kv, cache):
     return pl.pallas_call(
         cache_kernel,
+        grid=(1,),
         in_specs=[
             pl.BlockSpec(memory_space=pltpu.SMEM),
-            pl.BlockSpec(memory_space=pltpu.VMEM),
-            pl.BlockSpec(memory_space=pltpu.VMEM),
+            pl.BlockSpec(kv.shape, lambda i: (0, 0)),
+            pl.BlockSpec(cache.shape, lambda i: (0, 0, 0)),
         ],
-        out_specs=pl.BlockSpec(memory_space=pltpu.VMEM),
+        out_specs=pl.BlockSpec(cache.shape, lambda i: (0, 0, 0)),
         out_shape=jax.ShapeDtypeStruct(cache.shape, cache.dtype),
         compiler_params=pltpu.CompilerParams(vmem_limit_bytes=VMEM_LIMIT),
         cost_estimate=pl.CostEstimate(flops=0, bytes_accessed=8 * cache.size, transcendentals=0),
@@ -282,6 +283,11 @@
     paged_cache,
     page_table,
 ):
+    queries, residual, gate_weight, up_weight, paged_cache = [
+        pltpu.with_memory_space_constraint(a, pltpu.HBM)
+        for a in (queries, residual, gate_weight, up_weight, paged_cache)
+    ]
+    own_kv = pltpu.with_memory_space_constraint(rotated_keys_values, pltpu.HBM)
     rows, width = queries.shape
     tok_index = lax.axis_index("tok")
     tok_count = lax.axis_size("tok")
@@ -303,7 +309,7 @@
                 pairs.append((2 * z + y, 2 * ahead[steps][z] + (1 - y if flip else y)))
         return lax.ppermute(array, "grp", pairs)
 
-    packed = pack(rotated_keys_values, prompt_window_index)
+    packed = pack(own_kv, prompt_window_index)
     group_chunks = []
     for c in chunks:
         held = {0: packed[c]}

time: 203 us -> 202 us (level)
  local copies, waits for them, and re-layouts: 7.96 us -> 15.7 us
  Pallas kernels: 73.9 us -> 67.9 us
  waiting for transfers between devices: 58.5 us -> 55.7 us
    unnamed x80 -> x38, local copies, waits for them, and re-layouts: 3.08 us -> 9.59 us
    pallas_call x5, Pallas kernels: 54.6 us -> 51.4 us  [gated(): pl.pallas_call(functools.partial(gated_kernel, count, len(shards[0])), gr...]
    ppermute x35, waiting for transfers between devices: 51.5 us -> 48.9 us  [send(): return lax.ppermute(array, 'grp', pairs)]
  transfers between devices with their start and end apart: 48 -> 48, of which waited for: 12 -> 13; matrix products, arithmetic and copies ran while one was open for 3% -> 3% of each run, Pallas kernels for 36% -> 33%
where the time goes in v5:
time: 202 us; the launch traced here: 201 us
  Pallas kernels  67.9 us (34%)
  waiting for transfers between devices  55.7 us (28%)
  starting transfers between devices  46.8 us (23%)
  local copies, waits for them, and re-layouts  15.7 us (8%)
  between operations  14.3 us (7%)
    pallas_call x5, Pallas kernels, gated(): pl.pallas_call(functools.partial(gated_kernel, count, len(shards[0])), gr...  51.4 us
    ppermute x35, waiting for transfers between devices, send(): return lax.ppermute(array, 'grp', pairs)  48.9 us
    ppermute x35, starting transfers between devices, send(): return lax.ppermute(array, 'grp', pairs)  38.2 us
    pallas_call x4, Pallas kernels, attend(): pl.pallas_call(functools.partial(attend_kernel, chunk, shard_count, width...  12.8 us
    unnamed x38, local copies, waits for them, and re-layouts  9.59 us
    ppermute x12, starting transfers between devices, swap(): return lax.ppermute(array, 'tok', [(t, t ^ mask) for t in range(tok_count)])  8.55 us
    ppermute x12, waiting for transfers between devices, swap(): return lax.ppermute(array, 'tok', [(t, t ^ mask) for t in range(tok_count)])  6.76 us
    dynamic_update_slice x8, local copies, waits for them, and re-layouts, put(): return lax.dynamic_update_slice_in_dim(hidden, block, source * units, 1)  5.82 us
  transfers between devices with their start and end apart: 48, of which 13 were waited for; matrix products, arithmetic and copies ran while one was open for 3% of the time, Pallas kernels for 33%

profile of v5, /device:TPU:0, one launch (start us, length us, event | category | flops | bytes accessed | tf_op | source)
XLA Modules:
  0.0 201.1 jit_solution(5390445859531010859)
XLA Ops:
  7.2 0.6 copy-done.12
  7.9 1.1 shard_map.112
  9.0 0.5 collective-permute-start.3
  9.5 2.6 %collective-permute-start.4 = (bf16[144,512]{1,0:T(8,128)(2,1)S(1)}, bf16[144,512]{1,0:T(8,128)(2,1)S(1)}, u32[]{:S(2)}, u32[]{:S(2)}) collective-permute-start(bf16[144,512]{1,0:T(8,128)(2,1)S(1)} %get-tuple-element.53.refs_3_), channel_id=1, source_target_pairs={{0,2},{1,3},{2,0},{3,1},{4,6},{5,7},{6,4},{7,5},{8,10},{9,11},{10,... | collective-permute-start | bytes 442376 | tf_op jit(solution)/shard_map/ppermute | solution.py:303
  12.2 1.8 collective-permute-start.1
  14.1 5.5 %collective-permute-done.10.refs_5_ = bf16[128,512]{1,0:T(8,128)(2,1)S(1)} collective-permute-done((bf16[128,512]{1,0:T(8,128)(2,1)S(1)}, bf16[128,512]{1,0:T(8,128)(2,1)S(1)}, u32[]{:S(2)}, u32[]{:S(2)}) %collective-permute-start.10) | collective-permute-done | bytes 131104 | tf_op jit(solution)/shard_map/ppermute | solution.py:303
  19.6 1.9 collective-permute-start.7
  22.0 0.7 convert_bitcast_fusion
  23.2 0.7 copy-done.9
  23.9 3.2 %shard_map.113 = (bf16[128,5120]{1,0:T(8,128)(2,1)}, bf16[128,1280]{1,0:T(8,128)(2,1)S(1)}, f32[128,128]{1,0:T(8,128)S(1)}, f32[128,512]{1,0:T(8,128)S(1)}) custom-call(bf16[128,5120]{1,0:T(8,128)(2,1)} %refs_0_.7, bf16[128,5120]{1,0:T(8,128)(2,1)} %refs_1_.7, f32[1,5120]{1,0:T(1,128)S(1)} %bitcast.6, bf16[144,512]{1,0:T(8,128)(2,1)S(1)} %get-tuple-element.53.refs_3_, ...), custom_call_target="tpu_custom_call" | custom-call | flops 335544320 | bytes 1835008 | tf_op jit(solution)/shard_map/pallas_call | solution.py:171
  27.1 1.5 collective-permute-start.12
  28.6 1.6 collective-permute-start.13
  30.2 3.2 %shard_map.114 = (bf16[128,5120]{1,0:T(8,128)(2,1)}, bf16[128,1280]{1,0:T(8,128)(2,1)S(1)}, f32[128,128]{1,0:T(8,128)S(1)}) custom-call(bf16[128,5120]{1,0:T(8,128)(2,1)} %refs_0_.7, bf16[128,5120]{1,0:T(8,128)(2,1)} %refs_1_.7, f32[1,5120]{1,0:T(1,128)S(1)} %bitcast.7, ...), custom_call_target="tpu_custom_call", output_to_operand_aliasing={{0}: (9, {})} | custom-call | flops 335544320 | bytes 1835008 | tf_op jit(solution)/shard_map/pallas_call | solution.py:171
  34.4 0.8 collective-permute-done.6.refs_4_
  35.7 3.2 %shard_map.115 = (bf16[128,5120]{1,0:T(8,128)(2,1)}, bf16[128,1280]{1,0:T(8,128)(2,1)S(1)}, f32[128,128]{1,0:T(8,128)S(1)}) custom-call(bf16[128,5120]{1,0:T(8,128)(2,1)} %refs_0_.7, bf16[128,5120]{1,0:T(8,128)(2,1)} %refs_1_.7, f32[1,5120]{1,0:T(1,128)S(1)} %bitcast.8, ...), custom_call_target="tpu_custom_call", output_to_operand_aliasing={{0}: (9, {})} | custom-call | flops 335544320 | bytes 1835008 | tf_op jit(solution)/shard_map/pallas_call | solution.py:171
  38.9 3.3 %shard_map.116 = (bf16[128,5120]{1,0:T(8,128)(2,1)}, bf16[128,1408]{1,0:T(8,128)(2,1)S(1)}) custom-call(bf16[128,5120]{1,0:T(8,128)(2,1)} %refs_0_.7, bf16[128,5120]{1,0:T(8,128)(2,1)} %refs_1_.7, f32[1,5120]{1,0:T(1,128)S(1)} %bitcast.9, bf16[128,512]{1,0:T(8,128)(2,1)S(1)} %get-tuple-element.52.refs_3_, ...), custom_call_target="tpu_custom_call", output_to_operand_aliasing={{0}: (9, {})} | custom-call | flops 335544320 | bytes 1835008 | tf_op jit(solution)/shard_map/pallas_call | solution.py:171
  42.2 1.5 collective-permute-start.18
  43.7 2.6 %collective-permute-start.19 = (bf16[128,1408]{1,0:T(8,128)(2,1)S(1)}, bf16[128,1408]{1,0:T(8,128)(2,1)S(1)}, u32[]{:S(2)}, u32[]{:S(2)}) collective-permute-start(bf16[128,1408]{1,0:T(8,128)(2,1)S(1)} %get-tuple-element.67.refs_3_), channel_id=1, source_target_pairs={{0,8},{4,12},{8,24},{12,28},{16,0},{20,4},{24,16},{28,20},{1,9},{5... | collective-permute-start | bytes 1081352 | tf_op jit(solution)/shard_map/ppermute | solution.py:310
  47.7 15.2 %collective-permute-done.15.refs_1_ = bf16[128,1280]{1,0:T(8,128)(2,1)S(1)} collective-permute-done((bf16[128,1280]{1,0:T(8,128)(2,1)S(1)}, bf16[128,1280]{1,0:T(8,128)(2,1)S(1)}, u32[]{:S(2)}, u32[]{:S(2)}) %collective-permute-start.15) | collective-permute-done | bytes 327712 | tf_op jit(solution)/shard_map/ppermute | solution.py:310
  63.5 1.7 collective-permute-start.22
  65.2 4.9 %collective-permute-done.17.refs_2_ = bf16[128,1280]{1,0:T(8,128)(2,1)} collective-permute-done((bf16[128,1280]{1,0:T(8,128)(2,1)S(1)}, bf16[128,1280]{1,0:T(8,128)(2,1)}, u32[]{:S(2)}, u32[]{:S(2)}) %collective-permute-start.17) | collective-permute-done | bytes 327712 | tf_op jit(solution)/shard_map/ppermute | solution.py:310
  70.6 1.7 collective-permute-start.24
  72.3 1.5 collective-permute-start.25
  73.8 1.0 copy-done.6
  74.8 1.0 copy-done.8
  75.7 10.3 %shard_map.117 = (bf16[128,1024]{1,0:T(8,128)(2,1)S(1)}, bf16[128,1024]{1,0:T(8,128)(2,1)S(1)}) custom-call(bf16[128,1280]{1,0:T(8,128)(2,1)S(1)} %get-tuple-element.64.refs_0_, bf16[128,1280]{1,0:T(8,128)(2,1)S(1)} %get-tuple-element.65.refs_1_, bf16[128,1280]{1,0:T(8,128)(2,1)S(1)} %copy-done.8, bf16[128,1408]{1,0:T(8,128)(2,1)S(1)} %get-tuple-element.67.refs_3_, ...), custom_call_target="tpu_custom_call" | custom-call | flops 5368709120 | bytes 24117248 | tf_op jit(solution)/shard_map/pallas_call | solution.py:226
  86.1 1.4 collective-permute-start.26
  88.1 1.5 collective-permute-start.20
  89.7 0.6 collective-permute-start.31
  90.3 7.6 %collective-permute-done.26.refs_2_ = bf16[128,1280]{1,0:T(8,128)(2,1)S(1)} collective-permute-done((bf16[128,1280]{1,0:T(8,128)(2,1)}, bf16[128,1280]{1,0:T(8,128)(2,1)S(1)}, u32[]{:S(2)}, u32[]{:S(2)}) %collective-permute-start.26) | collective-permute-done | bytes 327712 | tf_op jit(solution)/shard_map/ppermute | solution.py:310
  99.3 6.3 %collective-permute-done.28.refs_3_ = bf16[128,1408]{1,0:T(8,128)(2,1)S(1)} collective-permute-done((bf16[128,1408]{1,0:T(8,128)(2,1)S(1)}, bf16[128,1408]{1,0:T(8,128)(2,1)S(1)}, u32[]{:S(2)}, u32[]{:S(2)}) %collective-permute-start.28) | collective-permute-done | bytes 360480 | tf_op jit(solution)/shard_map/ppermute | solution.py:310
  106.1 0.7 copy-done.17
  107.3 1.0 copy-done.4
  108.3 11.6 %shard_map.118 = (bf16[128,1024]{1,0:T(8,128)(2,1)}, bf16[128,1024]{1,0:T(8,128)(2,1)S(1)}) custom-call(bf16[128,1280]{1,0:T(8,128)(2,1)S(1)} %collective-permute-done.13.refs_0_, bf16[128,1280]{1,0:T(8,128)(2,1)S(1)} %copy-done.4, bf16[128,1280]{1,0:T(8,128)(2,1)} %collective-permute-done.17.refs_2_, bf16[128,1408]{1,0:T(8,128)(2,1)S(1)} %collective-permute-done.19.refs_3_, ...), custom_call_target="tpu_custom_call" | custom-call | flops 5368709120 | bytes 24117248 | tf_op jit(solution)/shard_map/pallas_call | solution.py:226
  119.9 1.0 collective-permute-start.36
  120.9 2.2 %collective-permute-start.29 = (bf16[128,1024]{1,0:T(8,128)(2,1)}, bf16[128,1024]{1,0:T(8,128)(2,1)}, u32[]{:S(2)}, u32[]{:S(2)}) collective-permute-start(bf16[128,1024]{1,0:T(8,128)(2,1)} %get-tuple-element.82), channel_id=1, source_target_pairs={{0,16},{4,20},{8,0},{12,4},{16,24},{20,28},{24,8},{28,12},{1,17},{... | collective-permute-start | bytes 786440 | tf_op jit(solution)/shard_map/ppermute | solution.py:310
  123.1 1.6 collective-permute-start.37
  124.7 0.9 collective-permute-done.35.refs_6_
  125.6 1.9 collective-permute-start.30
  127.8 1.0 constant_dynamic-update-slice_fusion.7
  128.8 1.0 constant_dynamic-update-slice_fusion.6
  129.7 2.1 %collective-permute-done.36.refs_2_ = bf16[128,1280]{1,0:T(8,128)(2,1)S(1)} collective-permute-done((bf16[128,1280]{1,0:T(8,128)(2,1)S(1)}, bf16[128,1280]{1,0:T(8,128)(2,1)S(1)}, u32[]{:S(2)}, u32[]{:S(2)}) %collective-permute-start.36) | collective-permute-done | bytes 327712 | tf_op jit(solution)/shard_map/ppermute | solution.py:310
  132.2 3.5 %collective-permute-done.29 = bf16[128,1024]{1,0:T(8,128)(2,1)} collective-permute-done((bf16[128,1024]{1,0:T(8,128)(2,1)}, bf16[128,1024]{1,0:T(8,128)(2,1)}, u32[]{:S(2)}, u32[]{:S(2)}) %collective-permute-start.29) | collective-permute-done | bytes 262176 | tf_op jit(solution)/shard_map/ppermute | solution.py:310
  135.6 1.6 collective-permute-start.43
  137.2 1.0 constant_dynamic-update-slice_fusion.5
  138.2 4.1 %collective-permute-done.30 = bf16[128,1024]{1,0:T(8,128)(2,1)S(1)} collective-permute-done((bf16[128,1024]{1,0:T(8,128)(2,1)}, bf16[128,1024]{1,0:T(8,128)(2,1)S(1)}, u32[]{:S(2)}, u32[]{:S(2)}) %collective-permute-start.30) | collective-permute-done | bytes 262176 | tf_op jit(solution)/shard_map/ppermute | solution.py:310
  142.3 1.0 collective-permute-start.44
  143.4 1.3 copy-done.16
  144.7 1.0 collective-permute-start.45
  145.7 1.0 copy-done.2
  146.6 11.7 %shard_map.119 = (bf16[128,1024]{1,0:T(8,128)(2,1)}, bf16[128,1024]{1,0:T(8,128)(2,1)S(1)}) custom-call(bf16[128,1280]{1,0:T(8,128)(2,1)S(1)} %collective-permute-done.22.refs_0_, bf16[128,1280]{1,0:T(8,128)(2,1)S(1)} %collective-permute-done.24.refs_1_, bf16[128,1280]{1,0:T(8,128)(2,1)S(1)} %collective-permute-done.26.refs_2_, ...), custom_call_target="tpu_custom_call" | custom-call | flops 5368709120 | bytes 24117248 | tf_op jit(solution)/shard_map/pallas_call | solution.py:226
  158.3 0.7 copy-done.14
  159.0 1.3 collective-permute-start.39
  160.3 8.8 %shard_map.120 = bf16[128,1024]{1,0:T(8,128)(2,1)S(1)} custom-call(bf16[128,1280]{1,0:T(8,128)(2,1)S(1)} %collective-permute-done.32.refs_0_, bf16[128,1280]{1,0:T(8,128)(2,1)S(1)} %collective-permute-done.34.refs_1_, bf16[128,1280]{1,0:T(8,128)(2,1)S(1)} %collective-permute-done.36.refs_2_, bf16[128,1408]{1,0:T(8,128)(2,1)S(1)} %collective-permute-done.38.refs_3_, ...), custom_call_target="tpu_custom_call" | custom-call | flops 2684354560 | bytes 22544384 | tf_op jit(solution)/shard_map/pallas_call | solution.py:226
  169.2 1.6 copy-done
  170.8 2.5 %shard_map.121 = bf16[16,16,2048]{2,1,0:T(8,128)(2,1)} custom-call(s32[16]{0:T(128)S(1)} %broadcast_add_fusion.page_ref, bf16[512,2048]{1,0:T(8,128)(2,1)S(1)} %copy-done, bf16[16,16,2048]{2,1,0:T(8,128)(2,1)} %cache_ref.1), custom_call_target="tpu_custom_call" | custom-call | bytes 4194304 | tf_op jit(solution)/shard_map/pallas_call | solution.py:260
  173.3 3.0 %collective-permute-start.40 = (bf16[128,1024]{1,0:T(8,128)(2,1)S(1)}, bf16[128,1024]{1,0:T(8,128)(2,1)S(1)}, u32[]{:S(2)}, u32[]{:S(2)}) collective-permute-start(bf16[128,1024]{1,0:T(8,128)(2,1)S(1)} %copy-done.15), channel_id=1, source_target_pairs={{0,28},{4,24},{8,20},{12,16},{16,12},{20,8},{24,4},{28,0},{1,29},{... | collective-permute-start | bytes 786440 | tf_op jit(solution)/shard_map/ppermute | solution.py:310
  176.3 9.0 %shard_map.122 = bf16[128,1024]{1,0:T(8,128)(2,1)S(1)} custom-call(bf16[128,1280]{1,0:T(8,128)(2,1)} %collective-permute-done.42.refs_0_, bf16[128,1280]{1,0:T(8,128)(2,1)} %collective-permute-done.43.refs_1_, bf16[128,1280]{1,0:T(8,128)(2,1)} %collective-permute-done.44.refs_2_, bf16[128,1408]{1,0:T(8,128)(2,1)S(1)} %collective-permute-done.45.refs_3_, ...), custom_call_target="tpu_custom_call" | custom-call | flops 2684354560 | bytes 22544384 | tf_op jit(solution)/shard_map/pallas_call | solution.py:226
  185.3 2.4 %collective-permute-start.46 = (bf16[128,1024]{1,0:T(8,128)(2,1)S(1)}, bf16[128,1024]{1,0:T(8,128)(2,1)S(1)}, u32[]{:S(2)}, u32[]{:S(2)}) collective-permute-start(bf16[128,1024]{1,0:T(8,128)(2,1)S(1)} %shard_map.122), channel_id=1, source_target_pairs={{0,12},{4,8},{8,28},{12,24},{16,4},{20,0},{24,20},{28,16},{1,13},{... | collective-permute-start | bytes 786440 | tf_op jit(solution)/shard_map/ppermute | solution.py:310
  187.7 0.7 constant_dynamic-update-slice_fusion.3
  188.4 0.7 constant_dynamic-update-slice_fusion.2
  189.1 0.7 constant_dynamic-update-slice_fusion.1
  189.9 3.7 %collective-permute-done.46 = bf16[128,1024]{1,0:T(8,128)(2,1)S(1)} collective-permute-done((bf16[128,1024]{1,0:T(8,128)(2,1)S(1)}, bf16[128,1024]{1,0:T(8,128)(2,1)S(1)}, u32[]{:S(2)}, u32[]{:S(2)}) %collective-permute-start.46) | collective-permute-done | bytes 262176 | tf_op jit(solution)/shard_map/ppermute | solution.py:310
  193.5 0.7 constant_dynamic-update-slice_fusion
  (97 shorter events, 9.0 us)
Async XLA Ops:
  7.2 23.0 %copy-start.10 = (f32[5120]{0:T(1024)S(1)}, f32[5120]{0:T(1024)}, u32[]{:S(2)}) copy-start(f32[5120]{0:T(1024)} %param.13) | copy-start | bytes 61444
  7.2 162.0 %all-gather.2.cloned.1.call-start = ((), (), s32[]{:S(2)}) async-start(), calls=%async_computation | async-start | bytes 2621440 | tf_op jit(solution)/shard_map/all_gather | solution.py:336
  9.0 12.5 %collective-permute-start.3 = (bf16[144,512]{1,0:T(8,128)(2,1)S(1)}, bf16[144,512]{1,0:T(8,128)(2,1)S(1)}, u32[]{:S(2)}, u32[]{:S(2)}) collective-permute-start(bf16[144,512]{1,0:T(8,128)(2,1)S(1)} %get-tuple-element.53.refs_3_), channel_id=1, source_target_pairs={{0,1},{1,0},{2,3},{3,2},{4,5},{5,4},{6,7},{7,6},{8,9},{9,8},{10,11... | collective-permute-start | bytes 442376 | tf_op jit(solution)/shard_map/ppermute | solution.py:303
  9.5 12.0 %collective-permute-start.4 = (bf16[144,512]{1,0:T(8,128)(2,1)S(1)}, bf16[144,512]{1,0:T(8,128)(2,1)S(1)}, u32[]{:S(2)}, u32[]{:S(2)}) collective-permute-start(bf16[144,512]{1,0:T(8,128)(2,1)S(1)} %get-tuple-element.53.refs_3_), channel_id=1, source_target_pairs={{0,2},{1,3},{2,0},{3,1},{4,6},{5,7},{6,4},{7,5},{8,10},{9,11},{10,... | collective-permute-start | bytes 442376 | tf_op jit(solution)/shard_map/ppermute | solution.py:303
  12.1 7.5 %collective-permute-start.10 = (bf16[128,512]{1,0:T(8,128)(2,1)S(1)}, bf16[128,512]{1,0:T(8,128)(2,1)S(1)}, u32[]{:S(2)}, u32[]{:S(2)}) collective-permute-start(bf16[128,512]{1,0:T(8,128)(2,1)S(1)} %get-tuple-element.56.refs_3_), channel_id=1, source_target_pairs={{0,2},{1,3},{2,0},{3,1},{4,6},{5,7},{6,4},{7,5},{8,10},{9,11},{10,... | collective-permute-start | bytes 393224 | tf_op jit(solution)/shard_map/ppermute | solution.py:303
  12.1 16.4 %collective-permute-start.9 = (bf16[128,512]{1,0:T(8,128)(2,1)S(1)}, bf16[128,512]{1,0:T(8,128)(2,1)S(1)}, u32[]{:S(2)}, u32[]{:S(2)}) collective-permute-start(bf16[128,512]{1,0:T(8,128)(2,1)S(1)} %get-tuple-element.56.refs_3_), channel_id=1, source_target_pairs={{0,1},{1,0},{2,3},{3,2},{4,5},{5,4},{6,7},{7,6},{8,9},{9,8},{10,11... | collective-permute-start | bytes 393224 | tf_op jit(solution)/shard_map/ppermute | solution.py:303
  12.2 21.6 %collective-permute-start.1 = (bf16[128,512]{1,0:T(8,128)(2,1)S(1)}, bf16[128,512]{1,0:T(8,128)(2,1)S(1)}, u32[]{:S(2)}, u32[]{:S(2)}) collective-permute-start(bf16[128,512]{1,0:T(8,128)(2,1)S(1)} %get-tuple-element.52.refs_3_), channel_id=1, source_target_pairs={{0,2},{1,3},{2,0},{3,1},{4,6},{5,7},{6,4},{7,5},{8,10},{9,11},{10,... | collective-permute-start | bytes 393224 | tf_op jit(solution)/shard_map/ppermute | solution.py:303
  19.6 14.3 %collective-permute-start.7 = (bf16[128,512]{1,0:T(8,128)(2,1)S(1)}, bf16[128,512]{1,0:T(8,128)(2,1)S(1)}, u32[]{:S(2)}, u32[]{:S(2)}) collective-permute-start(bf16[128,512]{1,0:T(8,128)(2,1)S(1)} %get-tuple-element.55.refs_3_), channel_id=1, source_target_pairs={{0,2},{1,3},{2,0},{3,1},{4,6},{5,7},{6,4},{7,5},{8,10},{9,11},{10,... | collective-permute-start | bytes 393224 | tf_op jit(solution)/shard_map/ppermute | solution.py:303
  21.5 8.7 %collective-permute-start.11 = (bf16[128,512]{1,0:T(8,128)(2,1)S(1)}, bf16[128,512]{1,0:T(8,128)(2,1)S(1)}, u32[]{:S(2)}, u32[]{:S(2)}) collective-permute-start(bf16[128,512]{1,0:T(8,128)(2,1)S(1)} %collective-permute-done.10.refs_5_), channel_id=1, source_target_pairs={{0,1},{1,0},{2,3},{3,2},{4,5},{5,4},{6,7},{7,6},{8,9},{9,8},{10,11... | collective-permute-start | bytes 393224 | tf_op jit(solution)/shard_map/ppermute | solution.py:303
  21.5 1.6 collective-permute-start.5
  23.1 0.7 copy-start.9
  27.1 19.3 %collective-permute-start.12 = (bf16[128,1280]{1,0:T(8,128)(2,1)S(1)}, bf16[128,1280]{1,0:T(8,128)(2,1)S(1)}, u32[]{:S(2)}, u32[]{:S(2)}) collective-permute-start(bf16[128,1280]{1,0:T(8,128)(2,1)S(1)} %get-tuple-element.64.refs_0_), channel_id=1, source_target_pairs={{0,4},{4,0},{8,12},{12,8},{16,20},{20,16},{24,28},{28,24},{1,5},{5... | collective-permute-start | bytes 983048 | tf_op jit(solution)/shard_map/ppermute | solution.py:310
  28.6 18.2 %collective-permute-start.13 = (bf16[128,1280]{1,0:T(8,128)(2,1)S(1)}, bf16[128,1280]{1,0:T(8,128)(2,1)S(1)}, u32[]{:S(2)}, u32[]{:S(2)}) collective-permute-start(bf16[128,1280]{1,0:T(8,128)(2,1)S(1)} %get-tuple-element.64.refs_0_), channel_id=1, source_target_pairs={{0,8},{4,12},{8,24},{12,28},{16,0},{20,4},{24,16},{28,20},{1,9},{5... | collective-permute-start | bytes 983048 | tf_op jit(solution)/shard_map/ppermute | solution.py:310
  33.3 13.9 %collective-permute-start.14 = (bf16[128,1280]{1,0:T(8,128)(2,1)S(1)}, bf16[128,1280]{1,0:T(8,128)(2,1)S(1)}, u32[]{:S(2)}, u32[]{:S(2)}) collective-permute-start(bf16[128,1280]{1,0:T(8,128)(2,1)S(1)} %get-tuple-element.65.refs_1_), channel_id=1, source_target_pairs={{0,4},{4,0},{8,12},{12,8},{16,20},{20,16},{24,28},{28,24},{1,5},{5... | collective-permute-start | bytes 983048 | tf_op jit(solution)/shard_map/ppermute | solution.py:310
  33.9 1.3 collective-permute-start.6
  33.9 1.5 collective-permute-start.8
  35.2 3.7 %collective-permute-start = (bf16[128,512]{1,0:T(8,128)(2,1)S(1)}, bf16[128,512]{1,0:T(8,128)(2,1)S(1)}, u32[]{:S(2)}, u32[]{:S(2)}) collective-permute-start(bf16[128,512]{1,0:T(8,128)(2,1)S(1)} %get-tuple-element.52.refs_3_), channel_id=1, source_target_pairs={{0,1},{1,0},{2,3},{3,2},{4,5},{5,4},{6,7},{7,6},{8,9},{9,8},{10,11... | collective-permute-start | bytes 393224 | tf_op jit(solution)/shard_map/ppermute | solution.py:303
  35.4 3.5 %collective-permute-start.2 = (bf16[128,512]{1,0:T(8,128)(2,1)S(1)}, bf16[128,512]{1,0:T(8,128)(2,1)S(1)}, u32[]{:S(2)}, u32[]{:S(2)}) collective-permute-start(bf16[128,512]{1,0:T(8,128)(2,1)S(1)} %collective-permute-done.1.refs_5_), channel_id=1, source_target_pairs={{0,1},{1,0},{2,3},{3,2},{4,5},{5,4},{6,7},{7,6},{8,9},{9,8},{10,11... | collective-permute-start | bytes 393224 | tf_op jit(solution)/shard_map/ppermute | solution.py:303
  38.9 8.4 %copy-start.7 = (bf16[128,1280]{1,0:T(8,128)(2,1)}, bf16[128,1280]{1,0:T(8,128)(2,1)S(1)}, u32[]{:S(2)}) copy-start(bf16[128,1280]{1,0:T(8,128)(2,1)S(1)} %get-tuple-element.66.refs_2_) | copy-start | bytes 983044
  42.2 28.4 %collective-permute-start.18 = (bf16[128,1408]{1,0:T(8,128)(2,1)S(1)}, bf16[128,1408]{1,0:T(8,128)(2,1)S(1)}, u32[]{:S(2)}, u32[]{:S(2)}) collective-permute-start(bf16[128,1408]{1,0:T(8,128)(2,1)S(1)} %get-tuple-element.67.refs_3_), channel_id=1, source_target_pairs={{0,4},{4,0},{8,12},{12,8},{16,20},{20,16},{24,28},{28,24},{1,5},{5... | collective-permute-start | bytes 1081352 | tf_op jit(solution)/shard_map/ppermute | solution.py:310
  43.7 28.5 %collective-permute-start.19 = (bf16[128,1408]{1,0:T(8,128)(2,1)S(1)}, bf16[128,1408]{1,0:T(8,128)(2,1)S(1)}, u32[]{:S(2)}, u32[]{:S(2)}) collective-permute-start(bf16[128,1408]{1,0:T(8,128)(2,1)S(1)} %get-tuple-element.67.refs_3_), channel_id=1, source_target_pairs={{0,8},{4,12},{8,24},{12,28},{16,0},{20,4},{24,16},{28,20},{1,9},{5... | collective-permute-start | bytes 1081352 | tf_op jit(solution)/shard_map/ppermute | solution.py:310
  46.3 16.6 %collective-permute-start.15 = (bf16[128,1280]{1,0:T(8,128)(2,1)S(1)}, bf16[128,1280]{1,0:T(8,128)(2,1)S(1)}, u32[]{:S(2)}, u32[]{:S(2)}) collective-permute-start(bf16[128,1280]{1,0:T(8,128)(2,1)S(1)} %get-tuple-element.65.refs_1_), channel_id=1, source_target_pairs={{0,8},{4,12},{8,24},{12,28},{16,0},{20,4},{24,16},{28,20},{1,9},{5... | collective-permute-start | bytes 983048 | tf_op jit(solution)/shard_map/ppermute | solution.py:310
  46.8 16.7 %collective-permute-start.16 = (bf16[128,1280]{1,0:T(8,128)(2,1)S(1)}, bf16[128,1280]{1,0:T(8,128)(2,1)}, u32[]{:S(2)}, u32[]{:S(2)}) collective-permute-start(bf16[128,1280]{1,0:T(8,128)(2,1)S(1)} %get-tuple-element.66.refs_2_), channel_id=1, source_target_pairs={{0,4},{4,0},{8,12},{12,8},{16,20},{20,16},{24,28},{28,24},{1,5},{5... | collective-permute-start | bytes 983048 | tf_op jit(solution)/shard_map/ppermute | solution.py:310
  47.3 16.2 %copy-start.5 = (bf16[128,1280]{1,0:T(8,128)(2,1)}, bf16[128,1280]{1,0:T(8,128)(2,1)S(1)}, u32[]{:S(2)}) copy-start(bf16[128,1280]{1,0:T(8,128)(2,1)S(1)} %collective-permute-done.14.refs_5_) | copy-start | bytes 983044
  47.3 22.8 %collective-permute-start.17 = (bf16[128,1280]{1,0:T(8,128)(2,1)S(1)}, bf16[128,1280]{1,0:T(8,128)(2,1)}, u32[]{:S(2)}, u32[]{:S(2)}) collective-permute-start(bf16[128,1280]{1,0:T(8,128)(2,1)S(1)} %get-tuple-element.66.refs_2_), channel_id=1, source_target_pairs={{0,8},{4,12},{8,24},{12,28},{16,0},{20,4},{24,16},{28,20},{1,9},{5... | collective-permute-start | bytes 983048 | tf_op jit(solution)/shard_map/ppermute | solution.py:310
  47.7 41.9 %copy-start.18 = (s32[1,64]{1,0:T(1,128)S(1)}, s32[1,64]{1,0:T(1,128)}, u32[]{:S(2)}) copy-start(s32[1,64]{1,0:T(1,128)} %param.17) | copy-start | bytes 772
  62.9 23.1 %copy-start.3 = (bf16[128,1280]{1,0:T(8,128)(2,1)}, bf16[128,1280]{1,0:T(8,128)(2,1)S(1)}, u32[]{:S(2)}) copy-start(bf16[128,1280]{1,0:T(8,128)(2,1)S(1)} %collective-permute-done.15.refs_1_) | copy-start | bytes 983044
  62.9 23.1 %collective-permute-start.21 = (bf16[128,1280]{1,0:T(8,128)(2,1)S(1)}, bf16[128,1280]{1,0:T(8,128)(2,1)S(1)}, u32[]{:S(2)}, u32[]{:S(2)}) collective-permute-start(bf16[128,1280]{1,0:T(8,128)(2,1)S(1)} %collective-permute-done.13.refs_0_), channel_id=1, source_target_pairs={{0,4},{4,0},{8,12},{12,8},{16,20},{20,16},{24,28},{28,24},{1,5},{5... | collective-permute-start | bytes 983048 | tf_op jit(solution)/shard_map/ppermute | solution.py:310
  63.5 24.0 %collective-permute-start.22 = (bf16[128,1280]{1,0:T(8,128)(2,1)S(1)}, bf16[128,1280]{1,0:T(8,128)(2,1)S(1)}, u32[]{:S(2)}, u32[]{:S(2)}) collective-permute-start(bf16[128,1280]{1,0:T(8,128)(2,1)S(1)} %collective-permute-done.13.refs_0_), channel_id=1, source_target_pairs={{0,8},{4,12},{8,24},{12,28},{16,0},{20,4},{24,16},{28,20},{1,9},{5... | collective-permute-start | bytes 983048 | tf_op jit(solution)/shard_map/ppermute | solution.py:310
  70.1 17.9 %collective-permute-start.23 = (bf16[128,1280]{1,0:T(8,128)(2,1)S(1)}, bf16[128,1280]{1,0:T(8,128)(2,1)S(1)}, u32[]{:S(2)}, u32[]{:S(2)}) collective-permute-start(bf16[128,1280]{1,0:T(8,128)(2,1)S(1)} %collective-permute-done.15.refs_1_), channel_id=1, source_target_pairs={{0,4},{4,0},{8,12},{12,8},{16,20},{20,16},{24,28},{28,24},{1,5},{5... | collective-permute-start | bytes 983048 | tf_op jit(solution)/shard_map/ppermute | solution.py:310
  70.6 17.5 %collective-permute-start.24 = (bf16[128,1280]{1,0:T(8,128)(2,1)S(1)}, bf16[128,1280]{1,0:T(8,128)(2,1)S(1)}, u32[]{:S(2)}, u32[]{:S(2)}) collective-permute-start(bf16[128,1280]{1,0:T(8,128)(2,1)S(1)} %collective-permute-done.15.refs_1_), channel_id=1, source_target_pairs={{0,8},{4,12},{8,24},{12,28},{16,0},{20,4},{24,16},{28,20},{1,9},{5... | collective-permute-start | bytes 983048 | tf_op jit(solution)/shard_map/ppermute | solution.py:310
  72.3 17.5 %collective-permute-start.25 = (bf16[128,1280]{1,0:T(8,128)(2,1)}, bf16[128,1280]{1,0:T(8,128)(2,1)S(1)}, u32[]{:S(2)}, u32[]{:S(2)}) collective-permute-start(bf16[128,1280]{1,0:T(8,128)(2,1)} %collective-permute-done.17.refs_2_), channel_id=1, source_target_pairs={{0,4},{4,0},{8,12},{12,8},{16,20},{20,16},{24,28},{28,24},{1,5},{5... | collective-permute-start | bytes 983048 | tf_op jit(solution)/shard_map/ppermute | solution.py:310
  73.8 1.0 copy-start.6
  74.8 1.0 copy-start.8
  86.1 20.0 %copy-start.11 = (bf16[128,1024]{1,0:T(8,128)(2,1)}, bf16[128,1024]{1,0:T(8,128)(2,1)S(1)}, u32[]{:S(2)}) copy-start(bf16[128,1024]{1,0:T(8,128)(2,1)S(1)} %get-tuple-element.72) | copy-start | bytes 786436
  86.1 11.8 %collective-permute-start.26 = (bf16[128,1280]{1,0:T(8,128)(2,1)}, bf16[128,1280]{1,0:T(8,128)(2,1)S(1)}, u32[]{:S(2)}, u32[]{:S(2)}) collective-permute-start(bf16[128,1280]{1,0:T(8,128)(2,1)} %collective-permute-done.17.refs_2_), channel_id=1, source_target_pairs={{0,8},{4,12},{8,24},{12,28},{16,0},{20,4},{24,16},{28,20},{1,9},{5... | collective-permute-start | bytes 983048 | tf_op jit(solution)/shard_map/ppermute | solution.py:310
  87.5 11.3 %collective-permute-start.27 = (bf16[128,1408]{1,0:T(8,128)(2,1)S(1)}, bf16[128,1408]{1,0:T(8,128)(2,1)S(1)}, u32[]{:S(2)}, u32[]{:S(2)}) collective-permute-start(bf16[128,1408]{1,0:T(8,128)(2,1)S(1)} %collective-permute-done.19.refs_3_), channel_id=1, source_target_pairs={{0,4},{4,0},{8,12},{12,8},{16,20},{20,16},{24,28},{28,24},{1,5},{5... | collective-permute-start | bytes 1081352 | tf_op jit(solution)/shard_map/ppermute | solution.py:310
  88.0 17.6 %collective-permute-start.28 = (bf16[128,1408]{1,0:T(8,128)(2,1)S(1)}, bf16[128,1408]{1,0:T(8,128)(2,1)S(1)}, u32[]{:S(2)}, u32[]{:S(2)}) collective-permute-start(bf16[128,1408]{1,0:T(8,128)(2,1)S(1)} %collective-permute-done.19.refs_3_), channel_id=1, source_target_pairs={{0,8},{4,12},{8,24},{12,28},{16,0},{20,4},{24,16},{28,20},{1,9},{5... | collective-permute-start | bytes 1081352 | tf_op jit(solution)/shard_map/ppermute | solution.py:310
  88.1 18.0 %collective-permute-start.20 = (bf16[128,1024]{1,0:T(8,128)(2,1)S(1)}, bf16[128,1024]{1,0:T(8,128)(2,1)S(1)}, u32[]{:S(2)}, u32[]{:S(2)}) collective-permute-start(bf16[128,1024]{1,0:T(8,128)(2,1)S(1)} %get-tuple-element.73), channel_id=1, source_target_pairs={{0,4},{4,0},{8,12},{12,8},{16,20},{20,16},{24,28},{28,24},{1,5},{5... | collective-permute-start | bytes 786440 | tf_op jit(solution)/shard_map/ppermute | solution.py:310
  89.7 30.2 %collective-permute-start.31 = (bf16[128,1280]{1,0:T(8,128)(2,1)S(1)}, bf16[128,1280]{1,0:T(8,128)(2,1)S(1)}, u32[]{:S(2)}, u32[]{:S(2)}) collective-permute-start(bf16[128,1280]{1,0:T(8,128)(2,1)S(1)} %collective-permute-done.22.refs_0_), channel_id=1, source_target_pairs={{0,4},{4,0},{8,12},{12,8},{16,20},{20,16},{24,28},{28,24},{1,5},{5... | collective-permute-start | bytes 983048 | tf_op jit(solution)/shard_map/ppermute | solution.py:310
  97.9 23.0 %collective-permute-start.32 = (bf16[128,1280]{1,0:T(8,128)(2,1)S(1)}, bf16[128,1280]{1,0:T(8,128)(2,1)S(1)}, u32[]{:S(2)}, u32[]{:S(2)}) collective-permute-start(bf16[128,1280]{1,0:T(8,128)(2,1)S(1)} %collective-permute-done.22.refs_0_), channel_id=1, source_target_pairs={{0,8},{4,12},{8,24},{12,28},{16,0},{20,4},{24,16},{28,20},{1,9},{5... | collective-permute-start | bytes 983048 | tf_op jit(solution)/shard_map/ppermute | solution.py:310
  98.8 24.3 %collective-permute-start.33 = (bf16[128,1280]{1,0:T(8,128)(2,1)S(1)}, bf16[128,1280]{1,0:T(8,128)(2,1)S(1)}, u32[]{:S(2)}, u32[]{:S(2)}) collective-permute-start(bf16[128,1280]{1,0:T(8,128)(2,1)S(1)} %collective-permute-done.24.refs_1_), channel_id=1, source_target_pairs={{0,4},{4,0},{8,12},{12,8},{16,20},{20,16},{24,28},{28,24},{1,5},{5... | collective-permute-start | bytes 983048 | tf_op jit(solution)/shard_map/ppermute | solution.py:310
  105.6 19.1 %collective-permute-start.34 = (bf16[128,1280]{1,0:T(8,128)(2,1)S(1)}, bf16[128,1280]{1,0:T(8,128)(2,1)S(1)}, u32[]{:S(2)}, u32[]{:S(2)}) collective-permute-start(bf16[128,1280]{1,0:T(8,128)(2,1)S(1)} %collective-permute-done.24.refs_1_), channel_id=1, source_target_pairs={{0,8},{4,12},{8,24},{12,28},{16,0},{20,4},{24,16},{28,20},{1,9},{5... | collective-permute-start | bytes 983048 | tf_op jit(solution)/shard_map/ppermute | solution.py:310
  106.8 18.9 %collective-permute-start.35 = (bf16[128,1280]{1,0:T(8,128)(2,1)S(1)}, bf16[128,1280]{1,0:T(8,128)(2,1)}, u32[]{:S(2)}, u32[]{:S(2)}) collective-permute-start(bf16[128,1280]{1,0:T(8,128)(2,1)S(1)} %collective-permute-done.26.refs_2_), channel_id=1, source_target_pairs={{0,4},{4,0},{8,12},{12,8},{16,20},{20,16},{24,28},{28,24},{1,5},{5... | collective-permute-start | bytes 983048 | tf_op jit(solution)/shard_map/ppermute | solution.py:310
  107.3 1.0 copy-start.4
  119.9 1.0 copy-start.13
  119.9 11.9 %collective-permute-start.36 = (bf16[128,1280]{1,0:T(8,128)(2,1)S(1)}, bf16[128,1280]{1,0:T(8,128)(2,1)S(1)}, u32[]{:S(2)}, u32[]{:S(2)}) collective-permute-start(bf16[128,1280]{1,0:T(8,128)(2,1)S(1)} %collective-permute-done.26.refs_2_), channel_id=1, source_target_pairs={{0,8},{4,12},{8,24},{12,28},{16,0},{20,4},{24,16},{28,20},{1,9},{5... | collective-permute-start | bytes 983048 | tf_op jit(solution)/shard_map/ppermute | solution.py:310
  120.9 14.7 %collective-permute-start.29 = (bf16[128,1024]{1,0:T(8,128)(2,1)}, bf16[128,1024]{1,0:T(8,128)(2,1)}, u32[]{:S(2)}, u32[]{:S(2)}) collective-permute-start(bf16[128,1024]{1,0:T(8,128)(2,1)} %get-tuple-element.82), channel_id=1, source_target_pairs={{0,16},{4,20},{8,0},{12,4},{16,24},{20,28},{24,8},{28,12},{1,17},{... | collective-permute-start | bytes 786440 | tf_op jit(solution)/shard_map/ppermute | solution.py:310
  123.1 20.2 %copy-start.1 = (bf16[128,1280]{1,0:T(8,128)(2,1)}, bf16[128,1280]{1,0:T(8,128)(2,1)S(1)}, u32[]{:S(2)}) copy-start(bf16[128,1280]{1,0:T(8,128)(2,1)S(1)} %collective-permute-done.33.refs_5_) | copy-start | bytes 983044
  123.1 20.2 %collective-permute-start.37 = (bf16[128,1408]{1,0:T(8,128)(2,1)S(1)}, bf16[128,1408]{1,0:T(8,128)(2,1)S(1)}, u32[]{:S(2)}, u32[]{:S(2)}) collective-permute-start(bf16[128,1408]{1,0:T(8,128)(2,1)S(1)} %collective-permute-done.28.refs_3_), channel_id=1, source_target_pairs={{0,4},{4,0},{8,12},{12,8},{16,20},{20,16},{24,28},{28,24},{1,5},{5... | collective-permute-start | bytes 1081352 | tf_op jit(solution)/shard_map/ppermute | solution.py:310
  124.7 18.7 %collective-permute-start.38 = (bf16[128,1408]{1,0:T(8,128)(2,1)S(1)}, bf16[128,1408]{1,0:T(8,128)(2,1)S(1)}, u32[]{:S(2)}, u32[]{:S(2)}) collective-permute-start(bf16[128,1408]{1,0:T(8,128)(2,1)S(1)} %collective-permute-done.28.refs_3_), channel_id=1, source_target_pairs={{0,8},{4,12},{8,24},{12,28},{16,0},{20,4},{24,16},{28,20},{1,9},{5... | collective-permute-start | bytes 1081352 | tf_op jit(solution)/shard_map/ppermute | solution.py:310
  125.6 16.6 %collective-permute-start.30 = (bf16[128,1024]{1,0:T(8,128)(2,1)}, bf16[128,1024]{1,0:T(8,128)(2,1)S(1)}, u32[]{:S(2)}, u32[]{:S(2)}) collective-permute-start(bf16[128,1024]{1,0:T(8,128)(2,1)} %copy-done.13), channel_id=1, source_target_pairs={{0,20},{4,16},{8,4},{12,0},{16,28},{20,24},{24,12},{28,8},{1,21},{... | collective-permute-start | bytes 786440 | tf_op jit(solution)/shard_map/ppermute | solution.py:310
  131.8 44.4 %collective-permute-start.42 = (bf16[128,1280]{1,0:T(8,128)(2,1)S(1)}, bf16[128,1280]{1,0:T(8,128)(2,1)}, u32[]{:S(2)}, u32[]{:S(2)}) collective-permute-start(bf16[128,1280]{1,0:T(8,128)(2,1)S(1)} %collective-permute-done.32.refs_0_), channel_id=1, source_target_pairs={{0,4},{4,0},{8,12},{12,8},{16,20},{20,16},{24,28},{28,24},{1,5},{5... | collective-permute-start | bytes 983048 | tf_op jit(solution)/shard_map/ppermute | solution.py:310
  135.6 40.6 %collective-permute-start.43 = (bf16[128,1280]{1,0:T(8,128)(2,1)S(1)}, bf16[128,1280]{1,0:T(8,128)(2,1)}, u32[]{:S(2)}, u32[]{:S(2)}) collective-permute-start(bf16[128,1280]{1,0:T(8,128)(2,1)S(1)} %collective-permute-done.34.refs_1_), channel_id=1, source_target_pairs={{0,4},{4,0},{8,12},{12,8},{16,20},{20,16},{24,28},{28,24},{1,5},{5... | collective-permute-start | bytes 983048 | tf_op jit(solution)/shard_map/ppermute | solution.py:310
  142.3 34.0 %collective-permute-start.44 = (bf16[128,1280]{1,0:T(8,128)(2,1)S(1)}, bf16[128,1280]{1,0:T(8,128)(2,1)}, u32[]{:S(2)}, u32[]{:S(2)}) collective-permute-start(bf16[128,1280]{1,0:T(8,128)(2,1)S(1)} %collective-permute-done.36.refs_2_), channel_id=1, source_target_pairs={{0,4},{4,0},{8,12},{12,8},{16,20},{20,16},{24,28},{28,24},{1,5},{5... | collective-permute-start | bytes 983048 | tf_op jit(solution)/shard_map/ppermute | solution.py:310
  143.3 1.3 copy-start.16
  144.7 28.6 %collective-permute-start.45 = (bf16[128,1408]{1,0:T(8,128)(2,1)S(1)}, bf16[128,1408]{1,0:T(8,128)(2,1)S(1)}, u32[]{:S(2)}, u32[]{:S(2)}) collective-permute-start(bf16[128,1408]{1,0:T(8,128)(2,1)S(1)} %collective-permute-done.38.refs_3_), channel_id=1, source_target_pairs={{0,4},{4,0},{8,12},{12,8},{16,20},{20,16},{24,28},{28,24},{1,5},{5... | collective-permute-start | bytes 1081352 | tf_op jit(solution)/shard_map/ppermute | solution.py:310
  145.7 1.0 copy-start.2
  159.0 28.7 %collective-permute-start.39 = (bf16[128,1024]{1,0:T(8,128)(2,1)}, bf16[128,1024]{1,0:T(8,128)(2,1)S(1)}, u32[]{:S(2)}, u32[]{:S(2)}) collective-permute-start(bf16[128,1024]{1,0:T(8,128)(2,1)} %get-tuple-element.92), channel_id=1, source_target_pairs={{0,24},{4,28},{8,16},{12,20},{16,8},{20,12},{24,0},{28,4},{1,25},{... | collective-permute-start | bytes 786440 | tf_op jit(solution)/shard_map/ppermute | solution.py:310
  169.2 1.6 copy-start
  170.8 2.5 %copy-start.15 = (bf16[128,1024]{1,0:T(8,128)(2,1)S(1)}, bf16[128,1024]{1,0:T(8,128)(2,1)}, u32[]{:S(2)}) copy-start(bf16[128,1024]{1,0:T(8,128)(2,1)} %copy-done.14) | copy-start | bytes 786436
  173.3 15.1 %collective-permute-start.40 = (bf16[128,1024]{1,0:T(8,128)(2,1)S(1)}, bf16[128,1024]{1,0:T(8,128)(2,1)S(1)}, u32[]{:S(2)}, u32[]{:S(2)}) collective-permute-start(bf16[128,1024]{1,0:T(8,128)(2,1)S(1)} %copy-done.15), channel_id=1, source_target_pairs={{0,28},{4,24},{8,20},{12,16},{16,12},{20,8},{24,4},{28,0},{1,29},{... | collective-permute-start | bytes 786440 | tf_op jit(solution)/shard_map/ppermute | solution.py:310
  176.2 12.9 %collective-permute-start.41 = (bf16[128,1024]{1,0:T(8,128)(2,1)S(1)}, bf16[128,1024]{1,0:T(8,128)(2,1)S(1)}, u32[]{:S(2)}, u32[]{:S(2)}) collective-permute-start(bf16[128,1024]{1,0:T(8,128)(2,1)S(1)} %shard_map.120), channel_id=1, source_target_pairs={{0,8},{4,12},{8,24},{12,28},{16,0},{20,4},{24,16},{28,20},{1,9},{5... | collective-permute-start | bytes 786440 | tf_op jit(solution)/shard_map/ppermute | solution.py:310
  185.3 8.2 %collective-permute-start.46 = (bf16[128,1024]{1,0:T(8,128)(2,1)S(1)}, bf16[128,1024]{1,0:T(8,128)(2,1)S(1)}, u32[]{:S(2)}, u32[]{:S(2)}) collective-permute-start(bf16[128,1024]{1,0:T(8,128)(2,1)S(1)} %shard_map.122), channel_id=1, source_target_pairs={{0,12},{4,8},{8,28},{12,24},{16,4},{20,0},{24,20},{28,16},{1,13},{... | collective-permute-start | bytes 786440 | tf_op jit(solution)/shard_map/ppermute | solution.py:310
  (3 other events, 2.1 us)
Sparse Core Ops, SparseCore 0:
  47.8 22.8 all-gather.1

commit v6 on v5

--- a/solution.py
+++ b/solution.py
@@ -13,7 +13,7 @@
 HEAD_SIZE = 128
 PAGE_TOKENS = 16
 GROUP_SPLIT = QUERY_HEADS // KEY_VALUE_HEADS
-HEAD_CHUNKS = (2, 2, 2, 2)
+HEAD_CHUNKS = (3, 5)
 SEG_ROWS = 16
 SCALE_COLUMNS = 128
 MASK_FILLER = -1e30
@@ -81,9 +81,9 @@
             bias_ref[:, m * rows : (m + 1) * rows] = jnp.where(live, 0.0, MASK_FILLER)
         total = jnp.zeros((rows, 1), jnp.float32)
     else:
-        bias_ref, square_in, _ = rest[:3]
-        attended_ref, scaled_ref = rest[3:5]
-        square_ref = None if last else rest[5]
+        bias_ref, square_in = rest[:2]
+        attended_ref, scaled_ref = rest[2:4]
+        square_ref = None if last else rest[4]
         total = square_in[:, :1]
     bias = bias_ref[...]
     bias = jnp.concatenate([bias] * GROUP_SPLIT, axis=0)
@@ -135,35 +135,33 @@
     first, last = chunk == 0, chunk == len(HEAD_CHUNKS) - 1
     width = heads * GROUP_SPLIT * HEAD_SIZE
     before = sum(HEAD_CHUNKS[:chunk]) * GROUP_SPLIT * HEAD_SIZE
-    assert before % width == 0
     shard_count = len(kv_chunks)
 
     def whole(shape):
         return pl.BlockSpec(shape, lambda i: (0, 0))
 
-    columns = pl.BlockSpec((rows, width), lambda i: (0, before // width))
-    in_specs = [columns, columns, pl.BlockSpec((1, width), lambda i: (0, before // width))]
+    columns = pl.BlockSpec((pl.Element(rows), pl.Element(width)), lambda i: (0, before))
+    gains = pl.BlockSpec((pl.Element(1), pl.Element(width)), lambda i: (0, before))
+    in_specs = [columns, columns, gains]
     in_specs += [whole(a.shape) for a in kv_chunks]
     operands = [queries, residual, gain] + list(kv_chunks)
     sent = width + (SCALE_COLUMNS if last else 0)
     shapes = [
-        jax.ShapeDtypeStruct((rows, width_all), jnp.bfloat16),
+        jax.ShapeDtypeStruct((rows, width), jnp.bfloat16),
         jax.ShapeDtypeStruct((rows, sent), jnp.bfloat16),
     ]
-    out_specs = [columns, whole((rows, sent))]
+    out_specs = [whole((rows, width)), whole((rows, sent))]
     square = jax.ShapeDtypeStruct((rows, 128), jnp.float32)
     bias = jax.ShapeDtypeStruct((rows, rows * shard_count), jnp.float32)
-    aliases = {}
     if first:
         operands += [place, own_seg]
         in_specs += [pl.BlockSpec(memory_space=pltpu.SMEM), whole(own_seg.shape)]
         shapes += [square, bias]
         out_specs += [whole(square.shape), whole(bias.shape)]
     else:
-        attended_so_far, square_so_far, bias_array = carried
-        operands += [bias_array, square_so_far, attended_so_far]
-        in_specs += [whole(bias.shape), whole(square.shape), pl.BlockSpec(memory_space=pl.ANY)]
-        aliases = {len(operands) - 1: 0}
+        square_so_far, bias_array = carried
+        operands += [bias_array, square_so_far]
+        in_specs += [whole(bias.shape), whole(square.shape)]
         if not last:
             shapes += [square]
             out_specs += [whole(square.shape)]
@@ -174,7 +172,6 @@
         in_specs=in_specs,
         out_specs=out_specs,
         out_shape=shapes,
-        input_output_aliases=aliases,
         compiler_params=pltpu.CompilerParams(vmem_limit_bytes=VMEM_LIMIT),
         cost_estimate=pl.CostEstimate(
             flops=4 * rows * width * keys,
@@ -299,6 +296,9 @@
     units = gate_weight.shape[1]
     chunks = range(len(HEAD_CHUNKS))
 
+    def after(array, *others):
+        return lax.optimization_barrier((array, *others))[0]
+
     def swap(array, mask):
         return lax.ppermute(array, "tok", [(t, t ^ mask) for t in range(tok_count)])
 
@@ -309,28 +309,34 @@
                 pairs.append((2 * z + y, 2 * ahead[steps][z] + (1 - y if flip else y)))
         return lax.ppermute(array, "grp", pairs)
 
+    own_seg = jnp.broadcast_to(prompt_window_index[0].astype(jnp.float32)[:, None], (rows, rows))
+    place = tok_index.astype(jnp.int32).reshape(1)
+    gain = ffn_gain.reshape(1, width)
     packed = pack(own_kv, prompt_window_index)
-    group_chunks = []
+    first_swaps = []
     for c in chunks:
         held = {0: packed[c]}
         mask = tok_count // 2
-        while mask:
+        while mask > 1:
             held.update({m ^ mask: swap(a, mask) for m, a in held.items()})
             mask //= 2
-        group_chunks.append([held[m] for m in range(tok_count)])
-
-    own_seg = jnp.broadcast_to(prompt_window_index[0].astype(jnp.float32)[:, None], (rows, rows))
-    place = tok_index.astype(jnp.int32).reshape(1)
-    gain = ffn_gain.reshape(1, width)
-    scaled, carried = [], None
+        first_swaps.append(held)
+    scaled, parts, carried = [], [], None
     for c in chunks:
-        made = attend(c, queries, residual, gain, group_chunks[c], place, own_seg, carried)
+        held = first_swaps[c]
+        if c:
+            held = {m: after(a, scaled[-1]) if m else a for m, a in held.items()}
+        if tok_count > 1:
+            held.update({m ^ 1: swap(a, 1) for m, a in held.items()})
+        keys_values = [held[m] for m in range(tok_count)]
+        made = attend(c, queries, residual, gain, keys_values, place, own_seg, carried)
         if c == 0:
             bias = made[3]
         if c < len(HEAD_CHUNKS) - 1:
-            carried = (made[0], made[2], bias)
+            carried = (made[2], bias)
+        parts.append(made[0])
         scaled.append(made[1])
-    attended = made[0]
+    attended = jnp.concatenate(parts, axis=1)
 
     late_kv, _ = lax.optimization_barrier((rotated_keys_values, scaled[-1]))
     group_kv = lax.all_gather(late_kv, "tok", axis=0, tiled=True)
@@ -349,28 +355,33 @@
         source = source + (1 - column if flip else column)
         return lax.dynamic_update_slice_in_dim(hidden, block, source * units, 1)
 
-    held = scaled
+    sent, arrived, waiting = [], [scaled], [(scaled, 0, False)]
     for step in range(line_count):
         other, following = [], []
         for c in chunks:
-            swapped = send(held[c], 0, True)
+            ready = arrived[-1][c]
+            number = len(sent)
+            behind = sent[0] if number == 1 else sent[number - 3] if number > 2 else ()
+            if behind:
+                ready = after(ready, *behind)
+            pair = [send(ready, 0, True)]
             if step + 1 < line_count:
-                forwarded = send(held[c], 1, False)
-                swapped, forwarded = lax.optimization_barrier((swapped, forwarded))
-                following.append(forwarded)
-            other.append(swapped)
-        if step + 1 < line_count:
-            own_block, other_block = gated([held, other], gate_weight, up_weight)
-        else:
-            (own_block,) = gated([held], gate_weight, up_weight)
-            other[-1], written = lax.optimization_barrier((other[-1], written))
-            (other_block,) = gated([other], gate_weight, up_weight)
-        if step:
-            own_block = send(own_block, line_count - step, False)
-        other_block = send(other_block, (line_count - step) % line_count, True)
-        hidden = put(hidden, own_block, step, False)
-        hidden = put(hidden, other_block, step, True)
-        held = following
+                pair.append(send(ready, 1, False))
+                following.append(pair[1])
+            other.append(pair[0])
+            sent.append(pair)
+        arrived.append(following)
+        waiting.append((other, step, True))
+        if following:
+            waiting.append((following, step + 1, False))
+        if step == line_count - 2:
+            waiting[-1] = ([*following[:-1], after(following[-1], written)], step + 1, False)
+        blocks = gated([shard for shard, _, _ in waiting], gate_weight, up_weight)
+        for block, (_, steps, flip) in zip(blocks, waiting):
+            if steps or flip:
+                block = send(block, (line_count - steps) % line_count, flip)
+            hidden = put(hidden, block, steps, flip)
+        waiting = []
     return (attended, hidden, written)
 
 

time: 202 us -> 197 us (0.975)
  waiting for transfers between devices: 55.7 us -> 70.8 us
  Pallas kernels: 67.9 us -> 54.8 us
  starting transfers between devices: 46.8 us -> 42.6 us
  local copies, waits for them, and re-layouts: 15.7 us -> 12.1 us
    ppermute x35 -> x21, waiting for transfers between devices: 48.9 us -> 62.3 us  [send(): return lax.ppermute(array, 'grp', pairs)]
    pallas_call x5 -> x4, Pallas kernels: 51.4 us -> 43.2 us  [gated(): pl.pallas_call(functools.partial(gated_kernel, count, len(shards[0])), gr...]
    unnamed x38 -> x22, local copies, waits for them, and re-layouts: 9.59 us -> 3.79 us
    pallas_call x4 -> x2, Pallas kernels: 12.8 us -> 7.86 us  [attend(): pl.pallas_call(functools.partial(attend_kernel, chunk, shard_count, width...]
    ppermute x12 -> x6, starting transfers between devices: 8.55 us -> 3.67 us  [swap(): return lax.ppermute(array, 'tok', [(t, t ^ mask) for t in range(tok_count)])]
    ppermute x12 -> x6, waiting for transfers between devices: 6.76 us -> 8.5 us  [swap(): return lax.ppermute(array, 'tok', [(t, t ^ mask) for t in range(tok_count)])]
    ppermute x35 -> x21, starting transfers between devices: 38.2 us -> 38.9 us  [send(): return lax.ppermute(array, 'grp', pairs)]
  transfers between devices with their start and end apart: 48 -> 28, of which waited for: 13 -> 10; matrix products, arithmetic and copies ran while one was open for 3% -> 5% of each run, Pallas kernels for 33% -> 27%
where the time goes in v6:
time: 197 us
  waiting for transfers between devices  70.8 us (36%)
  Pallas kernels  54.8 us (28%)
  starting transfers between devices  42.6 us (22%)
  between operations  14.3 us (7%)
  local copies, waits for them, and re-layouts  12.1 us (6%)
  other arithmetic  1.99 us (1%)
    ppermute x21, waiting for transfers between devices, send(): return lax.ppermute(array, 'grp', pairs)  62.3 us
    pallas_call x4, Pallas kernels, gated(): pl.pallas_call(functools.partial(gated_kernel, count, len(shards[0])), gr...  43.2 us
    ppermute x21, starting transfers between devices, send(): return lax.ppermute(array, 'grp', pairs)  38.9 us
    ppermute x6, waiting for transfers between devices, swap(): return lax.ppermute(array, 'tok', [(t, t ^ mask) for t in range(tok_count)])  8.5 us
    pallas_call x2, Pallas kernels, attend(): pl.pallas_call(functools.partial(attend_kernel, chunk, shard_count, width...  7.86 us
    dynamic_update_slice x8, local copies, waits for them, and re-layouts, put(): return lax.dynamic_update_slice_in_dim(hidden, block, source * units, 1)  6.71 us
  transfers between devices with their start and end apart: 28, of which 10 were waited for; matrix products, arithmetic and copies ran while one was open for 5% of the time, Pallas kernels for 27%

profile of v6, /device:TPU:0, one launch (start us, length us, event | category | flops | bytes accessed | tf_op | source)
XLA Modules:
  0.0 196.6 jit_solution(7028701258190419893)
XLA Ops:
  7.2 0.0 copy-start.4
  7.2 0.0 all-gather.2.cloned.1.call-start
  7.2 0.0 copy-start.5
  7.2 0.6 copy-done.5
  7.9 1.1 shard_map.112
  9.0 3.0 %collective-permute-start.1 = (bf16[144,768]{1,0:T(8,128)(2,1)S(1)}, bf16[144,768]{1,0:T(8,128)(2,1)S(1)}, u32[]{:S(2)}, u32[]{:S(2)}) collective-permute-start(bf16[144,768]{1,0:T(8,128)(2,1)S(1)} %get-tuple-element.27.refs_3_), channel_id=1, source_target_pairs={{0,2},{1,3},{2,0},{3,1},{4,6},{5,7},{6,4},{7,5},{8,10},{9,11},{10,... | collective-permute-start | bytes 663560 | tf_op jit(solution)/shard_map/ppermute | solution.py:303
  12.0 0.2 collective-permute-start.4
  12.1 6.1 %collective-permute-done.1.refs_5_ = bf16[144,768]{1,0:T(8,128)(2,1)S(1)} collective-permute-done((bf16[144,768]{1,0:T(8,128)(2,1)S(1)}, bf16[144,768]{1,0:T(8,128)(2,1)S(1)}, u32[]{:S(2)}, u32[]{:S(2)}) %collective-permute-start.1) | collective-permute-done | bytes 221216 | tf_op jit(solution)/shard_map/ppermute | solution.py:303
  18.2 0.7 convert_bitcast_fusion
  18.9 0.8 collective-permute-done.2.refs_6_
  19.7 0.1 broadcast_in_dim.24.refs_8_
  19.8 0.7 copy-done.3
  20.5 3.2 %shard_map.113 = (bf16[128,1920]{1,0:T(8,128)(2,1)S(1)}, bf16[128,1920]{1,0:T(8,128)(2,1)S(1)}, f32[128,128]{1,0:T(8,128)S(1)}, f32[128,512]{1,0:T(8,128)S(1)}) custom-call(bf16[128,5120]{1,0:T(8,128)(2,1)} %refs_0_.3, bf16[128,5120]{1,0:T(8,128)(2,1)} %refs_1_.3, f32[1,5120]{1,0:T(1,128)S(1)} %bitcast.6, bf16[144,768]{1,0:T(8,128)(2,1)S(1)} %get-tuple-element.27.refs_3_, ...), custom_call_target="tpu_custom_call" | custom-call | flops 503316480 | bytes 2752512 | tf_op jit(solution)/shard_map/pallas_call | solution.py:169
  23.7 0.0 copy-start.6
  23.7 2.1 %collective-permute-start.6 = (bf16[128,1920]{1,0:T(8,128)(2,1)S(1)}, bf16[128,1920]{1,0:T(8,128)(2,1)S(1)}, u32[]{:S(2)}, u32[]{:S(2)}) collective-permute-start(bf16[128,1920]{1,0:T(8,128)(2,1)S(1)} %get-tuple-element.30.refs_0_), channel_id=1, source_target_pairs={{0,4},{4,0},{8,12},{12,8},{16,20},{20,16},{24,28},{28,24},{1,5},{5... | collective-permute-start | bytes 1474568 | tf_op jit(solution)/shard_map/ppermute | solution.py:310
  25.9 1.6 collective-permute-start.7
  27.4 0.5 collective-permute-start.5
  27.9 1.1 collective-permute-done.3.refs_4_
  29.1 0.5 collective-permute-done.5.refs_6_
  29.5 4.7 %shard_map.114 = (bf16[128,3200]{1,0:T(8,128)(2,1)S(1)}, bf16[128,3328]{1,0:T(8,128)(2,1)S(1)}) custom-call(bf16[128,5120]{1,0:T(8,128)(2,1)} %refs_0_.3, bf16[128,5120]{1,0:T(8,128)(2,1)} %refs_1_.3, f32[1,5120]{1,0:T(1,128)S(1)} %bitcast.7, bf16[128,1280]{1,0:T(8,128)(2,1)S(1)} %get-tuple-element.29.refs_3_, ...), custom_call_target="tpu_custom_call" | custom-call | flops 838860800 | bytes 4587520 | tf_op jit(solution)/shard_map/pallas_call | solution.py:169
  34.2 3.1 %collective-permute-done.6.refs_2_ = bf16[128,1920]{1,0:T(8,128)(2,1)S(1)} collective-permute-done((bf16[128,1920]{1,0:T(8,128)(2,1)S(1)}, bf16[128,1920]{1,0:T(8,128)(2,1)S(1)}, u32[]{:S(2)}, u32[]{:S(2)}) %collective-permute-start.6) | collective-permute-done | bytes 491552 | tf_op jit(solution)/shard_map/ppermute | solution.py:310
  37.4 0.8 copy-done.8
  38.2 1.7 collective-permute-done.7.refs_4_
  39.8 0.7 collective-permute-start.9
  40.5 0.0 all-gather.2.cloned.1.call-update
  40.6 1.0 collective-permute-start.8
  41.6 19.1 %collective-permute-done.9.refs_5_ = bf16[128,3328]{1,0:T(8,128)(2,1)} collective-permute-done((bf16[128,3328]{1,0:T(8,128)(2,1)S(1)}, bf16[128,3328]{1,0:T(8,128)(2,1)}, u32[]{:S(2)}, u32[]{:S(2)}) %collective-permute-start.9) | collective-permute-done | bytes 852000 | tf_op jit(solution)/shard_map/ppermute | solution.py:310
  60.7 0.7 collective-permute-start.15
  61.4 0.1 select_reduce_fusion
  61.6 0.0 copy-start.7
  61.6 0.0 copy-start.9
  61.6 0.6 collective-permute-start.12
  62.2 3.5 %collective-permute-start.14 = (bf16[128,1920]{1,0:T(8,128)(2,1)}, bf16[128,1920]{1,0:T(8,128)(2,1)S(1)}, u32[]{:S(2)}, u32[]{:S(2)}) collective-permute-start(bf16[128,1920]{1,0:T(8,128)(2,1)} %collective-permute-done.7.refs_4_), channel_id=1, source_target_pairs={{0,8},{4,12},{8,24},{12,28},{16,0},{20,4},{24,16},{28,20},{1,9},{5... | collective-permute-start | bytes 1474568 | tf_op jit(solution)/shard_map/ppermute | solution.py:310
  65.7 1.5 collective-permute-start.13
  67.2 1.2 pad_maximum_fusion
  68.4 22.9 %collective-permute-done.14.refs_2_ = bf16[128,1920]{1,0:T(8,128)(2,1)S(1)} collective-permute-done((bf16[128,1920]{1,0:T(8,128)(2,1)}, bf16[128,1920]{1,0:T(8,128)(2,1)S(1)}, u32[]{:S(2)}, u32[]{:S(2)}) %collective-permute-start.14) | collective-permute-done | bytes 491552 | tf_op jit(solution)/shard_map/ppermute | solution.py:310
  91.3 1.1 collective-permute-start.18
  92.3 0.3 collective-permute-start.20
  92.7 3.3 %collective-permute-start.21 = (bf16[128,3328]{1,0:T(8,128)(2,1)S(1)}, bf16[128,3328]{1,0:T(8,128)(2,1)S(1)}, u32[]{:S(2)}, u32[]{:S(2)}) collective-permute-start(bf16[128,3328]{1,0:T(8,128)(2,1)S(1)} %collective-permute-done.15.refs_3_), channel_id=1, source_target_pairs={{0,8},{4,12},{8,24},{12,28},{16,0},{20,4},{24,16},{28,20},{1,9},{5... | collective-permute-start | bytes 2555912 | tf_op jit(solution)/shard_map/ppermute | solution.py:310
  95.9 13.0 %shard_map.115 = (bf16[128,1024]{1,0:T(8,128)(2,1)S(1)}, bf16[128,1024]{1,0:T(8,128)(2,1)S(1)}, bf16[128,1024]{1,0:T(8,128)(2,1)S(1)}) custom-call(bf16[128,1920]{1,0:T(8,128)(2,1)S(1)} %copy-done.7, bf16[128,3328]{1,0:T(8,128)(2,1)S(1)} %get-tuple-element.36.refs_1_, bf16[128,1920]{1,0:T(8,128)(2,1)S(1)} %copy-done.9, ...), custom_call_target="tpu_custom_call" | custom-call | flops 8053063680 | bytes 25690112 | tf_op jit(solution)/shard_map/pallas_call | solution.py:223
  108.9 1.6 collective-permute-start.10
  110.6 0.6 collective-permute-start.19
  111.1 10.9 %shard_map.116 = (bf16[128,1024]{1,0:T(8,128)(2,1)S(1)}, bf16[128,1024]{1,0:T(8,128)(2,1)}) custom-call(bf16[128,1920]{1,0:T(8,128)(2,1)S(1)} %collective-permute-done.12.refs_0_, bf16[128,3328]{1,0:T(8,128)(2,1)S(1)} %collective-permute-done.13.refs_1_, bf16[128,1920]{1,0:T(8,128)(2,1)S(1)} %collective-permute-done.14.refs_2_, ...), custom_call_target="tpu_custom_call" | custom-call | flops 5368709120 | bytes 24117248 | tf_op jit(solution)/shard_map/pallas_call | solution.py:223
  122.1 1.7 collective-permute-start.16
  123.8 1.5 broadcast_in_dim.25
  125.3 0.7 constant_dynamic-update-slice_fusion.7
  126.0 1.1 collective-permute-start.25
  127.1 0.7 constant_dynamic-update-slice_fusion.6
  127.8 0.7 constant_dynamic-update-slice_fusion.5
  128.6 14.7 %collective-permute-start.17 = (bf16[128,1024]{1,0:T(8,128)(2,1)}, bf16[128,1024]{1,0:T(8,128)(2,1)}, u32[]{:S(2)}, u32[]{:S(2)}) collective-permute-start(bf16[128,1024]{1,0:T(8,128)(2,1)} %get-tuple-element.42), channel_id=1, source_target_pairs={{0,24},{4,28},{8,16},{12,20},{16,8},{20,12},{24,0},{28,4},{1,25},{... | collective-permute-start | bytes 786440 | tf_op jit(solution)/shard_map/ppermute | solution.py:310
  143.2 0.2 collective-permute-start.24
  143.5 0.7 constant_dynamic-update-slice_fusion.4
  144.2 1.6 copy-done
  145.8 2.7 %shard_map.117 = bf16[16,16,2048]{2,1,0:T(8,128)(2,1)} custom-call(s32[16]{0:T(128)S(1)} %broadcast_add_fusion.page_ref, bf16[512,2048]{1,0:T(8,128)(2,1)S(1)} %copy-done, bf16[16,16,2048]{2,1,0:T(8,128)(2,1)} %cache_ref.1), custom_call_target="tpu_custom_call" | custom-call | bytes 4194304 | tf_op jit(solution)/shard_map/pallas_call | solution.py:257
  148.5 10.4 %shard_map.118 = (bf16[128,1024]{1,0:T(8,128)(2,1)S(1)}, bf16[128,1024]{1,0:T(8,128)(2,1)S(1)}) custom-call(bf16[128,1920]{1,0:T(8,128)(2,1)S(1)} %copy-done.2, bf16[128,3328]{1,0:T(8,128)(2,1)S(1)} %collective-permute-done.19.refs_1_, bf16[128,1920]{1,0:T(8,128)(2,1)} %collective-permute-done.20.refs_2_, ...), custom_call_target="tpu_custom_call" | custom-call | flops 5368709120 | bytes 24117248 | tf_op jit(solution)/shard_map/pallas_call | solution.py:223
  158.8 1.3 collective-permute-start.22
  160.2 11.7 %collective-permute-done.24.refs_0_ = bf16[128,1920]{1,0:T(8,128)(2,1)} collective-permute-done((bf16[128,1920]{1,0:T(8,128)(2,1)}, bf16[128,1920]{1,0:T(8,128)(2,1)}, u32[]{:S(2)}, u32[]{:S(2)}) %collective-permute-start.24) | collective-permute-done | bytes 491552 | tf_op jit(solution)/shard_map/ppermute | solution.py:310
  171.9 8.9 %shard_map.119 = bf16[128,1024]{1,0:T(8,128)(2,1)S(1)} custom-call(bf16[128,1920]{1,0:T(8,128)(2,1)} %collective-permute-done.24.refs_0_, bf16[128,3328]{1,0:T(8,128)(2,1)S(1)} %collective-permute-done.25.refs_1_, bf16[5120,1024]{1,0:T(8,128)(2,1)} %refs_2_.1, bf16[5120,1024]{1,0:T(8,128)(2,1)} %refs_3_.1), custom_call_target="tpu_custom_call" | custom-call | flops 2684354560 | bytes 22544384 | tf_op jit(solution)/shard_map/pallas_call | solution.py:223
  180.8 1.3 collective-permute-start.26
  182.2 1.7 constant_dynamic-update-slice_fusion.3
  183.8 0.7 constant_dynamic-update-slice_fusion.2
  184.5 0.7 constant_dynamic-update-slice_fusion.1
  185.3 3.8 %collective-permute-done.26 = bf16[128,1024]{1,0:T(8,128)(2,1)S(1)} collective-permute-done((bf16[128,1024]{1,0:T(8,128)(2,1)S(1)}, bf16[128,1024]{1,0:T(8,128)(2,1)S(1)}, u32[]{:S(2)}, u32[]{:S(2)}) %collective-permute-start.26) | collective-permute-done | bytes 262176 | tf_op jit(solution)/shard_map/ppermute | solution.py:310
  189.0 0.7 constant_dynamic-update-slice_fusion
  (39 shorter events, 0.1 us)
Async XLA Ops:
  7.2 22.4 %copy-start.4 = (f32[5120]{0:T(1024)S(1)}, f32[5120]{0:T(1024)}, u32[]{:S(2)}) copy-start(f32[5120]{0:T(1024)} %param.13) | copy-start | bytes 61444
  7.2 137.0 %all-gather.2.cloned.1.call-start = ((), (), s32[]{:S(2)}) async-start(), calls=%async_computation | async-start | bytes 2621440 | tf_op jit(solution)/shard_map/all_gather | solution.py:342
  7.2 0.7 copy-start.5
  9.0 9.3 %collective-permute-start.1 = (bf16[144,768]{1,0:T(8,128)(2,1)S(1)}, bf16[144,768]{1,0:T(8,128)(2,1)S(1)}, u32[]{:S(2)}, u32[]{:S(2)}) collective-permute-start(bf16[144,768]{1,0:T(8,128)(2,1)S(1)} %get-tuple-element.27.refs_3_), channel_id=1, source_target_pairs={{0,2},{1,3},{2,0},{3,1},{4,6},{5,7},{6,4},{7,5},{8,10},{9,11},{10,... | collective-permute-start | bytes 663560 | tf_op jit(solution)/shard_map/ppermute | solution.py:303
  12.0 6.9 %collective-permute-start = (bf16[144,768]{1,0:T(8,128)(2,1)S(1)}, bf16[144,768]{1,0:T(8,128)(2,1)S(1)}, u32[]{:S(2)}, u32[]{:S(2)}) collective-permute-start(bf16[144,768]{1,0:T(8,128)(2,1)S(1)} %get-tuple-element.27.refs_3_), channel_id=1, source_target_pairs={{0,1},{1,0},{2,3},{3,2},{4,5},{5,4},{6,7},{7,6},{8,9},{9,8},{10,11... | collective-permute-start | bytes 663560 | tf_op jit(solution)/shard_map/ppermute | solution.py:303
  12.0 15.5 %collective-permute-start.4 = (bf16[128,1280]{1,0:T(8,128)(2,1)S(1)}, bf16[128,1280]{1,0:T(8,128)(2,1)S(1)}, u32[]{:S(2)}, u32[]{:S(2)}) collective-permute-start(bf16[128,1280]{1,0:T(8,128)(2,1)S(1)} %get-tuple-element.29.refs_3_), channel_id=1, source_target_pairs={{0,2},{1,3},{2,0},{3,1},{4,6},{5,7},{6,4},{7,5},{8,10},{9,11},{10,... | collective-permute-start | bytes 983048 | tf_op jit(solution)/shard_map/ppermute | solution.py:303
  18.2 1.5 collective-permute-start.2
  19.8 0.7 copy-start.3
  23.7 10.5 %copy-start.6 = (bf16[128,1920]{1,0:T(8,128)(2,1)}, bf16[128,1920]{1,0:T(8,128)(2,1)S(1)}, u32[]{:S(2)}) copy-start(bf16[128,1920]{1,0:T(8,128)(2,1)S(1)} %get-tuple-element.30.refs_0_) | copy-start | bytes 1474564
  23.7 13.7 %collective-permute-start.6 = (bf16[128,1920]{1,0:T(8,128)(2,1)S(1)}, bf16[128,1920]{1,0:T(8,128)(2,1)S(1)}, u32[]{:S(2)}, u32[]{:S(2)}) collective-permute-start(bf16[128,1920]{1,0:T(8,128)(2,1)S(1)} %get-tuple-element.30.refs_0_), channel_id=1, source_target_pairs={{0,4},{4,0},{8,12},{12,8},{16,20},{20,16},{24,28},{28,24},{1,5},{5... | collective-permute-start | bytes 1474568 | tf_op jit(solution)/shard_map/ppermute | solution.py:310
  25.9 14.0 %collective-permute-start.7 = (bf16[128,1920]{1,0:T(8,128)(2,1)S(1)}, bf16[128,1920]{1,0:T(8,128)(2,1)}, u32[]{:S(2)}, u32[]{:S(2)}) collective-permute-start(bf16[128,1920]{1,0:T(8,128)(2,1)S(1)} %get-tuple-element.30.refs_0_), channel_id=1, source_target_pairs={{0,8},{4,12},{8,24},{12,28},{16,0},{20,4},{24,16},{28,20},{1,9},{5... | collective-permute-start | bytes 1474568 | tf_op jit(solution)/shard_map/ppermute | solution.py:310
  27.4 1.6 collective-permute-start.3
  27.4 2.1 %collective-permute-start.5 = (bf16[128,1280]{1,0:T(8,128)(2,1)S(1)}, bf16[128,1280]{1,0:T(8,128)(2,1)S(1)}, u32[]{:S(2)}, u32[]{:S(2)}) collective-permute-start(bf16[128,1280]{1,0:T(8,128)(2,1)S(1)} %collective-permute-done.4.refs_5_), channel_id=1, source_target_pairs={{0,1},{1,0},{2,3},{3,2},{4,5},{5,4},{6,7},{7,6},{8,9},{9,8},{10,11... | collective-permute-start | bytes 983048 | tf_op jit(solution)/shard_map/ppermute | solution.py:303
  29.5 11.0 %copy-start.10 = (s32[1,64]{1,0:T(1,128)S(1)}, s32[1,64]{1,0:T(1,128)}, u32[]{:S(2)}) copy-start(s32[1,64]{1,0:T(1,128)} %param.17) | copy-start | bytes 772
  37.4 0.8 copy-start.8
  39.8 20.8 %collective-permute-start.9 = (bf16[128,3328]{1,0:T(8,128)(2,1)S(1)}, bf16[128,3328]{1,0:T(8,128)(2,1)}, u32[]{:S(2)}, u32[]{:S(2)}) collective-permute-start(bf16[128,3328]{1,0:T(8,128)(2,1)S(1)} %get-tuple-element.36.refs_1_), channel_id=1, source_target_pairs={{0,8},{4,12},{8,24},{12,28},{16,0},{20,4},{24,16},{28,20},{1,9},{5... | collective-permute-start | bytes 2555912 | tf_op jit(solution)/shard_map/ppermute | solution.py:310
  40.6 50.7 %collective-permute-start.8 = (bf16[128,3328]{1,0:T(8,128)(2,1)S(1)}, bf16[128,3328]{1,0:T(8,128)(2,1)}, u32[]{:S(2)}, u32[]{:S(2)}) collective-permute-start(bf16[128,3328]{1,0:T(8,128)(2,1)S(1)} %get-tuple-element.36.refs_1_), channel_id=1, source_target_pairs={{0,4},{4,0},{8,12},{12,8},{16,20},{20,16},{24,28},{28,24},{1,5},{5... | collective-permute-start | bytes 2555912 | tf_op jit(solution)/shard_map/ppermute | solution.py:310
  60.7 32.0 %collective-permute-start.15 = (bf16[128,3328]{1,0:T(8,128)(2,1)}, bf16[128,3328]{1,0:T(8,128)(2,1)S(1)}, u32[]{:S(2)}, u32[]{:S(2)}) collective-permute-start(bf16[128,3328]{1,0:T(8,128)(2,1)} %collective-permute-done.9.refs_5_), channel_id=1, source_target_pairs={{0,8},{4,12},{8,24},{12,28},{16,0},{20,4},{24,16},{28,20},{1,9},{5... | collective-permute-start | bytes 2555912 | tf_op jit(solution)/shard_map/ppermute | solution.py:310
  61.6 34.3 %copy-start.7 = (bf16[128,1920]{1,0:T(8,128)(2,1)S(1)}, bf16[128,1920]{1,0:T(8,128)(2,1)}, u32[]{:S(2)}) copy-start(bf16[128,1920]{1,0:T(8,128)(2,1)} %copy-done.6) | copy-start | bytes 1474564
  61.6 34.3 %copy-start.9 = (bf16[128,1920]{1,0:T(8,128)(2,1)S(1)}, bf16[128,1920]{1,0:T(8,128)(2,1)}, u32[]{:S(2)}) copy-start(bf16[128,1920]{1,0:T(8,128)(2,1)} %copy-done.8) | copy-start | bytes 1474564
  61.6 31.0 %collective-permute-start.12 = (bf16[128,1920]{1,0:T(8,128)(2,1)}, bf16[128,1920]{1,0:T(8,128)(2,1)S(1)}, u32[]{:S(2)}, u32[]{:S(2)}) collective-permute-start(bf16[128,1920]{1,0:T(8,128)(2,1)} %collective-permute-done.7.refs_4_), channel_id=1, source_target_pairs={{0,4},{4,0},{8,12},{12,8},{16,20},{20,16},{24,28},{28,24},{1,5},{5... | collective-permute-start | bytes 1474568 | tf_op jit(solution)/shard_map/ppermute | solution.py:310
  62.2 29.1 %collective-permute-start.14 = (bf16[128,1920]{1,0:T(8,128)(2,1)}, bf16[128,1920]{1,0:T(8,128)(2,1)S(1)}, u32[]{:S(2)}, u32[]{:S(2)}) collective-permute-start(bf16[128,1920]{1,0:T(8,128)(2,1)} %collective-permute-done.7.refs_4_), channel_id=1, source_target_pairs={{0,8},{4,12},{8,24},{12,28},{16,0},{20,4},{24,16},{28,20},{1,9},{5... | collective-permute-start | bytes 1474568 | tf_op jit(solution)/shard_map/ppermute | solution.py:310
  65.7 44.9 %collective-permute-start.13 = (bf16[128,3328]{1,0:T(8,128)(2,1)}, bf16[128,3328]{1,0:T(8,128)(2,1)S(1)}, u32[]{:S(2)}, u32[]{:S(2)}) collective-permute-start(bf16[128,3328]{1,0:T(8,128)(2,1)} %collective-permute-done.9.refs_5_), channel_id=1, source_target_pairs={{0,4},{4,0},{8,12},{12,8},{16,20},{20,16},{24,28},{28,24},{1,5},{5... | collective-permute-start | bytes 2555912 | tf_op jit(solution)/shard_map/ppermute | solution.py:310
  91.3 19.3 %collective-permute-start.18 = (bf16[128,1920]{1,0:T(8,128)(2,1)S(1)}, bf16[128,1920]{1,0:T(8,128)(2,1)S(1)}, u32[]{:S(2)}, u32[]{:S(2)}) collective-permute-start(bf16[128,1920]{1,0:T(8,128)(2,1)S(1)} %collective-permute-done.14.refs_2_), channel_id=1, source_target_pairs={{0,4},{4,0},{8,12},{12,8},{16,20},{20,16},{24,28},{28,24},{1,5},{5... | collective-permute-start | bytes 1474568 | tf_op jit(solution)/shard_map/ppermute | solution.py:310
  92.3 29.7 %collective-permute-start.20 = (bf16[128,1920]{1,0:T(8,128)(2,1)S(1)}, bf16[128,1920]{1,0:T(8,128)(2,1)}, u32[]{:S(2)}, u32[]{:S(2)}) collective-permute-start(bf16[128,1920]{1,0:T(8,128)(2,1)S(1)} %collective-permute-done.14.refs_2_), channel_id=1, source_target_pairs={{0,8},{4,12},{8,24},{12,28},{16,0},{20,4},{24,16},{28,20},{1,9},{5... | collective-permute-start | bytes 1474568 | tf_op jit(solution)/shard_map/ppermute | solution.py:310
  92.7 33.4 %collective-permute-start.21 = (bf16[128,3328]{1,0:T(8,128)(2,1)S(1)}, bf16[128,3328]{1,0:T(8,128)(2,1)S(1)}, u32[]{:S(2)}, u32[]{:S(2)}) collective-permute-start(bf16[128,3328]{1,0:T(8,128)(2,1)S(1)} %collective-permute-done.15.refs_3_), channel_id=1, source_target_pairs={{0,8},{4,12},{8,24},{12,28},{16,0},{20,4},{24,16},{28,20},{1,9},{5... | collective-permute-start | bytes 2555912 | tf_op jit(solution)/shard_map/ppermute | solution.py:310
  108.9 18.2 %collective-permute-start.10 = (bf16[128,1024]{1,0:T(8,128)(2,1)S(1)}, bf16[128,1024]{1,0:T(8,128)(2,1)S(1)}, u32[]{:S(2)}, u32[]{:S(2)}) collective-permute-start(bf16[128,1024]{1,0:T(8,128)(2,1)S(1)} %get-tuple-element.38), channel_id=1, source_target_pairs={{0,4},{4,0},{8,12},{12,8},{16,20},{20,16},{24,28},{28,24},{1,5},{5... | collective-permute-start | bytes 786440 | tf_op jit(solution)/shard_map/ppermute | solution.py:310
  110.5 11.5 %copy-start.1 = (bf16[128,1920]{1,0:T(8,128)(2,1)}, bf16[128,1920]{1,0:T(8,128)(2,1)S(1)}, u32[]{:S(2)}) copy-start(bf16[128,1920]{1,0:T(8,128)(2,1)S(1)} %collective-permute-done.18.refs_0_) | copy-start | bytes 1474564
  110.5 17.3 %collective-permute-start.11 = (bf16[128,1024]{1,0:T(8,128)(2,1)S(1)}, bf16[128,1024]{1,0:T(8,128)(2,1)S(1)}, u32[]{:S(2)}, u32[]{:S(2)}) collective-permute-start(bf16[128,1024]{1,0:T(8,128)(2,1)S(1)} %get-tuple-element.39), channel_id=1, source_target_pairs={{0,16},{4,20},{8,0},{12,4},{16,24},{20,28},{24,8},{28,12},{1,17},{... | collective-permute-start | bytes 786440 | tf_op jit(solution)/shard_map/ppermute | solution.py:310
  110.6 37.9 %collective-permute-start.19 = (bf16[128,3328]{1,0:T(8,128)(2,1)S(1)}, bf16[128,3328]{1,0:T(8,128)(2,1)S(1)}, u32[]{:S(2)}, u32[]{:S(2)}) collective-permute-start(bf16[128,3328]{1,0:T(8,128)(2,1)S(1)} %collective-permute-done.15.refs_3_), channel_id=1, source_target_pairs={{0,4},{4,0},{8,12},{12,8},{16,20},{20,16},{24,28},{28,24},{1,5},{5... | collective-permute-start | bytes 2555912 | tf_op jit(solution)/shard_map/ppermute | solution.py:310
  122.1 21.4 %collective-permute-start.16 = (bf16[128,1024]{1,0:T(8,128)(2,1)S(1)}, bf16[128,1024]{1,0:T(8,128)(2,1)S(1)}, u32[]{:S(2)}, u32[]{:S(2)}) collective-permute-start(bf16[128,1024]{1,0:T(8,128)(2,1)S(1)} %get-tuple-element.41), channel_id=1, source_target_pairs={{0,20},{4,16},{8,4},{12,0},{16,28},{20,24},{24,12},{28,8},{1,21},{... | collective-permute-start | bytes 786440 | tf_op jit(solution)/shard_map/ppermute | solution.py:310
  126.0 45.9 %collective-permute-start.25 = (bf16[128,3328]{1,0:T(8,128)(2,1)S(1)}, bf16[128,3328]{1,0:T(8,128)(2,1)S(1)}, u32[]{:S(2)}, u32[]{:S(2)}) collective-permute-start(bf16[128,3328]{1,0:T(8,128)(2,1)S(1)} %collective-permute-done.21.refs_3_), channel_id=1, source_target_pairs={{0,4},{4,0},{8,12},{12,8},{16,20},{20,16},{24,28},{28,24},{1,5},{5... | collective-permute-start | bytes 2555912 | tf_op jit(solution)/shard_map/ppermute | solution.py:310
  128.6 53.6 %collective-permute-start.17 = (bf16[128,1024]{1,0:T(8,128)(2,1)}, bf16[128,1024]{1,0:T(8,128)(2,1)}, u32[]{:S(2)}, u32[]{:S(2)}) collective-permute-start(bf16[128,1024]{1,0:T(8,128)(2,1)} %get-tuple-element.42), channel_id=1, source_target_pairs={{0,24},{4,28},{8,16},{12,20},{16,8},{20,12},{24,0},{28,4},{1,25},{... | collective-permute-start | bytes 786440 | tf_op jit(solution)/shard_map/ppermute | solution.py:310
  143.2 28.7 %collective-permute-start.24 = (bf16[128,1920]{1,0:T(8,128)(2,1)}, bf16[128,1920]{1,0:T(8,128)(2,1)}, u32[]{:S(2)}, u32[]{:S(2)}) collective-permute-start(bf16[128,1920]{1,0:T(8,128)(2,1)} %collective-permute-done.20.refs_2_), channel_id=1, source_target_pairs={{0,4},{4,0},{8,12},{12,8},{16,20},{20,16},{24,28},{28,24},{1,5},{5... | collective-permute-start | bytes 1474568 | tf_op jit(solution)/shard_map/ppermute | solution.py:310
  144.2 1.6 copy-start
  145.8 2.7 %copy-start.2 = (bf16[128,1920]{1,0:T(8,128)(2,1)S(1)}, bf16[128,1920]{1,0:T(8,128)(2,1)}, u32[]{:S(2)}) copy-start(bf16[128,1920]{1,0:T(8,128)(2,1)} %copy-done.1) | copy-start | bytes 1474564
  158.8 25.0 %collective-permute-start.22 = (bf16[128,1024]{1,0:T(8,128)(2,1)S(1)}, bf16[128,1024]{1,0:T(8,128)(2,1)S(1)}, u32[]{:S(2)}, u32[]{:S(2)}) collective-permute-start(bf16[128,1024]{1,0:T(8,128)(2,1)S(1)} %get-tuple-element.47), channel_id=1, source_target_pairs={{0,28},{4,24},{8,20},{12,16},{16,12},{20,8},{24,4},{28,0},{1,29},{... | collective-permute-start | bytes 786440 | tf_op jit(solution)/shard_map/ppermute | solution.py:310
  160.2 24.4 %collective-permute-start.23 = (bf16[128,1024]{1,0:T(8,128)(2,1)S(1)}, bf16[128,1024]{1,0:T(8,128)(2,1)S(1)}, u32[]{:S(2)}, u32[]{:S(2)}) collective-permute-start(bf16[128,1024]{1,0:T(8,128)(2,1)S(1)} %get-tuple-element.48), channel_id=1, source_target_pairs={{0,8},{4,12},{8,24},{12,28},{16,0},{20,4},{24,16},{28,20},{1,9},{5... | collective-permute-start | bytes 786440 | tf_op jit(solution)/shard_map/ppermute | solution.py:310
  180.8 8.2 %collective-permute-start.26 = (bf16[128,1024]{1,0:T(8,128)(2,1)S(1)}, bf16[128,1024]{1,0:T(8,128)(2,1)S(1)}, u32[]{:S(2)}, u32[]{:S(2)}) collective-permute-start(bf16[128,1024]{1,0:T(8,128)(2,1)S(1)} %shard_map.119), channel_id=1, source_target_pairs={{0,12},{4,8},{8,28},{12,24},{16,4},{20,0},{24,20},{28,16},{1,13},{... | collective-permute-start | bytes 786440 | tf_op jit(solution)/shard_map/ppermute | solution.py:310
Sparse Core Ops, SparseCore 0:
  40.7 22.7 all-gather.1

commit v7 on v6

--- a/solution.py
+++ b/solution.py
@@ -356,12 +356,15 @@
         return lax.dynamic_update_slice_in_dim(hidden, block, source * units, 1)
 
     sent, arrived, waiting = [], [scaled], [(scaled, 0, False)]
+    products, late = [], []
     for step in range(line_count):
         other, following = [], []
         for c in chunks:
             ready = arrived[-1][c]
             number = len(sent)
-            behind = sent[0] if number == 1 else sent[number - 3] if number > 2 else ()
+            behind = sent[0] if number == 1 else sent[number - 2][:1] if number > 1 else []
+            if c == 0 and step > 1:
+                behind = [*behind, products[step - 2]]
             if behind:
                 ready = after(ready, *behind)
             pair = [send(ready, 0, True)]
@@ -377,7 +380,14 @@
         if step == line_count - 2:
             waiting[-1] = ([*following[:-1], after(following[-1], written)], step + 1, False)
         blocks = gated([shard for shard, _, _ in waiting], gate_weight, up_weight)
-        for block, (_, steps, flip) in zip(blocks, waiting):
+        products.append(blocks[-1])
+        late = [(after(block, blocks[-1]), steps, flip) for block, steps, flip in late]
+        made = late + [(block, steps, flip) for block, (_, steps, flip) in zip(blocks, waiting)]
+        late = []
+        if 0 < step < line_count - 2:
+            late = [entry for entry in made if entry[2]]
+            made = [entry for entry in made if not entry[2]]
+        for block, steps, flip in made:
             if steps or flip:
                 block = send(block, (line_count - steps) % line_count, flip)
             hidden = put(hidden, block, steps, flip)

time: 197 us -> 191 us (0.970)
  starting transfers between devices: 42.6 us -> 33.6 us
  local copies, waits for them, and re-layouts: 12.1 us -> 17 us
    ppermute x21, starting transfers between devices: 38.9 us -> 29.8 us  [send(): return lax.ppermute(array, 'grp', pairs)]
    unnamed x22 -> x44, local copies, waits for them, and re-layouts: 3.79 us -> 12.1 us
    dynamic_update_slice x8, local copies, waits for them, and re-layouts: 6.71 us -> 4.63 us  [put(): return lax.dynamic_update_slice_in_dim(hidden, block, source * units, 1)]
  transfers between devices with their start and end apart: 28 -> 28, of which waited for: 10 -> 13; matrix products, arithmetic and copies ran while one was open for 5% -> 3% of each run, Pallas kernels for 27% -> 28%
where the time goes in v7:
time: 191 us
  waiting for transfers between devices  69.7 us (36%)
  Pallas kernels  54.4 us (28%)
  starting transfers between devices  33.6 us (18%)
  local copies, waits for them, and re-layouts  17 us (9%)
  between operations  14.3 us (7%)
  other arithmetic  1.98 us (1%)
    ppermute x21, waiting for transfers between devices, send(): return lax.ppermute(array, 'grp', pairs)  61.2 us
    pallas_call x4, Pallas kernels, gated(): pl.pallas_call(functools.partial(gated_kernel, count, len(shards[0])), gr...  42.7 us
    ppermute x21, starting transfers between devices, send(): return lax.ppermute(array, 'grp', pairs)  29.8 us
    unnamed x44, local copies, waits for them, and re-layouts  12.1 us
    ppermute x6, waiting for transfers between devices, swap(): return lax.ppermute(array, 'tok', [(t, t ^ mask) for t in range(tok_count)])  8.5 us
    pallas_call x2, Pallas kernels, attend(): pl.pallas_call(functools.partial(attend_kernel, chunk, shard_count, width...  7.91 us
    dynamic_update_slice x8, local copies, waits for them, and re-layouts, put(): return lax.dynamic_update_slice_in_dim(hidden, block, source * units, 1)  4.63 us
  transfers between devices with their start and end apart: 28, of which 13 were waited for; matrix products, arithmetic and copies ran while one was open for 3% of the time, Pallas kernels for 28%

profile of v7, /device:TPU:0, one launch (start us, length us, event | category | flops | bytes accessed | tf_op | source)
XLA Modules:
  0.0 190.9 jit_solution(15725991734684298449)
XLA Ops:
  7.2 0.6 copy-done.9
  7.9 1.1 shard_map.112
  9.0 3.0 %collective-permute-start.1 = (bf16[144,768]{1,0:T(8,128)(2,1)S(1)}, bf16[144,768]{1,0:T(8,128)(2,1)S(1)}, u32[]{:S(2)}, u32[]{:S(2)}) collective-permute-start(bf16[144,768]{1,0:T(8,128)(2,1)S(1)} %get-tuple-element.29.refs_3_), channel_id=1, source_target_pairs={{0,2},{1,3},{2,0},{3,1},{4,6},{5,7},{6,4},{7,5},{8,10},{9,11},{10,... | collective-permute-start | bytes 663560 | tf_op jit(solution)/shard_map/ppermute | solution.py:303
  12.0 0.2 collective-permute-start.4
  12.1 6.1 %collective-permute-done.1.refs_5_ = bf16[144,768]{1,0:T(8,128)(2,1)S(1)} collective-permute-done((bf16[144,768]{1,0:T(8,128)(2,1)S(1)}, bf16[144,768]{1,0:T(8,128)(2,1)S(1)}, u32[]{:S(2)}, u32[]{:S(2)}) %collective-permute-start.1) | collective-permute-done | bytes 221216 | tf_op jit(solution)/shard_map/ppermute | solution.py:303
  18.2 0.7 convert_bitcast_fusion
  18.9 0.8 collective-permute-done.2.refs_6_
  19.8 0.7 copy-done.7
  20.5 3.2 %shard_map.113 = (bf16[128,1920]{1,0:T(8,128)(2,1)S(1)}, bf16[128,1920]{1,0:T(8,128)(2,1)S(1)}, f32[128,128]{1,0:T(8,128)S(1)}, f32[128,512]{1,0:T(8,128)S(1)}) custom-call(bf16[128,5120]{1,0:T(8,128)(2,1)} %refs_0_.3, bf16[128,5120]{1,0:T(8,128)(2,1)} %refs_1_.3, f32[1,5120]{1,0:T(1,128)S(1)} %bitcast.6, bf16[144,768]{1,0:T(8,128)(2,1)S(1)} %get-tuple-element.29.refs_3_, ...), custom_call_target="tpu_custom_call" | custom-call | flops 503316480 | bytes 2752512 | tf_op jit(solution)/shard_map/pallas_call | solution.py:169
  23.7 0.8 copy-done.3
  24.5 2.1 %collective-permute-start.7 = (bf16[128,1920]{1,0:T(8,128)(2,1)S(1)}, bf16[128,1920]{1,0:T(8,128)(2,1)S(1)}, u32[]{:S(2)}, u32[]{:S(2)}) collective-permute-start(bf16[128,1920]{1,0:T(8,128)(2,1)S(1)} %get-tuple-element.32.refs_0_), channel_id=1, source_target_pairs={{0,8},{4,12},{8,24},{12,28},{16,0},{20,4},{24,16},{28,20},{1,9},{5... | collective-permute-start | bytes 1474568 | tf_op jit(solution)/shard_map/ppermute | solution.py:310
  26.6 1.5 collective-permute-start.6
  28.2 0.5 collective-permute-start.5
  28.7 1.1 collective-permute-done.3.refs_4_
  29.8 0.5 collective-permute-done.5.refs_6_
  30.3 4.7 %shard_map.114 = (bf16[128,3200]{1,0:T(8,128)(2,1)S(1)}, bf16[128,3328]{1,0:T(8,128)(2,1)S(1)}) custom-call(bf16[128,5120]{1,0:T(8,128)(2,1)} %refs_0_.3, bf16[128,5120]{1,0:T(8,128)(2,1)} %refs_1_.3, f32[1,5120]{1,0:T(1,128)S(1)} %bitcast.7, bf16[128,1280]{1,0:T(8,128)(2,1)S(1)} %get-tuple-element.31.refs_3_, ...), custom_call_target="tpu_custom_call" | custom-call | flops 838860800 | bytes 4587520 | tf_op jit(solution)/shard_map/pallas_call | solution.py:169
  35.0 0.9 copy-done.1
  35.9 3.3 %collective-permute-done.7.refs_4_ = bf16[128,1920]{1,0:T(8,128)(2,1)S(1)} collective-permute-done((bf16[128,1920]{1,0:T(8,128)(2,1)S(1)}, bf16[128,1920]{1,0:T(8,128)(2,1)S(1)}, u32[]{:S(2)}, u32[]{:S(2)}) %collective-permute-start.7) | collective-permute-done | bytes 491552 | tf_op jit(solution)/shard_map/ppermute | solution.py:310
  39.2 0.4 collective-permute-done.6.refs_2_
  39.6 0.8 copy-done.16
  40.4 2.6 %collective-permute-start.9 = (bf16[128,3328]{1,0:T(8,128)(2,1)S(1)}, bf16[128,3328]{1,0:T(8,128)(2,1)S(1)}, u32[]{:S(2)}, u32[]{:S(2)}) collective-permute-start(bf16[128,3328]{1,0:T(8,128)(2,1)S(1)} %get-tuple-element.38.refs_1_), channel_id=1, source_target_pairs={{0,8},{4,12},{8,24},{12,28},{16,0},{20,4},{24,16},{28,20},{1,9},{5... | collective-permute-start | bytes 2555912 | tf_op jit(solution)/shard_map/ppermute | solution.py:310
  43.0 1.5 collective-permute-start.8
  44.7 16.8 %collective-permute-done.9.refs_5_ = bf16[128,3328]{1,0:T(8,128)(2,1)S(1)} collective-permute-done((bf16[128,3328]{1,0:T(8,128)(2,1)S(1)}, bf16[128,3328]{1,0:T(8,128)(2,1)S(1)}, u32[]{:S(2)}, u32[]{:S(2)}) %collective-permute-start.9) | collective-permute-done | bytes 852000 | tf_op jit(solution)/shard_map/ppermute | solution.py:310
  61.5 1.0 collective-permute-done.8.refs_3_
  62.6 0.9 copy-done.10
  63.5 1.7 collective-permute-start.15
  65.1 1.5 collective-permute-start.13
  66.7 1.2 collective-permute-start.14
  67.9 0.5 collective-permute-start.12
  68.4 1.2 copy-done.11
  69.5 1.0 copy-done.13
  70.6 1.0 copy-done.15
  71.6 1.0 copy-done.17
  72.6 12.3 %shard_map.115 = (bf16[128,1024]{1,0:T(8,128)(2,1)S(1)}, bf16[128,1024]{1,0:T(8,128)(2,1)S(1)}, bf16[128,1024]{1,0:T(8,128)(2,1)S(1)}) custom-call(bf16[128,1920]{1,0:T(8,128)(2,1)S(1)} %copy-done.15, bf16[128,3328]{1,0:T(8,128)(2,1)S(1)} %get-tuple-element.38.refs_1_, bf16[128,1920]{1,0:T(8,128)(2,1)S(1)} %copy-done.17, bf16[128,3328]{1,0:T(8,128)(2,1)S(1)} %copy-done.11, ...), custom_call_target="tpu_custom_call" | custom-call | flops 8053063680 | bytes 25690112 | tf_op jit(solution)/shard_map/pallas_call | solution.py:223
  84.9 1.6 collective-permute-start.10
  86.5 1.7 collective-permute-start.11
  88.3 0.3 collective-permute-start.20
  88.6 13.9 %collective-permute-done.14.refs_2_ = bf16[128,1920]{1,0:T(8,128)(2,1)S(1)} collective-permute-done((bf16[128,1920]{1,0:T(8,128)(2,1)}, bf16[128,1920]{1,0:T(8,128)(2,1)S(1)}, u32[]{:S(2)}, u32[]{:S(2)}) %collective-permute-start.14) | collective-permute-done | bytes 491552 | tf_op jit(solution)/shard_map/ppermute | solution.py:310
  102.4 1.5 collective-permute-start.18
  104.0 1.2 pad_maximum_fusion
  105.2 0.2 broadcast_in_dim.25
  105.4 0.6 collective-permute-start.17
  106.1 14.6 %collective-permute-done.20.refs_3_ = bf16[128,3328]{1,0:T(8,128)(2,1)S(1)} collective-permute-done((bf16[128,3328]{1,0:T(8,128)(2,1)S(1)}, bf16[128,3328]{1,0:T(8,128)(2,1)S(1)}, u32[]{:S(2)}, u32[]{:S(2)}) %collective-permute-start.20) | collective-permute-done | bytes 852000 | tf_op jit(solution)/shard_map/ppermute | solution.py:310
  120.7 3.6 %collective-permute-done.18.refs_1_ = bf16[128,3328]{1,0:T(8,128)(2,1)S(1)} collective-permute-done((bf16[128,3328]{1,0:T(8,128)(2,1)S(1)}, bf16[128,3328]{1,0:T(8,128)(2,1)S(1)}, u32[]{:S(2)}, u32[]{:S(2)}) %collective-permute-start.18) | collective-permute-done | bytes 852000 | tf_op jit(solution)/shard_map/ppermute | solution.py:310
  124.3 1.5 collective-permute-start.25
  125.9 10.9 %shard_map.116 = (bf16[128,1024]{1,0:T(8,128)(2,1)S(1)}, bf16[128,1024]{1,0:T(8,128)(2,1)}) custom-call(bf16[128,1920]{1,0:T(8,128)(2,1)S(1)} %collective-permute-done.12.refs_0_, bf16[128,3328]{1,0:T(8,128)(2,1)S(1)} %collective-permute-done.13.refs_1_, bf16[128,1920]{1,0:T(8,128)(2,1)S(1)} %collective-permute-done.14.refs_2_, ...), custom_call_target="tpu_custom_call" | custom-call | flops 5368709120 | bytes 24117248 | tf_op jit(solution)/shard_map/pallas_call | solution.py:223
  136.8 0.7 copy-done.18
  137.5 2.0 %collective-permute-start.16 = (bf16[128,1024]{1,0:T(8,128)(2,1)}, bf16[128,1024]{1,0:T(8,128)(2,1)}, u32[]{:S(2)}, u32[]{:S(2)}) collective-permute-start(bf16[128,1024]{1,0:T(8,128)(2,1)} %get-tuple-element.44), channel_id=1, source_target_pairs={{0,24},{4,28},{8,16},{12,20},{16,8},{20,12},{24,0},{28,4},{1,25},{... | collective-permute-start | bytes 786440 | tf_op jit(solution)/shard_map/ppermute | solution.py:310
  139.5 0.8 copy-done.5
  140.3 0.5 collective-permute-start.24
  140.8 1.6 copy-done
  142.4 2.7 %shard_map.117 = bf16[16,16,2048]{2,1,0:T(8,128)(2,1)} custom-call(s32[16]{0:T(128)S(1)} %broadcast_add_fusion.page_ref, bf16[512,2048]{1,0:T(8,128)(2,1)S(1)} %copy-done, bf16[16,16,2048]{2,1,0:T(8,128)(2,1)} %cache_ref.1), custom_call_target="tpu_custom_call" | custom-call | bytes 4194304 | tf_op jit(solution)/shard_map/pallas_call | solution.py:257
  145.1 10.4 %shard_map.118 = (bf16[128,1024]{1,0:T(8,128)(2,1)S(1)}, bf16[128,1024]{1,0:T(8,128)(2,1)S(1)}) custom-call(bf16[128,1920]{1,0:T(8,128)(2,1)S(1)} %copy-done.6, bf16[128,3328]{1,0:T(8,128)(2,1)S(1)} %collective-permute-done.18.refs_1_, bf16[128,1920]{1,0:T(8,128)(2,1)} %collective-permute-done.19.refs_2_, ...), custom_call_target="tpu_custom_call" | custom-call | flops 5368709120 | bytes 24117248 | tf_op jit(solution)/shard_map/pallas_call | solution.py:223
  155.6 1.7 constant_dynamic-update-slice_fusion.4
  157.3 3.0 %collective-permute-start.23 = (bf16[128,1024]{1,0:T(8,128)(2,1)S(1)}, bf16[128,1024]{1,0:T(8,128)(2,1)S(1)}, u32[]{:S(2)}, u32[]{:S(2)}) collective-permute-start(bf16[128,1024]{1,0:T(8,128)(2,1)S(1)} %get-tuple-element.50), channel_id=1, source_target_pairs={{0,8},{4,12},{8,24},{12,28},{16,0},{20,4},{24,16},{28,20},{1,9},{5... | collective-permute-start | bytes 786440 | tf_op jit(solution)/shard_map/ppermute | solution.py:310
  160.3 1.7 collective-permute-start.22
  162.0 4.1 %collective-permute-done.24.refs_0_ = bf16[128,1920]{1,0:T(8,128)(2,1)S(1)} collective-permute-done((bf16[128,1920]{1,0:T(8,128)(2,1)}, bf16[128,1920]{1,0:T(8,128)(2,1)S(1)}, u32[]{:S(2)}, u32[]{:S(2)}) %collective-permute-start.24) | collective-permute-done | bytes 491552 | tf_op jit(solution)/shard_map/ppermute | solution.py:310
  166.1 9.0 %shard_map.119 = bf16[128,1024]{1,0:T(8,128)(2,1)S(1)} custom-call(bf16[128,1920]{1,0:T(8,128)(2,1)S(1)} %collective-permute-done.24.refs_0_, bf16[128,3328]{1,0:T(8,128)(2,1)} %collective-permute-done.25.refs_1_, bf16[5120,1024]{1,0:T(8,128)(2,1)} %refs_2_.1, bf16[5120,1024]{1,0:T(8,128)(2,1)} %refs_3_.1), custom_call_target="tpu_custom_call" | custom-call | flops 2684354560 | bytes 22544384 | tf_op jit(solution)/shard_map/pallas_call | solution.py:223
  175.1 2.7 %collective-permute-start.26 = (bf16[128,1024]{1,0:T(8,128)(2,1)S(1)}, bf16[128,1024]{1,0:T(8,128)(2,1)S(1)}, u32[]{:S(2)}, u32[]{:S(2)}) collective-permute-start(bf16[128,1024]{1,0:T(8,128)(2,1)S(1)} %shard_map.119), channel_id=1, source_target_pairs={{0,12},{4,8},{8,28},{12,24},{16,4},{20,0},{24,20},{28,16},{1,13},{... | collective-permute-start | bytes 786440 | tf_op jit(solution)/shard_map/ppermute | solution.py:310
  177.8 0.7 constant_dynamic-update-slice_fusion.3
  178.5 0.7 constant_dynamic-update-slice_fusion.2
  179.3 0.7 constant_dynamic-update-slice_fusion.1
  180.0 3.3 %collective-permute-done.26 = bf16[128,1024]{1,0:T(8,128)(2,1)S(1)} collective-permute-done((bf16[128,1024]{1,0:T(8,128)(2,1)S(1)}, bf16[128,1024]{1,0:T(8,128)(2,1)S(1)}, u32[]{:S(2)}, u32[]{:S(2)}) %collective-permute-start.26) | collective-permute-done | bytes 262176 | tf_op jit(solution)/shard_map/ppermute | solution.py:310
  183.3 0.7 constant_dynamic-update-slice_fusion
  (61 shorter events, 0.5 us)
Async XLA Ops:
  7.2 23.1 %copy-start.8 = (f32[5120]{0:T(1024)S(1)}, f32[5120]{0:T(1024)}, u32[]{:S(2)}) copy-start(f32[5120]{0:T(1024)} %param.13) | copy-start | bytes 61444
  7.2 133.7 %all-gather.2.cloned.1.call-start = ((), (), s32[]{:S(2)}) async-start(), calls=%async_computation | async-start | bytes 2621440 | tf_op jit(solution)/shard_map/all_gather | solution.py:342
  7.2 0.7 copy-start.9
  9.0 9.3 %collective-permute-start.1 = (bf16[144,768]{1,0:T(8,128)(2,1)S(1)}, bf16[144,768]{1,0:T(8,128)(2,1)S(1)}, u32[]{:S(2)}, u32[]{:S(2)}) collective-permute-start(bf16[144,768]{1,0:T(8,128)(2,1)S(1)} %get-tuple-element.29.refs_3_), channel_id=1, source_target_pairs={{0,2},{1,3},{2,0},{3,1},{4,6},{5,7},{6,4},{7,5},{8,10},{9,11},{10,... | collective-permute-start | bytes 663560 | tf_op jit(solution)/shard_map/ppermute | solution.py:303
  12.0 6.9 %collective-permute-start = (bf16[144,768]{1,0:T(8,128)(2,1)S(1)}, bf16[144,768]{1,0:T(8,128)(2,1)S(1)}, u32[]{:S(2)}, u32[]{:S(2)}) collective-permute-start(bf16[144,768]{1,0:T(8,128)(2,1)S(1)} %get-tuple-element.29.refs_3_), channel_id=1, source_target_pairs={{0,1},{1,0},{2,3},{3,2},{4,5},{5,4},{6,7},{7,6},{8,9},{9,8},{10,11... | collective-permute-start | bytes 663560 | tf_op jit(solution)/shard_map/ppermute | solution.py:303
  12.0 16.2 %collective-permute-start.4 = (bf16[128,1280]{1,0:T(8,128)(2,1)S(1)}, bf16[128,1280]{1,0:T(8,128)(2,1)S(1)}, u32[]{:S(2)}, u32[]{:S(2)}) collective-permute-start(bf16[128,1280]{1,0:T(8,128)(2,1)S(1)} %get-tuple-element.31.refs_3_), channel_id=1, source_target_pairs={{0,2},{1,3},{2,0},{3,1},{4,6},{5,7},{6,4},{7,5},{8,10},{9,11},{10,... | collective-permute-start | bytes 983048 | tf_op jit(solution)/shard_map/ppermute | solution.py:303
  18.2 1.5 collective-permute-start.2
  19.8 0.7 copy-start.7
  23.7 0.8 copy-start.3
  24.5 10.5 %copy-start.14 = (bf16[128,1920]{1,0:T(8,128)(2,1)}, bf16[128,1920]{1,0:T(8,128)(2,1)S(1)}, u32[]{:S(2)}) copy-start(bf16[128,1920]{1,0:T(8,128)(2,1)S(1)} %get-tuple-element.32.refs_0_) | copy-start | bytes 1474564
  24.5 14.7 %collective-permute-start.7 = (bf16[128,1920]{1,0:T(8,128)(2,1)S(1)}, bf16[128,1920]{1,0:T(8,128)(2,1)S(1)}, u32[]{:S(2)}, u32[]{:S(2)}) collective-permute-start(bf16[128,1920]{1,0:T(8,128)(2,1)S(1)} %get-tuple-element.32.refs_0_), channel_id=1, source_target_pairs={{0,8},{4,12},{8,24},{12,28},{16,0},{20,4},{24,16},{28,20},{1,9},{5... | collective-permute-start | bytes 1474568 | tf_op jit(solution)/shard_map/ppermute | solution.py:310
  26.6 13.0 %collective-permute-start.6 = (bf16[128,1920]{1,0:T(8,128)(2,1)S(1)}, bf16[128,1920]{1,0:T(8,128)(2,1)S(1)}, u32[]{:S(2)}, u32[]{:S(2)}) collective-permute-start(bf16[128,1920]{1,0:T(8,128)(2,1)S(1)} %get-tuple-element.32.refs_0_), channel_id=1, source_target_pairs={{0,4},{4,0},{8,12},{12,8},{16,20},{20,16},{24,28},{28,24},{1,5},{5... | collective-permute-start | bytes 1474568 | tf_op jit(solution)/shard_map/ppermute | solution.py:310
  28.2 1.6 collective-permute-start.3
  28.2 2.1 %collective-permute-start.5 = (bf16[128,1280]{1,0:T(8,128)(2,1)S(1)}, bf16[128,1280]{1,0:T(8,128)(2,1)S(1)}, u32[]{:S(2)}, u32[]{:S(2)}) collective-permute-start(bf16[128,1280]{1,0:T(8,128)(2,1)S(1)} %collective-permute-done.4.refs_5_), channel_id=1, source_target_pairs={{0,1},{1,0},{2,3},{3,2},{4,5},{5,4},{6,7},{7,6},{8,9},{9,8},{10,11... | collective-permute-start | bytes 983048 | tf_op jit(solution)/shard_map/ppermute | solution.py:303
  30.3 14.3 %copy-start.21 = (s32[1,64]{1,0:T(1,128)S(1)}, s32[1,64]{1,0:T(1,128)}, u32[]{:S(2)}) copy-start(s32[1,64]{1,0:T(1,128)} %param.17) | copy-start | bytes 772
  35.0 0.9 copy-start.1
  39.2 1.3 copy-start.12
  39.6 0.8 copy-start.16
  40.4 21.1 %collective-permute-start.9 = (bf16[128,3328]{1,0:T(8,128)(2,1)S(1)}, bf16[128,3328]{1,0:T(8,128)(2,1)S(1)}, u32[]{:S(2)}, u32[]{:S(2)}) collective-permute-start(bf16[128,3328]{1,0:T(8,128)(2,1)S(1)} %get-tuple-element.38.refs_1_), channel_id=1, source_target_pairs={{0,8},{4,12},{8,24},{12,28},{16,0},{20,4},{24,16},{28,20},{1,9},{5... | collective-permute-start | bytes 2555912 | tf_op jit(solution)/shard_map/ppermute | solution.py:310
  43.0 19.6 %collective-permute-start.8 = (bf16[128,3328]{1,0:T(8,128)(2,1)S(1)}, bf16[128,3328]{1,0:T(8,128)(2,1)S(1)}, u32[]{:S(2)}, u32[]{:S(2)}) collective-permute-start(bf16[128,3328]{1,0:T(8,128)(2,1)S(1)} %get-tuple-element.38.refs_1_), channel_id=1, source_target_pairs={{0,4},{4,0},{8,12},{12,8},{16,20},{20,16},{24,28},{28,24},{1,5},{5... | collective-permute-start | bytes 2555912 | tf_op jit(solution)/shard_map/ppermute | solution.py:310
  62.6 0.9 copy-start.10
  63.5 23.1 %collective-permute-start.15 = (bf16[128,3328]{1,0:T(8,128)(2,1)S(1)}, bf16[128,3328]{1,0:T(8,128)(2,1)S(1)}, u32[]{:S(2)}, u32[]{:S(2)}) collective-permute-start(bf16[128,3328]{1,0:T(8,128)(2,1)S(1)} %collective-permute-done.9.refs_5_), channel_id=1, source_target_pairs={{0,8},{4,12},{8,24},{12,28},{16,0},{20,4},{24,16},{28,20},{1,9},{5... | collective-permute-start | bytes 2555912 | tf_op jit(solution)/shard_map/ppermute | solution.py:310
  65.1 23.1 %collective-permute-start.13 = (bf16[128,3328]{1,0:T(8,128)(2,1)S(1)}, bf16[128,3328]{1,0:T(8,128)(2,1)S(1)}, u32[]{:S(2)}, u32[]{:S(2)}) collective-permute-start(bf16[128,3328]{1,0:T(8,128)(2,1)S(1)} %collective-permute-done.9.refs_5_), channel_id=1, source_target_pairs={{0,4},{4,0},{8,12},{12,8},{16,20},{20,16},{24,28},{28,24},{1,5},{5... | collective-permute-start | bytes 2555912 | tf_op jit(solution)/shard_map/ppermute | solution.py:310
  66.7 37.3 %copy-start.2 = (bf16[128,3200]{1,0:T(8,128)(2,1)S(1)}, bf16[128,3200]{1,0:T(8,128)(2,1)}, u32[]{:S(2)}) copy-start(bf16[128,3200]{1,0:T(8,128)(2,1)} %copy-done.1) | copy-start | bytes 2457604
  66.7 37.3 %copy-start.4 = (bf16[128,1920]{1,0:T(8,128)(2,1)S(1)}, bf16[128,1920]{1,0:T(8,128)(2,1)}, u32[]{:S(2)}) copy-start(bf16[128,1920]{1,0:T(8,128)(2,1)} %copy-done.3) | copy-start | bytes 1474564
  66.7 35.8 %collective-permute-start.14 = (bf16[128,1920]{1,0:T(8,128)(2,1)}, bf16[128,1920]{1,0:T(8,128)(2,1)S(1)}, u32[]{:S(2)}, u32[]{:S(2)}) collective-permute-start(bf16[128,1920]{1,0:T(8,128)(2,1)} %copy-done.12), channel_id=1, source_target_pairs={{0,8},{4,12},{8,24},{12,28},{16,0},{20,4},{24,16},{28,20},{1,9},{5... | collective-permute-start | bytes 1474568 | tf_op jit(solution)/shard_map/ppermute | solution.py:310
  67.9 37.3 %collective-permute-start.12 = (bf16[128,1920]{1,0:T(8,128)(2,1)}, bf16[128,1920]{1,0:T(8,128)(2,1)S(1)}, u32[]{:S(2)}, u32[]{:S(2)}) collective-permute-start(bf16[128,1920]{1,0:T(8,128)(2,1)} %copy-done.12), channel_id=1, source_target_pairs={{0,4},{4,0},{8,12},{12,8},{16,20},{20,16},{24,28},{28,24},{1,5},{5... | collective-permute-start | bytes 1474568 | tf_op jit(solution)/shard_map/ppermute | solution.py:310
  68.4 1.2 copy-start.11
  69.5 1.0 copy-start.13
  70.5 1.0 copy-start.15
  71.6 1.0 copy-start.17
  84.9 20.5 %collective-permute-start.10 = (bf16[128,1024]{1,0:T(8,128)(2,1)S(1)}, bf16[128,1024]{1,0:T(8,128)(2,1)S(1)}, u32[]{:S(2)}, u32[]{:S(2)}) collective-permute-start(bf16[128,1024]{1,0:T(8,128)(2,1)S(1)} %get-tuple-element.40), channel_id=1, source_target_pairs={{0,4},{4,0},{8,12},{12,8},{16,20},{20,16},{24,28},{28,24},{1,5},{5... | collective-permute-start | bytes 786440 | tf_op jit(solution)/shard_map/ppermute | solution.py:310
  86.5 19.5 %collective-permute-start.11 = (bf16[128,1024]{1,0:T(8,128)(2,1)S(1)}, bf16[128,1024]{1,0:T(8,128)(2,1)S(1)}, u32[]{:S(2)}, u32[]{:S(2)}) collective-permute-start(bf16[128,1024]{1,0:T(8,128)(2,1)S(1)} %get-tuple-element.41), channel_id=1, source_target_pairs={{0,16},{4,20},{8,0},{12,4},{16,24},{20,28},{24,8},{28,12},{1,17},{... | collective-permute-start | bytes 786440 | tf_op jit(solution)/shard_map/ppermute | solution.py:310
  88.3 32.4 %collective-permute-start.20 = (bf16[128,3328]{1,0:T(8,128)(2,1)S(1)}, bf16[128,3328]{1,0:T(8,128)(2,1)S(1)}, u32[]{:S(2)}, u32[]{:S(2)}) collective-permute-start(bf16[128,3328]{1,0:T(8,128)(2,1)S(1)} %collective-permute-done.15.refs_3_), channel_id=1, source_target_pairs={{0,8},{4,12},{8,24},{12,28},{16,0},{20,4},{24,16},{28,20},{1,9},{5... | collective-permute-start | bytes 2555912 | tf_op jit(solution)/shard_map/ppermute | solution.py:310
  102.4 21.9 %collective-permute-start.18 = (bf16[128,3328]{1,0:T(8,128)(2,1)S(1)}, bf16[128,3328]{1,0:T(8,128)(2,1)S(1)}, u32[]{:S(2)}, u32[]{:S(2)}) collective-permute-start(bf16[128,3328]{1,0:T(8,128)(2,1)S(1)} %collective-permute-done.15.refs_3_), channel_id=1, source_target_pairs={{0,4},{4,0},{8,12},{12,8},{16,20},{20,16},{24,28},{28,24},{1,5},{5... | collective-permute-start | bytes 2555912 | tf_op jit(solution)/shard_map/ppermute | solution.py:310
  105.2 34.4 %collective-permute-start.19 = (bf16[128,1920]{1,0:T(8,128)(2,1)S(1)}, bf16[128,1920]{1,0:T(8,128)(2,1)}, u32[]{:S(2)}, u32[]{:S(2)}) collective-permute-start(bf16[128,1920]{1,0:T(8,128)(2,1)S(1)} %collective-permute-done.14.refs_2_), channel_id=1, source_target_pairs={{0,8},{4,12},{8,24},{12,28},{16,0},{20,4},{24,16},{28,20},{1,9},{5... | collective-permute-start | bytes 1474568 | tf_op jit(solution)/shard_map/ppermute | solution.py:310
  105.4 34.1 %collective-permute-start.17 = (bf16[128,1920]{1,0:T(8,128)(2,1)S(1)}, bf16[128,1920]{1,0:T(8,128)(2,1)S(1)}, u32[]{:S(2)}, u32[]{:S(2)}) collective-permute-start(bf16[128,1920]{1,0:T(8,128)(2,1)S(1)} %collective-permute-done.14.refs_2_), channel_id=1, source_target_pairs={{0,4},{4,0},{8,12},{12,8},{16,20},{20,16},{24,28},{28,24},{1,5},{5... | collective-permute-start | bytes 1474568 | tf_op jit(solution)/shard_map/ppermute | solution.py:310
  106.1 18.3 %copy-start.20 = (bf16[128,8192]{1,0:T(8,128)(2,1)}, bf16[128,8192]{1,0:T(8,128)(2,1)S(1)}, u32[]{:S(2)}) copy-start(bf16[128,8192]{1,0:T(8,128)(2,1)S(1)} %constant_dynamic-update-slice_fusion.5) | copy-start | bytes 6291460
  124.3 41.8 %collective-permute-start.25 = (bf16[128,3328]{1,0:T(8,128)(2,1)S(1)}, bf16[128,3328]{1,0:T(8,128)(2,1)}, u32[]{:S(2)}, u32[]{:S(2)}) collective-permute-start(bf16[128,3328]{1,0:T(8,128)(2,1)S(1)} %collective-permute-done.20.refs_3_), channel_id=1, source_target_pairs={{0,4},{4,0},{8,12},{12,8},{16,20},{20,16},{24,28},{28,24},{1,5},{5... | collective-permute-start | bytes 2555912 | tf_op jit(solution)/shard_map/ppermute | solution.py:310
  136.8 0.7 copy-start.18
  137.5 18.2 %collective-permute-start.16 = (bf16[128,1024]{1,0:T(8,128)(2,1)}, bf16[128,1024]{1,0:T(8,128)(2,1)}, u32[]{:S(2)}, u32[]{:S(2)}) collective-permute-start(bf16[128,1024]{1,0:T(8,128)(2,1)} %get-tuple-element.44), channel_id=1, source_target_pairs={{0,24},{4,28},{8,16},{12,20},{16,8},{20,12},{24,0},{28,4},{1,25},{... | collective-permute-start | bytes 786440 | tf_op jit(solution)/shard_map/ppermute | solution.py:310
  139.5 0.8 copy-start.5
  140.3 25.8 %collective-permute-start.24 = (bf16[128,1920]{1,0:T(8,128)(2,1)}, bf16[128,1920]{1,0:T(8,128)(2,1)S(1)}, u32[]{:S(2)}, u32[]{:S(2)}) collective-permute-start(bf16[128,1920]{1,0:T(8,128)(2,1)} %collective-permute-done.19.refs_2_), channel_id=1, source_target_pairs={{0,4},{4,0},{8,12},{12,8},{16,20},{20,16},{24,28},{28,24},{1,5},{5... | collective-permute-start | bytes 1474568 | tf_op jit(solution)/shard_map/ppermute | solution.py:310
  140.8 1.6 copy-start
  142.4 2.7 %copy-start.6 = (bf16[128,1920]{1,0:T(8,128)(2,1)S(1)}, bf16[128,1920]{1,0:T(8,128)(2,1)}, u32[]{:S(2)}) copy-start(bf16[128,1920]{1,0:T(8,128)(2,1)} %copy-done.5) | copy-start | bytes 1474564
  145.1 10.4 %copy-start.19 = (bf16[128,1024]{1,0:T(8,128)(2,1)S(1)}, bf16[128,1024]{1,0:T(8,128)(2,1)}, u32[]{:S(2)}) copy-start(bf16[128,1024]{1,0:T(8,128)(2,1)} %copy-done.18) | copy-start | bytes 786436
  155.6 22.3 %collective-permute-start.21 = (bf16[128,1024]{1,0:T(8,128)(2,1)S(1)}, bf16[128,1024]{1,0:T(8,128)(2,1)S(1)}, u32[]{:S(2)}, u32[]{:S(2)}) collective-permute-start(bf16[128,1024]{1,0:T(8,128)(2,1)S(1)} %copy-done.19), channel_id=1, source_target_pairs={{0,20},{4,16},{8,4},{12,0},{16,28},{20,24},{24,12},{28,8},{1,21},{... | collective-permute-start | bytes 786440 | tf_op jit(solution)/shard_map/ppermute | solution.py:310
  157.3 21.9 %collective-permute-start.23 = (bf16[128,1024]{1,0:T(8,128)(2,1)S(1)}, bf16[128,1024]{1,0:T(8,128)(2,1)S(1)}, u32[]{:S(2)}, u32[]{:S(2)}) collective-permute-start(bf16[128,1024]{1,0:T(8,128)(2,1)S(1)} %get-tuple-element.50), channel_id=1, source_target_pairs={{0,8},{4,12},{8,24},{12,28},{16,0},{20,4},{24,16},{28,20},{1,9},{5... | collective-permute-start | bytes 786440 | tf_op jit(solution)/shard_map/ppermute | solution.py:310
  160.3 18.3 %collective-permute-start.22 = (bf16[128,1024]{1,0:T(8,128)(2,1)S(1)}, bf16[128,1024]{1,0:T(8,128)(2,1)S(1)}, u32[]{:S(2)}, u32[]{:S(2)}) collective-permute-start(bf16[128,1024]{1,0:T(8,128)(2,1)S(1)} %get-tuple-element.52), channel_id=1, source_target_pairs={{0,28},{4,24},{8,20},{12,16},{16,12},{20,8},{24,4},{28,0},{1,29},{... | collective-permute-start | bytes 786440 | tf_op jit(solution)/shard_map/ppermute | solution.py:310
  175.1 8.2 %collective-permute-start.26 = (bf16[128,1024]{1,0:T(8,128)(2,1)S(1)}, bf16[128,1024]{1,0:T(8,128)(2,1)S(1)}, u32[]{:S(2)}, u32[]{:S(2)}) collective-permute-start(bf16[128,1024]{1,0:T(8,128)(2,1)S(1)} %shard_map.119), channel_id=1, source_target_pairs={{0,12},{4,8},{8,28},{12,24},{16,4},{20,0},{24,20},{28,16},{1,13},{... | collective-permute-start | bytes 786440 | tf_op jit(solution)/shard_map/ppermute | solution.py:310
Sparse Core Ops, SparseCore 0:
  44.7 20.6 all-gather.1

commit v8 on v7

--- a/solution.py
+++ b/solution.py
@@ -239,6 +239,57 @@
     )(*operands, gate_weight, up_weight)
 
 
+def part_kernel(width, final, *refs):
+    chunk_ref, gate_ref, up_ref = refs[:3]
+    tokens = chunk_ref[:, :width]
+    gate_sum = jnp.dot(tokens, gate_ref[...], preferred_element_type=jnp.float32)
+    up_sum = jnp.dot(tokens, up_ref[...], preferred_element_type=jnp.float32)
+    if final:
+        gate_part, up_part, scale_ref, out_ref = refs[3:]
+        scale = scale_ref[:, :1]
+        gate_sum = (gate_part[...] + gate_sum) * scale
+        up_sum = (up_part[...] + up_sum) * scale
+        out_ref[...] = (gate_sum / (1.0 + jnp.exp(-gate_sum)) * up_sum).astype(jnp.bfloat16)
+    else:
+        gate_part, up_part, scale_ref = refs[3:]
+        gate_part[...] = gate_sum
+        up_part[...] = up_sum
+        both = chunk_ref[:, -SCALE_COLUMNS:].astype(jnp.float32)
+        scale = both[:, :1] + both[:, SCALE_COLUMNS // 2 : SCALE_COLUMNS // 2 + 1]
+        scale_ref[...] = jnp.broadcast_to(scale, scale_ref.shape)
+
+
+def gated_part(chunk, array, gate_weight, up_weight, so_far):
+    rows = array.shape[0]
+    units = gate_weight.shape[1]
+    block = 256
+    before = sum(HEAD_CHUNKS[:chunk]) * GROUP_SPLIT * HEAD_SIZE
+    width = HEAD_CHUNKS[chunk] * GROUP_SPLIT * HEAD_SIZE
+    weights = pl.BlockSpec((pl.Element(width), pl.Element(block)), lambda i: (before, i * block))
+    whole = pl.BlockSpec(array.shape, lambda i: (0, 0))
+    part = pl.BlockSpec((rows, block), lambda i: (0, i))
+    scale = pl.BlockSpec((rows, 128), lambda i: (0, 0))
+    if so_far:
+        out_specs, shapes = part, jax.ShapeDtypeStruct((rows, units), jnp.bfloat16)
+    else:
+        out_specs = [part, part, scale]
+        shapes = [jax.ShapeDtypeStruct((rows, units), jnp.float32)] * 2
+        shapes.append(jax.ShapeDtypeStruct((rows, 128), jnp.float32))
+    return pl.pallas_call(
+        functools.partial(part_kernel, width, bool(so_far)),
+        grid=(units // block,),
+        in_specs=[whole, weights, weights] + ([part, part, scale] if so_far else []),
+        out_specs=out_specs,
+        out_shape=shapes,
+        compiler_params=pltpu.CompilerParams(vmem_limit_bytes=VMEM_LIMIT),
+        cost_estimate=pl.CostEstimate(
+            flops=4 * rows * width * units,
+            bytes_accessed=4 * width * units + 2 * rows * width + 8 * rows * units,
+            transcendentals=rows * units if so_far else 0,
+        ),
+    )(array, gate_weight, up_weight, *so_far)
+
+
 def cache_kernel(page_ref, kv_ref, cache_ref, out_ref):
     for i in range(out_ref.shape[0]):
         page = page_ref[i]
@@ -318,6 +369,8 @@
         held = {0: packed[c]}
         mask = tok_count // 2
         while mask > 1:
+            if c:
+                held = {m: after(a, *first_swaps[0].values()) for m, a in held.items()}
             held.update({m ^ mask: swap(a, mask) for m, a in held.items()})
             mask //= 2
         first_swaps.append(held)
@@ -379,7 +432,11 @@
             waiting.append((following, step + 1, False))
         if step == line_count - 2:
             waiting[-1] = ([*following[:-1], after(following[-1], written)], step + 1, False)
-        blocks = gated([shard for shard, _, _ in waiting], gate_weight, up_weight)
+        if step + 1 < line_count:
+            blocks = gated([shard for shard, _, _ in waiting], gate_weight, up_weight)
+        else:
+            shares = gated_part(1, other[1], gate_weight, up_weight, ())
+            blocks = [gated_part(0, other[0], gate_weight, up_weight, shares)]
         products.append(blocks[-1])
         late = [(after(block, blocks[-1]), steps, flip) for block, steps, flip in late]
         made = late + [(block, steps, flip) for block, (_, steps, flip) in zip(blocks, waiting)]

time: 191 us -> 190 us (level)
  Pallas kernels: 54.4 us -> 57 us
  waiting for transfers between devices: 69.7 us -> 67.5 us
    pallas_call x0 -> x2, Pallas kernels: none -> 11.6 us  [gated_part(): pl.pallas_call(functools.partial(part_kernel, width, bool(so_far)), grid=...]
    pallas_call x4 -> x3, Pallas kernels: 42.7 us -> 33.6 us  [gated(): pl.pallas_call(functools.partial(gated_kernel, count, len(shards[0])), gr...]
    ppermute x21, starting transfers between devices: 29.8 us -> 26.8 us  [send(): return lax.ppermute(array, 'grp', pairs)]
  transfers between devices with their start and end apart: 28 -> 28, of which waited for: 13 -> 12; matrix products, arithmetic and copies ran while one was open for 3% -> 3% of each run, Pallas kernels for 28% -> 29%
where the time goes in v8:
time: 190 us
  waiting for transfers between devices  67.5 us (36%)
  Pallas kernels  57 us (30%)
  starting transfers between devices  32.1 us (17%)
  local copies, waits for them, and re-layouts  17 us (9%)
  between operations  14.3 us (8%)
  other arithmetic  1.98 us (1%)
    ppermute x21, waiting for transfers between devices, send(): return lax.ppermute(array, 'grp', pairs)  59.6 us
    pallas_call x3, Pallas kernels, gated(): pl.pallas_call(functools.partial(gated_kernel, count, len(shards[0])), gr...  33.6 us
    ppermute x21, starting transfers between devices, send(): return lax.ppermute(array, 'grp', pairs)  26.8 us
    unnamed x44, local copies, waits for them, and re-layouts  12.1 us
    pallas_call x2, Pallas kernels, gated_part(): pl.pallas_call(functools.partial(part_kernel, width, bool(so_far)), grid=...  11.6 us
    pallas_call x2, Pallas kernels, attend(): pl.pallas_call(functools.partial(attend_kernel, chunk, shard_count, width...  7.91 us
    ppermute x6, waiting for transfers between devices, swap(): return lax.ppermute(array, 'tok', [(t, t ^ mask) for t in range(tok_count)])  7.83 us
    ppermute x6, starting transfers between devices, swap(): return lax.ppermute(array, 'tok', [(t, t ^ mask) for t in range(tok_count)])  5.26 us
  transfers between devices with their start and end apart: 28, of which 12 were waited for; matrix products, arithmetic and copies ran while one was open for 3% of the time, Pallas kernels for 29%

profile of v8, /device:TPU:0, one launch (start us, length us, event | category | flops | bytes accessed | tf_op | source)
XLA Modules:
  0.0 189.8 jit_solution(4274166675449982269)
XLA Ops:
  7.2 0.6 copy-done.9
  7.9 1.1 shard_map.112
  9.0 3.0 %collective-permute-start.1 = (bf16[144,768]{1,0:T(8,128)(2,1)S(1)}, bf16[144,768]{1,0:T(8,128)(2,1)S(1)}, u32[]{:S(2)}, u32[]{:S(2)}) collective-permute-start(bf16[144,768]{1,0:T(8,128)(2,1)S(1)} %get-tuple-element.33.refs_3_), channel_id=1, source_target_pairs={{0,2},{1,3},{2,0},{3,1},{4,6},{5,7},{6,4},{7,5},{8,10},{9,11},{10,... | collective-permute-start | bytes 663560 | tf_op jit(solution)/shard_map/ppermute | solution.py:354
  12.0 5.4 %collective-permute-done.1.refs_5_ = bf16[144,768]{1,0:T(8,128)(2,1)S(1)} collective-permute-done((bf16[144,768]{1,0:T(8,128)(2,1)S(1)}, bf16[144,768]{1,0:T(8,128)(2,1)S(1)}, u32[]{:S(2)}, u32[]{:S(2)}) %collective-permute-start.1) | collective-permute-done | bytes 221216 | tf_op jit(solution)/shard_map/ppermute | solution.py:354
  17.4 1.7 collective-permute-start.4
  19.1 0.7 convert_bitcast_fusion
  19.8 0.8 collective-permute-done.2.refs_6_
  20.7 0.7 copy-done.7
  21.4 3.2 %shard_map.113 = (bf16[128,1920]{1,0:T(8,128)(2,1)S(1)}, bf16[128,1920]{1,0:T(8,128)(2,1)S(1)}, f32[128,128]{1,0:T(8,128)S(1)}, f32[128,512]{1,0:T(8,128)S(1)}) custom-call(bf16[128,5120]{1,0:T(8,128)(2,1)} %refs_0_.3, bf16[128,5120]{1,0:T(8,128)(2,1)} %refs_1_.5, f32[1,5120]{1,0:T(1,128)S(1)} %bitcast.6, bf16[144,768]{1,0:T(8,128)(2,1)S(1)} %get-tuple-element.33.refs_3_, ...), custom_call_target="tpu_custom_call" | custom-call | flops 503316480 | bytes 2752512 | tf_op jit(solution)/shard_map/pallas_call | solution.py:169
  24.6 0.8 copy-done.3
  25.4 1.6 collective-permute-start.7
  27.0 1.5 collective-permute-start.6
  28.5 0.5 collective-permute-start.5
  29.0 1.1 collective-permute-done.3.refs_4_
  30.1 0.5 collective-permute-done.5.refs_6_
  30.6 4.7 %shard_map.114 = (bf16[128,3200]{1,0:T(8,128)(2,1)S(1)}, bf16[128,3328]{1,0:T(8,128)(2,1)S(1)}) custom-call(bf16[128,5120]{1,0:T(8,128)(2,1)} %refs_0_.3, bf16[128,5120]{1,0:T(8,128)(2,1)} %refs_1_.5, f32[1,5120]{1,0:T(1,128)S(1)} %bitcast.7, bf16[128,1280]{1,0:T(8,128)(2,1)S(1)} %get-tuple-element.36.refs_3_, ...), custom_call_target="tpu_custom_call" | custom-call | flops 838860800 | bytes 4587520 | tf_op jit(solution)/shard_map/pallas_call | solution.py:169
  35.4 0.9 copy-done.1
  36.2 3.3 %collective-permute-done.7.refs_4_ = bf16[128,1920]{1,0:T(8,128)(2,1)S(1)} collective-permute-done((bf16[128,1920]{1,0:T(8,128)(2,1)S(1)}, bf16[128,1920]{1,0:T(8,128)(2,1)S(1)}, u32[]{:S(2)}, u32[]{:S(2)}) %collective-permute-start.7) | collective-permute-done | bytes 491552 | tf_op jit(solution)/shard_map/ppermute | solution.py:361
  39.6 0.4 collective-permute-done.6.refs_2_
  40.0 0.8 copy-done.16
  40.7 2.6 %collective-permute-start.9 = (bf16[128,3328]{1,0:T(8,128)(2,1)S(1)}, bf16[128,3328]{1,0:T(8,128)(2,1)S(1)}, u32[]{:S(2)}, u32[]{:S(2)}) collective-permute-start(bf16[128,3328]{1,0:T(8,128)(2,1)S(1)} %get-tuple-element.43.refs_1_), channel_id=1, source_target_pairs={{0,8},{4,12},{8,24},{12,28},{16,0},{20,4},{24,16},{28,20},{1,9},{5... | collective-permute-start | bytes 2555912 | tf_op jit(solution)/shard_map/ppermute | solution.py:361
  43.3 1.5 collective-permute-start.8
  45.0 16.5 %collective-permute-done.9.refs_5_ = bf16[128,3328]{1,0:T(8,128)(2,1)S(1)} collective-permute-done((bf16[128,3328]{1,0:T(8,128)(2,1)S(1)}, bf16[128,3328]{1,0:T(8,128)(2,1)S(1)}, u32[]{:S(2)}, u32[]{:S(2)}) %collective-permute-start.9) | collective-permute-done | bytes 852000 | tf_op jit(solution)/shard_map/ppermute | solution.py:361
  61.6 1.3 collective-permute-done.8.refs_3_
  62.9 0.9 copy-done.10
  63.8 1.7 collective-permute-start.15
  65.5 1.5 collective-permute-start.13
  67.0 1.2 collective-permute-start.14
  68.2 0.5 collective-permute-start.12
  68.7 1.2 copy-done.11
  69.8 1.0 copy-done.13
  70.9 1.0 copy-done.15
  71.9 1.0 copy-done.17
  72.9 12.3 %shard_map.115 = (bf16[128,1024]{1,0:T(8,128)(2,1)S(1)}, bf16[128,1024]{1,0:T(8,128)(2,1)S(1)}, bf16[128,1024]{1,0:T(8,128)(2,1)S(1)}) custom-call(bf16[128,1920]{1,0:T(8,128)(2,1)S(1)} %copy-done.15, bf16[128,3328]{1,0:T(8,128)(2,1)S(1)} %get-tuple-element.43.refs_1_, bf16[128,1920]{1,0:T(8,128)(2,1)S(1)} %copy-done.17, bf16[128,3328]{1,0:T(8,128)(2,1)S(1)} %copy-done.11, ...), custom_call_target="tpu_custom_call" | custom-call | flops 8053063680 | bytes 25690112 | tf_op jit(solution)/shard_map/pallas_call | solution.py:223
  85.3 1.6 collective-permute-start.10
  86.8 1.7 collective-permute-start.11
  88.6 0.3 collective-permute-start.20
  88.9 13.9 %collective-permute-done.14.refs_2_ = bf16[128,1920]{1,0:T(8,128)(2,1)S(1)} collective-permute-done((bf16[128,1920]{1,0:T(8,128)(2,1)}, bf16[128,1920]{1,0:T(8,128)(2,1)S(1)}, u32[]{:S(2)}, u32[]{:S(2)}) %collective-permute-start.14) | collective-permute-done | bytes 491552 | tf_op jit(solution)/shard_map/ppermute | solution.py:361
  102.8 1.5 collective-permute-start.18
  104.3 1.2 pad_maximum_fusion
  105.5 0.2 broadcast_in_dim.25
  105.8 0.6 collective-permute-start.17
  106.4 14.6 %collective-permute-done.20.refs_3_ = bf16[128,3328]{1,0:T(8,128)(2,1)S(1)} collective-permute-done((bf16[128,3328]{1,0:T(8,128)(2,1)S(1)}, bf16[128,3328]{1,0:T(8,128)(2,1)S(1)}, u32[]{:S(2)}, u32[]{:S(2)}) %collective-permute-start.20) | collective-permute-done | bytes 852000 | tf_op jit(solution)/shard_map/ppermute | solution.py:361
  121.0 3.6 %collective-permute-done.18.refs_1_ = bf16[128,3328]{1,0:T(8,128)(2,1)S(1)} collective-permute-done((bf16[128,3328]{1,0:T(8,128)(2,1)S(1)}, bf16[128,3328]{1,0:T(8,128)(2,1)S(1)}, u32[]{:S(2)}, u32[]{:S(2)}) %collective-permute-start.18) | collective-permute-done | bytes 852000 | tf_op jit(solution)/shard_map/ppermute | solution.py:361
  124.6 1.5 collective-permute-start.25
  126.2 10.9 %shard_map.116 = (bf16[128,1024]{1,0:T(8,128)(2,1)S(1)}, bf16[128,1024]{1,0:T(8,128)(2,1)}) custom-call(bf16[128,1920]{1,0:T(8,128)(2,1)S(1)} %collective-permute-done.12.refs_0_, bf16[128,3328]{1,0:T(8,128)(2,1)S(1)} %collective-permute-done.13.refs_1_, bf16[128,1920]{1,0:T(8,128)(2,1)S(1)} %collective-permute-done.14.refs_2_, ...), custom_call_target="tpu_custom_call" | custom-call | flops 5368709120 | bytes 24117248 | tf_op jit(solution)/shard_map/pallas_call | solution.py:223
  137.1 0.7 copy-done.18
  137.8 2.0 %collective-permute-start.16 = (bf16[128,1024]{1,0:T(8,128)(2,1)}, bf16[128,1024]{1,0:T(8,128)(2,1)}, u32[]{:S(2)}, u32[]{:S(2)}) collective-permute-start(bf16[128,1024]{1,0:T(8,128)(2,1)} %get-tuple-element.49), channel_id=1, source_target_pairs={{0,24},{4,28},{8,16},{12,20},{16,8},{20,12},{24,0},{28,4},{1,25},{... | collective-permute-start | bytes 786440 | tf_op jit(solution)/shard_map/ppermute | solution.py:361
  139.9 0.8 copy-done.5
  140.7 0.5 collective-permute-start.24
  141.2 1.6 copy-done
  142.8 2.7 %shard_map.117 = bf16[16,16,2048]{2,1,0:T(8,128)(2,1)} custom-call(s32[16]{0:T(128)S(1)} %broadcast_add_fusion.page_ref, bf16[512,2048]{1,0:T(8,128)(2,1)S(1)} %copy-done, bf16[16,16,2048]{2,1,0:T(8,128)(2,1)} %cache_ref.1), custom_call_target="tpu_custom_call" | custom-call | bytes 4194304 | tf_op jit(solution)/shard_map/pallas_call | solution.py:308
  145.5 10.4 %shard_map.118 = (bf16[128,1024]{1,0:T(8,128)(2,1)S(1)}, bf16[128,1024]{1,0:T(8,128)(2,1)S(1)}) custom-call(bf16[128,1920]{1,0:T(8,128)(2,1)S(1)} %copy-done.6, bf16[128,3328]{1,0:T(8,128)(2,1)S(1)} %collective-permute-done.18.refs_1_, bf16[128,1920]{1,0:T(8,128)(2,1)} %collective-permute-done.19.refs_2_, ...), custom_call_target="tpu_custom_call" | custom-call | flops 5368709120 | bytes 24117248 | tf_op jit(solution)/shard_map/pallas_call | solution.py:223
  156.0 1.7 constant_dynamic-update-slice_fusion.4
  157.7 3.0 %collective-permute-start.23 = (bf16[128,1024]{1,0:T(8,128)(2,1)S(1)}, bf16[128,1024]{1,0:T(8,128)(2,1)S(1)}, u32[]{:S(2)}, u32[]{:S(2)}) collective-permute-start(bf16[128,1024]{1,0:T(8,128)(2,1)S(1)} %get-tuple-element.55), channel_id=1, source_target_pairs={{0,8},{4,12},{8,24},{12,28},{16,0},{20,4},{24,16},{28,20},{1,9},{5... | collective-permute-start | bytes 786440 | tf_op jit(solution)/shard_map/ppermute | solution.py:361
  160.6 1.7 collective-permute-start.22
  162.3 6.8 %shard_map.119 = (f32[128,1024]{1,0:T(8,128)S(1)}, f32[128,1024]{1,0:T(8,128)S(1)}, f32[128,128]{1,0:T(8,128)S(1)}) custom-call(bf16[128,3328]{1,0:T(8,128)(2,1)} %collective-permute-done.25.refs_0_, bf16[5120,1024]{1,0:T(8,128)(2,1)} %refs_1_.7, bf16[5120,1024]{1,0:T(8,128)(2,1)} %refs_2_.3), custom_call_target="tpu_custom_call" | custom-call | flops 1677721600 | bytes 14974976 | tf_op jit(solution)/shard_map/pallas_call | solution.py:278
  169.1 4.9 %shard_map.120 = bf16[128,1024]{1,0:T(8,128)(2,1)S(1)} custom-call(bf16[128,1920]{1,0:T(8,128)(2,1)S(1)} %collective-permute-done.24.refs_0_, bf16[5120,1024]{1,0:T(8,128)(2,1)} %refs_1_.7, bf16[5120,1024]{1,0:T(8,128)(2,1)} %refs_2_.3, f32[128,1024]{1,0:T(8,128)S(1)} %get-tuple-element.60.refs_3_, f32[128,1024]{1,0:T(8,128)S(1)} %get-tuple-element.61.refs_4_, ...), custom_call_target="tpu_custom_call" | custom-call | flops 1006632960 | bytes 9404416 | tf_op jit(solution)/shard_map/pallas_call | solution.py:278
  174.0 0.2 collective-permute-start.26
  174.2 0.7 constant_dynamic-update-slice_fusion.3
  174.9 0.7 constant_dynamic-update-slice_fusion.2
  175.6 0.7 constant_dynamic-update-slice_fusion.1
  176.3 5.9 %collective-permute-done.26 = bf16[128,1024]{1,0:T(8,128)(2,1)S(1)} collective-permute-done((bf16[128,1024]{1,0:T(8,128)(2,1)S(1)}, bf16[128,1024]{1,0:T(8,128)(2,1)S(1)}, u32[]{:S(2)}, u32[]{:S(2)}) %collective-permute-start.26) | collective-permute-done | bytes 262176 | tf_op jit(solution)/shard_map/ppermute | solution.py:361
  182.2 0.7 constant_dynamic-update-slice_fusion
  (62 shorter events, 0.5 us)
Async XLA Ops:
  7.2 23.4 %copy-start.8 = (f32[5120]{0:T(1024)S(1)}, f32[5120]{0:T(1024)}, u32[]{:S(2)}) copy-start(f32[5120]{0:T(1024)} %param.13) | copy-start | bytes 61444
  7.2 134.0 %all-gather.2.cloned.1.call-start = ((), (), s32[]{:S(2)}) async-start(), calls=%async_computation | async-start | bytes 2621440 | tf_op jit(solution)/shard_map/all_gather | solution.py:395
  7.2 0.7 copy-start.9
  9.0 8.4 %collective-permute-start.1 = (bf16[144,768]{1,0:T(8,128)(2,1)S(1)}, bf16[144,768]{1,0:T(8,128)(2,1)S(1)}, u32[]{:S(2)}, u32[]{:S(2)}) collective-permute-start(bf16[144,768]{1,0:T(8,128)(2,1)S(1)} %get-tuple-element.33.refs_3_), channel_id=1, source_target_pairs={{0,2},{1,3},{2,0},{3,1},{4,6},{5,7},{6,4},{7,5},{8,10},{9,11},{10,... | collective-permute-start | bytes 663560 | tf_op jit(solution)/shard_map/ppermute | solution.py:354
  12.0 7.8 %collective-permute-start = (bf16[144,768]{1,0:T(8,128)(2,1)S(1)}, bf16[144,768]{1,0:T(8,128)(2,1)S(1)}, u32[]{:S(2)}, u32[]{:S(2)}) collective-permute-start(bf16[144,768]{1,0:T(8,128)(2,1)S(1)} %get-tuple-element.33.refs_3_), channel_id=1, source_target_pairs={{0,1},{1,0},{2,3},{3,2},{4,5},{5,4},{6,7},{7,6},{8,9},{9,8},{10,11... | collective-permute-start | bytes 663560 | tf_op jit(solution)/shard_map/ppermute | solution.py:354
  17.4 11.1 %collective-permute-start.4 = (bf16[128,1280]{1,0:T(8,128)(2,1)S(1)}, bf16[128,1280]{1,0:T(8,128)(2,1)S(1)}, u32[]{:S(2)}, u32[]{:S(2)}) collective-permute-start(bf16[128,1280]{1,0:T(8,128)(2,1)S(1)} %get-tuple-element.36.refs_3_), channel_id=1, source_target_pairs={{0,2},{1,3},{2,0},{3,1},{4,6},{5,7},{6,4},{7,5},{8,10},{9,11},{10,... | collective-permute-start | bytes 983048 | tf_op jit(solution)/shard_map/ppermute | solution.py:354
  19.1 1.5 collective-permute-start.2
  20.7 0.7 copy-start.7
  24.6 0.8 copy-start.3
  25.4 9.9 %copy-start.14 = (bf16[128,1920]{1,0:T(8,128)(2,1)}, bf16[128,1920]{1,0:T(8,128)(2,1)S(1)}, u32[]{:S(2)}) copy-start(bf16[128,1920]{1,0:T(8,128)(2,1)S(1)} %get-tuple-element.37.refs_0_) | copy-start | bytes 1474564
  25.4 14.2 %collective-permute-start.7 = (bf16[128,1920]{1,0:T(8,128)(2,1)S(1)}, bf16[128,1920]{1,0:T(8,128)(2,1)S(1)}, u32[]{:S(2)}, u32[]{:S(2)}) collective-permute-start(bf16[128,1920]{1,0:T(8,128)(2,1)S(1)} %get-tuple-element.37.refs_0_), channel_id=1, source_target_pairs={{0,8},{4,12},{8,24},{12,28},{16,0},{20,4},{24,16},{28,20},{1,9},{5... | collective-permute-start | bytes 1474568 | tf_op jit(solution)/shard_map/ppermute | solution.py:361
  27.0 13.0 %collective-permute-start.6 = (bf16[128,1920]{1,0:T(8,128)(2,1)S(1)}, bf16[128,1920]{1,0:T(8,128)(2,1)S(1)}, u32[]{:S(2)}, u32[]{:S(2)}) collective-permute-start(bf16[128,1920]{1,0:T(8,128)(2,1)S(1)} %get-tuple-element.37.refs_0_), channel_id=1, source_target_pairs={{0,4},{4,0},{8,12},{12,8},{16,20},{20,16},{24,28},{28,24},{1,5},{5... | collective-permute-start | bytes 1474568 | tf_op jit(solution)/shard_map/ppermute | solution.py:361
  28.5 1.6 collective-permute-start.3
  28.5 2.1 %collective-permute-start.5 = (bf16[128,1280]{1,0:T(8,128)(2,1)S(1)}, bf16[128,1280]{1,0:T(8,128)(2,1)S(1)}, u32[]{:S(2)}, u32[]{:S(2)}) collective-permute-start(bf16[128,1280]{1,0:T(8,128)(2,1)S(1)} %collective-permute-done.4.refs_5_), channel_id=1, source_target_pairs={{0,1},{1,0},{2,3},{3,2},{4,5},{5,4},{6,7},{7,6},{8,9},{9,8},{10,11... | collective-permute-start | bytes 983048 | tf_op jit(solution)/shard_map/ppermute | solution.py:354
  30.6 14.3 %copy-start.21 = (s32[1,64]{1,0:T(1,128)S(1)}, s32[1,64]{1,0:T(1,128)}, u32[]{:S(2)}) copy-start(s32[1,64]{1,0:T(1,128)} %param.17) | copy-start | bytes 772
  35.3 0.9 copy-start.1
  39.6 1.2 copy-start.12
  40.0 0.8 copy-start.16
  40.7 20.8 %collective-permute-start.9 = (bf16[128,3328]{1,0:T(8,128)(2,1)S(1)}, bf16[128,3328]{1,0:T(8,128)(2,1)S(1)}, u32[]{:S(2)}, u32[]{:S(2)}) collective-permute-start(bf16[128,3328]{1,0:T(8,128)(2,1)S(1)} %get-tuple-element.43.refs_1_), channel_id=1, source_target_pairs={{0,8},{4,12},{8,24},{12,28},{16,0},{20,4},{24,16},{28,20},{1,9},{5... | collective-permute-start | bytes 2555912 | tf_op jit(solution)/shard_map/ppermute | solution.py:361
  43.3 19.6 %collective-permute-start.8 = (bf16[128,3328]{1,0:T(8,128)(2,1)S(1)}, bf16[128,3328]{1,0:T(8,128)(2,1)S(1)}, u32[]{:S(2)}, u32[]{:S(2)}) collective-permute-start(bf16[128,3328]{1,0:T(8,128)(2,1)S(1)} %get-tuple-element.43.refs_1_), channel_id=1, source_target_pairs={{0,4},{4,0},{8,12},{12,8},{16,20},{20,16},{24,28},{28,24},{1,5},{5... | collective-permute-start | bytes 2555912 | tf_op jit(solution)/shard_map/ppermute | solution.py:361
  62.9 0.9 copy-start.10
  63.8 23.1 %collective-permute-start.15 = (bf16[128,3328]{1,0:T(8,128)(2,1)S(1)}, bf16[128,3328]{1,0:T(8,128)(2,1)S(1)}, u32[]{:S(2)}, u32[]{:S(2)}) collective-permute-start(bf16[128,3328]{1,0:T(8,128)(2,1)S(1)} %collective-permute-done.9.refs_5_), channel_id=1, source_target_pairs={{0,8},{4,12},{8,24},{12,28},{16,0},{20,4},{24,16},{28,20},{1,9},{5... | collective-permute-start | bytes 2555912 | tf_op jit(solution)/shard_map/ppermute | solution.py:361
  65.5 23.1 %collective-permute-start.13 = (bf16[128,3328]{1,0:T(8,128)(2,1)S(1)}, bf16[128,3328]{1,0:T(8,128)(2,1)S(1)}, u32[]{:S(2)}, u32[]{:S(2)}) collective-permute-start(bf16[128,3328]{1,0:T(8,128)(2,1)S(1)} %collective-permute-done.9.refs_5_), channel_id=1, source_target_pairs={{0,4},{4,0},{8,12},{12,8},{16,20},{20,16},{24,28},{28,24},{1,5},{5... | collective-permute-start | bytes 2555912 | tf_op jit(solution)/shard_map/ppermute | solution.py:361
  67.0 37.3 %copy-start.2 = (bf16[128,3200]{1,0:T(8,128)(2,1)S(1)}, bf16[128,3200]{1,0:T(8,128)(2,1)}, u32[]{:S(2)}) copy-start(bf16[128,3200]{1,0:T(8,128)(2,1)} %copy-done.1) | copy-start | bytes 2457604
  67.0 37.3 %copy-start.4 = (bf16[128,1920]{1,0:T(8,128)(2,1)S(1)}, bf16[128,1920]{1,0:T(8,128)(2,1)}, u32[]{:S(2)}) copy-start(bf16[128,1920]{1,0:T(8,128)(2,1)} %copy-done.3) | copy-start | bytes 1474564
  67.0 35.8 %collective-permute-start.14 = (bf16[128,1920]{1,0:T(8,128)(2,1)}, bf16[128,1920]{1,0:T(8,128)(2,1)S(1)}, u32[]{:S(2)}, u32[]{:S(2)}) collective-permute-start(bf16[128,1920]{1,0:T(8,128)(2,1)} %copy-done.12), channel_id=1, source_target_pairs={{0,8},{4,12},{8,24},{12,28},{16,0},{20,4},{24,16},{28,20},{1,9},{5... | collective-permute-start | bytes 1474568 | tf_op jit(solution)/shard_map/ppermute | solution.py:361
  68.2 37.3 %collective-permute-start.12 = (bf16[128,1920]{1,0:T(8,128)(2,1)}, bf16[128,1920]{1,0:T(8,128)(2,1)S(1)}, u32[]{:S(2)}, u32[]{:S(2)}) collective-permute-start(bf16[128,1920]{1,0:T(8,128)(2,1)} %copy-done.12), channel_id=1, source_target_pairs={{0,4},{4,0},{8,12},{12,8},{16,20},{20,16},{24,28},{28,24},{1,5},{5... | collective-permute-start | bytes 1474568 | tf_op jit(solution)/shard_map/ppermute | solution.py:361
  68.7 1.2 copy-start.11
  69.8 1.0 copy-start.13
  70.9 1.0 copy-start.15
  71.9 1.0 copy-start.17
  85.3 20.5 %collective-permute-start.10 = (bf16[128,1024]{1,0:T(8,128)(2,1)S(1)}, bf16[128,1024]{1,0:T(8,128)(2,1)S(1)}, u32[]{:S(2)}, u32[]{:S(2)}) collective-permute-start(bf16[128,1024]{1,0:T(8,128)(2,1)S(1)} %get-tuple-element.45), channel_id=1, source_target_pairs={{0,4},{4,0},{8,12},{12,8},{16,20},{20,16},{24,28},{28,24},{1,5},{5... | collective-permute-start | bytes 786440 | tf_op jit(solution)/shard_map/ppermute | solution.py:361
  86.8 19.5 %collective-permute-start.11 = (bf16[128,1024]{1,0:T(8,128)(2,1)S(1)}, bf16[128,1024]{1,0:T(8,128)(2,1)S(1)}, u32[]{:S(2)}, u32[]{:S(2)}) collective-permute-start(bf16[128,1024]{1,0:T(8,128)(2,1)S(1)} %get-tuple-element.46), channel_id=1, source_target_pairs={{0,16},{4,20},{8,0},{12,4},{16,24},{20,28},{24,8},{28,12},{1,17},{... | collective-permute-start | bytes 786440 | tf_op jit(solution)/shard_map/ppermute | solution.py:361
  88.6 32.4 %collective-permute-start.20 = (bf16[128,3328]{1,0:T(8,128)(2,1)S(1)}, bf16[128,3328]{1,0:T(8,128)(2,1)S(1)}, u32[]{:S(2)}, u32[]{:S(2)}) collective-permute-start(bf16[128,3328]{1,0:T(8,128)(2,1)S(1)} %collective-permute-done.15.refs_3_), channel_id=1, source_target_pairs={{0,8},{4,12},{8,24},{12,28},{16,0},{20,4},{24,16},{28,20},{1,9},{5... | collective-permute-start | bytes 2555912 | tf_op jit(solution)/shard_map/ppermute | solution.py:361
  102.8 21.9 %collective-permute-start.18 = (bf16[128,3328]{1,0:T(8,128)(2,1)S(1)}, bf16[128,3328]{1,0:T(8,128)(2,1)S(1)}, u32[]{:S(2)}, u32[]{:S(2)}) collective-permute-start(bf16[128,3328]{1,0:T(8,128)(2,1)S(1)} %collective-permute-done.15.refs_3_), channel_id=1, source_target_pairs={{0,4},{4,0},{8,12},{12,8},{16,20},{20,16},{24,28},{28,24},{1,5},{5... | collective-permute-start | bytes 2555912 | tf_op jit(solution)/shard_map/ppermute | solution.py:361
  105.5 34.4 %collective-permute-start.19 = (bf16[128,1920]{1,0:T(8,128)(2,1)S(1)}, bf16[128,1920]{1,0:T(8,128)(2,1)}, u32[]{:S(2)}, u32[]{:S(2)}) collective-permute-start(bf16[128,1920]{1,0:T(8,128)(2,1)S(1)} %collective-permute-done.14.refs_2_), channel_id=1, source_target_pairs={{0,8},{4,12},{8,24},{12,28},{16,0},{20,4},{24,16},{28,20},{1,9},{5... | collective-permute-start | bytes 1474568 | tf_op jit(solution)/shard_map/ppermute | solution.py:361
  105.8 34.1 %collective-permute-start.17 = (bf16[128,1920]{1,0:T(8,128)(2,1)S(1)}, bf16[128,1920]{1,0:T(8,128)(2,1)S(1)}, u32[]{:S(2)}, u32[]{:S(2)}) collective-permute-start(bf16[128,1920]{1,0:T(8,128)(2,1)S(1)} %collective-permute-done.14.refs_2_), channel_id=1, source_target_pairs={{0,4},{4,0},{8,12},{12,8},{16,20},{20,16},{24,28},{28,24},{1,5},{5... | collective-permute-start | bytes 1474568 | tf_op jit(solution)/shard_map/ppermute | solution.py:361
  106.4 18.3 %copy-start.20 = (bf16[128,8192]{1,0:T(8,128)(2,1)}, bf16[128,8192]{1,0:T(8,128)(2,1)S(1)}, u32[]{:S(2)}) copy-start(bf16[128,8192]{1,0:T(8,128)(2,1)S(1)} %constant_dynamic-update-slice_fusion.5) | copy-start | bytes 6291460
  124.6 37.7 %collective-permute-start.25 = (bf16[128,3328]{1,0:T(8,128)(2,1)S(1)}, bf16[128,3328]{1,0:T(8,128)(2,1)}, u32[]{:S(2)}, u32[]{:S(2)}) collective-permute-start(bf16[128,3328]{1,0:T(8,128)(2,1)S(1)} %collective-permute-done.20.refs_3_), channel_id=1, source_target_pairs={{0,4},{4,0},{8,12},{12,8},{16,20},{20,16},{24,28},{28,24},{1,5},{5... | collective-permute-start | bytes 2555912 | tf_op jit(solution)/shard_map/ppermute | solution.py:361
  137.1 0.7 copy-start.18
  137.8 18.1 %collective-permute-start.16 = (bf16[128,1024]{1,0:T(8,128)(2,1)}, bf16[128,1024]{1,0:T(8,128)(2,1)}, u32[]{:S(2)}, u32[]{:S(2)}) collective-permute-start(bf16[128,1024]{1,0:T(8,128)(2,1)} %get-tuple-element.49), channel_id=1, source_target_pairs={{0,24},{4,28},{8,16},{12,20},{16,8},{20,12},{24,0},{28,4},{1,25},{... | collective-permute-start | bytes 786440 | tf_op jit(solution)/shard_map/ppermute | solution.py:361
  139.9 0.8 copy-start.5
  140.7 28.4 %collective-permute-start.24 = (bf16[128,1920]{1,0:T(8,128)(2,1)}, bf16[128,1920]{1,0:T(8,128)(2,1)S(1)}, u32[]{:S(2)}, u32[]{:S(2)}) collective-permute-start(bf16[128,1920]{1,0:T(8,128)(2,1)} %collective-permute-done.19.refs_2_), channel_id=1, source_target_pairs={{0,4},{4,0},{8,12},{12,8},{16,20},{20,16},{24,28},{28,24},{1,5},{5... | collective-permute-start | bytes 1474568 | tf_op jit(solution)/shard_map/ppermute | solution.py:361
  141.2 1.6 copy-start
  142.8 2.7 %copy-start.6 = (bf16[128,1920]{1,0:T(8,128)(2,1)S(1)}, bf16[128,1920]{1,0:T(8,128)(2,1)}, u32[]{:S(2)}) copy-start(bf16[128,1920]{1,0:T(8,128)(2,1)} %copy-done.5) | copy-start | bytes 1474564
  145.5 10.4 %copy-start.19 = (bf16[128,1024]{1,0:T(8,128)(2,1)S(1)}, bf16[128,1024]{1,0:T(8,128)(2,1)}, u32[]{:S(2)}) copy-start(bf16[128,1024]{1,0:T(8,128)(2,1)} %copy-done.18) | copy-start | bytes 786436
  155.9 18.3 %collective-permute-start.21 = (bf16[128,1024]{1,0:T(8,128)(2,1)S(1)}, bf16[128,1024]{1,0:T(8,128)(2,1)S(1)}, u32[]{:S(2)}, u32[]{:S(2)}) collective-permute-start(bf16[128,1024]{1,0:T(8,128)(2,1)S(1)} %copy-done.19), channel_id=1, source_target_pairs={{0,20},{4,16},{8,4},{12,0},{16,28},{20,24},{24,12},{28,8},{1,21},{... | collective-permute-start | bytes 786440 | tf_op jit(solution)/shard_map/ppermute | solution.py:361
  157.7 17.9 %collective-permute-start.23 = (bf16[128,1024]{1,0:T(8,128)(2,1)S(1)}, bf16[128,1024]{1,0:T(8,128)(2,1)S(1)}, u32[]{:S(2)}, u32[]{:S(2)}) collective-permute-start(bf16[128,1024]{1,0:T(8,128)(2,1)S(1)} %get-tuple-element.55), channel_id=1, source_target_pairs={{0,8},{4,12},{8,24},{12,28},{16,0},{20,4},{24,16},{28,20},{1,9},{5... | collective-permute-start | bytes 786440 | tf_op jit(solution)/shard_map/ppermute | solution.py:361
  160.6 14.3 %collective-permute-start.22 = (bf16[128,1024]{1,0:T(8,128)(2,1)S(1)}, bf16[128,1024]{1,0:T(8,128)(2,1)S(1)}, u32[]{:S(2)}, u32[]{:S(2)}) collective-permute-start(bf16[128,1024]{1,0:T(8,128)(2,1)S(1)} %get-tuple-element.57), channel_id=1, source_target_pairs={{0,28},{4,24},{8,20},{12,16},{16,12},{20,8},{24,4},{28,0},{1,29},{... | collective-permute-start | bytes 786440 | tf_op jit(solution)/shard_map/ppermute | solution.py:361
  174.0 8.2 %collective-permute-start.26 = (bf16[128,1024]{1,0:T(8,128)(2,1)S(1)}, bf16[128,1024]{1,0:T(8,128)(2,1)S(1)}, u32[]{:S(2)}, u32[]{:S(2)}) collective-permute-start(bf16[128,1024]{1,0:T(8,128)(2,1)S(1)} %shard_map.120), channel_id=1, source_target_pairs={{0,12},{4,8},{8,28},{12,24},{16,4},{20,0},{24,20},{28,16},{1,13},{... | collective-permute-start | bytes 786440 | tf_op jit(solution)/shard_map/ppermute | solution.py:361
Sparse Core Ops, SparseCore 0:
  45.0 19.6 all-gather.1

commit v9 on v8

--- a/solution.py
+++ b/solution.py
@@ -416,7 +416,7 @@
             ready = arrived[-1][c]
             number = len(sent)
             behind = sent[0] if number == 1 else sent[number - 2][:1] if number > 1 else []
-            if c == 0 and step > 1:
+            if step > 2 or (c == 0 and step > 1):
                 behind = [*behind, products[step - 2]]
             if behind:
                 ready = after(ready, *behind)
@@ -430,7 +430,7 @@
         waiting.append((other, step, True))
         if following:
             waiting.append((following, step + 1, False))
-        if step == line_count - 2:
+        if step == 1:
             waiting[-1] = ([*following[:-1], after(following[-1], written)], step + 1, False)
         if step + 1 < line_count:
             blocks = gated([shard for shard, _, _ in waiting], gate_weight, up_weight)

time: 190 us -> 192 us (1.011)
  local copies, waits for them, and re-layouts: 17 us -> 13.7 us
  starting transfers between devices: 32.1 us -> 35 us
    unnamed x44 -> x24, local copies, waits for them, and re-layouts: 12.1 us -> 5.4 us
    ppermute x21, starting transfers between devices: 26.8 us -> 29.7 us  [send(): return lax.ppermute(array, 'grp', pairs)]
    dynamic_update_slice x8, local copies, waits for them, and re-layouts: 4.63 us -> 6.71 us  [put(): return lax.dynamic_update_slice_in_dim(hidden, block, source * units, 1)]
  transfers between devices with their start and end apart: 28 -> 28, of which waited for: 12 -> 13; matrix products, arithmetic and copies ran while one was open for 3% -> 5% of each run, Pallas kernels for 29% -> 30%
where the time goes in v9:
time: 192 us
  waiting for transfers between devices  69 us (36%)
  Pallas kernels  57.6 us (30%)
  starting transfers between devices  35 us (18%)
  between operations  14.3 us (7%)
  local copies, waits for them, and re-layouts  13.7 us (7%)
  other arithmetic  1.99 us (1%)
    ppermute x21, waiting for transfers between devices, send(): return lax.ppermute(array, 'grp', pairs)  61.5 us
    pallas_call x3, Pallas kernels, gated(): pl.pallas_call(functools.partial(gated_kernel, count, len(shards[0])), gr...  34.7 us
    ppermute x21, starting transfers between devices, send(): return lax.ppermute(array, 'grp', pairs)  29.7 us
    pallas_call x2, Pallas kernels, gated_part(): pl.pallas_call(functools.partial(part_kernel, width, bool(so_far)), grid=...  11.3 us
    pallas_call x2, Pallas kernels, attend(): pl.pallas_call(functools.partial(attend_kernel, chunk, shard_count, width...  7.86 us
    ppermute x6, waiting for transfers between devices, swap(): return lax.ppermute(array, 'tok', [(t, t ^ mask) for t in range(tok_count)])  7.42 us
    dynamic_update_slice x8, local copies, waits for them, and re-layouts, put(): return lax.dynamic_update_slice_in_dim(hidden, block, source * units, 1)  6.71 us
    unnamed x24, local copies, waits for them, and re-layouts  5.4 us
  transfers between devices with their start and end apart: 28, of which 13 were waited for; matrix products, arithmetic and copies ran while one was open for 5% of the time, Pallas kernels for 30%

profile of v9, /device:TPU:0, one launch (start us, length us, event | category | flops | bytes accessed | tf_op | source)
XLA Modules:
  0.0 191.5 jit_solution(11292223105629130956)
XLA Ops:
  7.2 0.6 copy-done.4
  7.9 1.1 shard_map.112
  9.0 3.0 %collective-permute-start.1 = (bf16[144,768]{1,0:T(8,128)(2,1)S(1)}, bf16[144,768]{1,0:T(8,128)(2,1)S(1)}, u32[]{:S(2)}, u32[]{:S(2)}) collective-permute-start(bf16[144,768]{1,0:T(8,128)(2,1)S(1)} %get-tuple-element.33.refs_3_), channel_id=1, source_target_pairs={{0,2},{1,3},{2,0},{3,1},{4,6},{5,7},{6,4},{7,5},{8,10},{9,11},{10,... | collective-permute-start | bytes 663560 | tf_op jit(solution)/shard_map/ppermute | solution.py:354
  12.0 5.4 %collective-permute-done.1.refs_5_ = bf16[144,768]{1,0:T(8,128)(2,1)S(1)} collective-permute-done((bf16[144,768]{1,0:T(8,128)(2,1)S(1)}, bf16[144,768]{1,0:T(8,128)(2,1)S(1)}, u32[]{:S(2)}, u32[]{:S(2)}) %collective-permute-start.1) | collective-permute-done | bytes 221216 | tf_op jit(solution)/shard_map/ppermute | solution.py:354
  17.4 1.7 collective-permute-start.4
  19.1 0.5 collective-permute-start.2
  19.6 0.7 convert_bitcast_fusion
  20.3 0.3 collective-permute-done.refs_4_
  20.6 0.3 collective-permute-done.2.refs_6_
  20.9 0.1 broadcast_in_dim.24.refs_8_
  21.0 0.7 copy-done.3
  21.7 3.2 %shard_map.113 = (bf16[128,1920]{1,0:T(8,128)(2,1)S(1)}, bf16[128,1920]{1,0:T(8,128)(2,1)S(1)}, f32[128,128]{1,0:T(8,128)S(1)}, f32[128,512]{1,0:T(8,128)S(1)}) custom-call(bf16[128,5120]{1,0:T(8,128)(2,1)} %refs_0_.3, bf16[128,5120]{1,0:T(8,128)(2,1)} %refs_1_.5, f32[1,5120]{1,0:T(1,128)S(1)} %bitcast.6, bf16[144,768]{1,0:T(8,128)(2,1)S(1)} %get-tuple-element.33.refs_3_, ...), custom_call_target="tpu_custom_call" | custom-call | flops 503316480 | bytes 2752512 | tf_op jit(solution)/shard_map/pallas_call | solution.py:169
  24.9 1.4 collective-permute-done.4.refs_5_
  26.3 1.5 collective-permute-start.7
  27.8 1.5 collective-permute-start.6
  29.3 4.7 %shard_map.114 = (bf16[128,3200]{1,0:T(8,128)(2,1)S(1)}, bf16[128,3328]{1,0:T(8,128)(2,1)S(1)}) custom-call(bf16[128,5120]{1,0:T(8,128)(2,1)} %refs_0_.3, bf16[128,5120]{1,0:T(8,128)(2,1)} %refs_1_.5, f32[1,5120]{1,0:T(1,128)S(1)} %bitcast.7, bf16[128,1280]{1,0:T(8,128)(2,1)S(1)} %get-tuple-element.36.refs_3_, ...), custom_call_target="tpu_custom_call" | custom-call | flops 838860800 | bytes 4587520 | tf_op jit(solution)/shard_map/pallas_call | solution.py:169
  34.1 6.9 %collective-permute-done.7.refs_4_ = bf16[128,1920]{1,0:T(8,128)(2,1)} collective-permute-done((bf16[128,1920]{1,0:T(8,128)(2,1)S(1)}, bf16[128,1920]{1,0:T(8,128)(2,1)}, u32[]{:S(2)}, u32[]{:S(2)}) %collective-permute-start.7) | collective-permute-done | bytes 491552 | tf_op jit(solution)/shard_map/ppermute | solution.py:361
  40.9 0.3 collective-permute-done.6.refs_2_
  41.3 2.6 %collective-permute-start.9 = (bf16[128,3328]{1,0:T(8,128)(2,1)S(1)}, bf16[128,3328]{1,0:T(8,128)(2,1)}, u32[]{:S(2)}, u32[]{:S(2)}) collective-permute-start(bf16[128,3328]{1,0:T(8,128)(2,1)S(1)} %get-tuple-element.43.refs_1_), channel_id=1, source_target_pairs={{0,8},{4,12},{8,24},{12,28},{16,0},{20,4},{24,16},{28,20},{1,9},{5... | collective-permute-start | bytes 2555912 | tf_op jit(solution)/shard_map/ppermute | solution.py:361
  43.8 1.5 collective-permute-start.8
  45.4 0.9 copy-done.5
  46.3 16.2 %collective-permute-done.9.refs_5_ = bf16[128,3328]{1,0:T(8,128)(2,1)} collective-permute-done((bf16[128,3328]{1,0:T(8,128)(2,1)S(1)}, bf16[128,3328]{1,0:T(8,128)(2,1)}, u32[]{:S(2)}, u32[]{:S(2)}) %collective-permute-start.9) | collective-permute-done | bytes 852000 | tf_op jit(solution)/shard_map/ppermute | solution.py:361
  62.5 1.4 collective-permute-done.8.refs_3_
  63.9 1.5 collective-permute-start.15
  65.4 1.5 collective-permute-start.13
  67.0 0.1 select_reduce_fusion
  67.2 1.2 pad_maximum_fusion
  68.4 1.2 collective-permute-start.14
  69.6 0.5 collective-permute-start.12
  70.1 16.8 %collective-permute-done.15.refs_3_ = bf16[128,3328]{1,0:T(8,128)(2,1)S(1)} collective-permute-done((bf16[128,3328]{1,0:T(8,128)(2,1)}, bf16[128,3328]{1,0:T(8,128)(2,1)S(1)}, u32[]{:S(2)}, u32[]{:S(2)}) %collective-permute-start.15) | collective-permute-done | bytes 852000 | tf_op jit(solution)/shard_map/ppermute | solution.py:361
  86.9 0.6 collective-permute-done.13.refs_1_
  87.5 1.2 collective-permute-start.20
  88.7 1.5 collective-permute-start.18
  90.2 13.8 %shard_map.115 = (bf16[128,1024]{1,0:T(8,128)(2,1)S(1)}, bf16[128,1024]{1,0:T(8,128)(2,1)S(1)}, bf16[128,1024]{1,0:T(8,128)(2,1)}) custom-call(bf16[128,1920]{1,0:T(8,128)(2,1)S(1)} %copy-done.8, bf16[128,3328]{1,0:T(8,128)(2,1)S(1)} %copy-done.6, bf16[128,1920]{1,0:T(8,128)(2,1)} %collective-permute-done.6.refs_2_, ...), custom_call_target="tpu_custom_call" | custom-call | flops 8053063680 | bytes 25690112 | tf_op jit(solution)/shard_map/pallas_call | solution.py:223
  104.0 0.7 copy-done.9
  104.8 1.7 collective-permute-start.11
  106.5 0.8 copy-done.1
  107.3 0.3 collective-permute-start.19
  107.6 0.5 collective-permute-start.17
  108.1 1.5 broadcast_in_dim.25
  109.6 0.7 constant_dynamic-update-slice_fusion.7
  110.3 1.6 copy-done
  111.9 2.7 %shard_map.116 = bf16[16,16,2048]{2,1,0:T(8,128)(2,1)} custom-call(s32[16]{0:T(128)S(1)} %broadcast_add_fusion.page_ref, bf16[512,2048]{1,0:T(8,128)(2,1)S(1)} %copy-done, bf16[16,16,2048]{2,1,0:T(8,128)(2,1)} %cache_ref.1), custom_call_target="tpu_custom_call" | custom-call | bytes 4194304 | tf_op jit(solution)/shard_map/pallas_call | solution.py:308
  114.6 6.8 %collective-permute-done.20.refs_3_ = bf16[128,3328]{1,0:T(8,128)(2,1)S(1)} collective-permute-done((bf16[128,3328]{1,0:T(8,128)(2,1)S(1)}, bf16[128,3328]{1,0:T(8,128)(2,1)S(1)}, u32[]{:S(2)}, u32[]{:S(2)}) %collective-permute-start.20) | collective-permute-done | bytes 852000 | tf_op jit(solution)/shard_map/ppermute | solution.py:361
  121.4 1.5 collective-permute-start.10
  122.9 10.4 %shard_map.117 = (bf16[128,1024]{1,0:T(8,128)(2,1)S(1)}, bf16[128,1024]{1,0:T(8,128)(2,1)S(1)}) custom-call(bf16[128,1920]{1,0:T(8,128)(2,1)S(1)} %copy-done.2, bf16[128,3328]{1,0:T(8,128)(2,1)S(1)} %collective-permute-done.13.refs_1_, bf16[128,1920]{1,0:T(8,128)(2,1)} %collective-permute-done.14.refs_2_, ...), custom_call_target="tpu_custom_call" | custom-call | flops 5368709120 | bytes 24117248 | tf_op jit(solution)/shard_map/pallas_call | solution.py:223
  133.3 0.6 collective-permute-start.25
  133.9 0.7 constant_dynamic-update-slice_fusion.6
  134.6 1.7 constant_dynamic-update-slice_fusion.5
  136.3 1.9 collective-permute-start.16
  138.1 1.5 collective-permute-start.24
  139.7 10.5 %shard_map.118 = (bf16[128,1024]{1,0:T(8,128)(2,1)S(1)}, bf16[128,1024]{1,0:T(8,128)(2,1)S(1)}) custom-call(bf16[128,1920]{1,0:T(8,128)(2,1)} %collective-permute-done.17.refs_0_, bf16[128,3328]{1,0:T(8,128)(2,1)S(1)} %collective-permute-done.18.refs_1_, bf16[128,1920]{1,0:T(8,128)(2,1)} %collective-permute-done.19.refs_2_, ...), custom_call_target="tpu_custom_call" | custom-call | flops 5368709120 | bytes 24117248 | tf_op jit(solution)/shard_map/pallas_call | solution.py:223
  150.2 2.0 %collective-permute-start.22 = (bf16[128,1024]{1,0:T(8,128)(2,1)S(1)}, bf16[128,1024]{1,0:T(8,128)(2,1)S(1)}, u32[]{:S(2)}, u32[]{:S(2)}) collective-permute-start(bf16[128,1024]{1,0:T(8,128)(2,1)S(1)} %get-tuple-element.57), channel_id=1, source_target_pairs={{0,28},{4,24},{8,20},{12,16},{16,12},{20,8},{24,4},{28,0},{1,29},{... | collective-permute-start | bytes 786440 | tf_op jit(solution)/shard_map/ppermute | solution.py:361
  152.1 3.9 %collective-permute-start.21 = (bf16[128,1024]{1,0:T(8,128)(2,1)S(1)}, bf16[128,1024]{1,0:T(8,128)(2,1)S(1)}, u32[]{:S(2)}, u32[]{:S(2)}) collective-permute-start(bf16[128,1024]{1,0:T(8,128)(2,1)S(1)} %get-tuple-element.56), channel_id=1, source_target_pairs={{0,20},{4,16},{8,4},{12,0},{16,28},{20,24},{24,12},{28,8},{1,21},{... | collective-permute-start | bytes 786440 | tf_op jit(solution)/shard_map/ppermute | solution.py:361
  156.0 0.7 constant_dynamic-update-slice_fusion.4
  156.7 7.7 %collective-permute-done.25.refs_0_ = bf16[128,3328]{1,0:T(8,128)(2,1)S(1)} collective-permute-done((bf16[128,3328]{1,0:T(8,128)(2,1)S(1)}, bf16[128,3328]{1,0:T(8,128)(2,1)S(1)}, u32[]{:S(2)}, u32[]{:S(2)}) %collective-permute-start.25) | collective-permute-done | bytes 852000 | tf_op jit(solution)/shard_map/ppermute | solution.py:361
  164.4 6.5 %shard_map.119 = (f32[128,1024]{1,0:T(8,128)S(1)}, f32[128,1024]{1,0:T(8,128)S(1)}, f32[128,128]{1,0:T(8,128)S(1)}) custom-call(bf16[128,3328]{1,0:T(8,128)(2,1)S(1)} %collective-permute-done.25.refs_0_, bf16[5120,1024]{1,0:T(8,128)(2,1)} %refs_1_.7, bf16[5120,1024]{1,0:T(8,128)(2,1)} %refs_2_.3), custom_call_target="tpu_custom_call" | custom-call | flops 1677721600 | bytes 14974976 | tf_op jit(solution)/shard_map/pallas_call | solution.py:278
  170.9 4.8 %shard_map.120 = bf16[128,1024]{1,0:T(8,128)(2,1)S(1)} custom-call(bf16[128,1920]{1,0:T(8,128)(2,1)S(1)} %collective-permute-done.24.refs_0_, bf16[5120,1024]{1,0:T(8,128)(2,1)} %refs_1_.7, bf16[5120,1024]{1,0:T(8,128)(2,1)} %refs_2_.3, f32[128,1024]{1,0:T(8,128)S(1)} %get-tuple-element.60.refs_3_, f32[128,1024]{1,0:T(8,128)S(1)} %get-tuple-element.61.refs_4_, ...), custom_call_target="tpu_custom_call" | custom-call | flops 1006632960 | bytes 9404416 | tf_op jit(solution)/shard_map/pallas_call | solution.py:278
  175.8 1.3 collective-permute-start.26
  177.0 0.7 constant_dynamic-update-slice_fusion.3
  177.8 0.7 constant_dynamic-update-slice_fusion.2
  178.5 0.7 constant_dynamic-update-slice_fusion.1
  179.2 4.8 %collective-permute-done.26 = bf16[128,1024]{1,0:T(8,128)(2,1)S(1)} collective-permute-done((bf16[128,1024]{1,0:T(8,128)(2,1)S(1)}, bf16[128,1024]{1,0:T(8,128)(2,1)S(1)}, u32[]{:S(2)}, u32[]{:S(2)}) %collective-permute-start.26) | collective-permute-done | bytes 262176 | tf_op jit(solution)/shard_map/ppermute | solution.py:361
  184.0 0.7 constant_dynamic-update-slice_fusion
  (42 shorter events, 0.2 us)
Async XLA Ops:
  7.2 103.2 %all-gather.2.cloned.1.call-start = ((), (), s32[]{:S(2)}) async-start(), calls=%async_computation | async-start | bytes 2621440 | tf_op jit(solution)/shard_map/all_gather | solution.py:395
  7.2 0.7 copy-start.4
  9.0 8.4 %collective-permute-start.1 = (bf16[144,768]{1,0:T(8,128)(2,1)S(1)}, bf16[144,768]{1,0:T(8,128)(2,1)S(1)}, u32[]{:S(2)}, u32[]{:S(2)}) collective-permute-start(bf16[144,768]{1,0:T(8,128)(2,1)S(1)} %get-tuple-element.33.refs_3_), channel_id=1, source_target_pairs={{0,2},{1,3},{2,0},{3,1},{4,6},{5,7},{6,4},{7,5},{8,10},{9,11},{10,... | collective-permute-start | bytes 663560 | tf_op jit(solution)/shard_map/ppermute | solution.py:354
  17.4 8.9 %collective-permute-start.4 = (bf16[128,1280]{1,0:T(8,128)(2,1)S(1)}, bf16[128,1280]{1,0:T(8,128)(2,1)S(1)}, u32[]{:S(2)}, u32[]{:S(2)}) collective-permute-start(bf16[128,1280]{1,0:T(8,128)(2,1)S(1)} %get-tuple-element.36.refs_3_), channel_id=1, source_target_pairs={{0,2},{1,3},{2,0},{3,1},{4,6},{5,7},{6,4},{7,5},{8,10},{9,11},{10,... | collective-permute-start | bytes 983048 | tf_op jit(solution)/shard_map/ppermute | solution.py:354
  19.1 1.5 collective-permute-start
  19.1 1.8 collective-permute-start.2
  20.3 9.0 %collective-permute-start.3 = (bf16[128,1280]{1,0:T(8,128)(2,1)S(1)}, bf16[128,1280]{1,0:T(8,128)(2,1)S(1)}, u32[]{:S(2)}, u32[]{:S(2)}) collective-permute-start(bf16[128,1280]{1,0:T(8,128)(2,1)S(1)} %get-tuple-element.36.refs_3_), channel_id=1, source_target_pairs={{0,1},{1,0},{2,3},{3,2},{4,5},{5,4},{6,7},{7,6},{8,9},{9,8},{10,11... | collective-permute-start | bytes 983048 | tf_op jit(solution)/shard_map/ppermute | solution.py:354
  21.0 0.7 copy-start.3
  24.9 9.1 %copy-start.7 = (bf16[128,1920]{1,0:T(8,128)(2,1)}, bf16[128,1920]{1,0:T(8,128)(2,1)S(1)}, u32[]{:S(2)}) copy-start(bf16[128,1920]{1,0:T(8,128)(2,1)S(1)} %get-tuple-element.37.refs_0_) | copy-start | bytes 1474564
  26.3 3.0 %collective-permute-start.5 = (bf16[128,1280]{1,0:T(8,128)(2,1)S(1)}, bf16[128,1280]{1,0:T(8,128)(2,1)S(1)}, u32[]{:S(2)}, u32[]{:S(2)}) collective-permute-start(bf16[128,1280]{1,0:T(8,128)(2,1)S(1)} %collective-permute-done.4.refs_5_), channel_id=1, source_target_pairs={{0,1},{1,0},{2,3},{3,2},{4,5},{5,4},{6,7},{7,6},{8,9},{9,8},{10,11... | collective-permute-start | bytes 983048 | tf_op jit(solution)/shard_map/ppermute | solution.py:354
  26.3 14.6 %collective-permute-start.7 = (bf16[128,1920]{1,0:T(8,128)(2,1)S(1)}, bf16[128,1920]{1,0:T(8,128)(2,1)}, u32[]{:S(2)}, u32[]{:S(2)}) collective-permute-start(bf16[128,1920]{1,0:T(8,128)(2,1)S(1)} %get-tuple-element.37.refs_0_), channel_id=1, source_target_pairs={{0,8},{4,12},{8,24},{12,28},{16,0},{20,4},{24,16},{28,20},{1,9},{5... | collective-permute-start | bytes 1474568 | tf_op jit(solution)/shard_map/ppermute | solution.py:361
  27.8 13.5 %collective-permute-start.6 = (bf16[128,1920]{1,0:T(8,128)(2,1)S(1)}, bf16[128,1920]{1,0:T(8,128)(2,1)}, u32[]{:S(2)}, u32[]{:S(2)}) collective-permute-start(bf16[128,1920]{1,0:T(8,128)(2,1)S(1)} %get-tuple-element.37.refs_0_), channel_id=1, source_target_pairs={{0,4},{4,0},{8,12},{12,8},{16,20},{20,16},{24,28},{28,24},{1,5},{5... | collective-permute-start | bytes 1474568 | tf_op jit(solution)/shard_map/ppermute | solution.py:361
  29.3 16.9 %copy-start.11 = (s32[1,64]{1,0:T(1,128)S(1)}, s32[1,64]{1,0:T(1,128)}, u32[]{:S(2)}) copy-start(s32[1,64]{1,0:T(1,128)} %param.17) | copy-start | bytes 772
  41.3 21.3 %collective-permute-start.9 = (bf16[128,3328]{1,0:T(8,128)(2,1)S(1)}, bf16[128,3328]{1,0:T(8,128)(2,1)}, u32[]{:S(2)}, u32[]{:S(2)}) collective-permute-start(bf16[128,3328]{1,0:T(8,128)(2,1)S(1)} %get-tuple-element.43.refs_1_), channel_id=1, source_target_pairs={{0,8},{4,12},{8,24},{12,28},{16,0},{20,4},{24,16},{28,20},{1,9},{5... | collective-permute-start | bytes 2555912 | tf_op jit(solution)/shard_map/ppermute | solution.py:361
  43.8 20.1 %collective-permute-start.8 = (bf16[128,3328]{1,0:T(8,128)(2,1)S(1)}, bf16[128,3328]{1,0:T(8,128)(2,1)}, u32[]{:S(2)}, u32[]{:S(2)}) collective-permute-start(bf16[128,3328]{1,0:T(8,128)(2,1)S(1)} %get-tuple-element.43.refs_1_), channel_id=1, source_target_pairs={{0,4},{4,0},{8,12},{12,8},{16,20},{20,16},{24,28},{28,24},{1,5},{5... | collective-permute-start | bytes 2555912 | tf_op jit(solution)/shard_map/ppermute | solution.py:361
  45.4 0.9 copy-start.5
  63.9 23.0 %collective-permute-start.15 = (bf16[128,3328]{1,0:T(8,128)(2,1)}, bf16[128,3328]{1,0:T(8,128)(2,1)S(1)}, u32[]{:S(2)}, u32[]{:S(2)}) collective-permute-start(bf16[128,3328]{1,0:T(8,128)(2,1)} %collective-permute-done.9.refs_5_), channel_id=1, source_target_pairs={{0,8},{4,12},{8,24},{12,28},{16,0},{20,4},{24,16},{28,20},{1,9},{5... | collective-permute-start | bytes 2555912 | tf_op jit(solution)/shard_map/ppermute | solution.py:361
  65.4 22.1 %collective-permute-start.13 = (bf16[128,3328]{1,0:T(8,128)(2,1)}, bf16[128,3328]{1,0:T(8,128)(2,1)S(1)}, u32[]{:S(2)}, u32[]{:S(2)}) collective-permute-start(bf16[128,3328]{1,0:T(8,128)(2,1)} %collective-permute-done.9.refs_5_), channel_id=1, source_target_pairs={{0,4},{4,0},{8,12},{12,8},{16,20},{20,16},{24,28},{28,24},{1,5},{5... | collective-permute-start | bytes 2555912 | tf_op jit(solution)/shard_map/ppermute | solution.py:361
  67.2 23.1 %copy-start.6 = (bf16[128,3328]{1,0:T(8,128)(2,1)S(1)}, bf16[128,3328]{1,0:T(8,128)(2,1)}, u32[]{:S(2)}) copy-start(bf16[128,3328]{1,0:T(8,128)(2,1)} %copy-done.5) | copy-start | bytes 2555908
  67.2 23.1 %copy-start.8 = (bf16[128,1920]{1,0:T(8,128)(2,1)S(1)}, bf16[128,1920]{1,0:T(8,128)(2,1)}, u32[]{:S(2)}) copy-start(bf16[128,1920]{1,0:T(8,128)(2,1)} %copy-done.7) | copy-start | bytes 1474564
  68.4 38.1 %collective-permute-start.14 = (bf16[128,1920]{1,0:T(8,128)(2,1)}, bf16[128,1920]{1,0:T(8,128)(2,1)}, u32[]{:S(2)}, u32[]{:S(2)}) collective-permute-start(bf16[128,1920]{1,0:T(8,128)(2,1)} %collective-permute-done.7.refs_4_), channel_id=1, source_target_pairs={{0,8},{4,12},{8,24},{12,28},{16,0},{20,4},{24,16},{28,20},{1,9},{5... | collective-permute-start | bytes 1474568 | tf_op jit(solution)/shard_map/ppermute | solution.py:361
  69.6 36.9 %collective-permute-start.12 = (bf16[128,1920]{1,0:T(8,128)(2,1)}, bf16[128,1920]{1,0:T(8,128)(2,1)S(1)}, u32[]{:S(2)}, u32[]{:S(2)}) collective-permute-start(bf16[128,1920]{1,0:T(8,128)(2,1)} %collective-permute-done.7.refs_4_), channel_id=1, source_target_pairs={{0,4},{4,0},{8,12},{12,8},{16,20},{20,16},{24,28},{28,24},{1,5},{5... | collective-permute-start | bytes 1474568 | tf_op jit(solution)/shard_map/ppermute | solution.py:361
  87.5 33.9 %collective-permute-start.20 = (bf16[128,3328]{1,0:T(8,128)(2,1)S(1)}, bf16[128,3328]{1,0:T(8,128)(2,1)S(1)}, u32[]{:S(2)}, u32[]{:S(2)}) collective-permute-start(bf16[128,3328]{1,0:T(8,128)(2,1)S(1)} %collective-permute-done.15.refs_3_), channel_id=1, source_target_pairs={{0,8},{4,12},{8,24},{12,28},{16,0},{20,4},{24,16},{28,20},{1,9},{5... | collective-permute-start | bytes 2555912 | tf_op jit(solution)/shard_map/ppermute | solution.py:361
  88.7 44.6 %collective-permute-start.18 = (bf16[128,3328]{1,0:T(8,128)(2,1)S(1)}, bf16[128,3328]{1,0:T(8,128)(2,1)S(1)}, u32[]{:S(2)}, u32[]{:S(2)}) collective-permute-start(bf16[128,3328]{1,0:T(8,128)(2,1)S(1)} %collective-permute-done.15.refs_3_), channel_id=1, source_target_pairs={{0,4},{4,0},{8,12},{12,8},{16,20},{20,16},{24,28},{28,24},{1,5},{5... | collective-permute-start | bytes 2555912 | tf_op jit(solution)/shard_map/ppermute | solution.py:361
  104.0 0.7 copy-start.9
  104.8 29.8 %collective-permute-start.11 = (bf16[128,1024]{1,0:T(8,128)(2,1)}, bf16[128,1024]{1,0:T(8,128)(2,1)}, u32[]{:S(2)}, u32[]{:S(2)}) collective-permute-start(bf16[128,1024]{1,0:T(8,128)(2,1)} %get-tuple-element.46), channel_id=1, source_target_pairs={{0,16},{4,20},{8,0},{12,4},{16,24},{20,28},{24,8},{28,12},{1,17},{... | collective-permute-start | bytes 786440 | tf_op jit(solution)/shard_map/ppermute | solution.py:361
  106.5 0.8 copy-start.1
  107.3 30.8 %collective-permute-start.19 = (bf16[128,1920]{1,0:T(8,128)(2,1)}, bf16[128,1920]{1,0:T(8,128)(2,1)}, u32[]{:S(2)}, u32[]{:S(2)}) collective-permute-start(bf16[128,1920]{1,0:T(8,128)(2,1)} %collective-permute-done.14.refs_2_), channel_id=1, source_target_pairs={{0,8},{4,12},{8,24},{12,28},{16,0},{20,4},{24,16},{28,20},{1,9},{5... | collective-permute-start | bytes 1474568 | tf_op jit(solution)/shard_map/ppermute | solution.py:361
  107.6 30.6 %collective-permute-start.17 = (bf16[128,1920]{1,0:T(8,128)(2,1)}, bf16[128,1920]{1,0:T(8,128)(2,1)}, u32[]{:S(2)}, u32[]{:S(2)}) collective-permute-start(bf16[128,1920]{1,0:T(8,128)(2,1)} %collective-permute-done.14.refs_2_), channel_id=1, source_target_pairs={{0,4},{4,0},{8,12},{12,8},{16,20},{20,16},{24,28},{28,24},{1,5},{5... | collective-permute-start | bytes 1474568 | tf_op jit(solution)/shard_map/ppermute | solution.py:361
  110.3 1.6 copy-start
  111.9 9.5 %copy-start.10 = (bf16[128,1024]{1,0:T(8,128)(2,1)S(1)}, bf16[128,1024]{1,0:T(8,128)(2,1)}, u32[]{:S(2)}) copy-start(bf16[128,1024]{1,0:T(8,128)(2,1)} %copy-done.9) | copy-start | bytes 786436
  111.9 11.0 %copy-start.2 = (bf16[128,1920]{1,0:T(8,128)(2,1)S(1)}, bf16[128,1920]{1,0:T(8,128)(2,1)}, u32[]{:S(2)}) copy-start(bf16[128,1920]{1,0:T(8,128)(2,1)} %copy-done.1) | copy-start | bytes 1474564
  121.4 12.5 %collective-permute-start.10 = (bf16[128,1024]{1,0:T(8,128)(2,1)S(1)}, bf16[128,1024]{1,0:T(8,128)(2,1)S(1)}, u32[]{:S(2)}, u32[]{:S(2)}) collective-permute-start(bf16[128,1024]{1,0:T(8,128)(2,1)S(1)} %copy-done.10), channel_id=1, source_target_pairs={{0,4},{4,0},{8,12},{12,8},{16,20},{20,16},{24,28},{28,24},{1,5},{5... | collective-permute-start | bytes 786440 | tf_op jit(solution)/shard_map/ppermute | solution.py:361
  133.3 31.2 %collective-permute-start.25 = (bf16[128,3328]{1,0:T(8,128)(2,1)S(1)}, bf16[128,3328]{1,0:T(8,128)(2,1)S(1)}, u32[]{:S(2)}, u32[]{:S(2)}) collective-permute-start(bf16[128,3328]{1,0:T(8,128)(2,1)S(1)} %collective-permute-done.20.refs_3_), channel_id=1, source_target_pairs={{0,4},{4,0},{8,12},{12,8},{16,20},{20,16},{24,28},{28,24},{1,5},{5... | collective-permute-start | bytes 2555912 | tf_op jit(solution)/shard_map/ppermute | solution.py:361
  136.3 15.9 %collective-permute-start.16 = (bf16[128,1024]{1,0:T(8,128)(2,1)S(1)}, bf16[128,1024]{1,0:T(8,128)(2,1)S(1)}, u32[]{:S(2)}, u32[]{:S(2)}) collective-permute-start(bf16[128,1024]{1,0:T(8,128)(2,1)S(1)} %get-tuple-element.51), channel_id=1, source_target_pairs={{0,24},{4,28},{8,16},{12,20},{16,8},{20,12},{24,0},{28,4},{1,25},{... | collective-permute-start | bytes 786440 | tf_op jit(solution)/shard_map/ppermute | solution.py:361
  138.1 32.8 %collective-permute-start.24 = (bf16[128,1920]{1,0:T(8,128)(2,1)}, bf16[128,1920]{1,0:T(8,128)(2,1)S(1)}, u32[]{:S(2)}, u32[]{:S(2)}) collective-permute-start(bf16[128,1920]{1,0:T(8,128)(2,1)} %collective-permute-done.19.refs_2_), channel_id=1, source_target_pairs={{0,4},{4,0},{8,12},{12,8},{16,20},{20,16},{24,28},{28,24},{1,5},{5... | collective-permute-start | bytes 1474568 | tf_op jit(solution)/shard_map/ppermute | solution.py:361
  150.2 27.6 %collective-permute-start.22 = (bf16[128,1024]{1,0:T(8,128)(2,1)S(1)}, bf16[128,1024]{1,0:T(8,128)(2,1)S(1)}, u32[]{:S(2)}, u32[]{:S(2)}) collective-permute-start(bf16[128,1024]{1,0:T(8,128)(2,1)S(1)} %get-tuple-element.57), channel_id=1, source_target_pairs={{0,28},{4,24},{8,20},{12,16},{16,12},{20,8},{24,4},{28,0},{1,29},{... | collective-permute-start | bytes 786440 | tf_op jit(solution)/shard_map/ppermute | solution.py:361
  152.1 26.4 %collective-permute-start.23 = (bf16[128,1024]{1,0:T(8,128)(2,1)S(1)}, bf16[128,1024]{1,0:T(8,128)(2,1)S(1)}, u32[]{:S(2)}, u32[]{:S(2)}) collective-permute-start(bf16[128,1024]{1,0:T(8,128)(2,1)S(1)} %get-tuple-element.55), channel_id=1, source_target_pairs={{0,8},{4,12},{8,24},{12,28},{16,0},{20,4},{24,16},{28,20},{1,9},{5... | collective-permute-start | bytes 786440 | tf_op jit(solution)/shard_map/ppermute | solution.py:361
  152.1 24.9 %collective-permute-start.21 = (bf16[128,1024]{1,0:T(8,128)(2,1)S(1)}, bf16[128,1024]{1,0:T(8,128)(2,1)S(1)}, u32[]{:S(2)}, u32[]{:S(2)}) collective-permute-start(bf16[128,1024]{1,0:T(8,128)(2,1)S(1)} %get-tuple-element.56), channel_id=1, source_target_pairs={{0,20},{4,16},{8,4},{12,0},{16,28},{20,24},{24,12},{28,8},{1,21},{... | collective-permute-start | bytes 786440 | tf_op jit(solution)/shard_map/ppermute | solution.py:361
  175.8 8.2 %collective-permute-start.26 = (bf16[128,1024]{1,0:T(8,128)(2,1)S(1)}, bf16[128,1024]{1,0:T(8,128)(2,1)S(1)}, u32[]{:S(2)}, u32[]{:S(2)}) collective-permute-start(bf16[128,1024]{1,0:T(8,128)(2,1)S(1)} %shard_map.120), channel_id=1, source_target_pairs={{0,12},{4,8},{8,28},{12,24},{16,4},{20,0},{24,20},{28,16},{1,13},{... | collective-permute-start | bytes 786440 | tf_op jit(solution)/shard_map/ppermute | solution.py:361
Sparse Core Ops, SparseCore 0:
  34.2 22.3 all-gather.1

commit v10 on v9

--- a/solution.py
+++ b/solution.py
@@ -245,18 +245,16 @@
     gate_sum = jnp.dot(tokens, gate_ref[...], preferred_element_type=jnp.float32)
     up_sum = jnp.dot(tokens, up_ref[...], preferred_element_type=jnp.float32)
     if final:
-        gate_part, up_part, scale_ref, out_ref = refs[3:]
-        scale = scale_ref[:, :1]
+        gate_part, up_part, out_ref = refs[3:]
+        both = chunk_ref[:, -SCALE_COLUMNS:].astype(jnp.float32)
+        scale = both[:, :1] + both[:, SCALE_COLUMNS // 2 : SCALE_COLUMNS // 2 + 1]
         gate_sum = (gate_part[...] + gate_sum) * scale
         up_sum = (up_part[...] + up_sum) * scale
         out_ref[...] = (gate_sum / (1.0 + jnp.exp(-gate_sum)) * up_sum).astype(jnp.bfloat16)
     else:
-        gate_part, up_part, scale_ref = refs[3:]
+        gate_part, up_part = refs[3:]
         gate_part[...] = gate_sum
         up_part[...] = up_sum
-        both = chunk_ref[:, -SCALE_COLUMNS:].astype(jnp.float32)
-        scale = both[:, :1] + both[:, SCALE_COLUMNS // 2 : SCALE_COLUMNS // 2 + 1]
-        scale_ref[...] = jnp.broadcast_to(scale, scale_ref.shape)
 
 
 def gated_part(chunk, array, gate_weight, up_weight, so_far):
@@ -268,17 +266,15 @@
     weights = pl.BlockSpec((pl.Element(width), pl.Element(block)), lambda i: (before, i * block))
     whole = pl.BlockSpec(array.shape, lambda i: (0, 0))
     part = pl.BlockSpec((rows, block), lambda i: (0, i))
-    scale = pl.BlockSpec((rows, 128), lambda i: (0, 0))
     if so_far:
         out_specs, shapes = part, jax.ShapeDtypeStruct((rows, units), jnp.bfloat16)
     else:
-        out_specs = [part, part, scale]
+        out_specs = [part, part]
         shapes = [jax.ShapeDtypeStruct((rows, units), jnp.float32)] * 2
-        shapes.append(jax.ShapeDtypeStruct((rows, 128), jnp.float32))
     return pl.pallas_call(
         functools.partial(part_kernel, width, bool(so_far)),
         grid=(units // block,),
-        in_specs=[whole, weights, weights] + ([part, part, scale] if so_far else []),
+        in_specs=[whole, weights, weights] + ([part, part] if so_far else []),
         out_specs=out_specs,
         out_shape=shapes,
         compiler_params=pltpu.CompilerParams(vmem_limit_bytes=VMEM_LIMIT),
@@ -415,8 +411,8 @@
         for c in chunks:
             ready = arrived[-1][c]
             number = len(sent)
-            behind = sent[0] if number == 1 else sent[number - 2][:1] if number > 1 else []
-            if step > 2 or (c == 0 and step > 1):
+            behind = sent[number - 1] if c else sent[number - 2][:1] if step else []
+            if c == 0 and step > 1:
                 behind = [*behind, products[step - 2]]
             if behind:
                 ready = after(ready, *behind)
@@ -435,8 +431,8 @@
         if step + 1 < line_count:
             blocks = gated([shard for shard, _, _ in waiting], gate_weight, up_weight)
         else:
-            shares = gated_part(1, other[1], gate_weight, up_weight, ())
-            blocks = [gated_part(0, other[0], gate_weight, up_weight, shares)]
+            shares = gated_part(0, other[0], gate_weight, up_weight, ())
+            blocks = [gated_part(1, other[1], gate_weight, up_weight, shares)]
         products.append(blocks[-1])
         late = [(after(block, blocks[-1]), steps, flip) for block, steps, flip in late]
         made = late + [(block, steps, flip) for block, (_, steps, flip) in zip(blocks, waiting)]

time: 192 us -> 201 us (1.047)
  waiting for transfers between devices: 69 us -> 77.3 us
  local copies, waits for them, and re-layouts: 13.7 us -> 16.4 us
    unnamed x24 -> x52, local copies, waits for them, and re-layouts: 5.4 us -> 14.1 us
    ppermute x21, waiting for transfers between devices: 61.5 us -> 69 us  [send(): return lax.ppermute(array, 'grp', pairs)]
    dynamic_update_slice x8, local copies, waits for them, and re-layouts: 6.71 us -> 2.08 us  [put(): return lax.dynamic_update_slice_in_dim(hidden, block, source * units, 1)]
  transfers between devices with their start and end apart: 28 -> 28, of which waited for: 13 -> 13; matrix products, arithmetic and copies ran while one was open for 5% -> 2% of each run, Pallas kernels for 30% -> 25%
where the time goes in v10:
time: 201 us
  waiting for transfers between devices  77.3 us (38%)
  Pallas kernels  56.5 us (28%)
  starting transfers between devices  34.2 us (17%)
  local copies, waits for them, and re-layouts  16.4 us (8%)
  between operations  14.3 us (7%)
    ppermute x21, waiting for transfers between devices, send(): return lax.ppermute(array, 'grp', pairs)  69 us
    pallas_call x3, Pallas kernels, gated(): pl.pallas_call(functools.partial(gated_kernel, count, len(shards[0])), gr...  33.5 us
    ppermute x21, starting transfers between devices, send(): return lax.ppermute(array, 'grp', pairs)  28.9 us
    unnamed x52, local copies, waits for them, and re-layouts  14.1 us
    pallas_call x2, Pallas kernels, gated_part(): pl.pallas_call(functools.partial(part_kernel, width, bool(so_far)), grid=...  11.3 us
    ppermute x6, waiting for transfers between devices, swap(): return lax.ppermute(array, 'tok', [(t, t ^ mask) for t in range(tok_count)])  8.27 us
    pallas_call x2, Pallas kernels, attend(): pl.pallas_call(functools.partial(attend_kernel, chunk, shard_count, width...  7.86 us
    ppermute x6, starting transfers between devices, swap(): return lax.ppermute(array, 'tok', [(t, t ^ mask) for t in range(tok_count)])  5.26 us
  transfers between devices with their start and end apart: 28, of which 13 were waited for; matrix products, arithmetic and copies ran while one was open for 2% of the time, Pallas kernels for 25%

profile of v10, /device:TPU:0, one launch (start us, length us, event | category | flops | bytes accessed | tf_op | source)
XLA Modules:
  0.0 200.7 jit_solution(11600846880589873879)
XLA Ops:
  7.2 0.6 copy-done.17
  7.9 1.1 shard_map.112
  9.0 3.0 %collective-permute-start.1 = (bf16[144,768]{1,0:T(8,128)(2,1)S(1)}, bf16[144,768]{1,0:T(8,128)(2,1)S(1)}, u32[]{:S(2)}, u32[]{:S(2)}) collective-permute-start(bf16[144,768]{1,0:T(8,128)(2,1)S(1)} %get-tuple-element.32.refs_3_), channel_id=1, source_target_pairs={{0,2},{1,3},{2,0},{3,1},{4,6},{5,7},{6,4},{7,5},{8,10},{9,11},{10,... | collective-permute-start | bytes 663560 | tf_op jit(solution)/shard_map/ppermute | solution.py:350
  12.0 5.4 %collective-permute-done.1.refs_5_ = bf16[144,768]{1,0:T(8,128)(2,1)S(1)} collective-permute-done((bf16[144,768]{1,0:T(8,128)(2,1)S(1)}, bf16[144,768]{1,0:T(8,128)(2,1)S(1)}, u32[]{:S(2)}, u32[]{:S(2)}) %collective-permute-start.1) | collective-permute-done | bytes 221216 | tf_op jit(solution)/shard_map/ppermute | solution.py:350
  17.4 1.7 collective-permute-start.4
  19.1 0.5 collective-permute-start.2
  19.7 0.7 convert_bitcast_fusion
  20.3 0.3 collective-permute-done.refs_4_
  20.6 0.3 collective-permute-done.2.refs_6_
  21.0 0.7 copy-done.15
  21.7 3.2 %shard_map.113 = (bf16[128,1920]{1,0:T(8,128)(2,1)S(1)}, bf16[128,1920]{1,0:T(8,128)(2,1)S(1)}, f32[128,128]{1,0:T(8,128)S(1)}, f32[128,512]{1,0:T(8,128)S(1)}) custom-call(bf16[128,5120]{1,0:T(8,128)(2,1)} %refs_0_.3, bf16[128,5120]{1,0:T(8,128)(2,1)} %refs_1_.5, f32[1,5120]{1,0:T(1,128)S(1)} %bitcast.6, bf16[144,768]{1,0:T(8,128)(2,1)S(1)} %get-tuple-element.32.refs_3_, ...), custom_call_target="tpu_custom_call" | custom-call | flops 503316480 | bytes 2752512 | tf_op jit(solution)/shard_map/pallas_call | solution.py:169
  24.9 0.8 copy-done.3
  25.7 0.6 collective-permute-done.4.refs_5_
  26.3 1.6 collective-permute-done.5.refs_6_
  27.9 4.7 %shard_map.114 = (bf16[128,3200]{1,0:T(8,128)(2,1)S(1)}, bf16[128,3328]{1,0:T(8,128)(2,1)S(1)}) custom-call(bf16[128,5120]{1,0:T(8,128)(2,1)} %refs_0_.3, bf16[128,5120]{1,0:T(8,128)(2,1)} %refs_1_.5, f32[1,5120]{1,0:T(1,128)S(1)} %bitcast.7, bf16[128,1280]{1,0:T(8,128)(2,1)S(1)} %get-tuple-element.35.refs_3_, ...), custom_call_target="tpu_custom_call" | custom-call | flops 838860800 | bytes 4587520 | tf_op jit(solution)/shard_map/pallas_call | solution.py:169
  32.6 0.9 copy-done.1
  33.6 1.5 collective-permute-start.6
  35.1 1.6 collective-permute-start.7
  36.6 10.2 %collective-permute-done.6.refs_2_ = bf16[128,1920]{1,0:T(8,128)(2,1)S(1)} collective-permute-done((bf16[128,1920]{1,0:T(8,128)(2,1)S(1)}, bf16[128,1920]{1,0:T(8,128)(2,1)S(1)}, u32[]{:S(2)}, u32[]{:S(2)}) %collective-permute-start.6) | collective-permute-done | bytes 491552 | tf_op jit(solution)/shard_map/ppermute | solution.py:357
  46.9 0.8 copy-done.18
  47.7 1.3 collective-permute-done.7.refs_4_
  49.0 0.8 collective-permute-start.9
  49.7 1.0 collective-permute-start.8
  50.7 1.1 collective-permute-start.12
  51.8 3.4 %collective-permute-start.13 = (bf16[128,1920]{1,0:T(8,128)(2,1)S(1)}, bf16[128,1920]{1,0:T(8,128)(2,1)S(1)}, u32[]{:S(2)}, u32[]{:S(2)}) collective-permute-start(bf16[128,1920]{1,0:T(8,128)(2,1)S(1)} %collective-permute-done.7.refs_4_), channel_id=1, source_target_pairs={{0,8},{4,12},{8,24},{12,28},{16,0},{20,4},{24,16},{28,20},{1,9},{5... | collective-permute-start | bytes 1474568 | tf_op jit(solution)/shard_map/ppermute | solution.py:357
  55.1 0.8 copy-done.20
  55.9 23.9 %collective-permute-done.12.refs_0_ = bf16[128,1920]{1,0:T(8,128)(2,1)S(1)} collective-permute-done((bf16[128,1920]{1,0:T(8,128)(2,1)S(1)}, bf16[128,1920]{1,0:T(8,128)(2,1)S(1)}, u32[]{:S(2)}, u32[]{:S(2)}) %collective-permute-start.12) | collective-permute-done | bytes 491552 | tf_op jit(solution)/shard_map/ppermute | solution.py:357
  79.8 0.8 copy-done.9
  80.6 3.4 %collective-permute-start.15 = (bf16[128,3328]{1,0:T(8,128)(2,1)}, bf16[128,3328]{1,0:T(8,128)(2,1)S(1)}, u32[]{:S(2)}, u32[]{:S(2)}) collective-permute-start(bf16[128,3328]{1,0:T(8,128)(2,1)} %collective-permute-done.9.refs_5_), channel_id=1, source_target_pairs={{0,8},{4,12},{8,24},{12,28},{16,0},{20,4},{24,16},{28,20},{1,9},{5... | collective-permute-start | bytes 2555912 | tf_op jit(solution)/shard_map/ppermute | solution.py:357
  84.1 0.6 collective-permute-start.14
  84.7 1.0 copy-done.19
  85.7 1.0 copy-done.21
  86.7 12.8 %shard_map.115 = (bf16[128,1024]{1,0:T(8,128)(2,1)S(1)}, bf16[128,1024]{1,0:T(8,128)(2,1)S(1)}, bf16[128,1024]{1,0:T(8,128)(2,1)S(1)}) custom-call(bf16[128,1920]{1,0:T(8,128)(2,1)S(1)} %get-tuple-element.36.refs_0_, bf16[128,3328]{1,0:T(8,128)(2,1)S(1)} %get-tuple-element.42.refs_1_, bf16[128,1920]{1,0:T(8,128)(2,1)S(1)} %copy-done.19, ...), custom_call_target="tpu_custom_call" | custom-call | flops 8053063680 | bytes 25690112 | tf_op jit(solution)/shard_map/pallas_call | solution.py:223
  99.6 0.7 copy-done.13
  100.3 0.7 copy-done.22
  101.0 0.7 copy-done.23
  101.7 1.4 collective-permute-start.17
  103.1 0.3 collective-permute-start.18
  103.5 0.1 select_reduce_fusion
  103.6 2.6 %collective-permute-start.11 = (bf16[128,1024]{1,0:T(8,128)(2,1)}, bf16[128,1024]{1,0:T(8,128)(2,1)}, u32[]{:S(2)}, u32[]{:S(2)}) collective-permute-start(bf16[128,1024]{1,0:T(8,128)(2,1)} %copy-done.22), channel_id=1, source_target_pairs={{0,16},{4,20},{8,0},{12,4},{16,24},{20,28},{24,8},{28,12},{1,17},{... | collective-permute-start | bytes 786440 | tf_op jit(solution)/shard_map/ppermute | solution.py:357
  106.2 6.9 %collective-permute-done.17.refs_0_ = bf16[128,1920]{1,0:T(8,128)(2,1)S(1)} collective-permute-done((bf16[128,1920]{1,0:T(8,128)(2,1)S(1)}, bf16[128,1920]{1,0:T(8,128)(2,1)S(1)}, u32[]{:S(2)}, u32[]{:S(2)}) %collective-permute-start.17) | collective-permute-done | bytes 491552 | tf_op jit(solution)/shard_map/ppermute | solution.py:357
  113.2 0.8 copy-done.5
  113.9 0.7 collective-permute-start.10
  114.6 6.6 %collective-permute-done.18.refs_2_ = bf16[128,1920]{1,0:T(8,128)(2,1)S(1)} collective-permute-done((bf16[128,1920]{1,0:T(8,128)(2,1)S(1)}, bf16[128,1920]{1,0:T(8,128)(2,1)S(1)}, u32[]{:S(2)}, u32[]{:S(2)}) %collective-permute-start.18) | collective-permute-done | bytes 491552 | tf_op jit(solution)/shard_map/ppermute | solution.py:357
  121.3 0.8 copy-done.7
  122.1 1.6 copy-done
  123.7 2.7 %shard_map.116 = bf16[16,16,2048]{2,1,0:T(8,128)(2,1)} custom-call(s32[16]{0:T(128)S(1)} %broadcast_add_fusion.page_ref, bf16[512,2048]{1,0:T(8,128)(2,1)S(1)} %copy-done, bf16[16,16,2048]{2,1,0:T(8,128)(2,1)} %cache_ref.1), custom_call_target="tpu_custom_call" | custom-call | bytes 4194304 | tf_op jit(solution)/shard_map/pallas_call | solution.py:304
  126.4 10.4 %shard_map.117 = (bf16[128,1024]{1,0:T(8,128)(2,1)S(1)}, bf16[128,1024]{1,0:T(8,128)(2,1)S(1)}) custom-call(bf16[128,1920]{1,0:T(8,128)(2,1)S(1)} %copy-done.10, bf16[128,3328]{1,0:T(8,128)(2,1)S(1)} %collective-permute-done.14.refs_1_, bf16[128,1920]{1,0:T(8,128)(2,1)S(1)} %copy-done.12, bf16[128,3328]{1,0:T(8,128)(2,1)S(1)} %collective-permute-done.15.refs_3_, ...), custom_call_target="tpu_custom_call" | custom-call | flops 5368709120 | bytes 24117248 | tf_op jit(solution)/shard_map/pallas_call | solution.py:223
  136.9 2.1 %collective-permute-start.24 = (bf16[128,1920]{1,0:T(8,128)(2,1)S(1)}, bf16[128,1920]{1,0:T(8,128)(2,1)S(1)}, u32[]{:S(2)}, u32[]{:S(2)}) collective-permute-start(bf16[128,1920]{1,0:T(8,128)(2,1)S(1)} %copy-done.8), channel_id=1, source_target_pairs={{0,4},{4,0},{8,12},{12,8},{16,20},{20,16},{24,28},{28,24},{1,5},{5... | collective-permute-start | bytes 1474568 | tf_op jit(solution)/shard_map/ppermute | solution.py:357
  138.9 1.2 pad_maximum_fusion
  140.1 0.2 broadcast_in_dim.25
  140.4 11.3 %collective-permute-done.24.refs_0_ = bf16[128,1920]{1,0:T(8,128)(2,1)S(1)} collective-permute-done((bf16[128,1920]{1,0:T(8,128)(2,1)S(1)}, bf16[128,1920]{1,0:T(8,128)(2,1)S(1)}, u32[]{:S(2)}, u32[]{:S(2)}) %collective-permute-start.24) | collective-permute-done | bytes 491552 | tf_op jit(solution)/shard_map/ppermute | solution.py:357
  151.7 1.0 constant_dynamic-update-slice_fusion.6
  152.7 1.0 constant_dynamic-update-slice_fusion.5
  153.7 1.0 collective-permute-start.16
  154.7 10.3 %shard_map.118 = (bf16[128,1024]{1,0:T(8,128)(2,1)S(1)}, bf16[128,1024]{1,0:T(8,128)(2,1)S(1)}) custom-call(bf16[128,1920]{1,0:T(8,128)(2,1)S(1)} %copy-done.6, bf16[128,3328]{1,0:T(8,128)(2,1)S(1)} %collective-permute-done.19.refs_1_, bf16[128,1920]{1,0:T(8,128)(2,1)S(1)} %copy-done.8, bf16[128,3328]{1,0:T(8,128)(2,1)S(1)} %collective-permute-done.20.refs_3_, ...), custom_call_target="tpu_custom_call" | custom-call | flops 5368709120 | bytes 24117248 | tf_op jit(solution)/shard_map/pallas_call | solution.py:223
  165.0 4.4 %collective-permute-start.22 = (bf16[128,1024]{1,0:T(8,128)(2,1)S(1)}, bf16[128,1024]{1,0:T(8,128)(2,1)S(1)}, u32[]{:S(2)}, u32[]{:S(2)}) collective-permute-start(bf16[128,1024]{1,0:T(8,128)(2,1)S(1)} %get-tuple-element.56), channel_id=1, source_target_pairs={{0,28},{4,24},{8,20},{12,16},{16,12},{20,8},{24,4},{28,0},{1,29},{... | collective-permute-start | bytes 786440 | tf_op jit(solution)/shard_map/ppermute | solution.py:357
  169.4 2.4 %collective-permute-start.21 = (bf16[128,1024]{1,0:T(8,128)(2,1)S(1)}, bf16[128,1024]{1,0:T(8,128)(2,1)S(1)}, u32[]{:S(2)}, u32[]{:S(2)}) collective-permute-start(bf16[128,1024]{1,0:T(8,128)(2,1)S(1)} %get-tuple-element.55), channel_id=1, source_target_pairs={{0,20},{4,16},{8,4},{12,0},{16,28},{20,24},{24,12},{28,8},{1,21},{... | collective-permute-start | bytes 786440 | tf_op jit(solution)/shard_map/ppermute | solution.py:357
  171.8 4.8 %shard_map.119 = (f32[128,1024]{1,0:T(8,128)S(1)}, f32[128,1024]{1,0:T(8,128)S(1)}) custom-call(bf16[128,1920]{1,0:T(8,128)(2,1)S(1)} %collective-permute-done.24.refs_0_, bf16[5120,1024]{1,0:T(8,128)(2,1)} %refs_1_.7, bf16[5120,1024]{1,0:T(8,128)(2,1)} %refs_2_.3), custom_call_target="tpu_custom_call" | custom-call | flops 1006632960 | bytes 9404416 | tf_op jit(solution)/shard_map/pallas_call | solution.py:274
  176.6 6.5 %shard_map.120 = bf16[128,1024]{1,0:T(8,128)(2,1)S(1)} custom-call(bf16[128,3328]{1,0:T(8,128)(2,1)S(1)} %collective-permute-done.25.refs_0_, bf16[5120,1024]{1,0:T(8,128)(2,1)} %refs_1_.7, bf16[5120,1024]{1,0:T(8,128)(2,1)} %refs_2_.3, f32[128,1024]{1,0:T(8,128)S(1)} %get-tuple-element.59.refs_3_, f32[128,1024]{1,0:T(8,128)S(1)} %get-tuple-element.60.refs_4_), custom_call_target="tpu_custom_call" | custom-call | flops 1677721600 | bytes 14974976 | tf_op jit(solution)/shard_map/pallas_call | solution.py:274
  183.1 0.6 collective-permute-start.26
  183.8 3.6 %collective-permute-done.23 = bf16[128,1024]{1,0:T(8,128)(2,1)S(1)} collective-permute-done((bf16[128,1024]{1,0:T(8,128)(2,1)S(1)}, bf16[128,1024]{1,0:T(8,128)(2,1)S(1)}, u32[]{:S(2)}, u32[]{:S(2)}) %collective-permute-start.23) | collective-permute-done | bytes 262176 | tf_op jit(solution)/shard_map/ppermute | solution.py:357
  187.5 5.0 %collective-permute-done.26 = bf16[128,1024]{1,0:T(8,128)(2,1)S(1)} collective-permute-done((bf16[128,1024]{1,0:T(8,128)(2,1)S(1)}, bf16[128,1024]{1,0:T(8,128)(2,1)S(1)}, u32[]{:S(2)}, u32[]{:S(2)}) %collective-permute-start.26) | collective-permute-done | bytes 262176 | tf_op jit(solution)/shard_map/ppermute | solution.py:357
  192.6 1.3 copy-done.24
  (70 shorter events, 0.4 us)
Async XLA Ops:
  7.2 20.8 %copy-start.16 = (f32[5120]{0:T(1024)S(1)}, f32[5120]{0:T(1024)}, u32[]{:S(2)}) copy-start(f32[5120]{0:T(1024)} %param.13) | copy-start | bytes 61444
  7.2 114.9 %all-gather.2.cloned.1.call-start = ((), (), s32[]{:S(2)}) async-start(), calls=%async_computation | async-start | bytes 2621440 | tf_op jit(solution)/shard_map/all_gather | solution.py:391
  7.2 0.7 copy-start.17
  9.0 8.4 %collective-permute-start.1 = (bf16[144,768]{1,0:T(8,128)(2,1)S(1)}, bf16[144,768]{1,0:T(8,128)(2,1)S(1)}, u32[]{:S(2)}, u32[]{:S(2)}) collective-permute-start(bf16[144,768]{1,0:T(8,128)(2,1)S(1)} %get-tuple-element.32.refs_3_), channel_id=1, source_target_pairs={{0,2},{1,3},{2,0},{3,1},{4,6},{5,7},{6,4},{7,5},{8,10},{9,11},{10,... | collective-permute-start | bytes 663560 | tf_op jit(solution)/shard_map/ppermute | solution.py:350
  17.4 8.9 %collective-permute-start.4 = (bf16[128,1280]{1,0:T(8,128)(2,1)S(1)}, bf16[128,1280]{1,0:T(8,128)(2,1)S(1)}, u32[]{:S(2)}, u32[]{:S(2)}) collective-permute-start(bf16[128,1280]{1,0:T(8,128)(2,1)S(1)} %get-tuple-element.35.refs_3_), channel_id=1, source_target_pairs={{0,2},{1,3},{2,0},{3,1},{4,6},{5,7},{6,4},{7,5},{8,10},{9,11},{10,... | collective-permute-start | bytes 983048 | tf_op jit(solution)/shard_map/ppermute | solution.py:350
  19.1 1.5 collective-permute-start
  19.1 1.8 collective-permute-start.2
  20.3 6.0 %collective-permute-start.3 = (bf16[128,1280]{1,0:T(8,128)(2,1)S(1)}, bf16[128,1280]{1,0:T(8,128)(2,1)S(1)}, u32[]{:S(2)}, u32[]{:S(2)}) collective-permute-start(bf16[128,1280]{1,0:T(8,128)(2,1)S(1)} %get-tuple-element.35.refs_3_), channel_id=1, source_target_pairs={{0,1},{1,0},{2,3},{3,2},{4,5},{5,4},{6,7},{7,6},{8,9},{9,8},{10,11... | collective-permute-start | bytes 983048 | tf_op jit(solution)/shard_map/ppermute | solution.py:350
  21.0 0.7 copy-start.15
  24.9 0.8 copy-start.3
  26.3 1.6 collective-permute-start.5
  32.6 0.9 copy-start.1
  33.6 13.3 %collective-permute-start.6 = (bf16[128,1920]{1,0:T(8,128)(2,1)S(1)}, bf16[128,1920]{1,0:T(8,128)(2,1)S(1)}, u32[]{:S(2)}, u32[]{:S(2)}) collective-permute-start(bf16[128,1920]{1,0:T(8,128)(2,1)S(1)} %get-tuple-element.36.refs_0_), channel_id=1, source_target_pairs={{0,4},{4,0},{8,12},{12,8},{16,20},{20,16},{24,28},{28,24},{1,5},{5... | collective-permute-start | bytes 1474568 | tf_op jit(solution)/shard_map/ppermute | solution.py:357
  35.1 13.9 %collective-permute-start.7 = (bf16[128,1920]{1,0:T(8,128)(2,1)S(1)}, bf16[128,1920]{1,0:T(8,128)(2,1)S(1)}, u32[]{:S(2)}, u32[]{:S(2)}) collective-permute-start(bf16[128,1920]{1,0:T(8,128)(2,1)S(1)} %get-tuple-element.36.refs_0_), channel_id=1, source_target_pairs={{0,8},{4,12},{8,24},{12,28},{16,0},{20,4},{24,16},{28,20},{1,9},{5... | collective-permute-start | bytes 1474568 | tf_op jit(solution)/shard_map/ppermute | solution.py:357
  46.9 0.8 copy-start.18
  49.0 31.7 %collective-permute-start.9 = (bf16[128,3328]{1,0:T(8,128)(2,1)S(1)}, bf16[128,3328]{1,0:T(8,128)(2,1)}, u32[]{:S(2)}, u32[]{:S(2)}) collective-permute-start(bf16[128,3328]{1,0:T(8,128)(2,1)S(1)} %get-tuple-element.42.refs_1_), channel_id=1, source_target_pairs={{0,8},{4,12},{8,24},{12,28},{16,0},{20,4},{24,16},{28,20},{1,9},{5... | collective-permute-start | bytes 2555912 | tf_op jit(solution)/shard_map/ppermute | solution.py:357
  49.7 34.9 %collective-permute-start.8 = (bf16[128,3328]{1,0:T(8,128)(2,1)S(1)}, bf16[128,3328]{1,0:T(8,128)(2,1)}, u32[]{:S(2)}, u32[]{:S(2)}) collective-permute-start(bf16[128,3328]{1,0:T(8,128)(2,1)S(1)} %get-tuple-element.42.refs_1_), channel_id=1, source_target_pairs={{0,4},{4,0},{8,12},{12,8},{16,20},{20,16},{24,28},{28,24},{1,5},{5... | collective-permute-start | bytes 2555912 | tf_op jit(solution)/shard_map/ppermute | solution.py:357
  50.7 29.1 %collective-permute-start.12 = (bf16[128,1920]{1,0:T(8,128)(2,1)S(1)}, bf16[128,1920]{1,0:T(8,128)(2,1)S(1)}, u32[]{:S(2)}, u32[]{:S(2)}) collective-permute-start(bf16[128,1920]{1,0:T(8,128)(2,1)S(1)} %collective-permute-done.7.refs_4_), channel_id=1, source_target_pairs={{0,4},{4,0},{8,12},{12,8},{16,20},{20,16},{24,28},{28,24},{1,5},{5... | collective-permute-start | bytes 1474568 | tf_op jit(solution)/shard_map/ppermute | solution.py:357
  51.8 28.9 %collective-permute-start.13 = (bf16[128,1920]{1,0:T(8,128)(2,1)S(1)}, bf16[128,1920]{1,0:T(8,128)(2,1)S(1)}, u32[]{:S(2)}, u32[]{:S(2)}) collective-permute-start(bf16[128,1920]{1,0:T(8,128)(2,1)S(1)} %collective-permute-done.7.refs_4_), channel_id=1, source_target_pairs={{0,8},{4,12},{8,24},{12,28},{16,0},{20,4},{24,16},{28,20},{1,9},{5... | collective-permute-start | bytes 1474568 | tf_op jit(solution)/shard_map/ppermute | solution.py:357
  55.1 0.8 copy-start.20
  55.9 47.5 %copy-start.25 = (s32[1,64]{1,0:T(1,128)S(1)}, s32[1,64]{1,0:T(1,128)}, u32[]{:S(2)}) copy-start(s32[1,64]{1,0:T(1,128)} %param.17) | copy-start | bytes 772
  79.8 0.8 copy-start.9
  80.6 22.5 %copy-start.11 = (bf16[128,1920]{1,0:T(8,128)(2,1)}, bf16[128,1920]{1,0:T(8,128)(2,1)S(1)}, u32[]{:S(2)}) copy-start(bf16[128,1920]{1,0:T(8,128)(2,1)S(1)} %collective-permute-done.13.refs_2_) | copy-start | bytes 1474564
  80.6 41.4 %collective-permute-start.15 = (bf16[128,3328]{1,0:T(8,128)(2,1)}, bf16[128,3328]{1,0:T(8,128)(2,1)S(1)}, u32[]{:S(2)}, u32[]{:S(2)}) collective-permute-start(bf16[128,3328]{1,0:T(8,128)(2,1)} %collective-permute-done.9.refs_5_), channel_id=1, source_target_pairs={{0,8},{4,12},{8,24},{12,28},{16,0},{20,4},{24,16},{28,20},{1,9},{5... | collective-permute-start | bytes 2555912 | tf_op jit(solution)/shard_map/ppermute | solution.py:357
  84.1 42.4 %collective-permute-start.14 = (bf16[128,3328]{1,0:T(8,128)(2,1)}, bf16[128,3328]{1,0:T(8,128)(2,1)S(1)}, u32[]{:S(2)}, u32[]{:S(2)}) collective-permute-start(bf16[128,3328]{1,0:T(8,128)(2,1)} %collective-permute-done.9.refs_5_), channel_id=1, source_target_pairs={{0,4},{4,0},{8,12},{12,8},{16,20},{20,16},{24,28},{28,24},{1,5},{5... | collective-permute-start | bytes 2555912 | tf_op jit(solution)/shard_map/ppermute | solution.py:357
  84.7 1.0 copy-start.19
  85.7 1.0 copy-start.21
  99.6 0.7 copy-start.13
  100.3 0.7 copy-start.22
  101.0 0.7 copy-start.23
  101.7 11.5 %collective-permute-start.17 = (bf16[128,1920]{1,0:T(8,128)(2,1)S(1)}, bf16[128,1920]{1,0:T(8,128)(2,1)S(1)}, u32[]{:S(2)}, u32[]{:S(2)}) collective-permute-start(bf16[128,1920]{1,0:T(8,128)(2,1)S(1)} %collective-permute-done.13.refs_2_), channel_id=1, source_target_pairs={{0,4},{4,0},{8,12},{12,8},{16,20},{20,16},{24,28},{28,24},{1,5},{5... | collective-permute-start | bytes 1474568 | tf_op jit(solution)/shard_map/ppermute | solution.py:357
  103.1 18.1 %collective-permute-start.18 = (bf16[128,1920]{1,0:T(8,128)(2,1)S(1)}, bf16[128,1920]{1,0:T(8,128)(2,1)S(1)}, u32[]{:S(2)}, u32[]{:S(2)}) collective-permute-start(bf16[128,1920]{1,0:T(8,128)(2,1)S(1)} %collective-permute-done.13.refs_2_), channel_id=1, source_target_pairs={{0,8},{4,12},{8,24},{12,28},{16,0},{20,4},{24,16},{28,20},{1,9},{5... | collective-permute-start | bytes 1474568 | tf_op jit(solution)/shard_map/ppermute | solution.py:357
  103.6 49.1 %collective-permute-start.11 = (bf16[128,1024]{1,0:T(8,128)(2,1)}, bf16[128,1024]{1,0:T(8,128)(2,1)}, u32[]{:S(2)}, u32[]{:S(2)}) collective-permute-start(bf16[128,1024]{1,0:T(8,128)(2,1)} %copy-done.22), channel_id=1, source_target_pairs={{0,16},{4,20},{8,0},{12,4},{16,24},{20,28},{24,8},{28,12},{1,17},{... | collective-permute-start | bytes 786440 | tf_op jit(solution)/shard_map/ppermute | solution.py:357
  113.1 0.8 copy-start.5
  113.9 37.8 %collective-permute-start.10 = (bf16[128,1024]{1,0:T(8,128)(2,1)}, bf16[128,1024]{1,0:T(8,128)(2,1)}, u32[]{:S(2)}, u32[]{:S(2)}) collective-permute-start(bf16[128,1024]{1,0:T(8,128)(2,1)} %copy-done.23), channel_id=1, source_target_pairs={{0,4},{4,0},{8,12},{12,8},{16,20},{20,16},{24,28},{28,24},{1,5},{5... | collective-permute-start | bytes 786440 | tf_op jit(solution)/shard_map/ppermute | solution.py:357
  121.3 0.8 copy-start.7
  122.1 18.3 %collective-permute-start.20 = (bf16[128,3328]{1,0:T(8,128)(2,1)S(1)}, bf16[128,3328]{1,0:T(8,128)(2,1)S(1)}, u32[]{:S(2)}, u32[]{:S(2)}) collective-permute-start(bf16[128,3328]{1,0:T(8,128)(2,1)S(1)} %collective-permute-done.15.refs_3_), channel_id=1, source_target_pairs={{0,8},{4,12},{8,24},{12,28},{16,0},{20,4},{24,16},{28,20},{1,9},{5... | collective-permute-start | bytes 2555912 | tf_op jit(solution)/shard_map/ppermute | solution.py:357
  122.1 32.6 %collective-permute-start.19 = (bf16[128,3328]{1,0:T(8,128)(2,1)S(1)}, bf16[128,3328]{1,0:T(8,128)(2,1)S(1)}, u32[]{:S(2)}, u32[]{:S(2)}) collective-permute-start(bf16[128,3328]{1,0:T(8,128)(2,1)S(1)} %collective-permute-done.15.refs_3_), channel_id=1, source_target_pairs={{0,4},{4,0},{8,12},{12,8},{16,20},{20,16},{24,28},{28,24},{1,5},{5... | collective-permute-start | bytes 2555912 | tf_op jit(solution)/shard_map/ppermute | solution.py:357
  122.1 1.6 copy-start
  123.7 2.7 %copy-start.10 = (bf16[128,1920]{1,0:T(8,128)(2,1)S(1)}, bf16[128,1920]{1,0:T(8,128)(2,1)}, u32[]{:S(2)}) copy-start(bf16[128,1920]{1,0:T(8,128)(2,1)} %copy-done.9) | copy-start | bytes 1474564
  123.7 2.7 %copy-start.12 = (bf16[128,1920]{1,0:T(8,128)(2,1)S(1)}, bf16[128,1920]{1,0:T(8,128)(2,1)}, u32[]{:S(2)}) copy-start(bf16[128,1920]{1,0:T(8,128)(2,1)} %copy-done.11) | copy-start | bytes 1474564
  126.4 10.4 %copy-start.8 = (bf16[128,1920]{1,0:T(8,128)(2,1)S(1)}, bf16[128,1920]{1,0:T(8,128)(2,1)}, u32[]{:S(2)}) copy-start(bf16[128,1920]{1,0:T(8,128)(2,1)} %copy-done.7) | copy-start | bytes 1474564
  126.4 12.5 %copy-start.2 = (bf16[128,3200]{1,0:T(8,128)(2,1)S(1)}, bf16[128,3200]{1,0:T(8,128)(2,1)}, u32[]{:S(2)}) copy-start(bf16[128,3200]{1,0:T(8,128)(2,1)} %copy-done.1) | copy-start | bytes 2457604
  126.4 12.5 %copy-start.4 = (bf16[128,1920]{1,0:T(8,128)(2,1)S(1)}, bf16[128,1920]{1,0:T(8,128)(2,1)}, u32[]{:S(2)}) copy-start(bf16[128,1920]{1,0:T(8,128)(2,1)} %copy-done.3) | copy-start | bytes 1474564
  136.9 14.9 %collective-permute-start.24 = (bf16[128,1920]{1,0:T(8,128)(2,1)S(1)}, bf16[128,1920]{1,0:T(8,128)(2,1)S(1)}, u32[]{:S(2)}, u32[]{:S(2)}) collective-permute-start(bf16[128,1920]{1,0:T(8,128)(2,1)S(1)} %copy-done.8), channel_id=1, source_target_pairs={{0,4},{4,0},{8,12},{12,8},{16,20},{20,16},{24,28},{28,24},{1,5},{5... | collective-permute-start | bytes 1474568 | tf_op jit(solution)/shard_map/ppermute | solution.py:357
  138.9 1.4 copy-start.14
  140.1 14.6 %copy-start.6 = (bf16[128,1920]{1,0:T(8,128)(2,1)S(1)}, bf16[128,1920]{1,0:T(8,128)(2,1)}, u32[]{:S(2)}) copy-start(bf16[128,1920]{1,0:T(8,128)(2,1)} %copy-done.5) | copy-start | bytes 1474564
  151.7 24.9 %collective-permute-start.25 = (bf16[128,3328]{1,0:T(8,128)(2,1)S(1)}, bf16[128,3328]{1,0:T(8,128)(2,1)S(1)}, u32[]{:S(2)}, u32[]{:S(2)}) collective-permute-start(bf16[128,3328]{1,0:T(8,128)(2,1)S(1)} %collective-permute-done.20.refs_3_), channel_id=1, source_target_pairs={{0,4},{4,0},{8,12},{12,8},{16,20},{20,16},{24,28},{28,24},{1,5},{5... | collective-permute-start | bytes 2555912 | tf_op jit(solution)/shard_map/ppermute | solution.py:357
  153.7 18.1 %collective-permute-start.16 = (bf16[128,1024]{1,0:T(8,128)(2,1)S(1)}, bf16[128,1024]{1,0:T(8,128)(2,1)S(1)}, u32[]{:S(2)}, u32[]{:S(2)}) collective-permute-start(bf16[128,1024]{1,0:T(8,128)(2,1)S(1)} %get-tuple-element.50), channel_id=1, source_target_pairs={{0,24},{4,28},{8,16},{12,20},{16,8},{20,12},{24,0},{28,4},{1,25},{... | collective-permute-start | bytes 786440 | tf_op jit(solution)/shard_map/ppermute | solution.py:357
  165.0 18.8 %collective-permute-start.22 = (bf16[128,1024]{1,0:T(8,128)(2,1)S(1)}, bf16[128,1024]{1,0:T(8,128)(2,1)S(1)}, u32[]{:S(2)}, u32[]{:S(2)}) collective-permute-start(bf16[128,1024]{1,0:T(8,128)(2,1)S(1)} %get-tuple-element.56), channel_id=1, source_target_pairs={{0,28},{4,24},{8,20},{12,16},{16,12},{20,8},{24,4},{28,0},{1,29},{... | collective-permute-start | bytes 786440 | tf_op jit(solution)/shard_map/ppermute | solution.py:357
  169.4 18.1 %collective-permute-start.23 = (bf16[128,1024]{1,0:T(8,128)(2,1)S(1)}, bf16[128,1024]{1,0:T(8,128)(2,1)S(1)}, u32[]{:S(2)}, u32[]{:S(2)}) collective-permute-start(bf16[128,1024]{1,0:T(8,128)(2,1)S(1)} %get-tuple-element.54), channel_id=1, source_target_pairs={{0,8},{4,12},{8,24},{12,28},{16,0},{20,4},{24,16},{28,20},{1,9},{5... | collective-permute-start | bytes 786440 | tf_op jit(solution)/shard_map/ppermute | solution.py:357
  169.4 14.3 %collective-permute-start.21 = (bf16[128,1024]{1,0:T(8,128)(2,1)S(1)}, bf16[128,1024]{1,0:T(8,128)(2,1)S(1)}, u32[]{:S(2)}, u32[]{:S(2)}) collective-permute-start(bf16[128,1024]{1,0:T(8,128)(2,1)S(1)} %get-tuple-element.55), channel_id=1, source_target_pairs={{0,20},{4,16},{8,4},{12,0},{16,28},{20,24},{24,12},{28,8},{1,21},{... | collective-permute-start | bytes 786440 | tf_op jit(solution)/shard_map/ppermute | solution.py:357
  183.1 9.4 %collective-permute-start.26 = (bf16[128,1024]{1,0:T(8,128)(2,1)S(1)}, bf16[128,1024]{1,0:T(8,128)(2,1)S(1)}, u32[]{:S(2)}, u32[]{:S(2)}) collective-permute-start(bf16[128,1024]{1,0:T(8,128)(2,1)S(1)} %shard_map.120), channel_id=1, source_target_pairs={{0,12},{4,8},{8,28},{12,24},{16,4},{20,0},{24,20},{28,16},{1,13},{... | collective-permute-start | bytes 786440 | tf_op jit(solution)/shard_map/ppermute | solution.py:357
  192.5 1.3 copy-start.24
Sparse Core Ops, SparseCore 0:
  33.7 23.7 all-gather.1

commit v11 on v9

--- a/solution.py
+++ b/solution.py
@@ -147,7 +147,7 @@
     operands = [queries, residual, gain] + list(kv_chunks)
     sent = width + (SCALE_COLUMNS if last else 0)
     shapes = [
-        jax.ShapeDtypeStruct((rows, width), jnp.bfloat16),
+        pltpu.HBM((rows, width), jnp.bfloat16),
         jax.ShapeDtypeStruct((rows, sent), jnp.bfloat16),
     ]
     out_specs = [whole((rows, width)), whole((rows, sent))]
@@ -336,6 +336,7 @@
         for a in (queries, residual, gate_weight, up_weight, paged_cache)
     ]
     own_kv = pltpu.with_memory_space_constraint(rotated_keys_values, pltpu.HBM)
+    own_ids = pltpu.with_memory_space_constraint(prompt_window_index, pltpu.HBM)
     rows, width = queries.shape
     tok_index = lax.axis_index("tok")
     tok_count = lax.axis_size("tok")
@@ -362,8 +363,8 @@
 
     own_seg = jnp.broadcast_to(prompt_window_index[0].astype(jnp.float32)[:, None], (rows, rows))
     place = tok_index.astype(jnp.int32).reshape(1)
-    gain = ffn_gain.reshape(1, width)
-    packed = pack(own_kv, prompt_window_index)
+    gain = pltpu.with_memory_space_constraint(ffn_gain.reshape(1, width), pltpu.HBM)
+    packed = pack(own_kv, own_ids)
     first_swaps = []
     for c in chunks:
         held = {0: packed[c]}
@@ -416,7 +417,7 @@
             ready = arrived[-1][c]
             number = len(sent)
             behind = sent[0] if number == 1 else sent[number - 2][:1] if number > 1 else []
-            if step > 2 or (c == 0 and step > 1):
+            if c == 0 and step > 1:
                 behind = [*behind, products[step - 2]]
             if behind:
                 ready = after(ready, *behind)

time: 192 us -> 192 us (level)
  local copies, waits for them, and re-layouts: 13.7 us -> 10.5 us
  waiting for transfers between devices: 69 us -> 71.2 us
    dynamic_update_slice x8, local copies, waits for them, and re-layouts: 6.71 us -> 3.67 us  [put(): return lax.dynamic_update_slice_in_dim(hidden, block, source * units, 1)]
    ppermute x21, waiting for transfers between devices: 61.5 us -> 63.8 us  [send(): return lax.ppermute(array, 'grp', pairs)]
    unnamed x24 -> x26, local copies, waits for them, and re-layouts: 5.4 us -> 6.53 us
  transfers between devices with their start and end apart: 28 -> 28, of which waited for: 13 -> 12; matrix products, arithmetic and copies ran while one was open for 5% -> 3% of each run, Pallas kernels for 30% -> 30%
where the time goes in v11:
time: 192 us; the launch traced here: 191 us
  waiting for transfers between devices  71.2 us (37%)
  Pallas kernels  58.1 us (30%)
  starting transfers between devices  35.5 us (18%)
  between operations  14.2 us (7%)
  local copies, waits for them, and re-layouts  10.5 us (5%)
  other arithmetic  1.98 us (1%)
    ppermute x21, waiting for transfers between devices, send(): return lax.ppermute(array, 'grp', pairs)  63.8 us
    pallas_call x3, Pallas kernels, gated(): pl.pallas_call(functools.partial(gated_kernel, count, len(shards[0])), gr...  33.4 us
    ppermute x21, starting transfers between devices, send(): return lax.ppermute(array, 'grp', pairs)  30.2 us
    pallas_call x2, Pallas kernels, gated_part(): pl.pallas_call(functools.partial(part_kernel, width, bool(so_far)), grid=...  11.6 us
    pallas_call x2, Pallas kernels, attend(): pl.pallas_call(functools.partial(attend_kernel, chunk, shard_count, width...  9.37 us
    ppermute x6, waiting for transfers between devices, swap(): return lax.ppermute(array, 'tok', [(t, t ^ mask) for t in range(tok_count)])  7.44 us
    unnamed x26, local copies, waits for them, and re-layouts  6.53 us
    ppermute x6, starting transfers between devices, swap(): return lax.ppermute(array, 'tok', [(t, t ^ mask) for t in range(tok_count)])  5.26 us
  transfers between devices with their start and end apart: 28, of which 12 were waited for; matrix products, arithmetic and copies ran while one was open for 3% of the time, Pallas kernels for 30%

profile of v11, /device:TPU:0, one launch (start us, length us, event | category | flops | bytes accessed | tf_op | source)
XLA Modules:
  0.0 191.4 jit_solution(13057509596768146208)
XLA Ops:
  7.2 0.0 all-gather.2.cloned.1.call-start
  7.2 1.1 shard_map.112
  8.3 3.0 %collective-permute-start.1 = (bf16[144,768]{1,0:T(8,128)(2,1)S(1)}, bf16[144,768]{1,0:T(8,128)(2,1)S(1)}, u32[]{:S(2)}, u32[]{:S(2)}) collective-permute-start(bf16[144,768]{1,0:T(8,128)(2,1)S(1)} %get-tuple-element.33.refs_3_), channel_id=1, source_target_pairs={{0,2},{1,3},{2,0},{3,1},{4,6},{5,7},{6,4},{7,5},{8,10},{9,11},{10,... | collective-permute-start | bytes 663560 | tf_op jit(solution)/shard_map/ppermute | solution.py:355
  11.3 5.4 %collective-permute-done.1.refs_5_ = bf16[144,768]{1,0:T(8,128)(2,1)S(1)} collective-permute-done((bf16[144,768]{1,0:T(8,128)(2,1)S(1)}, bf16[144,768]{1,0:T(8,128)(2,1)S(1)}, u32[]{:S(2)}, u32[]{:S(2)}) %collective-permute-start.1) | collective-permute-done | bytes 221216 | tf_op jit(solution)/shard_map/ppermute | solution.py:355
  16.7 1.7 collective-permute-start.4
  18.5 0.5 collective-permute-start.2
  19.0 0.7 convert_bitcast_fusion
  19.6 0.0 collective-permute-start.3
  19.6 0.3 collective-permute-done.refs_4_
  20.0 0.3 collective-permute-done.2.refs_6_
  20.3 0.1 broadcast_in_dim.24.refs_8_
  20.3 3.9 %shard_map.113 = (bf16[128,1920]{1,0:T(8,128)(2,1)}, bf16[128,1920]{1,0:T(8,128)(2,1)S(1)}, f32[128,128]{1,0:T(8,128)S(1)}, f32[128,512]{1,0:T(8,128)S(1)}) custom-call(bf16[128,5120]{1,0:T(8,128)(2,1)} %refs_0_.3, bf16[128,5120]{1,0:T(8,128)(2,1)} %refs_1_.5, f32[1,5120]{1,0:T(1,128)} %bitcast.6, bf16[144,768]{1,0:T(8,128)(2,1)S(1)} %get-tuple-element.33.refs_3_, ...), custom_call_target="tpu_custom_call" | custom-call | flops 503316480 | bytes 2752512 | tf_op jit(solution)/shard_map/pallas_call | solution.py:169
  24.2 1.4 collective-permute-done.4.refs_5_
  25.6 1.5 collective-permute-start.7
  27.1 1.5 collective-permute-start.6
  28.7 5.5 %shard_map.114 = (bf16[128,3200]{1,0:T(8,128)(2,1)}, bf16[128,3328]{1,0:T(8,128)(2,1)S(1)}) custom-call(bf16[128,5120]{1,0:T(8,128)(2,1)} %refs_0_.3, bf16[128,5120]{1,0:T(8,128)(2,1)} %refs_1_.5, f32[1,5120]{1,0:T(1,128)} %bitcast.7, bf16[128,1280]{1,0:T(8,128)(2,1)S(1)} %get-tuple-element.36.refs_3_, bf16[128,1280]{1,0:T(8,128)(2,1)S(1)} %collective-permute-done.3.refs_4_, ...), custom_call_target="tpu_custom_call" | custom-call | flops 838860800 | bytes 4587520 | tf_op jit(solution)/shard_map/pallas_call | solution.py:169
  34.1 0.0 all-gather.2.cloned.1.call-update
  34.2 6.0 %collective-permute-done.7.refs_4_ = bf16[128,1920]{1,0:T(8,128)(2,1)S(1)} collective-permute-done((bf16[128,1920]{1,0:T(8,128)(2,1)S(1)}, bf16[128,1920]{1,0:T(8,128)(2,1)S(1)}, u32[]{:S(2)}, u32[]{:S(2)}) %collective-permute-start.7) | collective-permute-done | bytes 491552 | tf_op jit(solution)/shard_map/ppermute | solution.py:362
  40.2 0.8 copy-done.5
  41.0 2.2 %collective-permute-start.9 = (bf16[128,3328]{1,0:T(8,128)(2,1)S(1)}, bf16[128,3328]{1,0:T(8,128)(2,1)S(1)}, u32[]{:S(2)}, u32[]{:S(2)}) collective-permute-start(bf16[128,3328]{1,0:T(8,128)(2,1)S(1)} %get-tuple-element.43.refs_1_), channel_id=1, source_target_pairs={{0,8},{4,12},{8,24},{12,28},{16,0},{20,4},{24,16},{28,20},{1,9},{5... | collective-permute-start | bytes 2555912 | tf_op jit(solution)/shard_map/ppermute | solution.py:362
  43.2 1.5 collective-permute-start.8
  44.7 0.1 select_reduce_fusion
  44.8 17.6 %collective-permute-done.9.refs_5_ = bf16[128,3328]{1,0:T(8,128)(2,1)S(1)} collective-permute-done((bf16[128,3328]{1,0:T(8,128)(2,1)S(1)}, bf16[128,3328]{1,0:T(8,128)(2,1)S(1)}, u32[]{:S(2)}, u32[]{:S(2)}) %collective-permute-start.9) | collective-permute-done | bytes 852000 | tf_op jit(solution)/shard_map/ppermute | solution.py:362
  62.5 0.7 collective-permute-done.8.refs_3_
  63.2 0.9 copy-done.3
  64.1 2.2 %collective-permute-start.15 = (bf16[128,3328]{1,0:T(8,128)(2,1)S(1)}, bf16[128,3328]{1,0:T(8,128)(2,1)S(1)}, u32[]{:S(2)}, u32[]{:S(2)}) collective-permute-start(bf16[128,3328]{1,0:T(8,128)(2,1)S(1)} %collective-permute-done.9.refs_5_), channel_id=1, source_target_pairs={{0,8},{4,12},{8,24},{12,28},{16,0},{20,4},{24,16},{28,20},{1,9},{5... | collective-permute-start | bytes 2555912 | tf_op jit(solution)/shard_map/ppermute | solution.py:362
  66.3 1.5 collective-permute-start.13
  67.8 1.2 collective-permute-start.14
  69.0 0.5 collective-permute-start.12
  69.5 1.2 copy-done.4
  70.6 1.0 copy-done.6
  71.7 1.0 copy-done.8
  72.7 12.5 %shard_map.115 = (bf16[128,1024]{1,0:T(8,128)(2,1)S(1)}, bf16[128,1024]{1,0:T(8,128)(2,1)S(1)}, bf16[128,1024]{1,0:T(8,128)(2,1)S(1)}) custom-call(bf16[128,1920]{1,0:T(8,128)(2,1)S(1)} %copy-done.8, bf16[128,3328]{1,0:T(8,128)(2,1)S(1)} %get-tuple-element.43.refs_1_, bf16[128,1920]{1,0:T(8,128)(2,1)} %collective-permute-done.6.refs_2_, ...), custom_call_target="tpu_custom_call" | custom-call | flops 8053063680 | bytes 25690112 | tf_op jit(solution)/shard_map/pallas_call | solution.py:223
  85.2 1.6 collective-permute-start.10
  86.8 0.0 collective-permute-done.15.refs_3_
  86.9 1.7 collective-permute-start.11
  88.6 0.8 collective-permute-start.20
  89.3 13.8 %collective-permute-done.14.refs_2_ = bf16[128,1920]{1,0:T(8,128)(2,1)} collective-permute-done((bf16[128,1920]{1,0:T(8,128)(2,1)}, bf16[128,1920]{1,0:T(8,128)(2,1)}, u32[]{:S(2)}, u32[]{:S(2)}) %collective-permute-start.14) | collective-permute-done | bytes 491552 | tf_op jit(solution)/shard_map/ppermute | solution.py:362
  103.2 1.5 collective-permute-start.18
  104.7 1.2 pad_maximum_fusion
  105.9 0.2 broadcast_in_dim.25
  106.1 0.6 collective-permute-start.17
  106.8 0.0 copy-start.9
  106.8 14.5 %collective-permute-done.20.refs_3_ = bf16[128,3328]{1,0:T(8,128)(2,1)S(1)} collective-permute-done((bf16[128,3328]{1,0:T(8,128)(2,1)S(1)}, bf16[128,3328]{1,0:T(8,128)(2,1)S(1)}, u32[]{:S(2)}, u32[]{:S(2)}) %collective-permute-start.20) | collective-permute-done | bytes 852000 | tf_op jit(solution)/shard_map/ppermute | solution.py:362
  121.3 3.7 %collective-permute-done.18.refs_1_ = bf16[128,3328]{1,0:T(8,128)(2,1)S(1)} collective-permute-done((bf16[128,3328]{1,0:T(8,128)(2,1)S(1)}, bf16[128,3328]{1,0:T(8,128)(2,1)S(1)}, u32[]{:S(2)}, u32[]{:S(2)}) %collective-permute-start.18) | collective-permute-done | bytes 852000 | tf_op jit(solution)/shard_map/ppermute | solution.py:362
  125.0 1.5 collective-permute-start.25
  126.6 1.6 copy-done
  128.2 2.7 %shard_map.116 = bf16[16,16,2048]{2,1,0:T(8,128)(2,1)} custom-call(s32[16]{0:T(128)S(1)} %broadcast_add_fusion.page_ref, bf16[512,2048]{1,0:T(8,128)(2,1)S(1)} %copy-done, bf16[16,16,2048]{2,1,0:T(8,128)(2,1)} %cache_ref.1), custom_call_target="tpu_custom_call" | custom-call | bytes 4194304 | tf_op jit(solution)/shard_map/pallas_call | solution.py:308
  130.9 10.4 %shard_map.117 = (bf16[128,1024]{1,0:T(8,128)(2,1)S(1)}, bf16[128,1024]{1,0:T(8,128)(2,1)S(1)}) custom-call(bf16[128,1920]{1,0:T(8,128)(2,1)S(1)} %copy-done.2, bf16[128,3328]{1,0:T(8,128)(2,1)S(1)} %collective-permute-done.13.refs_1_, bf16[128,1920]{1,0:T(8,128)(2,1)} %collective-permute-done.14.refs_2_, ...), custom_call_target="tpu_custom_call" | custom-call | flops 5368709120 | bytes 24117248 | tf_op jit(solution)/shard_map/pallas_call | solution.py:223
  141.2 2.6 %collective-permute-start.16 = (bf16[128,1024]{1,0:T(8,128)(2,1)S(1)}, bf16[128,1024]{1,0:T(8,128)(2,1)S(1)}, u32[]{:S(2)}, u32[]{:S(2)}) collective-permute-start(bf16[128,1024]{1,0:T(8,128)(2,1)S(1)} %get-tuple-element.51), channel_id=1, source_target_pairs={{0,24},{4,28},{8,16},{12,20},{16,8},{20,12},{24,0},{28,4},{1,25},{... | collective-permute-start | bytes 786440 | tf_op jit(solution)/shard_map/ppermute | solution.py:362
  143.9 0.5 collective-permute-start.24
  144.4 10.5 %shard_map.118 = (bf16[128,1024]{1,0:T(8,128)(2,1)S(1)}, bf16[128,1024]{1,0:T(8,128)(2,1)S(1)}) custom-call(bf16[128,1920]{1,0:T(8,128)(2,1)} %collective-permute-done.17.refs_0_, bf16[128,3328]{1,0:T(8,128)(2,1)S(1)} %collective-permute-done.18.refs_1_, bf16[128,1920]{1,0:T(8,128)(2,1)} %collective-permute-done.19.refs_2_, ...), custom_call_target="tpu_custom_call" | custom-call | flops 5368709120 | bytes 24117248 | tf_op jit(solution)/shard_map/pallas_call | solution.py:223
  154.9 2.3 %collective-permute-start.22 = (bf16[128,1024]{1,0:T(8,128)(2,1)S(1)}, bf16[128,1024]{1,0:T(8,128)(2,1)S(1)}, u32[]{:S(2)}, u32[]{:S(2)}) collective-permute-start(bf16[128,1024]{1,0:T(8,128)(2,1)S(1)} %get-tuple-element.57), channel_id=1, source_target_pairs={{0,28},{4,24},{8,20},{12,16},{16,12},{20,8},{24,4},{28,0},{1,29},{... | collective-permute-start | bytes 786440 | tf_op jit(solution)/shard_map/ppermute | solution.py:362
  157.2 2.9 %collective-permute-start.21 = (bf16[128,1024]{1,0:T(8,128)(2,1)S(1)}, bf16[128,1024]{1,0:T(8,128)(2,1)S(1)}, u32[]{:S(2)}, u32[]{:S(2)}) collective-permute-start(bf16[128,1024]{1,0:T(8,128)(2,1)S(1)} %get-tuple-element.56), channel_id=1, source_target_pairs={{0,20},{4,16},{8,4},{12,0},{16,28},{20,24},{24,12},{28,8},{1,21},{... | collective-permute-start | bytes 786440 | tf_op jit(solution)/shard_map/ppermute | solution.py:362
  160.0 0.7 constant_dynamic-update-slice_fusion.4
  160.8 6.7 %shard_map.119 = (f32[128,1024]{1,0:T(8,128)S(1)}, f32[128,1024]{1,0:T(8,128)S(1)}, f32[128,128]{1,0:T(8,128)S(1)}) custom-call(bf16[128,3328]{1,0:T(8,128)(2,1)} %collective-permute-done.25.refs_0_, bf16[5120,1024]{1,0:T(8,128)(2,1)} %refs_1_.7, bf16[5120,1024]{1,0:T(8,128)(2,1)} %refs_2_.3), custom_call_target="tpu_custom_call" | custom-call | flops 1677721600 | bytes 14974976 | tf_op jit(solution)/shard_map/pallas_call | solution.py:278
  167.5 3.3 %collective-permute-done.24.refs_0_ = bf16[128,1920]{1,0:T(8,128)(2,1)S(1)} collective-permute-done((bf16[128,1920]{1,0:T(8,128)(2,1)}, bf16[128,1920]{1,0:T(8,128)(2,1)S(1)}, u32[]{:S(2)}, u32[]{:S(2)}) %collective-permute-start.24) | collective-permute-done | bytes 491552 | tf_op jit(solution)/shard_map/ppermute | solution.py:362
  170.8 4.8 %shard_map.120 = bf16[128,1024]{1,0:T(8,128)(2,1)S(1)} custom-call(bf16[128,1920]{1,0:T(8,128)(2,1)S(1)} %collective-permute-done.24.refs_0_, bf16[5120,1024]{1,0:T(8,128)(2,1)} %refs_1_.7, bf16[5120,1024]{1,0:T(8,128)(2,1)} %refs_2_.3, f32[128,1024]{1,0:T(8,128)S(1)} %get-tuple-element.60.refs_3_, f32[128,1024]{1,0:T(8,128)S(1)} %get-tuple-element.61.refs_4_, ...), custom_call_target="tpu_custom_call" | custom-call | flops 1006632960 | bytes 9404416 | tf_op jit(solution)/shard_map/pallas_call | solution.py:278
  175.6 2.0 %collective-permute-start.26 = (bf16[128,1024]{1,0:T(8,128)(2,1)S(1)}, bf16[128,1024]{1,0:T(8,128)(2,1)S(1)}, u32[]{:S(2)}, u32[]{:S(2)}) collective-permute-start(bf16[128,1024]{1,0:T(8,128)(2,1)S(1)} %shard_map.120), channel_id=1, source_target_pairs={{0,12},{4,8},{8,28},{12,24},{16,4},{20,0},{24,20},{28,16},{1,13},{... | collective-permute-start | bytes 786440 | tf_op jit(solution)/shard_map/ppermute | solution.py:362
  177.7 0.7 constant_dynamic-update-slice_fusion.3
  178.4 0.7 constant_dynamic-update-slice_fusion.2
  179.1 0.7 constant_dynamic-update-slice_fusion.1
  179.8 4.0 %collective-permute-done.26 = bf16[128,1024]{1,0:T(8,128)(2,1)S(1)} collective-permute-done((bf16[128,1024]{1,0:T(8,128)(2,1)S(1)}, bf16[128,1024]{1,0:T(8,128)(2,1)S(1)}, u32[]{:S(2)}, u32[]{:S(2)}) %collective-permute-start.26) | collective-permute-done | bytes 262176 | tf_op jit(solution)/shard_map/ppermute | solution.py:362
  183.8 0.7 constant_dynamic-update-slice_fusion
  (44 shorter events, 0.2 us)
Async XLA Ops:
  7.2 119.4 %all-gather.2.cloned.1.call-start = ((), (), s32[]{:S(2)}) async-start(), calls=%async_computation | async-start | bytes 2621440 | tf_op jit(solution)/shard_map/all_gather | solution.py:396
  8.3 8.4 %collective-permute-start.1 = (bf16[144,768]{1,0:T(8,128)(2,1)S(1)}, bf16[144,768]{1,0:T(8,128)(2,1)S(1)}, u32[]{:S(2)}, u32[]{:S(2)}) collective-permute-start(bf16[144,768]{1,0:T(8,128)(2,1)S(1)} %get-tuple-element.33.refs_3_), channel_id=1, source_target_pairs={{0,2},{1,3},{2,0},{3,1},{4,6},{5,7},{6,4},{7,5},{8,10},{9,11},{10,... | collective-permute-start | bytes 663560 | tf_op jit(solution)/shard_map/ppermute | solution.py:355
  16.7 8.9 %collective-permute-start.4 = (bf16[128,1280]{1,0:T(8,128)(2,1)S(1)}, bf16[128,1280]{1,0:T(8,128)(2,1)S(1)}, u32[]{:S(2)}, u32[]{:S(2)}) collective-permute-start(bf16[128,1280]{1,0:T(8,128)(2,1)S(1)} %get-tuple-element.36.refs_3_), channel_id=1, source_target_pairs={{0,2},{1,3},{2,0},{3,1},{4,6},{5,7},{6,4},{7,5},{8,10},{9,11},{10,... | collective-permute-start | bytes 983048 | tf_op jit(solution)/shard_map/ppermute | solution.py:355
  18.5 1.5 collective-permute-start
  18.5 1.8 collective-permute-start.2
  19.6 9.0 %collective-permute-start.3 = (bf16[128,1280]{1,0:T(8,128)(2,1)S(1)}, bf16[128,1280]{1,0:T(8,128)(2,1)S(1)}, u32[]{:S(2)}, u32[]{:S(2)}) collective-permute-start(bf16[128,1280]{1,0:T(8,128)(2,1)S(1)} %get-tuple-element.36.refs_3_), channel_id=1, source_target_pairs={{0,1},{1,0},{2,3},{3,2},{4,5},{5,4},{6,7},{7,6},{8,9},{9,8},{10,11... | collective-permute-start | bytes 983048 | tf_op jit(solution)/shard_map/ppermute | solution.py:355
  24.2 9.9 %copy-start.7 = (bf16[128,1920]{1,0:T(8,128)(2,1)}, bf16[128,1920]{1,0:T(8,128)(2,1)S(1)}, u32[]{:S(2)}) copy-start(bf16[128,1920]{1,0:T(8,128)(2,1)S(1)} %get-tuple-element.37.refs_0_) | copy-start | bytes 1474564
  25.6 3.0 %collective-permute-start.5 = (bf16[128,1280]{1,0:T(8,128)(2,1)S(1)}, bf16[128,1280]{1,0:T(8,128)(2,1)S(1)}, u32[]{:S(2)}, u32[]{:S(2)}) collective-permute-start(bf16[128,1280]{1,0:T(8,128)(2,1)S(1)} %collective-permute-done.4.refs_5_), channel_id=1, source_target_pairs={{0,1},{1,0},{2,3},{3,2},{4,5},{5,4},{6,7},{7,6},{8,9},{9,8},{10,11... | collective-permute-start | bytes 983048 | tf_op jit(solution)/shard_map/ppermute | solution.py:355
  25.6 14.5 %collective-permute-start.7 = (bf16[128,1920]{1,0:T(8,128)(2,1)S(1)}, bf16[128,1920]{1,0:T(8,128)(2,1)S(1)}, u32[]{:S(2)}, u32[]{:S(2)}) collective-permute-start(bf16[128,1920]{1,0:T(8,128)(2,1)S(1)} %get-tuple-element.37.refs_0_), channel_id=1, source_target_pairs={{0,8},{4,12},{8,24},{12,28},{16,0},{20,4},{24,16},{28,20},{1,9},{5... | collective-permute-start | bytes 1474568 | tf_op jit(solution)/shard_map/ppermute | solution.py:362
  27.1 13.8 %collective-permute-start.6 = (bf16[128,1920]{1,0:T(8,128)(2,1)S(1)}, bf16[128,1920]{1,0:T(8,128)(2,1)}, u32[]{:S(2)}, u32[]{:S(2)}) collective-permute-start(bf16[128,1920]{1,0:T(8,128)(2,1)S(1)} %get-tuple-element.37.refs_0_), channel_id=1, source_target_pairs={{0,4},{4,0},{8,12},{12,8},{16,20},{20,16},{24,28},{28,24},{1,5},{5... | collective-permute-start | bytes 1474568 | tf_op jit(solution)/shard_map/ppermute | solution.py:362
  28.7 16.0 %copy-start.12 = (s32[1,64]{1,0:T(1,128)S(1)}, s32[1,64]{1,0:T(1,128)}, u32[]{:S(2)}) copy-start(s32[1,64]{1,0:T(1,128)} %param.17) | copy-start | bytes 772
  40.2 0.8 copy-start.5
  41.0 21.5 %collective-permute-start.9 = (bf16[128,3328]{1,0:T(8,128)(2,1)S(1)}, bf16[128,3328]{1,0:T(8,128)(2,1)S(1)}, u32[]{:S(2)}, u32[]{:S(2)}) collective-permute-start(bf16[128,3328]{1,0:T(8,128)(2,1)S(1)} %get-tuple-element.43.refs_1_), channel_id=1, source_target_pairs={{0,8},{4,12},{8,24},{12,28},{16,0},{20,4},{24,16},{28,20},{1,9},{5... | collective-permute-start | bytes 2555912 | tf_op jit(solution)/shard_map/ppermute | solution.py:362
  43.2 20.0 %collective-permute-start.8 = (bf16[128,3328]{1,0:T(8,128)(2,1)S(1)}, bf16[128,3328]{1,0:T(8,128)(2,1)S(1)}, u32[]{:S(2)}, u32[]{:S(2)}) collective-permute-start(bf16[128,3328]{1,0:T(8,128)(2,1)S(1)} %get-tuple-element.43.refs_1_), channel_id=1, source_target_pairs={{0,4},{4,0},{8,12},{12,8},{16,20},{20,16},{24,28},{28,24},{1,5},{5... | collective-permute-start | bytes 2555912 | tf_op jit(solution)/shard_map/ppermute | solution.py:362
  63.2 0.9 copy-start.3
  64.1 22.8 %collective-permute-start.15 = (bf16[128,3328]{1,0:T(8,128)(2,1)S(1)}, bf16[128,3328]{1,0:T(8,128)(2,1)S(1)}, u32[]{:S(2)}, u32[]{:S(2)}) collective-permute-start(bf16[128,3328]{1,0:T(8,128)(2,1)S(1)} %collective-permute-done.9.refs_5_), channel_id=1, source_target_pairs={{0,8},{4,12},{8,24},{12,28},{16,0},{20,4},{24,16},{28,20},{1,9},{5... | collective-permute-start | bytes 2555912 | tf_op jit(solution)/shard_map/ppermute | solution.py:362
  66.3 22.3 %collective-permute-start.13 = (bf16[128,3328]{1,0:T(8,128)(2,1)S(1)}, bf16[128,3328]{1,0:T(8,128)(2,1)S(1)}, u32[]{:S(2)}, u32[]{:S(2)}) collective-permute-start(bf16[128,3328]{1,0:T(8,128)(2,1)S(1)} %collective-permute-done.9.refs_5_), channel_id=1, source_target_pairs={{0,4},{4,0},{8,12},{12,8},{16,20},{20,16},{24,28},{28,24},{1,5},{5... | collective-permute-start | bytes 2555912 | tf_op jit(solution)/shard_map/ppermute | solution.py:362
  67.8 35.4 %collective-permute-start.14 = (bf16[128,1920]{1,0:T(8,128)(2,1)}, bf16[128,1920]{1,0:T(8,128)(2,1)}, u32[]{:S(2)}, u32[]{:S(2)}) collective-permute-start(bf16[128,1920]{1,0:T(8,128)(2,1)} %copy-done.5), channel_id=1, source_target_pairs={{0,8},{4,12},{8,24},{12,28},{16,0},{20,4},{24,16},{28,20},{1,9},{5... | collective-permute-start | bytes 1474568 | tf_op jit(solution)/shard_map/ppermute | solution.py:362
  69.0 36.9 %collective-permute-start.12 = (bf16[128,1920]{1,0:T(8,128)(2,1)}, bf16[128,1920]{1,0:T(8,128)(2,1)S(1)}, u32[]{:S(2)}, u32[]{:S(2)}) collective-permute-start(bf16[128,1920]{1,0:T(8,128)(2,1)} %copy-done.5), channel_id=1, source_target_pairs={{0,4},{4,0},{8,12},{12,8},{16,20},{20,16},{24,28},{28,24},{1,5},{5... | collective-permute-start | bytes 1474568 | tf_op jit(solution)/shard_map/ppermute | solution.py:362
  69.5 1.2 copy-start.4
  70.6 1.0 copy-start.6
  71.7 1.0 copy-start.8
  72.7 32.0 %copy-start.10 = (bf16[128,3200]{1,0:T(8,128)(2,1)S(1)}, bf16[128,3200]{1,0:T(8,128)(2,1)}, u32[]{:S(2)}) copy-start(bf16[128,3200]{1,0:T(8,128)(2,1)} %get-tuple-element.41) | copy-start | bytes 2457604
  72.7 32.0 %copy-start.11 = (bf16[128,1920]{1,0:T(8,128)(2,1)S(1)}, bf16[128,1920]{1,0:T(8,128)(2,1)}, u32[]{:S(2)}) copy-start(bf16[128,1920]{1,0:T(8,128)(2,1)} %get-tuple-element.34) | copy-start | bytes 1474564
  85.2 20.9 %collective-permute-start.10 = (bf16[128,1024]{1,0:T(8,128)(2,1)S(1)}, bf16[128,1024]{1,0:T(8,128)(2,1)S(1)}, u32[]{:S(2)}, u32[]{:S(2)}) collective-permute-start(bf16[128,1024]{1,0:T(8,128)(2,1)S(1)} %get-tuple-element.45), channel_id=1, source_target_pairs={{0,4},{4,0},{8,12},{12,8},{16,20},{20,16},{24,28},{28,24},{1,5},{5... | collective-permute-start | bytes 786440 | tf_op jit(solution)/shard_map/ppermute | solution.py:362
  86.9 19.9 %collective-permute-start.11 = (bf16[128,1024]{1,0:T(8,128)(2,1)S(1)}, bf16[128,1024]{1,0:T(8,128)(2,1)S(1)}, u32[]{:S(2)}, u32[]{:S(2)}) collective-permute-start(bf16[128,1024]{1,0:T(8,128)(2,1)S(1)} %get-tuple-element.46), channel_id=1, source_target_pairs={{0,16},{4,20},{8,0},{12,4},{16,24},{20,28},{24,8},{28,12},{1,17},{... | collective-permute-start | bytes 786440 | tf_op jit(solution)/shard_map/ppermute | solution.py:362
  88.6 32.7 %collective-permute-start.20 = (bf16[128,3328]{1,0:T(8,128)(2,1)S(1)}, bf16[128,3328]{1,0:T(8,128)(2,1)S(1)}, u32[]{:S(2)}, u32[]{:S(2)}) collective-permute-start(bf16[128,3328]{1,0:T(8,128)(2,1)S(1)} %collective-permute-done.15.refs_3_), channel_id=1, source_target_pairs={{0,8},{4,12},{8,24},{12,28},{16,0},{20,4},{24,16},{28,20},{1,9},{5... | collective-permute-start | bytes 2555912 | tf_op jit(solution)/shard_map/ppermute | solution.py:362
  103.2 21.9 %collective-permute-start.18 = (bf16[128,3328]{1,0:T(8,128)(2,1)S(1)}, bf16[128,3328]{1,0:T(8,128)(2,1)S(1)}, u32[]{:S(2)}, u32[]{:S(2)}) collective-permute-start(bf16[128,3328]{1,0:T(8,128)(2,1)S(1)} %collective-permute-done.15.refs_3_), channel_id=1, source_target_pairs={{0,4},{4,0},{8,12},{12,8},{16,20},{20,16},{24,28},{28,24},{1,5},{5... | collective-permute-start | bytes 2555912 | tf_op jit(solution)/shard_map/ppermute | solution.py:362
  105.9 19.2 %copy-start.1 = (bf16[128,1920]{1,0:T(8,128)(2,1)}, bf16[128,1920]{1,0:T(8,128)(2,1)S(1)}, u32[]{:S(2)}) copy-start(bf16[128,1920]{1,0:T(8,128)(2,1)S(1)} %collective-permute-done.12.refs_0_) | copy-start | bytes 1474564
  105.9 38.0 %collective-permute-start.19 = (bf16[128,1920]{1,0:T(8,128)(2,1)}, bf16[128,1920]{1,0:T(8,128)(2,1)}, u32[]{:S(2)}, u32[]{:S(2)}) collective-permute-start(bf16[128,1920]{1,0:T(8,128)(2,1)} %collective-permute-done.14.refs_2_), channel_id=1, source_target_pairs={{0,8},{4,12},{8,24},{12,28},{16,0},{20,4},{24,16},{28,20},{1,9},{5... | collective-permute-start | bytes 1474568 | tf_op jit(solution)/shard_map/ppermute | solution.py:362
  106.1 37.7 %collective-permute-start.17 = (bf16[128,1920]{1,0:T(8,128)(2,1)}, bf16[128,1920]{1,0:T(8,128)(2,1)}, u32[]{:S(2)}, u32[]{:S(2)}) collective-permute-start(bf16[128,1920]{1,0:T(8,128)(2,1)} %collective-permute-done.14.refs_2_), channel_id=1, source_target_pairs={{0,4},{4,0},{8,12},{12,8},{16,20},{20,16},{24,28},{28,24},{1,5},{5... | collective-permute-start | bytes 1474568 | tf_op jit(solution)/shard_map/ppermute | solution.py:362
  106.8 18.3 %copy-start.9 = (bf16[128,8192]{1,0:T(8,128)(2,1)}, bf16[128,8192]{1,0:T(8,128)(2,1)S(1)}, u32[]{:S(2)}) copy-start(bf16[128,8192]{1,0:T(8,128)(2,1)S(1)} %constant_dynamic-update-slice_fusion.5) | copy-start | bytes 6291460
  125.0 35.7 %collective-permute-start.25 = (bf16[128,3328]{1,0:T(8,128)(2,1)S(1)}, bf16[128,3328]{1,0:T(8,128)(2,1)}, u32[]{:S(2)}, u32[]{:S(2)}) collective-permute-start(bf16[128,3328]{1,0:T(8,128)(2,1)S(1)} %collective-permute-done.20.refs_3_), channel_id=1, source_target_pairs={{0,4},{4,0},{8,12},{12,8},{16,20},{20,16},{24,28},{28,24},{1,5},{5... | collective-permute-start | bytes 2555912 | tf_op jit(solution)/shard_map/ppermute | solution.py:362
  126.6 1.6 copy-start
  128.2 2.7 %copy-start.2 = (bf16[128,1920]{1,0:T(8,128)(2,1)S(1)}, bf16[128,1920]{1,0:T(8,128)(2,1)}, u32[]{:S(2)}) copy-start(bf16[128,1920]{1,0:T(8,128)(2,1)} %copy-done.1) | copy-start | bytes 1474564
  141.2 15.9 %collective-permute-start.16 = (bf16[128,1024]{1,0:T(8,128)(2,1)S(1)}, bf16[128,1024]{1,0:T(8,128)(2,1)S(1)}, u32[]{:S(2)}, u32[]{:S(2)}) collective-permute-start(bf16[128,1024]{1,0:T(8,128)(2,1)S(1)} %get-tuple-element.51), channel_id=1, source_target_pairs={{0,24},{4,28},{8,16},{12,20},{16,8},{20,12},{24,0},{28,4},{1,25},{... | collective-permute-start | bytes 786440 | tf_op jit(solution)/shard_map/ppermute | solution.py:362
  143.9 26.9 %collective-permute-start.24 = (bf16[128,1920]{1,0:T(8,128)(2,1)}, bf16[128,1920]{1,0:T(8,128)(2,1)S(1)}, u32[]{:S(2)}, u32[]{:S(2)}) collective-permute-start(bf16[128,1920]{1,0:T(8,128)(2,1)} %collective-permute-done.19.refs_2_), channel_id=1, source_target_pairs={{0,4},{4,0},{8,12},{12,8},{16,20},{20,16},{24,28},{28,24},{1,5},{5... | collective-permute-start | bytes 1474568 | tf_op jit(solution)/shard_map/ppermute | solution.py:362
  154.9 23.5 %collective-permute-start.22 = (bf16[128,1024]{1,0:T(8,128)(2,1)S(1)}, bf16[128,1024]{1,0:T(8,128)(2,1)S(1)}, u32[]{:S(2)}, u32[]{:S(2)}) collective-permute-start(bf16[128,1024]{1,0:T(8,128)(2,1)S(1)} %get-tuple-element.57), channel_id=1, source_target_pairs={{0,28},{4,24},{8,20},{12,16},{16,12},{20,8},{24,4},{28,0},{1,29},{... | collective-permute-start | bytes 786440 | tf_op jit(solution)/shard_map/ppermute | solution.py:362
  157.2 21.9 %collective-permute-start.23 = (bf16[128,1024]{1,0:T(8,128)(2,1)S(1)}, bf16[128,1024]{1,0:T(8,128)(2,1)S(1)}, u32[]{:S(2)}, u32[]{:S(2)}) collective-permute-start(bf16[128,1024]{1,0:T(8,128)(2,1)S(1)} %get-tuple-element.55), channel_id=1, source_target_pairs={{0,8},{4,12},{8,24},{12,28},{16,0},{20,4},{24,16},{28,20},{1,9},{5... | collective-permute-start | bytes 786440 | tf_op jit(solution)/shard_map/ppermute | solution.py:362
  157.2 20.5 %collective-permute-start.21 = (bf16[128,1024]{1,0:T(8,128)(2,1)S(1)}, bf16[128,1024]{1,0:T(8,128)(2,1)S(1)}, u32[]{:S(2)}, u32[]{:S(2)}) collective-permute-start(bf16[128,1024]{1,0:T(8,128)(2,1)S(1)} %get-tuple-element.56), channel_id=1, source_target_pairs={{0,20},{4,16},{8,4},{12,0},{16,28},{20,24},{24,12},{28,8},{1,21},{... | collective-permute-start | bytes 786440 | tf_op jit(solution)/shard_map/ppermute | solution.py:362
  175.6 8.2 %collective-permute-start.26 = (bf16[128,1024]{1,0:T(8,128)(2,1)S(1)}, bf16[128,1024]{1,0:T(8,128)(2,1)S(1)}, u32[]{:S(2)}, u32[]{:S(2)}) collective-permute-start(bf16[128,1024]{1,0:T(8,128)(2,1)S(1)} %shard_map.120), channel_id=1, source_target_pairs={{0,12},{4,8},{8,28},{12,24},{16,4},{20,0},{24,20},{28,16},{1,13},{... | collective-permute-start | bytes 786440 | tf_op jit(solution)/shard_map/ppermute | solution.py:362
Sparse Core Ops, SparseCore 0:
  34.3 22.3 all-gather.1

commit v12 on v11

--- a/solution.py
+++ b/solution.py
@@ -13,7 +13,7 @@
 HEAD_SIZE = 128
 PAGE_TOKENS = 16
 GROUP_SPLIT = QUERY_HEADS // KEY_VALUE_HEADS
-HEAD_CHUNKS = (3, 5)
+HEAD_CHUNKS = (2, 6)
 SEG_ROWS = 16
 SCALE_COLUMNS = 128
 MASK_FILLER = -1e30

time: 192 us -> 193 us (level)
  local copies, waits for them, and re-layouts: 10.5 us -> 14.3 us
    unnamed x26 -> x34, local copies, waits for them, and re-layouts: 6.53 us -> 10.4 us
  transfers between devices with their start and end apart: 28 -> 28, of which waited for: 12 -> 15; matrix products, arithmetic and copies ran while one was open for 3% -> 3% of each run, Pallas kernels for 30% -> 30%
where the time goes in v12:
time: 193 us
  waiting for transfers between devices  70 us (36%)
  Pallas kernels  58.1 us (30%)
  starting transfers between devices  34.4 us (18%)
  local copies, waits for them, and re-layouts  14.3 us (7%)
  between operations  14.2 us (7%)
  other arithmetic  1.97 us (1%)
    ppermute x21, waiting for transfers between devices, send(): return lax.ppermute(array, 'grp', pairs)  62 us
    pallas_call x3, Pallas kernels, gated(): pl.pallas_call(functools.partial(gated_kernel, count, len(shards[0])), gr...  33.5 us
    ppermute x21, starting transfers between devices, send(): return lax.ppermute(array, 'grp', pairs)  29.1 us
    pallas_call x2, Pallas kernels, gated_part(): pl.pallas_call(functools.partial(part_kernel, width, bool(so_far)), grid=...  11.5 us
    unnamed x34, local copies, waits for them, and re-layouts  10.4 us
    pallas_call x2, Pallas kernels, attend(): pl.pallas_call(functools.partial(attend_kernel, chunk, shard_count, width...  9.35 us
    ppermute x6, waiting for transfers between devices, swap(): return lax.ppermute(array, 'tok', [(t, t ^ mask) for t in range(tok_count)])  7.97 us
    ppermute x6, starting transfers between devices, swap(): return lax.ppermute(array, 'tok', [(t, t ^ mask) for t in range(tok_count)])  5.26 us
  transfers between devices with their start and end apart: 28, of which 15 were waited for; matrix products, arithmetic and copies ran while one was open for 3% of the time, Pallas kernels for 30%

profile of v12, /device:TPU:0, one launch (start us, length us, event | category | flops | bytes accessed | tf_op | source)
XLA Modules:
  0.0 192.9 jit_solution(6932920599411376490)
XLA Ops:
  7.2 1.1 shard_map.112
  8.3 3.0 %collective-permute-start.1 = (bf16[144,512]{1,0:T(8,128)(2,1)S(1)}, bf16[144,512]{1,0:T(8,128)(2,1)S(1)}, u32[]{:S(2)}, u32[]{:S(2)}) collective-permute-start(bf16[144,512]{1,0:T(8,128)(2,1)S(1)} %get-tuple-element.33.refs_3_), channel_id=1, source_target_pairs={{0,2},{1,3},{2,0},{3,1},{4,6},{5,7},{6,4},{7,5},{8,10},{9,11},{10,... | collective-permute-start | bytes 442376 | tf_op jit(solution)/shard_map/ppermute | solution.py:355
  11.3 3.8 %collective-permute-done.1.refs_5_ = bf16[144,512]{1,0:T(8,128)(2,1)S(1)} collective-permute-done((bf16[144,512]{1,0:T(8,128)(2,1)S(1)}, bf16[144,512]{1,0:T(8,128)(2,1)S(1)}, u32[]{:S(2)}, u32[]{:S(2)}) %collective-permute-start.1) | collective-permute-done | bytes 147488 | tf_op jit(solution)/shard_map/ppermute | solution.py:355
  15.1 1.7 collective-permute-start.4
  16.9 0.5 collective-permute-start.2
  17.4 0.7 convert_bitcast_fusion
  18.1 0.2 collective-permute-done.refs_4_
  18.3 0.2 collective-permute-done.2.refs_6_
  18.5 3.2 %shard_map.113 = (bf16[128,1280]{1,0:T(8,128)(2,1)}, bf16[128,1280]{1,0:T(8,128)(2,1)S(1)}, f32[128,128]{1,0:T(8,128)S(1)}, f32[128,512]{1,0:T(8,128)S(1)}) custom-call(bf16[128,5120]{1,0:T(8,128)(2,1)} %refs_0_.3, bf16[128,5120]{1,0:T(8,128)(2,1)} %refs_1_.5, f32[1,5120]{1,0:T(1,128)} %bitcast.6, bf16[144,512]{1,0:T(8,128)(2,1)S(1)} %get-tuple-element.33.refs_3_, ...), custom_call_target="tpu_custom_call" | custom-call | flops 335544320 | bytes 1835008 | tf_op jit(solution)/shard_map/pallas_call | solution.py:169
  21.7 3.7 %collective-permute-done.4.refs_5_ = bf16[128,1536]{1,0:T(8,128)(2,1)S(1)} collective-permute-done((bf16[128,1536]{1,0:T(8,128)(2,1)S(1)}, bf16[128,1536]{1,0:T(8,128)(2,1)S(1)}, u32[]{:S(2)}, u32[]{:S(2)}) %collective-permute-start.4) | collective-permute-done | bytes 393248 | tf_op jit(solution)/shard_map/ppermute | solution.py:355
  25.5 1.5 collective-permute-start.7
  27.0 1.5 collective-permute-start.6
  28.5 6.2 %shard_map.114 = (bf16[128,3840]{1,0:T(8,128)(2,1)}, bf16[128,3968]{1,0:T(8,128)(2,1)S(1)}) custom-call(bf16[128,5120]{1,0:T(8,128)(2,1)} %refs_0_.3, bf16[128,5120]{1,0:T(8,128)(2,1)} %refs_1_.5, f32[1,5120]{1,0:T(1,128)} %bitcast.7, bf16[128,1536]{1,0:T(8,128)(2,1)S(1)} %get-tuple-element.36.refs_3_, bf16[128,1536]{1,0:T(8,128)(2,1)S(1)} %collective-permute-done.3.refs_4_, ...), custom_call_target="tpu_custom_call" | custom-call | flops 1006632960 | bytes 5505024 | tf_op jit(solution)/shard_map/pallas_call | solution.py:169
  34.7 1.9 collective-permute-done.7.refs_4_
  36.6 0.2 collective-permute-done.6.refs_2_
  36.8 0.7 copy-done.11
  37.5 2.6 %collective-permute-start.9 = (bf16[128,3968]{1,0:T(8,128)(2,1)S(1)}, bf16[128,3968]{1,0:T(8,128)(2,1)S(1)}, u32[]{:S(2)}, u32[]{:S(2)}) collective-permute-start(bf16[128,3968]{1,0:T(8,128)(2,1)S(1)} %get-tuple-element.43.refs_1_), channel_id=1, source_target_pairs={{0,8},{4,12},{8,24},{12,28},{16,0},{20,4},{24,16},{28,20},{1,9},{5... | collective-permute-start | bytes 3047432 | tf_op jit(solution)/shard_map/ppermute | solution.py:362
  40.1 1.5 collective-permute-start.8
  41.6 1.0 copy-done.5
  42.6 19.7 %collective-permute-done.9.refs_5_ = bf16[128,3968]{1,0:T(8,128)(2,1)S(1)} collective-permute-done((bf16[128,3968]{1,0:T(8,128)(2,1)S(1)}, bf16[128,3968]{1,0:T(8,128)(2,1)S(1)}, u32[]{:S(2)}, u32[]{:S(2)}) %collective-permute-start.9) | collective-permute-done | bytes 1015840 | tf_op jit(solution)/shard_map/ppermute | solution.py:362
  62.3 1.4 collective-permute-done.8.refs_3_
  63.7 1.6 collective-permute-start.15
  65.3 1.5 collective-permute-start.13
  66.8 1.0 copy-done.7
  67.9 1.1 collective-permute-start.14
  69.1 0.5 collective-permute-start.12
  69.6 20.4 %collective-permute-done.15.refs_3_ = bf16[128,3968]{1,0:T(8,128)(2,1)S(1)} collective-permute-done((bf16[128,3968]{1,0:T(8,128)(2,1)S(1)}, bf16[128,3968]{1,0:T(8,128)(2,1)S(1)}, u32[]{:S(2)}, u32[]{:S(2)}) %collective-permute-start.15) | collective-permute-done | bytes 1015840 | tf_op jit(solution)/shard_map/ppermute | solution.py:362
  90.0 0.7 collective-permute-done.13.refs_1_
  90.7 1.1 collective-permute-start.20
  91.8 1.5 collective-permute-start.18
  93.3 1.2 copy-done.6
  94.5 1.2 copy-done.8
  95.7 1.0 copy-done.10
  96.7 1.0 copy-done.12
  97.7 12.8 %shard_map.115 = (bf16[128,1024]{1,0:T(8,128)(2,1)S(1)}, bf16[128,1024]{1,0:T(8,128)(2,1)S(1)}, bf16[128,1024]{1,0:T(8,128)(2,1)S(1)}) custom-call(bf16[128,1280]{1,0:T(8,128)(2,1)S(1)} %copy-done.10, bf16[128,3968]{1,0:T(8,128)(2,1)S(1)} %copy-done.6, bf16[128,1280]{1,0:T(8,128)(2,1)S(1)} %copy-done.12, bf16[128,3968]{1,0:T(8,128)(2,1)} %collective-permute-done.8.refs_3_, ...), custom_call_target="tpu_custom_call" | custom-call | flops 8053063680 | bytes 25690112 | tf_op jit(solution)/shard_map/pallas_call | solution.py:223
  110.5 0.6 collective-permute-start.10
  111.1 1.9 collective-permute-start.11
  112.9 1.2 pad_maximum_fusion
  114.3 0.2 broadcast_in_dim.25
  114.5 7.8 %collective-permute-done.10 = bf16[128,1024]{1,0:T(8,128)(2,1)S(1)} collective-permute-done((bf16[128,1024]{1,0:T(8,128)(2,1)S(1)}, bf16[128,1024]{1,0:T(8,128)(2,1)S(1)}, u32[]{:S(2)}, u32[]{:S(2)}) %collective-permute-start.10) | collective-permute-done | bytes 262176 | tf_op jit(solution)/shard_map/ppermute | solution.py:362
  122.4 1.5 collective-permute-start.17
  124.0 0.5 collective-permute-done.20.refs_3_
  124.5 0.8 copy-done.13
  125.3 1.0 copy-done.1
  126.2 1.2 collective-permute-start.25
  127.4 1.6 copy-done
  129.0 2.7 %shard_map.116 = bf16[16,16,2048]{2,1,0:T(8,128)(2,1)} custom-call(s32[16]{0:T(128)S(1)} %broadcast_add_fusion.page_ref, bf16[512,2048]{1,0:T(8,128)(2,1)S(1)} %copy-done, bf16[16,16,2048]{2,1,0:T(8,128)(2,1)} %cache_ref.1), custom_call_target="tpu_custom_call" | custom-call | bytes 4194304 | tf_op jit(solution)/shard_map/pallas_call | solution.py:308
  131.7 10.4 %shard_map.117 = (bf16[128,1024]{1,0:T(8,128)(2,1)S(1)}, bf16[128,1024]{1,0:T(8,128)(2,1)S(1)}) custom-call(bf16[128,1280]{1,0:T(8,128)(2,1)S(1)} %copy-done.4, bf16[128,3968]{1,0:T(8,128)(2,1)S(1)} %collective-permute-done.13.refs_1_, bf16[128,1280]{1,0:T(8,128)(2,1)S(1)} %collective-permute-done.14.refs_2_, ...), custom_call_target="tpu_custom_call" | custom-call | flops 5368709120 | bytes 24117248 | tf_op jit(solution)/shard_map/pallas_call | solution.py:223
  142.0 3.4 %collective-permute-start.16 = (bf16[128,1024]{1,0:T(8,128)(2,1)S(1)}, bf16[128,1024]{1,0:T(8,128)(2,1)S(1)}, u32[]{:S(2)}, u32[]{:S(2)}) collective-permute-start(bf16[128,1024]{1,0:T(8,128)(2,1)S(1)} %get-tuple-element.51), channel_id=1, source_target_pairs={{0,24},{4,28},{8,16},{12,20},{16,8},{20,12},{24,0},{28,4},{1,25},{... | collective-permute-start | bytes 786440 | tf_op jit(solution)/shard_map/ppermute | solution.py:362
  145.4 0.5 collective-permute-start.24
  145.9 10.4 %shard_map.118 = (bf16[128,1024]{1,0:T(8,128)(2,1)S(1)}, bf16[128,1024]{1,0:T(8,128)(2,1)S(1)}) custom-call(bf16[128,1280]{1,0:T(8,128)(2,1)} %collective-permute-done.17.refs_0_, bf16[128,3968]{1,0:T(8,128)(2,1)S(1)} %copy-done.2, bf16[128,1280]{1,0:T(8,128)(2,1)} %collective-permute-done.19.refs_2_, bf16[128,3968]{1,0:T(8,128)(2,1)S(1)} %collective-permute-done.20.refs_3_, ...), custom_call_target="tpu_custom_call" | custom-call | flops 5368709120 | bytes 24117248 | tf_op jit(solution)/shard_map/pallas_call | solution.py:223
  156.3 1.6 collective-permute-start.22
  157.9 3.2 %collective-permute-start.21 = (bf16[128,1024]{1,0:T(8,128)(2,1)S(1)}, bf16[128,1024]{1,0:T(8,128)(2,1)S(1)}, u32[]{:S(2)}, u32[]{:S(2)}) collective-permute-start(bf16[128,1024]{1,0:T(8,128)(2,1)S(1)} %get-tuple-element.56), channel_id=1, source_target_pairs={{0,20},{4,16},{8,4},{12,0},{16,28},{20,24},{24,12},{28,8},{1,21},{... | collective-permute-start | bytes 786440 | tf_op jit(solution)/shard_map/ppermute | solution.py:362
  161.1 0.7 constant_dynamic-update-slice_fusion.4
  161.8 7.5 %shard_map.119 = (f32[128,1024]{1,0:T(8,128)S(1)}, f32[128,1024]{1,0:T(8,128)S(1)}, f32[128,128]{1,0:T(8,128)S(1)}) custom-call(bf16[128,3968]{1,0:T(8,128)(2,1)} %collective-permute-done.25.refs_0_, bf16[5120,1024]{1,0:T(8,128)(2,1)} %refs_1_.7, bf16[5120,1024]{1,0:T(8,128)(2,1)} %refs_2_.3), custom_call_target="tpu_custom_call" | custom-call | flops 2013265920 | bytes 17760256 | tf_op jit(solution)/shard_map/pallas_call | solution.py:278
  169.4 4.0 %shard_map.120 = bf16[128,1024]{1,0:T(8,128)(2,1)S(1)} custom-call(bf16[128,1280]{1,0:T(8,128)(2,1)S(1)} %collective-permute-done.24.refs_0_, bf16[5120,1024]{1,0:T(8,128)(2,1)} %refs_1_.7, bf16[5120,1024]{1,0:T(8,128)(2,1)} %refs_2_.3, f32[128,1024]{1,0:T(8,128)S(1)} %get-tuple-element.60.refs_3_, f32[128,1024]{1,0:T(8,128)S(1)} %get-tuple-element.61.refs_4_, ...), custom_call_target="tpu_custom_call" | custom-call | flops 671088640 | bytes 6619136 | tf_op jit(solution)/shard_map/pallas_call | solution.py:278
  173.3 0.6 collective-permute-start.26
  174.0 1.6 collective-permute-done.21
  175.5 0.7 constant_dynamic-update-slice_fusion.3
  176.3 0.7 constant_dynamic-update-slice_fusion.2
  177.0 4.6 %collective-permute-done.23 = bf16[128,1024]{1,0:T(8,128)(2,1)S(1)} collective-permute-done((bf16[128,1024]{1,0:T(8,128)(2,1)S(1)}, bf16[128,1024]{1,0:T(8,128)(2,1)S(1)}, u32[]{:S(2)}, u32[]{:S(2)}) %collective-permute-start.23) | collective-permute-done | bytes 262176 | tf_op jit(solution)/shard_map/ppermute | solution.py:362
  181.5 0.7 constant_dynamic-update-slice_fusion.1
  182.3 3.1 %collective-permute-done.26 = bf16[128,1024]{1,0:T(8,128)(2,1)S(1)} collective-permute-done((bf16[128,1024]{1,0:T(8,128)(2,1)S(1)}, bf16[128,1024]{1,0:T(8,128)(2,1)S(1)}, u32[]{:S(2)}, u32[]{:S(2)}) %collective-permute-start.26) | collective-permute-done | bytes 262176 | tf_op jit(solution)/shard_map/ppermute | solution.py:362
  185.3 0.7 constant_dynamic-update-slice_fusion
  (52 shorter events, 0.6 us)
Async XLA Ops:
  7.2 120.3 %all-gather.2.cloned.1.call-start = ((), (), s32[]{:S(2)}) async-start(), calls=%async_computation | async-start | bytes 2621440 | tf_op jit(solution)/shard_map/all_gather | solution.py:396
  8.3 6.9 %collective-permute-start.1 = (bf16[144,512]{1,0:T(8,128)(2,1)S(1)}, bf16[144,512]{1,0:T(8,128)(2,1)S(1)}, u32[]{:S(2)}, u32[]{:S(2)}) collective-permute-start(bf16[144,512]{1,0:T(8,128)(2,1)S(1)} %get-tuple-element.33.refs_3_), channel_id=1, source_target_pairs={{0,2},{1,3},{2,0},{3,1},{4,6},{5,7},{6,4},{7,5},{8,10},{9,11},{10,... | collective-permute-start | bytes 442376 | tf_op jit(solution)/shard_map/ppermute | solution.py:355
  15.1 10.3 %collective-permute-start.4 = (bf16[128,1536]{1,0:T(8,128)(2,1)S(1)}, bf16[128,1536]{1,0:T(8,128)(2,1)S(1)}, u32[]{:S(2)}, u32[]{:S(2)}) collective-permute-start(bf16[128,1536]{1,0:T(8,128)(2,1)S(1)} %get-tuple-element.36.refs_3_), channel_id=1, source_target_pairs={{0,2},{1,3},{2,0},{3,1},{4,6},{5,7},{6,4},{7,5},{8,10},{9,11},{10,... | collective-permute-start | bytes 1179656 | tf_op jit(solution)/shard_map/ppermute | solution.py:355
  16.9 1.4 collective-permute-start
  16.9 1.6 collective-permute-start.2
  18.1 10.4 %collective-permute-start.3 = (bf16[128,1536]{1,0:T(8,128)(2,1)S(1)}, bf16[128,1536]{1,0:T(8,128)(2,1)S(1)}, u32[]{:S(2)}, u32[]{:S(2)}) collective-permute-start(bf16[128,1536]{1,0:T(8,128)(2,1)S(1)} %get-tuple-element.36.refs_3_), channel_id=1, source_target_pairs={{0,1},{1,0},{2,3},{3,2},{4,5},{5,4},{6,7},{7,6},{8,9},{9,8},{10,11... | collective-permute-start | bytes 1179656 | tf_op jit(solution)/shard_map/ppermute | solution.py:355
  21.7 12.9 %copy-start.9 = (bf16[128,1280]{1,0:T(8,128)(2,1)}, bf16[128,1280]{1,0:T(8,128)(2,1)S(1)}, u32[]{:S(2)}) copy-start(bf16[128,1280]{1,0:T(8,128)(2,1)S(1)} %get-tuple-element.37.refs_0_) | copy-start | bytes 983044
  25.4 3.0 %collective-permute-start.5 = (bf16[128,1536]{1,0:T(8,128)(2,1)S(1)}, bf16[128,1536]{1,0:T(8,128)(2,1)S(1)}, u32[]{:S(2)}, u32[]{:S(2)}) collective-permute-start(bf16[128,1536]{1,0:T(8,128)(2,1)S(1)} %collective-permute-done.4.refs_5_), channel_id=1, source_target_pairs={{0,1},{1,0},{2,3},{3,2},{4,5},{5,4},{6,7},{7,6},{8,9},{9,8},{10,11... | collective-permute-start | bytes 1179656 | tf_op jit(solution)/shard_map/ppermute | solution.py:355
  25.5 11.1 %collective-permute-start.7 = (bf16[128,1280]{1,0:T(8,128)(2,1)S(1)}, bf16[128,1280]{1,0:T(8,128)(2,1)}, u32[]{:S(2)}, u32[]{:S(2)}) collective-permute-start(bf16[128,1280]{1,0:T(8,128)(2,1)S(1)} %get-tuple-element.37.refs_0_), channel_id=1, source_target_pairs={{0,8},{4,12},{8,24},{12,28},{16,0},{20,4},{24,16},{28,20},{1,9},{5... | collective-permute-start | bytes 983048 | tf_op jit(solution)/shard_map/ppermute | solution.py:362
  27.0 9.8 %collective-permute-start.6 = (bf16[128,1280]{1,0:T(8,128)(2,1)S(1)}, bf16[128,1280]{1,0:T(8,128)(2,1)S(1)}, u32[]{:S(2)}, u32[]{:S(2)}) collective-permute-start(bf16[128,1280]{1,0:T(8,128)(2,1)S(1)} %get-tuple-element.37.refs_0_), channel_id=1, source_target_pairs={{0,4},{4,0},{8,12},{12,8},{16,20},{20,16},{24,28},{28,24},{1,5},{5... | collective-permute-start | bytes 983048 | tf_op jit(solution)/shard_map/ppermute | solution.py:362
  28.5 39.3 %copy-start.16 = (s32[1,64]{1,0:T(1,128)S(1)}, s32[1,64]{1,0:T(1,128)}, u32[]{:S(2)}) copy-start(s32[1,64]{1,0:T(1,128)} %param.17) | copy-start | bytes 772
  36.8 0.7 copy-start.11
  37.5 24.8 %collective-permute-start.9 = (bf16[128,3968]{1,0:T(8,128)(2,1)S(1)}, bf16[128,3968]{1,0:T(8,128)(2,1)S(1)}, u32[]{:S(2)}, u32[]{:S(2)}) collective-permute-start(bf16[128,3968]{1,0:T(8,128)(2,1)S(1)} %get-tuple-element.43.refs_1_), channel_id=1, source_target_pairs={{0,8},{4,12},{8,24},{12,28},{16,0},{20,4},{24,16},{28,20},{1,9},{5... | collective-permute-start | bytes 3047432 | tf_op jit(solution)/shard_map/ppermute | solution.py:362
  40.1 23.6 %collective-permute-start.8 = (bf16[128,3968]{1,0:T(8,128)(2,1)S(1)}, bf16[128,3968]{1,0:T(8,128)(2,1)}, u32[]{:S(2)}, u32[]{:S(2)}) collective-permute-start(bf16[128,3968]{1,0:T(8,128)(2,1)S(1)} %get-tuple-element.43.refs_1_), channel_id=1, source_target_pairs={{0,4},{4,0},{8,12},{12,8},{16,20},{20,16},{24,28},{28,24},{1,5},{5... | collective-permute-start | bytes 3047432 | tf_op jit(solution)/shard_map/ppermute | solution.py:362
  41.6 1.0 copy-start.5
  63.7 26.3 %collective-permute-start.15 = (bf16[128,3968]{1,0:T(8,128)(2,1)S(1)}, bf16[128,3968]{1,0:T(8,128)(2,1)S(1)}, u32[]{:S(2)}, u32[]{:S(2)}) collective-permute-start(bf16[128,3968]{1,0:T(8,128)(2,1)S(1)} %collective-permute-done.9.refs_5_), channel_id=1, source_target_pairs={{0,8},{4,12},{8,24},{12,28},{16,0},{20,4},{24,16},{28,20},{1,9},{5... | collective-permute-start | bytes 3047432 | tf_op jit(solution)/shard_map/ppermute | solution.py:362
  65.3 25.4 %collective-permute-start.13 = (bf16[128,3968]{1,0:T(8,128)(2,1)S(1)}, bf16[128,3968]{1,0:T(8,128)(2,1)S(1)}, u32[]{:S(2)}, u32[]{:S(2)}) collective-permute-start(bf16[128,3968]{1,0:T(8,128)(2,1)S(1)} %collective-permute-done.9.refs_5_), channel_id=1, source_target_pairs={{0,4},{4,0},{8,12},{12,8},{16,20},{20,16},{24,28},{28,24},{1,5},{5... | collective-permute-start | bytes 3047432 | tf_op jit(solution)/shard_map/ppermute | solution.py:362
  66.8 1.0 copy-start.7
  67.9 43.1 %collective-permute-start.14 = (bf16[128,1280]{1,0:T(8,128)(2,1)}, bf16[128,1280]{1,0:T(8,128)(2,1)S(1)}, u32[]{:S(2)}, u32[]{:S(2)}) collective-permute-start(bf16[128,1280]{1,0:T(8,128)(2,1)} %collective-permute-done.7.refs_4_), channel_id=1, source_target_pairs={{0,8},{4,12},{8,24},{12,28},{16,0},{20,4},{24,16},{28,20},{1,9},{5... | collective-permute-start | bytes 983048 | tf_op jit(solution)/shard_map/ppermute | solution.py:362
  69.1 45.0 %collective-permute-start.12 = (bf16[128,1280]{1,0:T(8,128)(2,1)}, bf16[128,1280]{1,0:T(8,128)(2,1)S(1)}, u32[]{:S(2)}, u32[]{:S(2)}) collective-permute-start(bf16[128,1280]{1,0:T(8,128)(2,1)} %collective-permute-done.7.refs_4_), channel_id=1, source_target_pairs={{0,4},{4,0},{8,12},{12,8},{16,20},{20,16},{24,28},{28,24},{1,5},{5... | collective-permute-start | bytes 983048 | tf_op jit(solution)/shard_map/ppermute | solution.py:362
  90.7 33.7 %collective-permute-start.20 = (bf16[128,3968]{1,0:T(8,128)(2,1)S(1)}, bf16[128,3968]{1,0:T(8,128)(2,1)S(1)}, u32[]{:S(2)}, u32[]{:S(2)}) collective-permute-start(bf16[128,3968]{1,0:T(8,128)(2,1)S(1)} %collective-permute-done.15.refs_3_), channel_id=1, source_target_pairs={{0,8},{4,12},{8,24},{12,28},{16,0},{20,4},{24,16},{28,20},{1,9},{5... | collective-permute-start | bytes 3047432 | tf_op jit(solution)/shard_map/ppermute | solution.py:362
  91.8 32.7 %collective-permute-start.18 = (bf16[128,3968]{1,0:T(8,128)(2,1)S(1)}, bf16[128,3968]{1,0:T(8,128)(2,1)S(1)}, u32[]{:S(2)}, u32[]{:S(2)}) collective-permute-start(bf16[128,3968]{1,0:T(8,128)(2,1)S(1)} %collective-permute-done.15.refs_3_), channel_id=1, source_target_pairs={{0,4},{4,0},{8,12},{12,8},{16,20},{20,16},{24,28},{28,24},{1,5},{5... | collective-permute-start | bytes 3047432 | tf_op jit(solution)/shard_map/ppermute | solution.py:362
  93.3 1.2 copy-start.6
  94.5 1.2 copy-start.8
  95.7 1.0 copy-start.10
  96.7 1.0 copy-start.12
  97.7 15.2 %copy-start.14 = (bf16[128,3840]{1,0:T(8,128)(2,1)S(1)}, bf16[128,3840]{1,0:T(8,128)(2,1)}, u32[]{:S(2)}) copy-start(bf16[128,3840]{1,0:T(8,128)(2,1)} %get-tuple-element.41) | copy-start | bytes 2949124
  97.7 15.2 %copy-start.15 = (bf16[128,1280]{1,0:T(8,128)(2,1)S(1)}, bf16[128,1280]{1,0:T(8,128)(2,1)}, u32[]{:S(2)}) copy-start(bf16[128,1280]{1,0:T(8,128)(2,1)} %get-tuple-element.34) | copy-start | bytes 983044
  110.5 11.9 %collective-permute-start.10 = (bf16[128,1024]{1,0:T(8,128)(2,1)S(1)}, bf16[128,1024]{1,0:T(8,128)(2,1)S(1)}, u32[]{:S(2)}, u32[]{:S(2)}) collective-permute-start(bf16[128,1024]{1,0:T(8,128)(2,1)S(1)} %get-tuple-element.45), channel_id=1, source_target_pairs={{0,4},{4,0},{8,12},{12,8},{16,20},{20,16},{24,28},{28,24},{1,5},{5... | collective-permute-start | bytes 786440 | tf_op jit(solution)/shard_map/ppermute | solution.py:362
  111.1 12.8 %collective-permute-start.11 = (bf16[128,1024]{1,0:T(8,128)(2,1)S(1)}, bf16[128,1024]{1,0:T(8,128)(2,1)S(1)}, u32[]{:S(2)}, u32[]{:S(2)}) collective-permute-start(bf16[128,1024]{1,0:T(8,128)(2,1)S(1)} %get-tuple-element.46), channel_id=1, source_target_pairs={{0,16},{4,20},{8,0},{12,4},{16,24},{20,28},{24,8},{28,12},{1,17},{... | collective-permute-start | bytes 786440 | tf_op jit(solution)/shard_map/ppermute | solution.py:362
  114.1 10.4 %copy-start.3 = (bf16[128,1280]{1,0:T(8,128)(2,1)}, bf16[128,1280]{1,0:T(8,128)(2,1)S(1)}, u32[]{:S(2)}) copy-start(bf16[128,1280]{1,0:T(8,128)(2,1)S(1)} %collective-permute-done.12.refs_0_) | copy-start | bytes 983044
  114.1 31.3 %collective-permute-start.19 = (bf16[128,1280]{1,0:T(8,128)(2,1)S(1)}, bf16[128,1280]{1,0:T(8,128)(2,1)}, u32[]{:S(2)}, u32[]{:S(2)}) collective-permute-start(bf16[128,1280]{1,0:T(8,128)(2,1)S(1)} %collective-permute-done.14.refs_2_), channel_id=1, source_target_pairs={{0,8},{4,12},{8,24},{12,28},{16,0},{20,4},{24,16},{28,20},{1,9},{5... | collective-permute-start | bytes 983048 | tf_op jit(solution)/shard_map/ppermute | solution.py:362
  122.4 23.0 %collective-permute-start.17 = (bf16[128,1280]{1,0:T(8,128)(2,1)S(1)}, bf16[128,1280]{1,0:T(8,128)(2,1)}, u32[]{:S(2)}, u32[]{:S(2)}) collective-permute-start(bf16[128,1280]{1,0:T(8,128)(2,1)S(1)} %collective-permute-done.14.refs_2_), channel_id=1, source_target_pairs={{0,4},{4,0},{8,12},{12,8},{16,20},{20,16},{24,28},{28,24},{1,5},{5... | collective-permute-start | bytes 983048 | tf_op jit(solution)/shard_map/ppermute | solution.py:362
  123.9 1.3 copy-start.13
  125.3 1.0 copy-start.1
  126.2 35.6 %collective-permute-start.25 = (bf16[128,3968]{1,0:T(8,128)(2,1)S(1)}, bf16[128,3968]{1,0:T(8,128)(2,1)}, u32[]{:S(2)}, u32[]{:S(2)}) collective-permute-start(bf16[128,3968]{1,0:T(8,128)(2,1)S(1)} %collective-permute-done.20.refs_3_), channel_id=1, source_target_pairs={{0,4},{4,0},{8,12},{12,8},{16,20},{20,16},{24,28},{28,24},{1,5},{5... | collective-permute-start | bytes 3047432 | tf_op jit(solution)/shard_map/ppermute | solution.py:362
  127.4 1.6 copy-start
  129.0 2.7 %copy-start.4 = (bf16[128,1280]{1,0:T(8,128)(2,1)S(1)}, bf16[128,1280]{1,0:T(8,128)(2,1)}, u32[]{:S(2)}) copy-start(bf16[128,1280]{1,0:T(8,128)(2,1)} %copy-done.3) | copy-start | bytes 983044
  131.7 14.2 %copy-start.2 = (bf16[128,3968]{1,0:T(8,128)(2,1)S(1)}, bf16[128,3968]{1,0:T(8,128)(2,1)}, u32[]{:S(2)}) copy-start(bf16[128,3968]{1,0:T(8,128)(2,1)} %copy-done.1) | copy-start | bytes 3047428
  142.0 15.8 %collective-permute-start.16 = (bf16[128,1024]{1,0:T(8,128)(2,1)S(1)}, bf16[128,1024]{1,0:T(8,128)(2,1)S(1)}, u32[]{:S(2)}, u32[]{:S(2)}) collective-permute-start(bf16[128,1024]{1,0:T(8,128)(2,1)S(1)} %get-tuple-element.51), channel_id=1, source_target_pairs={{0,24},{4,28},{8,16},{12,20},{16,8},{20,12},{24,0},{28,4},{1,25},{... | collective-permute-start | bytes 786440 | tf_op jit(solution)/shard_map/ppermute | solution.py:362
  145.4 24.0 %collective-permute-start.24 = (bf16[128,1280]{1,0:T(8,128)(2,1)}, bf16[128,1280]{1,0:T(8,128)(2,1)S(1)}, u32[]{:S(2)}, u32[]{:S(2)}) collective-permute-start(bf16[128,1280]{1,0:T(8,128)(2,1)} %collective-permute-done.19.refs_2_), channel_id=1, source_target_pairs={{0,4},{4,0},{8,12},{12,8},{16,20},{20,16},{24,28},{28,24},{1,5},{5... | collective-permute-start | bytes 983048 | tf_op jit(solution)/shard_map/ppermute | solution.py:362
  156.3 19.9 %collective-permute-start.22 = (bf16[128,1024]{1,0:T(8,128)(2,1)S(1)}, bf16[128,1024]{1,0:T(8,128)(2,1)S(1)}, u32[]{:S(2)}, u32[]{:S(2)}) collective-permute-start(bf16[128,1024]{1,0:T(8,128)(2,1)S(1)} %get-tuple-element.57), channel_id=1, source_target_pairs={{0,28},{4,24},{8,20},{12,16},{16,12},{20,8},{24,4},{28,0},{1,29},{... | collective-permute-start | bytes 786440 | tf_op jit(solution)/shard_map/ppermute | solution.py:362
  157.9 23.7 %collective-permute-start.23 = (bf16[128,1024]{1,0:T(8,128)(2,1)S(1)}, bf16[128,1024]{1,0:T(8,128)(2,1)S(1)}, u32[]{:S(2)}, u32[]{:S(2)}) collective-permute-start(bf16[128,1024]{1,0:T(8,128)(2,1)S(1)} %get-tuple-element.55), channel_id=1, source_target_pairs={{0,8},{4,12},{8,24},{12,28},{16,0},{20,4},{24,16},{28,20},{1,9},{5... | collective-permute-start | bytes 786440 | tf_op jit(solution)/shard_map/ppermute | solution.py:362
  157.9 17.6 %collective-permute-start.21 = (bf16[128,1024]{1,0:T(8,128)(2,1)S(1)}, bf16[128,1024]{1,0:T(8,128)(2,1)S(1)}, u32[]{:S(2)}, u32[]{:S(2)}) collective-permute-start(bf16[128,1024]{1,0:T(8,128)(2,1)S(1)} %get-tuple-element.56), channel_id=1, source_target_pairs={{0,20},{4,16},{8,4},{12,0},{16,28},{20,24},{24,12},{28,8},{1,21},{... | collective-permute-start | bytes 786440 | tf_op jit(solution)/shard_map/ppermute | solution.py:362
  173.3 12.0 %collective-permute-start.26 = (bf16[128,1024]{1,0:T(8,128)(2,1)S(1)}, bf16[128,1024]{1,0:T(8,128)(2,1)S(1)}, u32[]{:S(2)}, u32[]{:S(2)}) collective-permute-start(bf16[128,1024]{1,0:T(8,128)(2,1)S(1)} %shard_map.120), channel_id=1, source_target_pairs={{0,12},{4,8},{8,28},{12,24},{16,4},{20,0},{24,20},{28,16},{1,13},{... | collective-permute-start | bytes 786440 | tf_op jit(solution)/shard_map/ppermute | solution.py:362
Sparse Core Ops, SparseCore 0:
  42.7 20.5 all-gather.1

commit v13 on v11

--- a/solution.py
+++ b/solution.py
@@ -417,8 +417,8 @@
             ready = arrived[-1][c]
             number = len(sent)
             behind = sent[0] if number == 1 else sent[number - 2][:1] if number > 1 else []
-            if c == 0 and step > 1:
-                behind = [*behind, products[step - 2]]
+            if step > 1 and (c == 0 or step + 1 < line_count):
+                behind = [*behind, products[step - 1 if c == 0 and step + 1 < line_count else step - 2]]
             if behind:
                 ready = after(ready, *behind)
             pair = [send(ready, 0, True)]

time: 192 us -> 199 us (1.036)
  waiting for transfers between devices: 71.2 us -> 76.8 us
  local copies, waits for them, and re-layouts: 10.5 us -> 12.5 us
    ppermute x21, waiting for transfers between devices: 63.8 us -> 67.7 us  [send(): return lax.ppermute(array, 'grp', pairs)]
    unnamed x26 -> x30, local copies, waits for them, and re-layouts: 6.53 us -> 10.2 us
  transfers between devices with their start and end apart: 28 -> 28, of which waited for: 12 -> 15; matrix products, arithmetic and copies ran while one was open for 3% -> 2% of each run, Pallas kernels for 30% -> 26%
where the time goes in v13:
time: 199 us; the launch traced here: 198 us
  waiting for transfers between devices  76.8 us (39%)
  Pallas kernels  57.2 us (29%)
  starting transfers between devices  35.6 us (18%)
  between operations  14.3 us (7%)
  local copies, waits for them, and re-layouts  12.5 us (6%)
  other arithmetic  1.99 us (1%)
    ppermute x21, waiting for transfers between devices, send(): return lax.ppermute(array, 'grp', pairs)  67.7 us
    pallas_call x3, Pallas kernels, gated(): pl.pallas_call(functools.partial(gated_kernel, count, len(shards[0])), gr...  33.2 us
    ppermute x21, starting transfers between devices, send(): return lax.ppermute(array, 'grp', pairs)  30.3 us
    pallas_call x2, Pallas kernels, gated_part(): pl.pallas_call(functools.partial(part_kernel, width, bool(so_far)), grid=...  11.3 us
    unnamed x30, local copies, waits for them, and re-layouts  10.2 us
    ppermute x6, waiting for transfers between devices, swap(): return lax.ppermute(array, 'tok', [(t, t ^ mask) for t in range(tok_count)])  9.13 us
    pallas_call x2, Pallas kernels, attend(): pl.pallas_call(functools.partial(attend_kernel, chunk, shard_count, width...  9.1 us
    ppermute x6, starting transfers between devices, swap(): return lax.ppermute(array, 'tok', [(t, t ^ mask) for t in range(tok_count)])  5.26 us
  transfers between devices with their start and end apart: 28, of which 15 were waited for; matrix products, arithmetic and copies ran while one was open for 2% of the time, Pallas kernels for 26%

profile of v13, /device:TPU:0, one launch (start us, length us, event | category | flops | bytes accessed | tf_op | source)
XLA Modules:
  0.0 198.3 jit_solution(3634726226021131764)
XLA Ops:
  7.2 1.1 shard_map.112
  8.3 3.0 %collective-permute-start.1 = (bf16[144,768]{1,0:T(8,128)(2,1)S(1)}, bf16[144,768]{1,0:T(8,128)(2,1)S(1)}, u32[]{:S(2)}, u32[]{:S(2)}) collective-permute-start(bf16[144,768]{1,0:T(8,128)(2,1)S(1)} %get-tuple-element.33.refs_3_), channel_id=1, source_target_pairs={{0,2},{1,3},{2,0},{3,1},{4,6},{5,7},{6,4},{7,5},{8,10},{9,11},{10,... | collective-permute-start | bytes 663560 | tf_op jit(solution)/shard_map/ppermute | solution.py:355
  11.3 5.4 %collective-permute-done.1.refs_5_ = bf16[144,768]{1,0:T(8,128)(2,1)S(1)} collective-permute-done((bf16[144,768]{1,0:T(8,128)(2,1)S(1)}, bf16[144,768]{1,0:T(8,128)(2,1)S(1)}, u32[]{:S(2)}, u32[]{:S(2)}) %collective-permute-start.1) | collective-permute-done | bytes 221216 | tf_op jit(solution)/shard_map/ppermute | solution.py:355
  16.7 1.7 collective-permute-start.4
  18.5 0.5 collective-permute-start.2
  19.0 0.7 convert_bitcast_fusion
  19.6 0.3 collective-permute-done.refs_4_
  20.0 0.3 collective-permute-done.2.refs_6_
  20.3 0.1 broadcast_in_dim.24.refs_8_
  20.3 3.8 %shard_map.113 = (bf16[128,1920]{1,0:T(8,128)(2,1)}, bf16[128,1920]{1,0:T(8,128)(2,1)S(1)}, f32[128,128]{1,0:T(8,128)S(1)}, f32[128,512]{1,0:T(8,128)S(1)}) custom-call(bf16[128,5120]{1,0:T(8,128)(2,1)} %refs_0_.3, bf16[128,5120]{1,0:T(8,128)(2,1)} %refs_1_.5, f32[1,5120]{1,0:T(1,128)} %bitcast.6, bf16[144,768]{1,0:T(8,128)(2,1)S(1)} %get-tuple-element.33.refs_3_, ...), custom_call_target="tpu_custom_call" | custom-call | flops 503316480 | bytes 2752512 | tf_op jit(solution)/shard_map/pallas_call | solution.py:169
  24.2 1.5 collective-permute-done.4.refs_5_
  25.6 1.6 collective-permute-done.5.refs_6_
  27.3 5.3 %shard_map.114 = (bf16[128,3200]{1,0:T(8,128)(2,1)}, bf16[128,3328]{1,0:T(8,128)(2,1)S(1)}) custom-call(bf16[128,5120]{1,0:T(8,128)(2,1)} %refs_0_.3, bf16[128,5120]{1,0:T(8,128)(2,1)} %refs_1_.5, f32[1,5120]{1,0:T(1,128)} %bitcast.7, bf16[128,1280]{1,0:T(8,128)(2,1)S(1)} %get-tuple-element.36.refs_3_, bf16[128,1280]{1,0:T(8,128)(2,1)S(1)} %collective-permute-done.3.refs_4_, ...), custom_call_target="tpu_custom_call" | custom-call | flops 838860800 | bytes 4587520 | tf_op jit(solution)/shard_map/pallas_call | solution.py:169
  32.6 1.6 collective-permute-start.7
  34.1 1.5 collective-permute-start.6
  35.6 11.2 %collective-permute-done.7.refs_4_ = bf16[128,1920]{1,0:T(8,128)(2,1)} collective-permute-done((bf16[128,1920]{1,0:T(8,128)(2,1)S(1)}, bf16[128,1920]{1,0:T(8,128)(2,1)}, u32[]{:S(2)}, u32[]{:S(2)}) %collective-permute-start.7) | collective-permute-done | bytes 491552 | tf_op jit(solution)/shard_map/ppermute | solution.py:362
  46.9 0.2 collective-permute-done.6.refs_2_
  47.1 2.6 %collective-permute-start.9 = (bf16[128,3328]{1,0:T(8,128)(2,1)S(1)}, bf16[128,3328]{1,0:T(8,128)(2,1)}, u32[]{:S(2)}, u32[]{:S(2)}) collective-permute-start(bf16[128,3328]{1,0:T(8,128)(2,1)S(1)} %get-tuple-element.43.refs_1_), channel_id=1, source_target_pairs={{0,8},{4,12},{8,24},{12,28},{16,0},{20,4},{24,16},{28,20},{1,9},{5... | collective-permute-start | bytes 2555912 | tf_op jit(solution)/shard_map/ppermute | solution.py:362
  49.7 1.5 collective-permute-start.8
  51.2 0.9 copy-done.3
  52.1 15.9 %collective-permute-done.9.refs_5_ = bf16[128,3328]{1,0:T(8,128)(2,1)} collective-permute-done((bf16[128,3328]{1,0:T(8,128)(2,1)S(1)}, bf16[128,3328]{1,0:T(8,128)(2,1)}, u32[]{:S(2)}, u32[]{:S(2)}) %collective-permute-start.9) | collective-permute-done | bytes 852000 | tf_op jit(solution)/shard_map/ppermute | solution.py:362
  68.1 1.3 collective-permute-done.8.refs_3_
  69.4 0.9 copy-done.5
  70.3 1.5 collective-permute-start.15
  71.8 1.5 collective-permute-start.13
  73.3 1.3 collective-permute-start.14
  74.6 0.5 collective-permute-start.12
  75.1 1.2 copy-done.4
  76.2 1.2 copy-done.6
  77.4 1.0 copy-done.8
  78.4 12.7 %shard_map.115 = (bf16[128,1024]{1,0:T(8,128)(2,1)S(1)}, bf16[128,1024]{1,0:T(8,128)(2,1)S(1)}, bf16[128,1024]{1,0:T(8,128)(2,1)S(1)}) custom-call(bf16[128,1920]{1,0:T(8,128)(2,1)S(1)} %copy-done.8, bf16[128,3328]{1,0:T(8,128)(2,1)S(1)} %copy-done.4, bf16[128,1920]{1,0:T(8,128)(2,1)S(1)} %collective-permute-done.6.refs_2_, bf16[128,3328]{1,0:T(8,128)(2,1)S(1)} %copy-done.6, ...), custom_call_target="tpu_custom_call" | custom-call | flops 8053063680 | bytes 25690112 | tf_op jit(solution)/shard_map/pallas_call | solution.py:223
  91.1 0.7 copy-done.1
  91.8 0.7 copy-done.9
  92.5 0.7 copy-done.10
  93.3 0.6 collective-permute-done.13.refs_1_
  93.9 1.3 collective-permute-start.20
  95.2 0.1 select_reduce_fusion
  95.3 1.7 collective-permute-start.11
  97.0 1.5 collective-permute-start.10
  98.5 1.6 copy-done
  100.1 2.5 %shard_map.116 = bf16[16,16,2048]{2,1,0:T(8,128)(2,1)} custom-call(s32[16]{0:T(128)S(1)} %broadcast_add_fusion.page_ref, bf16[512,2048]{1,0:T(8,128)(2,1)S(1)} %copy-done, bf16[16,16,2048]{2,1,0:T(8,128)(2,1)} %cache_ref.1), custom_call_target="tpu_custom_call" | custom-call | bytes 4194304 | tf_op jit(solution)/shard_map/pallas_call | solution.py:308
  102.5 1.3 collective-permute-done.14.refs_2_
  103.9 1.5 collective-permute-start.18
  105.4 10.3 %shard_map.117 = (bf16[128,1024]{1,0:T(8,128)(2,1)S(1)}, bf16[128,1024]{1,0:T(8,128)(2,1)S(1)}) custom-call(bf16[128,1920]{1,0:T(8,128)(2,1)S(1)} %collective-permute-done.12.refs_0_, bf16[128,3328]{1,0:T(8,128)(2,1)S(1)} %collective-permute-done.13.refs_1_, bf16[128,1920]{1,0:T(8,128)(2,1)S(1)} %collective-permute-done.14.refs_2_, ...), custom_call_target="tpu_custom_call" | custom-call | flops 5368709120 | bytes 24117248 | tf_op jit(solution)/shard_map/pallas_call | solution.py:223
  115.7 0.7 collective-permute-start.19
  116.4 11.3 %collective-permute-done.20.refs_3_ = bf16[128,3328]{1,0:T(8,128)(2,1)S(1)} collective-permute-done((bf16[128,3328]{1,0:T(8,128)(2,1)S(1)}, bf16[128,3328]{1,0:T(8,128)(2,1)S(1)}, u32[]{:S(2)}, u32[]{:S(2)}) %collective-permute-start.20) | collective-permute-done | bytes 852000 | tf_op jit(solution)/shard_map/ppermute | solution.py:362
  127.7 1.5 collective-permute-start.17
  129.2 1.2 pad_maximum_fusion
  130.4 0.2 broadcast_in_dim.25
  130.7 0.6 collective-permute-start.25
  131.3 1.0 constant_dynamic-update-slice_fusion.6
  132.2 1.0 constant_dynamic-update-slice_fusion.5
  133.2 2.1 %collective-permute-start.16 = (bf16[128,1024]{1,0:T(8,128)(2,1)S(1)}, bf16[128,1024]{1,0:T(8,128)(2,1)S(1)}, u32[]{:S(2)}, u32[]{:S(2)}) collective-permute-start(bf16[128,1024]{1,0:T(8,128)(2,1)S(1)} %get-tuple-element.51), channel_id=1, source_target_pairs={{0,24},{4,28},{8,16},{12,20},{16,8},{20,12},{24,0},{28,4},{1,25},{... | collective-permute-start | bytes 786440 | tf_op jit(solution)/shard_map/ppermute | solution.py:362
  135.4 8.3 %collective-permute-done.19.refs_2_ = bf16[128,1920]{1,0:T(8,128)(2,1)S(1)} collective-permute-done((bf16[128,1920]{1,0:T(8,128)(2,1)S(1)}, bf16[128,1920]{1,0:T(8,128)(2,1)S(1)}, u32[]{:S(2)}, u32[]{:S(2)}) %collective-permute-start.19) | collective-permute-done | bytes 491552 | tf_op jit(solution)/shard_map/ppermute | solution.py:362
  143.6 1.5 collective-permute-start.24
  145.2 10.3 %shard_map.118 = (bf16[128,1024]{1,0:T(8,128)(2,1)S(1)}, bf16[128,1024]{1,0:T(8,128)(2,1)S(1)}) custom-call(bf16[128,1920]{1,0:T(8,128)(2,1)S(1)} %collective-permute-done.17.refs_0_, bf16[128,3328]{1,0:T(8,128)(2,1)S(1)} %collective-permute-done.18.refs_1_, bf16[128,1920]{1,0:T(8,128)(2,1)S(1)} %collective-permute-done.19.refs_2_, ...), custom_call_target="tpu_custom_call" | custom-call | flops 5368709120 | bytes 24117248 | tf_op jit(solution)/shard_map/pallas_call | solution.py:223
  155.5 2.9 %collective-permute-start.22 = (bf16[128,1024]{1,0:T(8,128)(2,1)S(1)}, bf16[128,1024]{1,0:T(8,128)(2,1)S(1)}, u32[]{:S(2)}, u32[]{:S(2)}) collective-permute-start(bf16[128,1024]{1,0:T(8,128)(2,1)S(1)} %get-tuple-element.57), channel_id=1, source_target_pairs={{0,28},{4,24},{8,20},{12,16},{16,12},{20,8},{24,4},{28,0},{1,29},{... | collective-permute-start | bytes 786440 | tf_op jit(solution)/shard_map/ppermute | solution.py:362
  158.5 12.0 %collective-permute-done.25.refs_0_ = bf16[128,3328]{1,0:T(8,128)(2,1)S(1)} collective-permute-done((bf16[128,3328]{1,0:T(8,128)(2,1)S(1)}, bf16[128,3328]{1,0:T(8,128)(2,1)S(1)}, u32[]{:S(2)}, u32[]{:S(2)}) %collective-permute-start.25) | collective-permute-done | bytes 852000 | tf_op jit(solution)/shard_map/ppermute | solution.py:362
  170.5 6.5 %shard_map.119 = (f32[128,1024]{1,0:T(8,128)S(1)}, f32[128,1024]{1,0:T(8,128)S(1)}, f32[128,128]{1,0:T(8,128)S(1)}) custom-call(bf16[128,3328]{1,0:T(8,128)(2,1)S(1)} %collective-permute-done.25.refs_0_, bf16[5120,1024]{1,0:T(8,128)(2,1)} %refs_1_.7, bf16[5120,1024]{1,0:T(8,128)(2,1)} %refs_2_.3), custom_call_target="tpu_custom_call" | custom-call | flops 1677721600 | bytes 14974976 | tf_op jit(solution)/shard_map/pallas_call | solution.py:278
  176.9 0.1 collective-permute-start.23
  177.0 4.8 %shard_map.120 = bf16[128,1024]{1,0:T(8,128)(2,1)S(1)} custom-call(bf16[128,1920]{1,0:T(8,128)(2,1)S(1)} %collective-permute-done.24.refs_0_, bf16[5120,1024]{1,0:T(8,128)(2,1)} %refs_1_.7, bf16[5120,1024]{1,0:T(8,128)(2,1)} %refs_2_.3, f32[128,1024]{1,0:T(8,128)S(1)} %get-tuple-element.60.refs_3_, f32[128,1024]{1,0:T(8,128)S(1)} %get-tuple-element.61.refs_4_, ...), custom_call_target="tpu_custom_call" | custom-call | flops 1006632960 | bytes 9404416 | tf_op jit(solution)/shard_map/pallas_call | solution.py:278
  181.8 2.7 %collective-permute-start.26 = (bf16[128,1024]{1,0:T(8,128)(2,1)S(1)}, bf16[128,1024]{1,0:T(8,128)(2,1)S(1)}, u32[]{:S(2)}, u32[]{:S(2)}) collective-permute-start(bf16[128,1024]{1,0:T(8,128)(2,1)S(1)} %shard_map.120), channel_id=1, source_target_pairs={{0,12},{4,8},{8,28},{12,24},{16,4},{20,0},{24,20},{28,16},{1,13},{... | collective-permute-start | bytes 786440 | tf_op jit(solution)/shard_map/ppermute | solution.py:362
  184.7 5.4 %collective-permute-done.26 = bf16[128,1024]{1,0:T(8,128)(2,1)S(1)} collective-permute-done((bf16[128,1024]{1,0:T(8,128)(2,1)S(1)}, bf16[128,1024]{1,0:T(8,128)(2,1)S(1)}, u32[]{:S(2)}, u32[]{:S(2)}) %collective-permute-start.26) | collective-permute-done | bytes 262176 | tf_op jit(solution)/shard_map/ppermute | solution.py:362
  190.1 1.3 copy-done.11
  (48 shorter events, 0.4 us)
Async XLA Ops:
  7.2 91.3 %all-gather.2.cloned.1.call-start = ((), (), s32[]{:S(2)}) async-start(), calls=%async_computation | async-start | bytes 2621440 | tf_op jit(solution)/shard_map/all_gather | solution.py:396
  8.3 8.4 %collective-permute-start.1 = (bf16[144,768]{1,0:T(8,128)(2,1)S(1)}, bf16[144,768]{1,0:T(8,128)(2,1)S(1)}, u32[]{:S(2)}, u32[]{:S(2)}) collective-permute-start(bf16[144,768]{1,0:T(8,128)(2,1)S(1)} %get-tuple-element.33.refs_3_), channel_id=1, source_target_pairs={{0,2},{1,3},{2,0},{3,1},{4,6},{5,7},{6,4},{7,5},{8,10},{9,11},{10,... | collective-permute-start | bytes 663560 | tf_op jit(solution)/shard_map/ppermute | solution.py:355
  16.7 8.9 %collective-permute-start.4 = (bf16[128,1280]{1,0:T(8,128)(2,1)S(1)}, bf16[128,1280]{1,0:T(8,128)(2,1)S(1)}, u32[]{:S(2)}, u32[]{:S(2)}) collective-permute-start(bf16[128,1280]{1,0:T(8,128)(2,1)S(1)} %get-tuple-element.36.refs_3_), channel_id=1, source_target_pairs={{0,2},{1,3},{2,0},{3,1},{4,6},{5,7},{6,4},{7,5},{8,10},{9,11},{10,... | collective-permute-start | bytes 983048 | tf_op jit(solution)/shard_map/ppermute | solution.py:355
  18.5 1.5 collective-permute-start
  18.5 1.8 collective-permute-start.2
  19.6 6.0 %collective-permute-start.3 = (bf16[128,1280]{1,0:T(8,128)(2,1)S(1)}, bf16[128,1280]{1,0:T(8,128)(2,1)S(1)}, u32[]{:S(2)}, u32[]{:S(2)}) collective-permute-start(bf16[128,1280]{1,0:T(8,128)(2,1)S(1)} %get-tuple-element.36.refs_3_), channel_id=1, source_target_pairs={{0,1},{1,0},{2,3},{3,2},{4,5},{5,4},{6,7},{7,6},{8,9},{9,8},{10,11... | collective-permute-start | bytes 983048 | tf_op jit(solution)/shard_map/ppermute | solution.py:355
  24.2 9.9 %copy-start.7 = (bf16[128,1920]{1,0:T(8,128)(2,1)}, bf16[128,1920]{1,0:T(8,128)(2,1)S(1)}, u32[]{:S(2)}) copy-start(bf16[128,1920]{1,0:T(8,128)(2,1)S(1)} %get-tuple-element.37.refs_0_) | copy-start | bytes 1474564
  25.6 1.6 collective-permute-start.5
  27.3 46.0 %copy-start.14 = (s32[1,64]{1,0:T(1,128)S(1)}, s32[1,64]{1,0:T(1,128)}, u32[]{:S(2)}) copy-start(s32[1,64]{1,0:T(1,128)} %param.17) | copy-start | bytes 772
  32.6 14.3 %collective-permute-start.7 = (bf16[128,1920]{1,0:T(8,128)(2,1)S(1)}, bf16[128,1920]{1,0:T(8,128)(2,1)}, u32[]{:S(2)}, u32[]{:S(2)}) collective-permute-start(bf16[128,1920]{1,0:T(8,128)(2,1)S(1)} %get-tuple-element.37.refs_0_), channel_id=1, source_target_pairs={{0,8},{4,12},{8,24},{12,28},{16,0},{20,4},{24,16},{28,20},{1,9},{5... | collective-permute-start | bytes 1474568 | tf_op jit(solution)/shard_map/ppermute | solution.py:362
  34.1 13.0 %collective-permute-start.6 = (bf16[128,1920]{1,0:T(8,128)(2,1)S(1)}, bf16[128,1920]{1,0:T(8,128)(2,1)S(1)}, u32[]{:S(2)}, u32[]{:S(2)}) collective-permute-start(bf16[128,1920]{1,0:T(8,128)(2,1)S(1)} %get-tuple-element.37.refs_0_), channel_id=1, source_target_pairs={{0,4},{4,0},{8,12},{12,8},{16,20},{20,16},{24,28},{28,24},{1,5},{5... | collective-permute-start | bytes 1474568 | tf_op jit(solution)/shard_map/ppermute | solution.py:362
  47.1 21.0 %collective-permute-start.9 = (bf16[128,3328]{1,0:T(8,128)(2,1)S(1)}, bf16[128,3328]{1,0:T(8,128)(2,1)}, u32[]{:S(2)}, u32[]{:S(2)}) collective-permute-start(bf16[128,3328]{1,0:T(8,128)(2,1)S(1)} %get-tuple-element.43.refs_1_), channel_id=1, source_target_pairs={{0,8},{4,12},{8,24},{12,28},{16,0},{20,4},{24,16},{28,20},{1,9},{5... | collective-permute-start | bytes 2555912 | tf_op jit(solution)/shard_map/ppermute | solution.py:362
  49.7 19.7 %collective-permute-start.8 = (bf16[128,3328]{1,0:T(8,128)(2,1)S(1)}, bf16[128,3328]{1,0:T(8,128)(2,1)S(1)}, u32[]{:S(2)}, u32[]{:S(2)}) collective-permute-start(bf16[128,3328]{1,0:T(8,128)(2,1)S(1)} %get-tuple-element.43.refs_1_), channel_id=1, source_target_pairs={{0,4},{4,0},{8,12},{12,8},{16,20},{20,16},{24,28},{28,24},{1,5},{5... | collective-permute-start | bytes 2555912 | tf_op jit(solution)/shard_map/ppermute | solution.py:362
  51.2 0.9 copy-start.3
  69.4 0.9 copy-start.5
  70.3 23.0 %collective-permute-start.15 = (bf16[128,3328]{1,0:T(8,128)(2,1)}, bf16[128,3328]{1,0:T(8,128)(2,1)S(1)}, u32[]{:S(2)}, u32[]{:S(2)}) collective-permute-start(bf16[128,3328]{1,0:T(8,128)(2,1)} %collective-permute-done.9.refs_5_), channel_id=1, source_target_pairs={{0,8},{4,12},{8,24},{12,28},{16,0},{20,4},{24,16},{28,20},{1,9},{5... | collective-permute-start | bytes 2555912 | tf_op jit(solution)/shard_map/ppermute | solution.py:362
  71.8 22.1 %collective-permute-start.13 = (bf16[128,3328]{1,0:T(8,128)(2,1)}, bf16[128,3328]{1,0:T(8,128)(2,1)S(1)}, u32[]{:S(2)}, u32[]{:S(2)}) collective-permute-start(bf16[128,3328]{1,0:T(8,128)(2,1)} %collective-permute-done.9.refs_5_), channel_id=1, source_target_pairs={{0,4},{4,0},{8,12},{12,8},{16,20},{20,16},{24,28},{28,24},{1,5},{5... | collective-permute-start | bytes 2555912 | tf_op jit(solution)/shard_map/ppermute | solution.py:362
  73.3 30.6 %collective-permute-start.14 = (bf16[128,1920]{1,0:T(8,128)(2,1)}, bf16[128,1920]{1,0:T(8,128)(2,1)S(1)}, u32[]{:S(2)}, u32[]{:S(2)}) collective-permute-start(bf16[128,1920]{1,0:T(8,128)(2,1)} %collective-permute-done.7.refs_4_), channel_id=1, source_target_pairs={{0,8},{4,12},{8,24},{12,28},{16,0},{20,4},{24,16},{28,20},{1,9},{5... | collective-permute-start | bytes 1474568 | tf_op jit(solution)/shard_map/ppermute | solution.py:362
  74.6 30.8 %collective-permute-start.12 = (bf16[128,1920]{1,0:T(8,128)(2,1)}, bf16[128,1920]{1,0:T(8,128)(2,1)S(1)}, u32[]{:S(2)}, u32[]{:S(2)}) collective-permute-start(bf16[128,1920]{1,0:T(8,128)(2,1)} %collective-permute-done.7.refs_4_), channel_id=1, source_target_pairs={{0,4},{4,0},{8,12},{12,8},{16,20},{20,16},{24,28},{28,24},{1,5},{5... | collective-permute-start | bytes 1474568 | tf_op jit(solution)/shard_map/ppermute | solution.py:362
  75.1 1.2 copy-start.4
  76.2 1.2 copy-start.6
  77.4 1.0 copy-start.8
  91.1 0.7 copy-start.1
  91.8 0.7 copy-start.9
  92.5 0.7 copy-start.10
  93.9 33.8 %collective-permute-start.20 = (bf16[128,3328]{1,0:T(8,128)(2,1)S(1)}, bf16[128,3328]{1,0:T(8,128)(2,1)S(1)}, u32[]{:S(2)}, u32[]{:S(2)}) collective-permute-start(bf16[128,3328]{1,0:T(8,128)(2,1)S(1)} %collective-permute-done.15.refs_3_), channel_id=1, source_target_pairs={{0,8},{4,12},{8,24},{12,28},{16,0},{20,4},{24,16},{28,20},{1,9},{5... | collective-permute-start | bytes 2555912 | tf_op jit(solution)/shard_map/ppermute | solution.py:362
  95.3 37.0 %collective-permute-start.11 = (bf16[128,1024]{1,0:T(8,128)(2,1)}, bf16[128,1024]{1,0:T(8,128)(2,1)}, u32[]{:S(2)}, u32[]{:S(2)}) collective-permute-start(bf16[128,1024]{1,0:T(8,128)(2,1)} %copy-done.9), channel_id=1, source_target_pairs={{0,16},{4,20},{8,0},{12,4},{16,24},{20,28},{24,8},{28,12},{1,17},{... | collective-permute-start | bytes 786440 | tf_op jit(solution)/shard_map/ppermute | solution.py:362
  97.0 34.3 %collective-permute-start.10 = (bf16[128,1024]{1,0:T(8,128)(2,1)}, bf16[128,1024]{1,0:T(8,128)(2,1)}, u32[]{:S(2)}, u32[]{:S(2)}) collective-permute-start(bf16[128,1024]{1,0:T(8,128)(2,1)} %copy-done.10), channel_id=1, source_target_pairs={{0,4},{4,0},{8,12},{12,8},{16,20},{20,16},{24,28},{28,24},{1,5},{5... | collective-permute-start | bytes 786440 | tf_op jit(solution)/shard_map/ppermute | solution.py:362
  98.5 1.6 copy-start
  102.5 26.7 %copy-start.12 = (bf16[128,3200]{1,0:T(8,128)(2,1)S(1)}, bf16[128,3200]{1,0:T(8,128)(2,1)}, u32[]{:S(2)}) copy-start(bf16[128,3200]{1,0:T(8,128)(2,1)} %get-tuple-element.41) | copy-start | bytes 2457604
  102.5 26.7 %copy-start.13 = (bf16[128,1920]{1,0:T(8,128)(2,1)S(1)}, bf16[128,1920]{1,0:T(8,128)(2,1)}, u32[]{:S(2)}) copy-start(bf16[128,1920]{1,0:T(8,128)(2,1)} %get-tuple-element.34) | copy-start | bytes 1474564
  103.9 26.8 %collective-permute-start.18 = (bf16[128,3328]{1,0:T(8,128)(2,1)S(1)}, bf16[128,3328]{1,0:T(8,128)(2,1)S(1)}, u32[]{:S(2)}, u32[]{:S(2)}) collective-permute-start(bf16[128,3328]{1,0:T(8,128)(2,1)S(1)} %collective-permute-done.15.refs_3_), channel_id=1, source_target_pairs={{0,4},{4,0},{8,12},{12,8},{16,20},{20,16},{24,28},{28,24},{1,5},{5... | collective-permute-start | bytes 2555912 | tf_op jit(solution)/shard_map/ppermute | solution.py:362
  115.7 27.9 %collective-permute-start.19 = (bf16[128,1920]{1,0:T(8,128)(2,1)S(1)}, bf16[128,1920]{1,0:T(8,128)(2,1)S(1)}, u32[]{:S(2)}, u32[]{:S(2)}) collective-permute-start(bf16[128,1920]{1,0:T(8,128)(2,1)S(1)} %collective-permute-done.14.refs_2_), channel_id=1, source_target_pairs={{0,8},{4,12},{8,24},{12,28},{16,0},{20,4},{24,16},{28,20},{1,9},{5... | collective-permute-start | bytes 1474568 | tf_op jit(solution)/shard_map/ppermute | solution.py:362
  127.7 15.9 %collective-permute-start.17 = (bf16[128,1920]{1,0:T(8,128)(2,1)S(1)}, bf16[128,1920]{1,0:T(8,128)(2,1)S(1)}, u32[]{:S(2)}, u32[]{:S(2)}) collective-permute-start(bf16[128,1920]{1,0:T(8,128)(2,1)S(1)} %collective-permute-done.14.refs_2_), channel_id=1, source_target_pairs={{0,4},{4,0},{8,12},{12,8},{16,20},{20,16},{24,28},{28,24},{1,5},{5... | collective-permute-start | bytes 1474568 | tf_op jit(solution)/shard_map/ppermute | solution.py:362
  129.2 1.4 copy-start.2
  130.7 39.8 %collective-permute-start.25 = (bf16[128,3328]{1,0:T(8,128)(2,1)S(1)}, bf16[128,3328]{1,0:T(8,128)(2,1)S(1)}, u32[]{:S(2)}, u32[]{:S(2)}) collective-permute-start(bf16[128,3328]{1,0:T(8,128)(2,1)S(1)} %collective-permute-done.20.refs_3_), channel_id=1, source_target_pairs={{0,4},{4,0},{8,12},{12,8},{16,20},{20,16},{24,28},{28,24},{1,5},{5... | collective-permute-start | bytes 2555912 | tf_op jit(solution)/shard_map/ppermute | solution.py:362
  133.2 22.3 %collective-permute-start.16 = (bf16[128,1024]{1,0:T(8,128)(2,1)S(1)}, bf16[128,1024]{1,0:T(8,128)(2,1)S(1)}, u32[]{:S(2)}, u32[]{:S(2)}) collective-permute-start(bf16[128,1024]{1,0:T(8,128)(2,1)S(1)} %get-tuple-element.51), channel_id=1, source_target_pairs={{0,24},{4,28},{8,16},{12,20},{16,8},{20,12},{24,0},{28,4},{1,25},{... | collective-permute-start | bytes 786440 | tf_op jit(solution)/shard_map/ppermute | solution.py:362
  143.6 33.4 %collective-permute-start.24 = (bf16[128,1920]{1,0:T(8,128)(2,1)S(1)}, bf16[128,1920]{1,0:T(8,128)(2,1)S(1)}, u32[]{:S(2)}, u32[]{:S(2)}) collective-permute-start(bf16[128,1920]{1,0:T(8,128)(2,1)S(1)} %collective-permute-done.19.refs_2_), channel_id=1, source_target_pairs={{0,4},{4,0},{8,12},{12,8},{16,20},{20,16},{24,28},{28,24},{1,5},{5... | collective-permute-start | bytes 1474568 | tf_op jit(solution)/shard_map/ppermute | solution.py:362
  155.4 29.1 %collective-permute-start.21 = (bf16[128,1024]{1,0:T(8,128)(2,1)S(1)}, bf16[128,1024]{1,0:T(8,128)(2,1)S(1)}, u32[]{:S(2)}, u32[]{:S(2)}) collective-permute-start(bf16[128,1024]{1,0:T(8,128)(2,1)S(1)} %get-tuple-element.56), channel_id=1, source_target_pairs={{0,20},{4,16},{8,4},{12,0},{16,28},{20,24},{24,12},{28,8},{1,21},{... | collective-permute-start | bytes 786440 | tf_op jit(solution)/shard_map/ppermute | solution.py:362
  155.5 29.1 %collective-permute-start.22 = (bf16[128,1024]{1,0:T(8,128)(2,1)S(1)}, bf16[128,1024]{1,0:T(8,128)(2,1)S(1)}, u32[]{:S(2)}, u32[]{:S(2)}) collective-permute-start(bf16[128,1024]{1,0:T(8,128)(2,1)S(1)} %get-tuple-element.57), channel_id=1, source_target_pairs={{0,28},{4,24},{8,20},{12,16},{16,12},{20,8},{24,4},{28,0},{1,29},{... | collective-permute-start | bytes 786440 | tf_op jit(solution)/shard_map/ppermute | solution.py:362
  176.9 7.7 %collective-permute-start.23 = (bf16[128,1024]{1,0:T(8,128)(2,1)S(1)}, bf16[128,1024]{1,0:T(8,128)(2,1)S(1)}, u32[]{:S(2)}, u32[]{:S(2)}) collective-permute-start(bf16[128,1024]{1,0:T(8,128)(2,1)S(1)} %get-tuple-element.55), channel_id=1, source_target_pairs={{0,8},{4,12},{8,24},{12,28},{16,0},{20,4},{24,16},{28,20},{1,9},{5... | collective-permute-start | bytes 786440 | tf_op jit(solution)/shard_map/ppermute | solution.py:362
  181.8 8.2 %collective-permute-start.26 = (bf16[128,1024]{1,0:T(8,128)(2,1)S(1)}, bf16[128,1024]{1,0:T(8,128)(2,1)S(1)}, u32[]{:S(2)}, u32[]{:S(2)}) collective-permute-start(bf16[128,1024]{1,0:T(8,128)(2,1)S(1)} %shard_map.120), channel_id=1, source_target_pairs={{0,12},{4,8},{8,28},{12,24},{16,4},{20,0},{24,20},{28,16},{1,13},{... | collective-permute-start | bytes 786440 | tf_op jit(solution)/shard_map/ppermute | solution.py:362
  190.1 1.3 copy-start.11
Sparse Core Ops, SparseCore 0:
  32.7 23.7 all-gather.1
